TPU v7x, 32 devices: a whole 2x2x4 slice. The times are simulated.
32 devices in a mesh: dp: 8 (over y, x, core), blk: 4 (over z).
Axes of the slice: x: 2, y: 2, z: 4, core: 2. Of those that a mesh axis runs over, the one named last changes fastest.
Arguments:
- self_feat: bfloat16 [16384, 256], P(('dp', 'blk')), may hold values from -6 to 6
- nbr_mask: int32 [16384, 8], P(('dp', 'blk')), may hold values 0 or 1
- neighbour_slot: int32 [32, 4096], P(('dp', 'blk')), may hold values from 0 to 4095, each once within a row
- serve_rows: int32 [128, 1024], P(('dp', 'blk')), may hold values from 0 to 8191
- feat_store: bfloat16 [32768, 256], P('blk'), may hold values from -6 to 6
- w_self: bfloat16 [256, 1024], replicated, may hold values from -0.375 to 0.375
- w_nbr: bfloat16 [256, 1024], replicated, may hold values from -0.375 to 0.375
- w_out: bfloat16 [1024, 256], replicated, may hold values from -0.1875 to 0.1875
Outputs:
- grad_self: float32 [256, 1024], replicated
- grad_nbr: float32 [256, 1024], replicated
- grad_out: float32 [1024, 256], replicated
All inputs are finite; a program needn't handle non-finite values. No bound on the sum of `nbr_mask` on one device may be relied on, other than what follows from the above.
Results may differ from a plain program's by a relative error of at most 0.0077.
Values may be sent and summed in bfloat16 or wider, within the bound.
No kernel may reach another device: no remote copies, remote signals or barrier semaphores. Data moves between devices by JAX's collectives and lax.ppermute only.
A program may use at most 64 MiB of HBM per device.

v0:
```python
import jax
import jax.numpy as jnp
from jax import lax
from jax.sharding import PartitionSpec as P

MARGIN = 0.5


def forward_nodes(self_rows, node_mask, neighbours, w_self, w_nbr, w_out):
    first_col = lax.broadcasted_iota(jnp.int32, node_mask.shape, 1) == 0
    valid_slots = jnp.where(first_col, 1, node_mask).astype(jnp.float32)
    live_count = jnp.sum(valid_slots, 1, keepdims=True)
    pooled = (
        jnp.sum(neighbours.astype(jnp.float32) * valid_slots[:, :, None], 1) / live_count
    ).astype(jnp.bfloat16)
    pre_act = jnp.dot(self_rows, w_self, preferred_element_type=jnp.float32) + jnp.dot(
        pooled, w_nbr, preferred_element_type=jnp.float32
    )
    hidden = (pre_act * jax.nn.sigmoid(pre_act)).astype(jnp.bfloat16)
    projected = jnp.dot(hidden, w_out, preferred_element_type=jnp.float32)
    inv_norm = lax.rsqrt(jnp.mean(projected * projected, 1, keepdims=True) + 1e-06)
    embedding = (projected * inv_norm).astype(jnp.bfloat16)
    return (pooled, pre_act, hidden, projected, inv_norm, embedding)


def pair_weights(queries, own_items, cycle_items, position):
    score_scale = queries.shape[1] ** (-0.5)
    scores = jnp.dot(queries, cycle_items.T, preferred_element_type=jnp.float32) * score_scale
    positive_item = (
        jnp.sum(queries.astype(jnp.float32) * own_items.astype(jnp.float32), 1, keepdims=True)
        * score_scale
    )
    weights = jax.nn.sigmoid(scores - positive_item + MARGIN) / scores.shape[1]
    columns = lax.broadcasted_iota(jnp.int32, scores.shape, 1)
    own_column = lax.broadcasted_iota(jnp.int32, scores.shape, 0) + position * queries.shape[0]
    row_total = jnp.sum(weights, 1, keepdims=True)
    tile = jnp.where(columns == own_column, weights - row_total, weights).astype(jnp.bfloat16)
    return (tile, positive_item, row_total)


def backward_nodes(self_rows, pooled, pre_act, hidden, projected, inv_norm, d_embed, w_out):
    contract = (((0,), (0,)), ((), ()))
    interior_term = jnp.mean(d_embed * projected, 1, keepdims=True)
    d_proj = (inv_norm * d_embed - projected * inv_norm**3 * interior_term).astype(jnp.bfloat16)
    g_out = lax.dot_general(hidden, d_proj, contract, preferred_element_type=jnp.float32)
    d_hidden = lax.dot_general(
        d_proj, w_out, (((1,), (1,)), ((), ())), preferred_element_type=jnp.float32
    )
    gate_sig = jax.nn.sigmoid(pre_act)
    d_pre = (d_hidden * gate_sig * (1.0 + pre_act * (1.0 - gate_sig))).astype(jnp.bfloat16)
    g_self = lax.dot_general(self_rows, d_pre, contract, preferred_element_type=jnp.float32)
    g_nbr = lax.dot_general(pooled, d_pre, contract, preferred_element_type=jnp.float32)
    return (g_self, g_nbr, g_out)


def on_device(self_feat, nbr_mask, neighbour_slot, serve_rows, feat_store, w_self, w_nbr, w_out):
    node_total = self_feat.shape[0]
    pair_total = node_total // 2
    fanout_cols = nbr_mask.shape[1]
    feat_width = feat_store.shape[1]
    outgoing = feat_store[serve_rows]
    received_rows = lax.all_to_all(outgoing, "blk", split_axis=0, concat_axis=0, tiled=True)
    neighbours = received_rows.reshape(-1, feat_width)[neighbour_slot[0]].reshape(
        node_total, fanout_cols, feat_width
    )
    pooled, pre_act, hidden, projected, inv_norm, embedding = forward_nodes(
        self_feat, nbr_mask, neighbours, w_self, w_nbr, w_out
    )
    queries = embedding[:pair_total]
    own_items = embedding[pair_total:]
    cycle_items = lax.all_gather(own_items, "blk", axis=0, tiled=True)
    position = lax.axis_index("blk")
    weight_tile, positive_item, row_total = pair_weights(queries, own_items, cycle_items, position)
    score_scale = queries.shape[1] ** (-0.5)
    d_query = jnp.dot(weight_tile, cycle_items, preferred_element_type=jnp.float32) * score_scale
    contract = (((0,), (0,)), ((), ()))
    d_items = lax.psum_scatter(
        lax.dot_general(weight_tile, queries, contract, preferred_element_type=jnp.float32)
        * score_scale,
        "blk",
        scatter_dimension=0,
        tiled=True,
    )
    d_embed = jnp.concatenate([d_query, d_items], 0)
    grads = backward_nodes(self_feat, pooled, pre_act, hidden, projected, inv_norm, d_embed, w_out)
    grad_self, grad_nbr, grad_out = lax.psum((grads[0], grads[1], grads[2]), ("dp", "blk"))
    return (grad_self, grad_nbr, grad_out)


def solution(mesh):
    in_specs = (
        P(("dp", "blk"), None),
        P(("dp", "blk"), None),
        P(("dp", "blk"), None),
        P(("dp", "blk"), None),
        P("blk", None),
        P(),
        P(),
        P(),
    )
    out_specs = (P(), P(), P())
    return jax.shard_map(
        on_device, mesh=mesh, in_specs=in_specs, out_specs=out_specs, check_vma=False
    )
```

profile of v0, /device:TPU:0, one launch (start us, length us, event | category | flops | bytes accessed | tf_op | source)
XLA Modules:
  0.0 306.3 jit_solution(14688047699911241302)
XLA Ops:
  7.2 0.8 fusion.11
  8.0 18.6 %gather_fusion = bf16[4096,256]{1,0:T(8,128)(2,1)} fusion(bf16[8192,256]{1,0:T(8,128)(2,1)} %param.12, s32[4096]{0:T(1024)S(1)} %bitcast_clamp_fusion), kind=kCustom, calls=%fused_computation | custom fusion | bytes 4210688 | tf_op jit(solution)/shard_map/gather | solution.py:61
  26.6 6.5 %all-to-all-start = ((bf16[4,1024,256]{2,1,0:T(8,128)(2,1)}), bf16[4,1024,256]{2,1,0:T(8,128)(2,1)S(1)}, u32[]{:S(2)}, u32[]{:S(2)}) async-start(bf16[4,1024,256]{2,1,0:T(8,128)(2,1)} %bitcast.29), calls=%async_computation | async-start | bytes 4194304 | tf_op jit(solution)/shard_map/all_to_all | solution.py:62
  33.0 0.1 fusion.15
  33.1 0.1 copy.15
  33.3 2.8 fusion.17
  36.1 45.1 %all-to-all-done = bf16[4,1024,256]{2,1,0:T(8,128)(2,1)S(1)} async-done(((bf16[4,1024,256]{2,1,0:T(8,128)(2,1)}), bf16[4,1024,256]{2,1,0:T(8,128)(2,1)S(1)}, u32[]{:S(2)}, u32[]{:S(2)}) %all-to-all-start) | async-done | bytes 2097184 | tf_op jit(solution)/shard_map/all_to_all | solution.py:62
  81.2 16.9 %gather_fusion.1 = bf16[4096,256]{1,0:T(8,128)(2,1)} fusion(bf16[4096,256]{1,0:T(8,128)(2,1)S(1)} %bitcast.28, s32[4096]{0:T(1024)S(1)} %broadcast_clamp_fusion), kind=kCustom, calls=%fused_computation.1 | custom fusion | bytes 4210688 | tf_op jit(solution)/shard_map/gather | solution.py:63
  98.2 4.2 %fusion = f32[512,256]{1,0:T(8,128)S(1)} fusion(bf16[4096,256]{1,0:T(8,128)(2,1)} %gather_fusion.1, f32[512,8]{1,0:T(8,128)S(1)} %copy.15), kind=kLoop, calls=%fused_computation.3 | loop fusion | flops 3014656 | bytes 2637824 | tf_op jit(solution)/shard_map/reduce_sum | solution.py:14
  102.4 2.1 multiply_convert_fusion.1
  104.5 0.5 multiply_reduce_fusion.1
  105.1 0.1 multiply_reduce_fusion.2
  105.1 16.0 %all_gather.3 = bf16[1024,256]{0,1:T(8,128)(2,1)S(1)} all-gather(bf16[256,256]{0,1:T(8,128)(2,1)S(1)} %slice.13), channel_id=1, replica_groups=mesh['dp'=8,'blk'=4] {'blk'}, dimensions={0}, use_global_device_ids=true | all-gather | bytes 655360 | tf_op jit(solution)/shard_map/all_gather | solution.py:71
  121.1 0.6 fusion.16
  121.7 0.2 copy-done.8
  121.9 1.4 convolution_multiply_fusion
  123.3 0.0 reduce-scatter.2.cloned.1.call-update
  123.4 0.0 all-reduce.3.cloned.1.call-start
  123.4 1.5 convolution_multiply_fusion.2
  124.9 24.7 %reduce-scatter.2.cloned.1.call-done = f32[256,256]{0,1:T(8,128)} async-done(((f32[1024,256]{0,1:T(8,128)}), f32[256,256]{0,1:T(8,128)}) %reduce-scatter.2.cloned.1.call-update) | async-done | bytes 262160 | tf_op jit(solution)/shard_map/reduce_scatter | solution.py:77
  149.6 1.0 multiply_reduce_fusion
  150.6 1.2 subtract_convert_fusion
  151.9 1.5 fusion.18
  153.3 1.0 multiply_convert_fusion
  154.3 0.0 copy-done.10
  154.4 1.5 fusion.12
  155.9 1.4 convolution_bitcast_fusion
  157.4 0.0 all-reduce.3.cloned.1.call-update
  157.4 137.4 %all-reduce.3.cloned.1.call-done = (f32[256,1024]{0,1:T(8,128)}, f32[256,1024]{1,0:T(8,128)}, f32[1024,256]{1,0:T(8,128)}) async-done(((f32[256,1024]{0,1:T(8,128)}, f32[256,1024]{1,0:T(8,128)}, f32[1024,256]{1,0:T(8,128)}), (f32[256,1024]{0,1:T(8,128)}, f32[256,1024]{1,0:T(8,128)}, f32[1024,256]{1,0:T(8,128)})) %all-reduce.3.cloned.1.call-update) | async-done | bytes 3145744 | tf_op jit(solution)/shard_map/psum | solution.py:86
  294.8 2.7 copy.18
  297.5 1.0 copy.26
  298.5 1.0 copy.27
  (37 shorter events, 0.2 us)
Async XLA Ops:
  7.2 95.2 %copy-start = (bf16[256,1024]{1,0:T(8,128)(2,1)S(1)}, bf16[256,1024]{1,0:T(8,128)(2,1)}, u32[]{:S(2)}) copy-start(bf16[256,1024]{1,0:T(8,128)(2,1)} %param.14) | copy-start | bytes 1572868
  26.6 6.5 %copy-start.11 = (s32[512,8]{0,1:T(8,128)S(1)}, s32[512,8]{0,1:T(8,128)}, u32[]{:S(2)}) copy-start(s32[512,8]{0,1:T(8,128)} %param.9) | copy-start | bytes 49156
  26.6 6.7 %copy-start.12 = (s32[1,4096]{1,0:T(1,128)S(1)}, s32[1,4096]{1,0:T(1,128)}, u32[]{:S(2)}) copy-start(s32[1,4096]{1,0:T(1,128)} %param.10) | copy-start | bytes 49156
  26.6 6.8 %copy-start.4 = (bf16[512,256]{1,0:T(8,128)(2,1)S(1)}, bf16[512,256]{1,0:T(8,128)(2,1)}, u32[]{:S(2)}) copy-start(bf16[512,256]{1,0:T(8,128)(2,1)} %param.8) | copy-start | bytes 786436
  26.6 54.7 %all-to-all-start = ((bf16[4,1024,256]{2,1,0:T(8,128)(2,1)}), bf16[4,1024,256]{2,1,0:T(8,128)(2,1)S(1)}, u32[]{:S(2)}, u32[]{:S(2)}) async-start(bf16[4,1024,256]{2,1,0:T(8,128)(2,1)} %bitcast.29), calls=%async_computation | async-start | bytes 4194304 | tf_op jit(solution)/shard_map/all_to_all | solution.py:62
  33.0 116.6 %reduce-scatter.2.cloned.1.call-start = ((), (), s32[]{:S(2)}) async-start(), calls=%async_computation.2 | async-start | bytes 1310720 | tf_op jit(solution)/shard_map/reduce_scatter | solution.py:77
  98.2 4.2 %copy-start.1 = (f32[512,1024]{1,0:T(8,128)S(1)}, f32[512,1024]{1,0:T(8,128)}, u32[]{:S(2)}) copy-start(f32[512,1024]{1,0:T(8,128)} %fusion.17) | copy-start | bytes 6291460
  102.4 2.1 copy-start.9
  102.4 2.1 copy-start.6
  121.1 0.8 copy-start.8
  123.4 171.5 %all-reduce.3.cloned.1.call-start = ((), (), s32[]{:S(2)}) async-start(), calls=%async_computation.3 | async-start | bytes 6291456 | tf_op jit(solution)/shard_map/psum | solution.py:86
  150.6 2.7 copy-start.7
  150.6 2.7 copy-start.13
  153.3 1.0 copy-start.10
  154.4 1.5 copy-start.5
  294.8 2.7 copy-start.3
  294.8 3.7 %copy-start.2 = (f32[1024,256]{1,0:T(8,128)S(1)}, f32[1024,256]{1,0:T(8,128)}, u32[]{:S(2)}) copy-start(f32[1024,256]{1,0:T(8,128)} %get-tuple-element.24) | copy-start | bytes 3145732
Sparse Core Ops, SparseCore 0:
  123.5 26.0 reduce-scatter.1
  157.5 137.2 all-reduce.2
where the time goes:
time: 307 us; the launch traced here: 306 us
  waiting for transfers between devices  207 us (67%)
  local copies, waits for them, and re-layouts  40.6 us (13%)
  blocking collectives  16 us (5%)
  matrix products  14.3 us (5%)
  between operations  14.2 us (5%)
  other arithmetic  7.5 us (2%)
  starting transfers between devices  6.5 us (2%)
    psum x1, waiting for transfers between devices, on_device(): lax.psum((grads[0], grads[1], grads[2]), ('dp', 'blk'))  137 us
    all_to_all x1, waiting for transfers between devices, on_device(): lax.all_to_all(outgoing, 'blk', split_axis=0, concat_axis=0, tiled=True)  45.1 us
    reduce_scatter x1, waiting for transfers between devices, on_device(): lax.psum_scatter(lax.dot_general(weight_tile, queries, contract, preferre...  24.7 us
    gather x1, local copies, waits for them, and re-layouts, on_device(): outgoing = feat_store[serve_rows]  18.6 us
    gather x1, local copies, waits for them, and re-layouts, on_device(): received_rows.reshape(-1, feat_width)[neighbour_slot[0]]  16.9 us
    all_gather x1, blocking collectives, on_device(): cycle_items = lax.all_gather(own_items, 'blk', axis=0, tiled=True)  16 us
    all_to_all x1, starting transfers between devices, on_device(): lax.all_to_all(outgoing, 'blk', split_axis=0, concat_axis=0, tiled=True)  6.46 us
  transfers between devices with their start and end apart: 3, of which 3 were waited for; matrix products, arithmetic and copies ran while one was open for 1% of the time, Pallas kernels for 0%

commit v1 on v0

v1 whole, which is shorter than its diff:
```python
import jax
import jax.numpy as jnp
from jax import lax
from jax.sharding import PartitionSpec as P

MARGIN = 0.5
AXES = ("dp", "blk")
BF16 = jnp.bfloat16
F32 = jnp.float32
OVER_ROWS = (((0,), (0,)), ((), ()))


def exchange(value, sizes, flip_dp, flip_blk):
    dp_size, blk_size = sizes
    pairs = [
        (g * blk_size + b, (g ^ flip_dp) * blk_size + (b ^ flip_blk))
        for g in range(dp_size)
        for b in range(blk_size)
    ]
    return lax.ppermute(value, AXES, pairs)


def block_of(array, index, count):
    rows = array.shape[0] // count
    return lax.dynamic_slice_in_dim(array, index * rows, rows, 0)


def in_order(parts, own):
    ordered = []
    for place in range(len(parts)):
        block = parts[place]
        for own_value in range(1, len(parts)):
            block = jnp.where(own == own_value, parts[place ^ own_value], block)
        ordered.append(block)
    return jnp.concatenate(ordered, 0)


def reduce_blocks(array, own, count, send):
    arrived = [send(block_of(array, own ^ j, count).astype(BF16), j) for j in range(1, count)]
    total = block_of(array, own, count)
    for part in arrived:
        total = total + part.astype(F32)
    return total


def gather_blocks(block, own, count, send):
    return in_order([block] + [send(block, j) for j in range(1, count)], own)


def node_of_arrival(neighbour_slot, valid, count):
    slots = neighbour_slot.shape[1]
    low = 128
    node = lax.broadcasted_iota(jnp.int32, (1, slots), 1) // (slots // valid.shape[0])
    flat_valid = valid.reshape(1, slots)
    high_hot = lax.broadcasted_iota(jnp.int32, (slots // low, slots), 0) == neighbour_slot // low
    low_hot = lax.broadcasted_iota(jnp.int32, (low, slots), 0) == neighbour_slot % low
    upper = ((node // 16 + 1) * flat_valid).astype(F32)
    lower = ((node % 16) * flat_valid).astype(F32)
    codes = jnp.concatenate(
        [jnp.where(low_hot, upper, 0.0), jnp.where(low_hot, lower, 0.0)], 0
    ).astype(BF16)
    found = lax.dot_general(
        high_hot.astype(BF16), codes, (((1,), (1,)), ((), ())), preferred_element_type=F32
    )
    found = found.astype(jnp.int32)
    return ((found[:, :low] - 1) * 16 + found[:, low:]).reshape(count, slots // count)


def pooled_mean(nbr_mask, neighbour_slot, serve_rows, feat_store, own, sizes):
    blk_size = sizes[1]
    nodes = nbr_mask.shape[0]
    first_col = lax.broadcasted_iota(jnp.int32, nbr_mask.shape, 1) == 0
    valid = jnp.where(first_col, 1, nbr_mask)
    live_count = jnp.sum(valid.astype(F32), 1, keepdims=True)
    node_at = node_of_arrival(neighbour_slot, valid, blk_size)
    order = sorted(range(1, blk_size), key=lambda j: (j != blk_size // 2, j))
    wanted = {
        j: exchange(block_of(node_at, own ^ j, blk_size), sizes, 0, j) for j in order
    }
    wanted[0] = block_of(node_at, own, blk_size)
    row_node = lax.broadcasted_iota(jnp.int32, (nodes, serve_rows.shape[1]), 0)
    total = None
    for j in order + [0]:
        served = block_of(serve_rows, own ^ j, blk_size)[0]
        rows = feat_store.at[served].get(mode="promise_in_bounds")
        pick = (row_node == wanted[j]).astype(BF16)
        part = jnp.dot(pick, rows, preferred_element_type=F32)
        if j:
            part = exchange(part.astype(BF16), sizes, 0, j).astype(F32)
        total = part if total is None else total + part
    return (total / live_count).astype(BF16)


def pair_gradients(embedding, own, sizes):
    blk_size = sizes[1]
    pairs = embedding.shape[0] // 2
    scale = embedding.shape[1] ** (-0.5)
    queries, items = embedding[:pairs], embedding[pairs:]
    order = sorted(range(1, blk_size), key=lambda j: (j != blk_size // 2, j))
    other_items = [exchange(items, sizes, 0, j) for j in order]
    other_queries = [exchange(queries, sizes, 0, j) for j in order]
    cycle = jnp.concatenate([items] + other_items, 0)
    columns = cycle.shape[0]

    def positive_of(q, i):
        return jnp.sum(q.astype(F32) * i.astype(F32), 1, keepdims=True) * scale

    def weights_of(q, i, positive):
        scores = lax.dot_general(q, i, (((1,), (1,)), ((), ())), preferred_element_type=F32)
        return jax.nn.sigmoid(scores * scale - positive + MARGIN) / columns

    weights = weights_of(queries, cycle, positive_of(queries, items))
    row_total = jnp.sum(weights, 1, keepdims=True)
    diagonal = lax.broadcasted_iota(jnp.int32, weights.shape, 0) == lax.broadcasted_iota(
        jnp.int32, weights.shape, 1
    )
    tile = jnp.where(diagonal, weights - row_total, weights).astype(BF16)
    d_query = jnp.dot(tile, cycle, preferred_element_type=F32) * scale
    remote_queries = jnp.concatenate(other_queries, 0)
    remote_tile = weights_of(
        remote_queries, items, positive_of(remote_queries, cycle[pairs:])
    ).astype(BF16)
    d_item = (
        lax.dot_general(tile[:, :pairs], queries, OVER_ROWS, preferred_element_type=F32)
        + lax.dot_general(remote_tile, remote_queries, OVER_ROWS, preferred_element_type=F32)
    ) * scale
    return jnp.concatenate([d_query, d_item], 0)


def sum_staged(g_in, g_out, group, own, sizes):
    dp_size, blk_size = sizes
    width = g_in.shape[1]
    side = g_out.shape[1]
    plane = dp_size // 2
    core = group % 2
    across = group // 2

    def half(index):
        g_in_half = block_of(g_in, index, 2)
        g_out_half = block_of(g_out, index, 2)
        rows = g_out_half.shape[0] * side // width
        folded = jnp.concatenate(
            [g_out_half[k * rows : (k + 1) * rows] for k in range(width // side)], 1
        )
        return jnp.concatenate([g_in_half, folded], 0)

    def unfold(folded):
        return jnp.concatenate(
            [folded[:, k * side : (k + 1) * side] for k in range(width // side)], 0
        )

    def over_core(v, j):
        return exchange(v, sizes, j, 0)

    def over_plane(v, j):
        return exchange(v, sizes, 2 * j, 0)

    def over_blk(v, j):
        return exchange(v, sizes, 0, j)

    total = half(core) + over_core(half(1 - core).astype(BF16), 1).astype(F32)
    total = reduce_blocks(total, across, plane, over_plane)
    total = reduce_blocks(total, own, blk_size, over_blk)
    block = total.astype(BF16)
    block = gather_blocks(block, own, blk_size, over_blk)
    block = gather_blocks(block, across, plane, over_plane)
    other = over_core(block, 1)
    first = jnp.where(core == 0, block, other)
    second = jnp.where(core == 0, other, block)
    cut = g_in.shape[0] // 2
    grad_out = jnp.concatenate([unfold(first[cut:]), unfold(second[cut:])], 0)
    return (first[:cut].astype(F32), second[:cut].astype(F32), grad_out.astype(F32))


def on_device(sizes, self_feat, nbr_mask, neighbour_slot, serve_rows, feat_store, w_self, w_nbr, w_out):
    dp_size, blk_size = sizes
    group = lax.axis_index("dp")
    own = lax.axis_index("blk")
    pooled = pooled_mean(nbr_mask, neighbour_slot, serve_rows, feat_store, own, sizes)
    pre_act = jnp.dot(self_feat, w_self, preferred_element_type=F32) + jnp.dot(
        pooled, w_nbr, preferred_element_type=F32
    )
    gate_sig = jax.nn.sigmoid(pre_act)
    hidden = (pre_act * gate_sig).astype(BF16)
    projected = jnp.dot(hidden, w_out, preferred_element_type=F32)
    inv_norm = lax.rsqrt(jnp.mean(projected * projected, 1, keepdims=True) + 1e-06)
    embedding = (projected * inv_norm).astype(BF16)
    d_embed = pair_gradients(embedding, own, sizes)
    interior_term = jnp.mean(d_embed * projected, 1, keepdims=True)
    d_proj = (inv_norm * d_embed - projected * inv_norm**3 * interior_term).astype(BF16)
    g_out = lax.dot_general(hidden, d_proj, OVER_ROWS, preferred_element_type=F32)
    d_hidden = lax.dot_general(d_proj, w_out, (((1,), (1,)), ((), ())), preferred_element_type=F32)
    d_pre = (d_hidden * gate_sig * (1.0 + pre_act * (1.0 - gate_sig))).astype(BF16)
    inputs = jnp.concatenate([self_feat, pooled], 1)
    g_in = lax.dot_general(inputs, d_pre, OVER_ROWS, preferred_element_type=F32)
    staged = (dp_size & (dp_size - 1)) == 0 and dp_size > 1
    if staged and g_in.shape[0] % (8 * dp_size * blk_size) == 0:
        return sum_staged(g_in, g_out, group, own, sizes)
    g_in, grad_out = lax.psum((g_in, g_out), AXES)
    cut = g_in.shape[0] // 2
    return (g_in[:cut], g_in[cut:], grad_out)


def solution(mesh):
    sizes = (mesh.shape["dp"], mesh.shape["blk"])
    in_specs = (
        P(("dp", "blk"), None),
        P(("dp", "blk"), None),
        P(("dp", "blk"), None),
        P(("dp", "blk"), None),
        P("blk", None),
        P(),
        P(),
        P(),
    )
    out_specs = (P(), P(), P())

    def body(*arrays):
        return on_device(sizes, *arrays)

    return jax.shard_map(
        body, mesh=mesh, in_specs=in_specs, out_specs=out_specs, check_vma=False
    )
```

time: 307 us -> 145 us (0.47)
  waiting for transfers between devices: 207 us -> 51.6 us
  starting transfers between devices: 6.5 us -> 37.8 us
  blocking collectives: 16 us -> 0 us
  between operations: 14.2 us -> 1.41 us
  local copies, waits for them, and re-layouts: 40.6 us -> 28.7 us
  matrix products: 14.3 us -> 17.9 us
    psum x1 -> x0, waiting for transfers between devices: 137 us -> none  [on_device(): lax.psum((grads[0], grads[1], grads[2]), ('dp', 'blk'))]
    ppermute x0 -> x26, waiting for transfers between devices: none -> 51.6 us  [exchange(): return lax.ppermute(value, AXES, pairs)]
    all_to_all x1 -> x0, waiting for transfers between devices: 45.1 us -> none  [on_device(): lax.all_to_all(outgoing, 'blk', split_axis=0, concat_axis=0, tiled=True)]
    ppermute x0 -> x26, starting transfers between devices: none -> 37.8 us  [exchange(): return lax.ppermute(value, AXES, pairs)]
    reduce_scatter x1 -> x0, waiting for transfers between devices: 24.7 us -> none  [on_device(): lax.psum_scatter(lax.dot_general(weight_tile, queries, contract, preferre...]
    all_gather x1 -> x0, blocking collectives: 16 us -> none  [on_device(): cycle_items = lax.all_gather(own_items, 'blk', axis=0, tiled=True)]
    gather x2 -> x4, local copies, waits for them, and re-layouts: 35.5 us -> 24.9 us  [pooled_mean(): rows = feat_store.at[served].get(mode='promise_in_bounds')]
    all_to_all x1 -> x0, starting transfers between devices: 6.46 us -> none  [on_device(): lax.all_to_all(outgoing, 'blk', split_axis=0, concat_axis=0, tiled=True)]
  transfers between devices with their start and end apart: 3 -> 26, of which waited for: 3 -> 14; matrix products, arithmetic and copies ran while one was open for 1% -> 21% of each run, Pallas kernels for 0% -> 0%
where the time goes in v1:
time: 145 us; the launch traced here: 144 us
  waiting for transfers between devices  51.6 us (36%)
  starting transfers between devices  37.8 us (26%)
  local copies, waits for them, and re-layouts  28.7 us (20%)
  matrix products  17.9 us (12%)
  other arithmetic  6.67 us (5%)
    ppermute x26, waiting for transfers between devices, exchange(): return lax.ppermute(value, AXES, pairs)  51.6 us
    ppermute x26, starting transfers between devices, exchange(): return lax.ppermute(value, AXES, pairs)  37.8 us
    gather x4, local copies, waits for them, and re-layouts, pooled_mean(): rows = feat_store.at[served].get(mode='promise_in_bounds')  24.9 us
    dot_general x1, matrix products, on_device(): g_in = lax.dot_general(inputs, d_pre, OVER_ROWS, preferred_element_type=F32)  4.48 us
    dot_general x1, matrix products, on_device(): jnp.dot(pooled, w_nbr, preferred_element_type=F32)  3.67 us
  transfers between devices with their start and end apart: 26, of which 14 were waited for; matrix products, arithmetic and copies ran while one was open for 21% of the time, Pallas kernels for 0%

profile of v1, /device:TPU:0, one launch (start us, length us, event | category | flops | bytes accessed | tf_op | source)
XLA Modules:
  0.0 144.2 jit_solution(5849140327218413181)
XLA Ops:
  3.9 4.1 %collective-permute-start = (s32[1,1024]{1,0:T(1,128)S(1)}, s32[1,1024]{1,0:T(1,128)S(1)}, u32[]{:S(2)}, u32[]{:S(2)}) collective-permute-start(s32[1,1024]{1,0:T(1,128)S(1)} %get-tuple-element.32), channel_id=1, source_target_pairs={{0,2},{1,3},{2,0},{3,1},{4,6},{5,7},{6,4},{7,5},{8,10},{9,11},{10,... | collective-permute-start | bytes 12296 | tf_op jit(solution)/shard_map/ppermute | solution.py:20
  8.0 1.6 %collective-permute-start.2 = (s32[1,1024]{1,0:T(1,128)S(1)}, s32[1,1024]{1,0:T(1,128)S(1)}, u32[]{:S(2)}, u32[]{:S(2)}) collective-permute-start(s32[1,1024]{1,0:T(1,128)S(1)} %get-tuple-element.35), channel_id=1, source_target_pairs={{0,1},{1,0},{2,3},{3,2},{4,5},{5,4},{6,7},{7,6},{8,9},{9,8},{10,11... | collective-permute-start | bytes 12296 | tf_op jit(solution)/shard_map/ppermute | solution.py:20
  9.6 1.8 %fusion.84 = f32[512,1024]{1,0:T(8,128)} fusion(bf16[512,256]{1,0:T(8,128)(2,1)S(1)} %copy-done.5, bf16[256,1024]{1,0:T(8,128)(2,1)S(1)} %copy-done.3), kind=kOutput, calls=%fused_computation.193 | convolution fusion | flops 268435456 | bytes 2883584 | tf_op jit(solution)/shard_map/dot_general | solution.py:180
  11.4 6.2 %gather_fusion = bf16[1024,256]{1,0:T(8,128)(2,1)S(1)} fusion(bf16[8192,256]{1,0:T(8,128)(2,1)} %param.12, s32[1024]{0:T(1024)S(1)} %broadcast_clamp_fusion.3), kind=kCustom, calls=%fused_computation | custom fusion | bytes 1052672 | tf_op jit(solution)/shard_map/gather | solution.py:85
  17.6 6.2 %gather_fusion.1 = bf16[1024,256]{1,0:T(8,128)(2,1)S(1)} fusion(bf16[8192,256]{1,0:T(8,128)(2,1)} %param.12, s32[1024]{0:T(1024)S(1)} %broadcast_clamp_fusion.2), kind=kCustom, calls=%fused_computation.1 | custom fusion | bytes 1052672 | tf_op jit(solution)/shard_map/gather | solution.py:85
  23.8 6.2 %gather_fusion.2 = bf16[1024,256]{1,0:T(8,128)(2,1)S(1)} fusion(bf16[8192,256]{1,0:T(8,128)(2,1)} %param.12, s32[1024]{0:T(1024)S(1)} %broadcast_clamp_fusion.1), kind=kCustom, calls=%fused_computation.2 | custom fusion | bytes 1052672 | tf_op jit(solution)/shard_map/gather | solution.py:85
  30.5 2.0 %collective-permute-start.1 = (bf16[512,256]{1,0:T(8,128)(2,1)S(1)}, bf16[512,256]{1,0:T(8,128)(2,1)S(1)}, u32[]{:S(2)}, u32[]{:S(2)}) collective-permute-start(bf16[512,256]{1,0:T(8,128)(2,1)S(1)} %fusion.27), channel_id=1, source_target_pairs={{0,2},{1,3},{2,0},{3,1},{4,6},{5,7},{6,4},{7,5},{8,10},{9,11},{10,... | collective-permute-start | bytes 786440 | tf_op jit(solution)/shard_map/ppermute | solution.py:20
  32.9 2.6 %collective-permute-start.3 = (bf16[512,256]{1,0:T(8,128)(2,1)S(1)}, bf16[512,256]{1,0:T(8,128)(2,1)S(1)}, u32[]{:S(2)}, u32[]{:S(2)}) collective-permute-start(bf16[512,256]{1,0:T(8,128)(2,1)S(1)} %fusion.26), channel_id=1, source_target_pairs={{0,1},{1,0},{2,3},{3,2},{4,5},{5,4},{6,7},{7,6},{8,9},{9,8},{10,11... | collective-permute-start | bytes 786440 | tf_op jit(solution)/shard_map/ppermute | solution.py:20
  36.1 6.4 %gather_fusion.3 = bf16[1024,256]{1,0:T(8,128)(2,1)S(1)} fusion(bf16[8192,256]{1,0:T(8,128)(2,1)} %param.12, s32[1024]{0:T(1024)S(1)} %broadcast_clamp_fusion), kind=kCustom, calls=%fused_computation.3 | custom fusion | bytes 1052672 | tf_op jit(solution)/shard_map/gather | solution.py:85
  42.9 8.4 %collective-permute-done.1 = bf16[512,256]{1,0:T(8,128)(2,1)S(1)} collective-permute-done((bf16[512,256]{1,0:T(8,128)(2,1)S(1)}, bf16[512,256]{1,0:T(8,128)(2,1)S(1)}, u32[]{:S(2)}, u32[]{:S(2)}) %collective-permute-start.1) | collective-permute-done | bytes 262176 | tf_op jit(solution)/shard_map/ppermute | solution.py:20
  51.5 3.7 %multiply_convert_fusion.1 = (bf16[512,1024]{1,0:T(8,128)(2,1)S(1)}, f32[512,1024]{1,0:T(8,128)}) fusion(f32[512,1024]{1,0:T(8,128)} %fusion.84, bf16[512,256]{1,0:T(8,128)(2,1)S(1)} %divide_convert_fusion, bf16[256,1024]{1,0:T(8,128)(2,1)S(1)} %copy-done), kind=kOutput, calls=%fused_computation.9 | convolution fusion | flops 271581184 | bytes 6029312 | tf_op jit(solution)/shard_map/dot_general | solution.py:180
  55.8 6.2 %collective-permute-start.6 = (bf16[256,256]{0,1:T(8,128)(2,1)S(1)}, bf16[256,256]{0,1:T(8,128)(2,1)S(1)}, u32[]{:S(2)}, u32[]{:S(2)}) collective-permute-start(bf16[256,256]{0,1:T(8,128)(2,1)S(1)} %get-tuple-element.27), channel_id=1, source_target_pairs={{0,2},{1,3},{2,0},{3,1},{4,6},{5,7},{6,4},{7,5},{8,10},{9,11},{10,... | collective-permute-start | bytes 393224 | tf_op jit(solution)/shard_map/ppermute | solution.py:20
  62.0 1.5 %collective-permute-start.8 = (bf16[256,256]{0,1:T(8,128)(2,1)S(1)}, bf16[256,256]{0,1:T(8,128)(2,1)S(1)}, u32[]{:S(2)}, u32[]{:S(2)}) collective-permute-start(bf16[256,256]{0,1:T(8,128)(2,1)S(1)} %get-tuple-element.27), channel_id=1, source_target_pairs={{0,3},{1,2},{2,1},{3,0},{4,7},{5,6},{6,5},{7,4},{8,11},{9,10},{10,... | collective-permute-start | bytes 393224 | tf_op jit(solution)/shard_map/ppermute | solution.py:20
  63.6 2.0 %collective-permute-start.9 = (bf16[256,256]{0,1:T(8,128)(2,1)S(1)}, bf16[256,256]{0,1:T(8,128)(2,1)S(1)}, u32[]{:S(2)}, u32[]{:S(2)}) collective-permute-start(bf16[256,256]{0,1:T(8,128)(2,1)S(1)} %get-tuple-element.26), channel_id=1, source_target_pairs={{0,2},{1,3},{2,0},{3,1},{4,6},{5,7},{6,4},{7,5},{8,10},{9,11},{10,... | collective-permute-start | bytes 393224 | tf_op jit(solution)/shard_map/ppermute | solution.py:20
  66.5 13.2 %collective-permute-done.9 = bf16[256,256]{0,1:T(8,128)(2,1)S(1)} collective-permute-done((bf16[256,256]{0,1:T(8,128)(2,1)S(1)}, bf16[256,256]{0,1:T(8,128)(2,1)S(1)}, u32[]{:S(2)}, u32[]{:S(2)}) %collective-permute-start.9) | collective-permute-done | bytes 131104 | tf_op jit(solution)/shard_map/ppermute | solution.py:20
  80.5 6.3 %collective-permute-done.11 = bf16[256,256]{0,1:T(8,128)(2,1)S(1)} collective-permute-done((bf16[256,256]{0,1:T(8,128)(2,1)S(1)}, bf16[256,256]{0,1:T(8,128)(2,1)S(1)}, u32[]{:S(2)}, u32[]{:S(2)}) %collective-permute-start.11) | collective-permute-done | bytes 131104 | tf_op jit(solution)/shard_map/ppermute | solution.py:20
  88.6 1.5 %fusion.29 = f32[256,256]{0,1:T(8,128)S(1)} fusion(f32[256,256]{0,1:T(8,128)} %fusion.48, bf16[768,256]{0,1:T(8,128)(2,1)S(1)} %constant_dynamic-update-slice_fusion, f32[768]{0:T(1024)S(1)} %broadcast_multiply_fusion, bf16[512,256]{0,1:T(8,128)(2,1)S(1)} %multiply_convert_fusion.2), kind=kOutput, calls=%fused_computation.49 | convolution fusion | flops 203030528 | bytes 1445888 | tf_op jit(solution)/shard_map/dot_general | solution.py:125
  92.8 4.5 %fusion.15 = f32[512,1024]{1,0:T(8,128)} fusion(f32[512,1024]{1,0:T(8,128)} %get-tuple-element.47, bf16[512,256]{0,1:T(8,128)(2,1)S(1)} %subtract_convert_fusion, bf16[1024,256]{1,0:T(8,128)(2,1)S(1)} %copy-done.2, bf16[512,256]{1,0:T(8,128)(2,1)} %copy-done.4, bf16[512,256]{1,0:T(8,128)(2,1)} %param.8), kind=kOutput, calls=%fused_computation.33 | convolution fusion | flops 811073536 | bytes 5505024 | tf_op jit(solution)/shard_map/dot_general | solution.py:195
  101.4 1.5 %collective-permute-start.13 = (bf16[96,1024]{1,0:T(8,128)(2,1)S(1)}, bf16[96,1024]{1,0:T(8,128)(2,1)S(1)}, u32[]{:S(2)}, u32[]{:S(2)}) collective-permute-start(bf16[96,1024]{1,0:T(8,128)(2,1)S(1)} %get-tuple-element.9), channel_id=1, source_target_pairs={{0,8},{1,9},{2,10},{3,11},{4,12},{5,13},{6,14},{7,15},{8,0},{9,1},... | collective-permute-start | bytes 589832 | tf_op jit(solution)/shard_map/ppermute | solution.py:20
  104.9 4.3 %collective-permute-done.13 = bf16[96,1024]{1,0:T(8,128)(2,1)S(1)} collective-permute-done((bf16[96,1024]{1,0:T(8,128)(2,1)S(1)}, bf16[96,1024]{1,0:T(8,128)(2,1)S(1)}, u32[]{:S(2)}, u32[]{:S(2)}) %collective-permute-start.13) | collective-permute-done | bytes 196640 | tf_op jit(solution)/shard_map/ppermute | solution.py:20
  109.2 4.6 %collective-permute-done.14 = bf16[96,1024]{1,0:T(8,128)(2,1)S(1)} collective-permute-done((bf16[96,1024]{1,0:T(8,128)(2,1)S(1)}, bf16[96,1024]{1,0:T(8,128)(2,1)S(1)}, u32[]{:S(2)}, u32[]{:S(2)}) %collective-permute-start.14) | collective-permute-done | bytes 196640 | tf_op jit(solution)/shard_map/ppermute | solution.py:20
  114.0 1.5 %collective-permute-start.17 = (bf16[24,1024]{1,0:T(8,128)(2,1)S(1)}, bf16[24,1024]{1,0:T(8,128)(2,1)S(1)}, u32[]{:S(2)}, u32[]{:S(2)}) collective-permute-start(bf16[24,1024]{1,0:T(8,128)(2,1)S(1)} %get-tuple-element.21), channel_id=1, source_target_pairs={{0,2},{1,3},{2,0},{3,1},{4,6},{5,7},{6,4},{7,5},{8,10},{9,11},{10,... | collective-permute-start | bytes 147464 | tf_op jit(solution)/shard_map/ppermute | solution.py:20
  115.6 2.8 %collective-permute-start.18 = (bf16[24,1024]{1,0:T(8,128)(2,1)S(1)}, bf16[24,1024]{1,0:T(8,128)(2,1)S(1)}, u32[]{:S(2)}, u32[]{:S(2)}) collective-permute-start(bf16[24,1024]{1,0:T(8,128)(2,1)S(1)} %get-tuple-element.20), channel_id=1, source_target_pairs={{0,3},{1,2},{2,1},{3,0},{4,7},{5,6},{6,5},{7,4},{8,11},{9,10},{10,... | collective-permute-start | bytes 147464 | tf_op jit(solution)/shard_map/ppermute | solution.py:20
  119.7 1.8 %collective-permute-done.18 = bf16[24,1024]{1,0:T(8,128)(2,1)S(1)} collective-permute-done((bf16[24,1024]{1,0:T(8,128)(2,1)S(1)}, bf16[24,1024]{1,0:T(8,128)(2,1)S(1)}, u32[]{:S(2)}, u32[]{:S(2)}) %collective-permute-start.18) | collective-permute-done | bytes 49184 | tf_op jit(solution)/shard_map/ppermute | solution.py:20
  121.5 2.9 %collective-permute-start.19 = (bf16[24,1024]{1,0:T(8,128)(2,1)S(1)}, bf16[24,1024]{1,0:T(8,128)(2,1)S(1)}, u32[]{:S(2)}, u32[]{:S(2)}) collective-permute-start(bf16[24,1024]{1,0:T(8,128)(2,1)S(1)} %add_convert_fusion), channel_id=1, source_target_pairs={{0,3},{1,2},{2,1},{3,0},{4,7},{5,6},{6,5},{7,4},{8,11},{9,10},{10,... | collective-permute-start | bytes 147464 | tf_op jit(solution)/shard_map/ppermute | solution.py:20
  124.4 1.6 %collective-permute-start.21 = (bf16[24,1024]{1,0:T(8,128)(2,1)S(1)}, bf16[24,1024]{1,0:T(8,128)(2,1)S(1)}, u32[]{:S(2)}, u32[]{:S(2)}) collective-permute-start(bf16[24,1024]{1,0:T(8,128)(2,1)S(1)} %add_convert_fusion), channel_id=1, source_target_pairs={{0,1},{1,0},{2,3},{3,2},{4,5},{5,4},{6,7},{7,6},{8,9},{9,8},{10,11... | collective-permute-start | bytes 147464 | tf_op jit(solution)/shard_map/ppermute | solution.py:20
  127.5 1.9 %collective-permute-done.20 = bf16[24,1024]{1,0:T(8,128)(2,1)S(1)} collective-permute-done((bf16[24,1024]{1,0:T(8,128)(2,1)S(1)}, bf16[24,1024]{1,0:T(8,128)(2,1)S(1)}, u32[]{:S(2)}, u32[]{:S(2)}) %collective-permute-start.20) | collective-permute-done | bytes 49184 | tf_op jit(solution)/shard_map/ppermute | solution.py:20
  129.4 1.6 %collective-permute-start.22 = (bf16[96,1024]{1,0:T(8,128)(2,1)S(1)}, bf16[96,1024]{1,0:T(8,128)(2,1)S(1)}, u32[]{:S(2)}, u32[]{:S(2)}) collective-permute-start(bf16[96,1024]{1,0:T(8,128)(2,1)S(1)} %pad_maximum_fusion.3), channel_id=1, source_target_pairs={{0,24},{1,25},{2,26},{3,27},{4,28},{5,29},{6,30},{7,31},{8,16},{9,... | collective-permute-start | bytes 589832 | tf_op jit(solution)/shard_map/ppermute | solution.py:20
  133.0 3.2 %collective-permute-done.22 = bf16[96,1024]{1,0:T(8,128)(2,1)S(1)} collective-permute-done((bf16[96,1024]{1,0:T(8,128)(2,1)S(1)}, bf16[96,1024]{1,0:T(8,128)(2,1)S(1)}, u32[]{:S(2)}, u32[]{:S(2)}) %collective-permute-start.22) | collective-permute-done | bytes 196640 | tf_op jit(solution)/shard_map/ppermute | solution.py:20
  136.2 2.0 %collective-permute-done.23 = bf16[96,1024]{1,0:T(8,128)(2,1)S(1)} collective-permute-done((bf16[96,1024]{1,0:T(8,128)(2,1)S(1)}, bf16[96,1024]{1,0:T(8,128)(2,1)S(1)}, u32[]{:S(2)}, u32[]{:S(2)}) %collective-permute-start.23) | collective-permute-done | bytes 196640 | tf_op jit(solution)/shard_map/ppermute | solution.py:20
  138.7 2.3 %collective-permute-done.25 = bf16[384,1024]{1,0:T(8,128)(2,1)S(1)} collective-permute-done((bf16[384,1024]{1,0:T(8,128)(2,1)S(1)}, bf16[384,1024]{1,0:T(8,128)(2,1)S(1)}, u32[]{:S(2)}, u32[]{:S(2)}) %collective-permute-start.25) | collective-permute-done | bytes 786464 | tf_op jit(solution)/shard_map/ppermute | solution.py:20
  141.5 1.6 %slice_convert_fusion = (f32[256,1024]{1,0:T(8,128)}, f32[256,1024]{1,0:T(8,128)}) fusion(bf16[384,1024]{1,0:T(8,128)(2,1)S(1)} %get-tuple-element.7, bf16[384,1024]{1,0:T(8,128)(2,1)S(1)} %get-tuple-element.8), kind=kLoop, calls=%fused_computation.64 | loop fusion | flops 524288 | bytes 3145728 | tf_op jit(solution)/shard_map/convert_element_type | solution.py:172
  (118 shorter events, 25.0 us)
Async XLA Ops:
  0.6 50.8 %copy-start = (bf16[256,1024]{1,0:T(8,128)(2,1)S(1)}, bf16[256,1024]{1,0:T(8,128)(2,1)}, u32[]{:S(2)}) copy-start(bf16[256,1024]{1,0:T(8,128)(2,1)} %param.14) | copy-start | bytes 1572868
  3.0 6.5 %copy-start.10 = (s32[4,1024]{1,0:T(4,128)S(1)}, s32[4,1024]{1,0:T(4,128)}, u32[]{:S(2)}) copy-start(s32[4,1024]{1,0:T(4,128)} %param.11) | copy-start | bytes 49156
  3.1 6.6 %copy-start.3 = (bf16[256,1024]{1,0:T(8,128)(2,1)S(1)}, bf16[256,1024]{1,0:T(8,128)(2,1)}, u32[]{:S(2)}) copy-start(bf16[256,1024]{1,0:T(8,128)(2,1)} %param.13) | copy-start | bytes 1572868
  3.1 6.6 %copy-start.5 = (bf16[512,256]{1,0:T(8,128)(2,1)S(1)}, bf16[512,256]{1,0:T(8,128)(2,1)}, u32[]{:S(2)}) copy-start(bf16[512,256]{1,0:T(8,128)(2,1)} %param.8) | copy-start | bytes 786436
  3.9 26.1 %collective-permute-start = (s32[1,1024]{1,0:T(1,128)S(1)}, s32[1,1024]{1,0:T(1,128)S(1)}, u32[]{:S(2)}, u32[]{:S(2)}) collective-permute-start(s32[1,1024]{1,0:T(1,128)S(1)} %get-tuple-element.32), channel_id=1, source_target_pairs={{0,2},{1,3},{2,0},{3,1},{4,6},{5,7},{6,4},{7,5},{8,10},{9,11},{10,... | collective-permute-start | bytes 12296 | tf_op jit(solution)/shard_map/ppermute | solution.py:20
  8.0 24.5 %collective-permute-start.2 = (s32[1,1024]{1,0:T(1,128)S(1)}, s32[1,1024]{1,0:T(1,128)S(1)}, u32[]{:S(2)}, u32[]{:S(2)}) collective-permute-start(s32[1,1024]{1,0:T(1,128)S(1)} %get-tuple-element.35), channel_id=1, source_target_pairs={{0,1},{1,0},{2,3},{3,2},{4,5},{5,4},{6,7},{7,6},{8,9},{9,8},{10,11... | collective-permute-start | bytes 12296 | tf_op jit(solution)/shard_map/ppermute | solution.py:20
  9.6 25.9 %collective-permute-start.4 = (s32[1,1024]{1,0:T(1,128)S(1)}, s32[1,1024]{1,0:T(1,128)S(1)}, u32[]{:S(2)}, u32[]{:S(2)}) collective-permute-start(s32[1,1024]{1,0:T(1,128)S(1)} %get-tuple-element.34), channel_id=1, source_target_pairs={{0,3},{1,2},{2,1},{3,0},{4,7},{5,6},{6,5},{7,4},{8,11},{9,10},{10,... | collective-permute-start | bytes 12296 | tf_op jit(solution)/shard_map/ppermute | solution.py:20
  30.5 20.8 %collective-permute-start.1 = (bf16[512,256]{1,0:T(8,128)(2,1)S(1)}, bf16[512,256]{1,0:T(8,128)(2,1)S(1)}, u32[]{:S(2)}, u32[]{:S(2)}) collective-permute-start(bf16[512,256]{1,0:T(8,128)(2,1)S(1)} %fusion.27), channel_id=1, source_target_pairs={{0,2},{1,3},{2,0},{3,1},{4,6},{5,7},{6,4},{7,5},{8,10},{9,11},{10,... | collective-permute-start | bytes 786440 | tf_op jit(solution)/shard_map/ppermute | solution.py:20
  32.9 18.4 %collective-permute-start.3 = (bf16[512,256]{1,0:T(8,128)(2,1)S(1)}, bf16[512,256]{1,0:T(8,128)(2,1)S(1)}, u32[]{:S(2)}, u32[]{:S(2)}) collective-permute-start(bf16[512,256]{1,0:T(8,128)(2,1)S(1)} %fusion.26), channel_id=1, source_target_pairs={{0,1},{1,0},{2,3},{3,2},{4,5},{5,4},{6,7},{7,6},{8,9},{9,8},{10,11... | collective-permute-start | bytes 786440 | tf_op jit(solution)/shard_map/ppermute | solution.py:20
  36.0 15.3 %collective-permute-start.5 = (bf16[512,256]{1,0:T(8,128)(2,1)S(1)}, bf16[512,256]{1,0:T(8,128)(2,1)S(1)}, u32[]{:S(2)}, u32[]{:S(2)}) collective-permute-start(bf16[512,256]{1,0:T(8,128)(2,1)S(1)} %fusion.25), channel_id=1, source_target_pairs={{0,3},{1,2},{2,1},{3,0},{4,7},{5,6},{6,5},{7,4},{8,11},{9,10},{10,... | collective-permute-start | bytes 786440 | tf_op jit(solution)/shard_map/ppermute | solution.py:20
  51.5 3.7 %copy-start.4 = (bf16[512,256]{1,0:T(8,128)(2,1)}, bf16[512,256]{1,0:T(8,128)(2,1)S(1)}, u32[]{:S(2)}) copy-start(bf16[512,256]{1,0:T(8,128)(2,1)S(1)} %divide_convert_fusion) | copy-start | bytes 786436
  55.8 31.8 %copy-start.6 = (bf16[256,256]{0,1:T(8,128)(2,1)}, bf16[256,256]{0,1:T(8,128)(2,1)S(1)}, u32[]{:S(2)}) copy-start(bf16[256,256]{0,1:T(8,128)(2,1)S(1)} %get-tuple-element.27) | copy-start | bytes 393220
  55.8 31.0 %collective-permute-start.6 = (bf16[256,256]{0,1:T(8,128)(2,1)S(1)}, bf16[256,256]{0,1:T(8,128)(2,1)S(1)}, u32[]{:S(2)}, u32[]{:S(2)}) collective-permute-start(bf16[256,256]{0,1:T(8,128)(2,1)S(1)} %get-tuple-element.27), channel_id=1, source_target_pairs={{0,2},{1,3},{2,0},{3,1},{4,6},{5,7},{6,4},{7,5},{8,10},{9,11},{10,... | collective-permute-start | bytes 393224 | tf_op jit(solution)/shard_map/ppermute | solution.py:20
  62.0 24.8 %collective-permute-start.7 = (bf16[256,256]{0,1:T(8,128)(2,1)S(1)}, bf16[256,256]{0,1:T(8,128)(2,1)S(1)}, u32[]{:S(2)}, u32[]{:S(2)}) collective-permute-start(bf16[256,256]{0,1:T(8,128)(2,1)S(1)} %get-tuple-element.27), channel_id=1, source_target_pairs={{0,1},{1,0},{2,3},{3,2},{4,5},{5,4},{6,7},{7,6},{8,9},{9,8},{10,11... | collective-permute-start | bytes 393224 | tf_op jit(solution)/shard_map/ppermute | solution.py:20
  62.0 24.8 %collective-permute-start.8 = (bf16[256,256]{0,1:T(8,128)(2,1)S(1)}, bf16[256,256]{0,1:T(8,128)(2,1)S(1)}, u32[]{:S(2)}, u32[]{:S(2)}) collective-permute-start(bf16[256,256]{0,1:T(8,128)(2,1)S(1)} %get-tuple-element.27), channel_id=1, source_target_pairs={{0,3},{1,2},{2,1},{3,0},{4,7},{5,6},{6,5},{7,4},{8,11},{9,10},{10,... | collective-permute-start | bytes 393224 | tf_op jit(solution)/shard_map/ppermute | solution.py:20
  63.6 16.1 %collective-permute-start.9 = (bf16[256,256]{0,1:T(8,128)(2,1)S(1)}, bf16[256,256]{0,1:T(8,128)(2,1)S(1)}, u32[]{:S(2)}, u32[]{:S(2)}) collective-permute-start(bf16[256,256]{0,1:T(8,128)(2,1)S(1)} %get-tuple-element.26), channel_id=1, source_target_pairs={{0,2},{1,3},{2,0},{3,1},{4,6},{5,7},{6,4},{7,5},{8,10},{9,11},{10,... | collective-permute-start | bytes 393224 | tf_op jit(solution)/shard_map/ppermute | solution.py:20
  65.6 14.9 %collective-permute-start.10 = (bf16[256,256]{0,1:T(8,128)(2,1)S(1)}, bf16[256,256]{0,1:T(8,128)(2,1)S(1)}, u32[]{:S(2)}, u32[]{:S(2)}) collective-permute-start(bf16[256,256]{0,1:T(8,128)(2,1)S(1)} %get-tuple-element.26), channel_id=1, source_target_pairs={{0,1},{1,0},{2,3},{3,2},{4,5},{5,4},{6,7},{7,6},{8,9},{9,8},{10,11... | collective-permute-start | bytes 393224 | tf_op jit(solution)/shard_map/ppermute | solution.py:20
  79.7 7.1 %collective-permute-start.11 = (bf16[256,256]{0,1:T(8,128)(2,1)S(1)}, bf16[256,256]{0,1:T(8,128)(2,1)S(1)}, u32[]{:S(2)}, u32[]{:S(2)}) collective-permute-start(bf16[256,256]{0,1:T(8,128)(2,1)S(1)} %get-tuple-element.26), channel_id=1, source_target_pairs={{0,3},{1,2},{2,1},{3,0},{4,7},{5,6},{6,5},{7,4},{8,11},{9,10},{10,... | collective-permute-start | bytes 393224 | tf_op jit(solution)/shard_map/ppermute | solution.py:20
  98.7 2.4 %collective-permute-start.12 = (bf16[384,1024]{1,0:T(8,128)(2,1)S(1)}, bf16[384,1024]{1,0:T(8,128)(2,1)S(1)}, u32[]{:S(2)}, u32[]{:S(2)}) collective-permute-start(bf16[384,1024]{1,0:T(8,128)(2,1)S(1)} %maximum_maximum_fusion), channel_id=1, source_target_pairs={{0,4},{1,5},{2,6},{3,7},{4,0},{5,1},{6,2},{7,3},{8,12},{9,13},{10,... | collective-permute-start | bytes 2359304 | tf_op jit(solution)/shard_map/ppermute | solution.py:20
  101.4 7.8 %collective-permute-start.13 = (bf16[96,1024]{1,0:T(8,128)(2,1)S(1)}, bf16[96,1024]{1,0:T(8,128)(2,1)S(1)}, u32[]{:S(2)}, u32[]{:S(2)}) collective-permute-start(bf16[96,1024]{1,0:T(8,128)(2,1)S(1)} %get-tuple-element.9), channel_id=1, source_target_pairs={{0,8},{1,9},{2,10},{3,11},{4,12},{5,13},{6,14},{7,15},{8,0},{9,1},... | collective-permute-start | bytes 589832 | tf_op jit(solution)/shard_map/ppermute | solution.py:20
  102.9 10.9 %collective-permute-start.14 = (bf16[96,1024]{1,0:T(8,128)(2,1)S(1)}, bf16[96,1024]{1,0:T(8,128)(2,1)S(1)}, u32[]{:S(2)}, u32[]{:S(2)}) collective-permute-start(bf16[96,1024]{1,0:T(8,128)(2,1)S(1)} %get-tuple-element.11), channel_id=1, source_target_pairs={{0,16},{1,17},{2,18},{3,19},{4,20},{5,21},{6,22},{7,23},{8,24},{9,... | collective-permute-start | bytes 589832 | tf_op jit(solution)/shard_map/ppermute | solution.py:20
  104.4 9.4 %collective-permute-start.15 = (bf16[96,1024]{1,0:T(8,128)(2,1)S(1)}, bf16[96,1024]{1,0:T(8,128)(2,1)S(1)}, u32[]{:S(2)}, u32[]{:S(2)}) collective-permute-start(bf16[96,1024]{1,0:T(8,128)(2,1)S(1)} %get-tuple-element.10), channel_id=1, source_target_pairs={{0,24},{1,25},{2,26},{3,27},{4,28},{5,29},{6,30},{7,31},{8,16},{9,... | collective-permute-start | bytes 589832 | tf_op jit(solution)/shard_map/ppermute | solution.py:20
  113.9 4.5 %collective-permute-start.16 = (bf16[24,1024]{1,0:T(8,128)(2,1)S(1)}, bf16[24,1024]{1,0:T(8,128)(2,1)S(1)}, u32[]{:S(2)}, u32[]{:S(2)}) collective-permute-start(bf16[24,1024]{1,0:T(8,128)(2,1)S(1)} %get-tuple-element.19), channel_id=1, source_target_pairs={{0,1},{1,0},{2,3},{3,2},{4,5},{5,4},{6,7},{7,6},{8,9},{9,8},{10,11... | collective-permute-start | bytes 147464 | tf_op jit(solution)/shard_map/ppermute | solution.py:20
  114.0 5.7 %collective-permute-start.17 = (bf16[24,1024]{1,0:T(8,128)(2,1)S(1)}, bf16[24,1024]{1,0:T(8,128)(2,1)S(1)}, u32[]{:S(2)}, u32[]{:S(2)}) collective-permute-start(bf16[24,1024]{1,0:T(8,128)(2,1)S(1)} %get-tuple-element.21), channel_id=1, source_target_pairs={{0,2},{1,3},{2,0},{3,1},{4,6},{5,7},{6,4},{7,5},{8,10},{9,11},{10,... | collective-permute-start | bytes 147464 | tf_op jit(solution)/shard_map/ppermute | solution.py:20
  115.6 5.9 %collective-permute-start.18 = (bf16[24,1024]{1,0:T(8,128)(2,1)S(1)}, bf16[24,1024]{1,0:T(8,128)(2,1)S(1)}, u32[]{:S(2)}, u32[]{:S(2)}) collective-permute-start(bf16[24,1024]{1,0:T(8,128)(2,1)S(1)} %get-tuple-element.20), channel_id=1, source_target_pairs={{0,3},{1,2},{2,1},{3,0},{4,7},{5,6},{6,5},{7,4},{8,11},{9,10},{10,... | collective-permute-start | bytes 147464 | tf_op jit(solution)/shard_map/ppermute | solution.py:20
  121.5 6.0 %collective-permute-start.19 = (bf16[24,1024]{1,0:T(8,128)(2,1)S(1)}, bf16[24,1024]{1,0:T(8,128)(2,1)S(1)}, u32[]{:S(2)}, u32[]{:S(2)}) collective-permute-start(bf16[24,1024]{1,0:T(8,128)(2,1)S(1)} %add_convert_fusion), channel_id=1, source_target_pairs={{0,3},{1,2},{2,1},{3,0},{4,7},{5,6},{6,5},{7,4},{8,11},{9,10},{10,... | collective-permute-start | bytes 147464 | tf_op jit(solution)/shard_map/ppermute | solution.py:20
  124.4 5.0 %collective-permute-start.20 = (bf16[24,1024]{1,0:T(8,128)(2,1)S(1)}, bf16[24,1024]{1,0:T(8,128)(2,1)S(1)}, u32[]{:S(2)}, u32[]{:S(2)}) collective-permute-start(bf16[24,1024]{1,0:T(8,128)(2,1)S(1)} %add_convert_fusion), channel_id=1, source_target_pairs={{0,2},{1,3},{2,0},{3,1},{4,6},{5,7},{6,4},{7,5},{8,10},{9,11},{10,... | collective-permute-start | bytes 147464 | tf_op jit(solution)/shard_map/ppermute | solution.py:20
  124.4 5.0 %collective-permute-start.21 = (bf16[24,1024]{1,0:T(8,128)(2,1)S(1)}, bf16[24,1024]{1,0:T(8,128)(2,1)S(1)}, u32[]{:S(2)}, u32[]{:S(2)}) collective-permute-start(bf16[24,1024]{1,0:T(8,128)(2,1)S(1)} %add_convert_fusion), channel_id=1, source_target_pairs={{0,1},{1,0},{2,3},{3,2},{4,5},{5,4},{6,7},{7,6},{8,9},{9,8},{10,11... | collective-permute-start | bytes 147464 | tf_op jit(solution)/shard_map/ppermute | solution.py:20
  129.4 6.7 %collective-permute-start.22 = (bf16[96,1024]{1,0:T(8,128)(2,1)S(1)}, bf16[96,1024]{1,0:T(8,128)(2,1)S(1)}, u32[]{:S(2)}, u32[]{:S(2)}) collective-permute-start(bf16[96,1024]{1,0:T(8,128)(2,1)S(1)} %pad_maximum_fusion.3), channel_id=1, source_target_pairs={{0,24},{1,25},{2,26},{3,27},{4,28},{5,29},{6,30},{7,31},{8,16},{9,... | collective-permute-start | bytes 589832 | tf_op jit(solution)/shard_map/ppermute | solution.py:20
  131.0 7.2 %collective-permute-start.23 = (bf16[96,1024]{1,0:T(8,128)(2,1)S(1)}, bf16[96,1024]{1,0:T(8,128)(2,1)S(1)}, u32[]{:S(2)}, u32[]{:S(2)}) collective-permute-start(bf16[96,1024]{1,0:T(8,128)(2,1)S(1)} %pad_maximum_fusion.3), channel_id=1, source_target_pairs={{0,16},{1,17},{2,18},{3,19},{4,20},{5,21},{6,22},{7,23},{8,24},{9,... | collective-permute-start | bytes 589832 | tf_op jit(solution)/shard_map/ppermute | solution.py:20
  132.2 6.1 %collective-permute-start.24 = (bf16[96,1024]{1,0:T(8,128)(2,1)S(1)}, bf16[96,1024]{1,0:T(8,128)(2,1)S(1)}, u32[]{:S(2)}, u32[]{:S(2)}) collective-permute-start(bf16[96,1024]{1,0:T(8,128)(2,1)S(1)} %pad_maximum_fusion.3), channel_id=1, source_target_pairs={{0,8},{1,9},{2,10},{3,11},{4,12},{5,13},{6,14},{7,15},{8,0},{9,1},... | collective-permute-start | bytes 589832 | tf_op jit(solution)/shard_map/ppermute | solution.py:20
  138.7 2.4 %collective-permute-start.25 = (bf16[384,1024]{1,0:T(8,128)(2,1)S(1)}, bf16[384,1024]{1,0:T(8,128)(2,1)S(1)}, u32[]{:S(2)}, u32[]{:S(2)}) collective-permute-start(bf16[384,1024]{1,0:T(8,128)(2,1)S(1)} %pad_maximum_fusion), channel_id=1, source_target_pairs={{0,4},{1,5},{2,6},{3,7},{4,0},{5,1},{6,2},{7,3},{8,12},{9,13},{10,... | collective-permute-start | bytes 2359304 | tf_op jit(solution)/shard_map/ppermute | solution.py:20
  (5 other events, 7.1 us)

commit v2 on v1

--- a/solution.py
+++ b/solution.py
@@ -73,32 +73,42 @@
     valid = jnp.where(first_col, 1, nbr_mask)
     live_count = jnp.sum(valid.astype(F32), 1, keepdims=True)
     node_at = node_of_arrival(neighbour_slot, valid, blk_size)
-    order = sorted(range(1, blk_size), key=lambda j: (j != blk_size // 2, j))
+    order = sorted(range(1, blk_size), key=lambda j: (j < blk_size // 2, j))
     wanted = {
         j: exchange(block_of(node_at, own ^ j, blk_size), sizes, 0, j) for j in order
     }
     wanted[0] = block_of(node_at, own, blk_size)
     row_node = lax.broadcasted_iota(jnp.int32, (nodes, serve_rows.shape[1]), 0)
     total = None
+    sent = None
     for j in order + [0]:
         served = block_of(serve_rows, own ^ j, blk_size)[0]
+        if sent is not None:
+            served, sent = lax.optimization_barrier((served, sent))
+            arrived = exchange(sent, sizes, 0, previous).astype(F32)
+            total = arrived if total is None else total + arrived
         rows = feat_store.at[served].get(mode="promise_in_bounds")
         pick = (row_node == wanted[j]).astype(BF16)
         part = jnp.dot(pick, rows, preferred_element_type=F32)
-        if j:
-            part = exchange(part.astype(BF16), sizes, 0, j).astype(F32)
-        total = part if total is None else total + part
-    return (total / live_count).astype(BF16)
-
-
-def pair_gradients(embedding, own, sizes):
+        sent, previous = part.astype(BF16), j
+    return ((total + part) / live_count).astype(BF16)
+
+
+def spread(block, sizes):
     blk_size = sizes[1]
-    pairs = embedding.shape[0] // 2
-    scale = embedding.shape[1] ** (-0.5)
-    queries, items = embedding[:pairs], embedding[pairs:]
-    order = sorted(range(1, blk_size), key=lambda j: (j != blk_size // 2, j))
-    other_items = [exchange(items, sizes, 0, j) for j in order]
-    other_queries = [exchange(queries, sizes, 0, j) for j in order]
+    known = {0: block}
+    bit = blk_size // 2
+    while bit:
+        known.update({j ^ bit: exchange(v, sizes, 0, bit) for j, v in list(known.items())})
+        bit //= 2
+    return [known[j] for j in range(1, blk_size)]
+
+
+def pair_gradients(queries, items, sizes):
+    pairs = queries.shape[0]
+    scale = queries.shape[1] ** (-0.5)
+    other_items = spread(items, sizes)
+    other_queries = spread(queries, sizes)
     cycle = jnp.concatenate([items] + other_items, 0)
     columns = cycle.shape[0]
 
@@ -111,11 +121,10 @@
 
     weights = weights_of(queries, cycle, positive_of(queries, items))
     row_total = jnp.sum(weights, 1, keepdims=True)
-    diagonal = lax.broadcasted_iota(jnp.int32, weights.shape, 0) == lax.broadcasted_iota(
-        jnp.int32, weights.shape, 1
-    )
-    tile = jnp.where(diagonal, weights - row_total, weights).astype(BF16)
-    d_query = jnp.dot(tile, cycle, preferred_element_type=F32) * scale
+    tile = weights.astype(BF16)
+    d_query = (
+        jnp.dot(tile, cycle, preferred_element_type=F32) - row_total * items.astype(F32)
+    ) * scale
     remote_queries = jnp.concatenate(other_queries, 0)
     remote_tile = weights_of(
         remote_queries, items, positive_of(remote_queries, cycle[pairs:])
@@ -123,8 +132,9 @@
     d_item = (
         lax.dot_general(tile[:, :pairs], queries, OVER_ROWS, preferred_element_type=F32)
         + lax.dot_general(remote_tile, remote_queries, OVER_ROWS, preferred_element_type=F32)
+        - row_total * queries.astype(F32)
     ) * scale
-    return jnp.concatenate([d_query, d_item], 0)
+    return d_query, d_item
 
 
 def sum_staged(g_in, g_out, group, own, sizes):
@@ -185,14 +195,20 @@
     projected = jnp.dot(hidden, w_out, preferred_element_type=F32)
     inv_norm = lax.rsqrt(jnp.mean(projected * projected, 1, keepdims=True) + 1e-06)
     embedding = (projected * inv_norm).astype(BF16)
-    d_embed = pair_gradients(embedding, own, sizes)
-    interior_term = jnp.mean(d_embed * projected, 1, keepdims=True)
-    d_proj = (inv_norm * d_embed - projected * inv_norm**3 * interior_term).astype(BF16)
-    g_out = lax.dot_general(hidden, d_proj, OVER_ROWS, preferred_element_type=F32)
-    d_hidden = lax.dot_general(d_proj, w_out, (((1,), (1,)), ((), ())), preferred_element_type=F32)
-    d_pre = (d_hidden * gate_sig * (1.0 + pre_act * (1.0 - gate_sig))).astype(BF16)
+    pairs = embedding.shape[0] // 2
     inputs = jnp.concatenate([self_feat, pooled], 1)
-    g_in = lax.dot_general(inputs, d_pre, OVER_ROWS, preferred_element_type=F32)
+    g_in = g_out = 0.0
+    for half, d_embed in enumerate(pair_gradients(embedding[:pairs], embedding[pairs:], sizes)):
+        rows = slice(half * pairs, (half + 1) * pairs)
+        inv, proj, pre, sig = inv_norm[rows], projected[rows], pre_act[rows], gate_sig[rows]
+        interior_term = jnp.mean(d_embed * proj, 1, keepdims=True)
+        d_proj = (inv * d_embed - proj * inv**3 * interior_term).astype(BF16)
+        d_hidden = lax.dot_general(
+            d_proj, w_out, (((1,), (1,)), ((), ())), preferred_element_type=F32
+        )
+        d_pre = (d_hidden * sig * (1.0 + pre * (1.0 - sig))).astype(BF16)
+        g_out += lax.dot_general(hidden[rows], d_proj, OVER_ROWS, preferred_element_type=F32)
+        g_in += lax.dot_general(inputs[rows], d_pre, OVER_ROWS, preferred_element_type=F32)
     staged = (dp_size & (dp_size - 1)) == 0 and dp_size > 1
     if staged and g_in.shape[0] % (8 * dp_size * blk_size) == 0:
         return sum_staged(g_in, g_out, group, own, sizes)

time: 145 us -> 136 us (0.938)
  waiting for transfers between devices: 51.6 us -> 41.8 us
  starting transfers between devices: 37.8 us -> 31 us
  other arithmetic: 6.67 us -> 11.3 us
  matrix products: 17.9 us -> 19.9 us
  local copies, waits for them, and re-layouts: 28.7 us -> 30.3 us
    ppermute x26, waiting for transfers between devices: 51.6 us -> 41.8 us  [exchange(): return lax.ppermute(value, AXES, pairs)]
    ppermute x26, starting transfers between devices: 37.8 us -> 31 us  [exchange(): return lax.ppermute(value, AXES, pairs)]
    slice x2, local copies, waits for them, and re-layouts: 0.06 us -> 1.94 us  [half(): g_out_half[k * rows:(k + 1) * rows]]
    convert_element_type x3 -> x2, other arithmetic: 0.35 us -> 2.2 us  [the longest x1 1.12 us: on_device(): d_proj = (inv * d_embed - proj * inv ** 3 * interior_term).astype(BF16)]
    dot_general x3 -> x5, matrix products: 6.4 us -> 7.84 us  [the longest x2 6.11 us: on_device(): lax.dot_general(inputs[rows], d_pre, OVER_ROWS, preferred_element_type=F32)]
  transfers between devices with their start and end apart: 26 -> 26, of which waited for: 14 -> 16; matrix products, arithmetic and copies ran while one was open for 21% -> 22% of each run, Pallas kernels for 0% -> 0%
where the time goes in v2:
time: 136 us
  waiting for transfers between devices  41.8 us (31%)
  starting transfers between devices  31 us (23%)
  local copies, waits for them, and re-layouts  30.3 us (22%)
  matrix products  19.9 us (15%)
  other arithmetic  11.3 us (8%)
    ppermute x26, waiting for transfers between devices, exchange(): return lax.ppermute(value, AXES, pairs)  41.8 us
    ppermute x26, starting transfers between devices, exchange(): return lax.ppermute(value, AXES, pairs)  31 us
    gather x4, local copies, waits for them, and re-layouts, pooled_mean(): rows = feat_store.at[served].get(mode='promise_in_bounds')  24.9 us
    dot_general x2, matrix products, on_device(): lax.dot_general(inputs[rows], d_pre, OVER_ROWS, preferred_element_type=F32)  6.11 us
    dot_general x1, matrix products, pair_gradients(): lax.dot_general(remote_tile, remote_queries, OVER_ROWS, preferred_element...  2.92 us
    dot_general x1, matrix products, on_device(): jnp.dot(pooled, w_nbr, preferred_element_type=F32)  2.73 us
  transfers between devices with their start and end apart: 26, of which 16 were waited for; matrix products, arithmetic and copies ran while one was open for 22% of the time, Pallas kernels for 0%

profile of v2, /device:TPU:0, one launch (start us, length us, event | category | flops | bytes accessed | tf_op | source)
XLA Modules:
  0.0 135.5 jit_solution(11872465397126642787)
XLA Ops:
  3.9 3.1 %collective-permute-start.4 = (s32[1,1024]{1,0:T(1,128)S(1)}, s32[1,1024]{1,0:T(1,128)S(1)}, u32[]{:S(2)}, u32[]{:S(2)}) collective-permute-start(s32[1,1024]{1,0:T(1,128)S(1)} %get-tuple-element.53), channel_id=1, source_target_pairs={{0,1},{1,0},{2,3},{3,2},{4,5},{5,4},{6,7},{7,6},{8,9},{9,8},{10,11... | collective-permute-start | bytes 12296 | tf_op jit(solution)/shard_map/ppermute | solution.py:20
  7.0 2.5 %collective-permute-start.2 = (s32[1,1024]{1,0:T(1,128)S(1)}, s32[1,1024]{1,0:T(1,128)S(1)}, u32[]{:S(2)}, u32[]{:S(2)}) collective-permute-start(s32[1,1024]{1,0:T(1,128)S(1)} %get-tuple-element.54), channel_id=1, source_target_pairs={{0,3},{1,2},{2,1},{3,0},{4,7},{5,6},{6,5},{7,4},{8,11},{9,10},{10,... | collective-permute-start | bytes 12296 | tf_op jit(solution)/shard_map/ppermute | solution.py:20
  9.6 6.2 %gather_fusion = bf16[1024,256]{1,0:T(8,128)(2,1)S(1)} fusion(bf16[8192,256]{1,0:T(8,128)(2,1)} %param.12, s32[1024]{0:T(1024)S(1)} %broadcast_clamp_fusion), kind=kCustom, calls=%fused_computation | custom fusion | bytes 1052672 | tf_op jit(solution)/shard_map/gather | solution.py:90
  16.3 2.9 %collective-permute-start.1 = (bf16[512,256]{1,0:T(8,128)(2,1)S(1)}, bf16[512,256]{1,0:T(8,128)(2,1)S(1)}, u32[]{:S(2)}, u32[]{:S(2)}) collective-permute-start(bf16[512,256]{1,0:T(8,128)(2,1)S(1)} %fusion.31), channel_id=1, source_target_pairs={{0,2},{1,3},{2,0},{3,1},{4,6},{5,7},{6,4},{7,5},{8,10},{9,11},{10,... | collective-permute-start | bytes 786440 | tf_op jit(solution)/shard_map/ppermute | solution.py:20
  19.2 6.2 %gather_fusion.1 = bf16[1024,256]{1,0:T(8,128)(2,1)S(1)} fusion(bf16[8192,256]{1,0:T(8,128)(2,1)} %param.12, s32[1024]{0:T(1024)S(1)} %fusion.81), kind=kCustom, calls=%fused_computation.1 | custom fusion | bytes 1052672 | tf_op jit(solution)/shard_map/gather | solution.py:90
  27.3 6.2 %gather_fusion.2 = bf16[1024,256]{1,0:T(8,128)(2,1)S(1)} fusion(bf16[8192,256]{1,0:T(8,128)(2,1)} %param.12, s32[1024]{0:T(1024)S(1)} %fusion.82), kind=kCustom, calls=%fused_computation.2 | custom fusion | bytes 1052672 | tf_op jit(solution)/shard_map/gather | solution.py:90
  34.1 1.8 %fusion.105 = f32[512,1024]{1,0:T(8,128)} fusion(bf16[512,256]{1,0:T(8,128)(2,1)S(1)} %copy-done.4, bf16[256,1024]{1,0:T(8,128)(2,1)S(1)} %copy-done.8), kind=kOutput, calls=%fused_computation.219 | convolution fusion | flops 268435456 | bytes 2883584 | tf_op jit(solution)/shard_map/dot_general | solution.py:190
  35.9 6.4 %gather_fusion.3 = bf16[1024,256]{1,0:T(8,128)(2,1)S(1)} fusion(bf16[8192,256]{1,0:T(8,128)(2,1)} %param.12, s32[1024]{0:T(1024)S(1)} %fusion.83), kind=kCustom, calls=%fused_computation.3 | custom fusion | bytes 1052672 | tf_op jit(solution)/shard_map/gather | solution.py:90
  43.9 2.7 %add_divide_fusion = (f32[512,1024]{1,0:T(8,128)}, bf16[512,1024]{1,0:T(8,128)(2,1)S(1)}, f32[512,1024]{1,0:T(8,128)}) fusion(f32[512,1024]{1,0:T(8,128)S(1)} %copy-done.5, bf16[512,256]{1,0:T(8,128)(2,1)S(1)} %divide_convert_fusion, bf16[256,1024]{1,0:T(8,128)(2,1)S(1)} %copy-done), kind=kOutput, calls=%fused_computation.9 | convolution fusion | flops 271581184 | bytes 8126464 | tf_op jit(solution)/shard_map/dot_general | solution.py:190
  47.3 2.1 %collective-permute-start.9 = (bf16[256,256]{0,1:T(8,128)(2,1)S(1)}, bf16[256,256]{0,1:T(8,128)(2,1)S(1)}, u32[]{:S(2)}, u32[]{:S(2)}) collective-permute-start(bf16[256,256]{0,1:T(8,128)(2,1)S(1)} %get-tuple-element.46), channel_id=1, source_target_pairs={{0,1},{1,0},{2,3},{3,2},{4,5},{5,4},{6,7},{7,6},{8,9},{9,8},{10,11... | collective-permute-start | bytes 393224 | tf_op jit(solution)/shard_map/ppermute | solution.py:20
  50.4 1.8 %collective-permute-start.7 = (bf16[256,256]{0,1:T(8,128)(2,1)S(1)}, bf16[256,256]{0,1:T(8,128)(2,1)S(1)}, u32[]{:S(2)}, u32[]{:S(2)}) collective-permute-start(bf16[256,256]{0,1:T(8,128)(2,1)S(1)} %get-tuple-element.47), channel_id=1, source_target_pairs={{0,2},{1,3},{2,0},{3,1},{4,6},{5,7},{6,4},{7,5},{8,10},{9,11},{10,... | collective-permute-start | bytes 393224 | tf_op jit(solution)/shard_map/ppermute | solution.py:20
  52.4 6.9 %collective-permute-done.10 = bf16[256,256]{0,1:T(8,128)(2,1)S(1)} collective-permute-done((bf16[256,256]{0,1:T(8,128)(2,1)S(1)}, bf16[256,256]{0,1:T(8,128)(2,1)S(1)}, u32[]{:S(2)}, u32[]{:S(2)}) %collective-permute-start.10) | collective-permute-done | bytes 131104 | tf_op jit(solution)/shard_map/ppermute | solution.py:20
  59.6 2.4 %collective-permute-done.7 = bf16[256,256]{0,1:T(8,128)(2,1)S(1)} collective-permute-done((bf16[256,256]{0,1:T(8,128)(2,1)S(1)}, bf16[256,256]{0,1:T(8,128)(2,1)S(1)}, u32[]{:S(2)}, u32[]{:S(2)}) %collective-permute-start.7) | collective-permute-done | bytes 131104 | tf_op jit(solution)/shard_map/ppermute | solution.py:20
  62.3 2.4 %collective-permute-done.11 = bf16[256,256]{0,1:T(8,128)(2,1)S(1)} collective-permute-done((bf16[256,256]{0,1:T(8,128)(2,1)S(1)}, bf16[256,256]{0,1:T(8,128)(2,1)S(1)}, u32[]{:S(2)}, u32[]{:S(2)}) %collective-permute-start.11) | collective-permute-done | bytes 131104 | tf_op jit(solution)/shard_map/ppermute | solution.py:20
  64.7 2.2 %collective-permute-done.8 = bf16[256,256]{0,1:T(8,128)(2,1)S(1)} collective-permute-done((bf16[256,256]{0,1:T(8,128)(2,1)S(1)}, bf16[256,256]{0,1:T(8,128)(2,1)S(1)}, u32[]{:S(2)}, u32[]{:S(2)}) %collective-permute-start.8) | collective-permute-done | bytes 131104 | tf_op jit(solution)/shard_map/ppermute | solution.py:20
  70.2 2.9 %multiply_reduce_fusion.2 = (f32[256]{0:T(256)}, f32[256]{0:T(256)}, f32[256,256]{0,1:T(8,128)}) fusion(f32[512,256]{0,1:T(8,128)S(1)} %get-tuple-element.71, f32[256,256]{0,1:T(8,128)} %convolution_subtract_fusion, bf16[512,256]{0,1:T(8,128)(2,1)S(1)} %multiply_convert_fusion.1, f32[256]{0:T(256)} %copy-done.10, f32[256,256]{0,1:T(8,128)} %fusion.64, ...), kind=kOutput, calls=%fused_computation.107 | convolution fusion | flops 203554304 | bytes 2365440 | tf_op jit(solution)/shard_map/dot_general | solution.py:134
  76.7 2.4 %fusion.27 = f32[512,1024]{1,0:T(8,128)S(1)} fusion(bf16[256,256]{0,1:T(8,128)(2,1)} %copy-done.6, bf16[1024,256]{1,0:T(8,128)(2,1)S(1)} %copy-done.2, f32[512,1024]{1,0:T(8,128)} %get-tuple-element.69, f32[512,1024]{1,0:T(8,128)} %get-tuple-element.21, bf16[512,256]{1,0:T(8,128)(2,1)S(1)} %copy-done.4, bf16[512,256]{1,0:T(8,128)(2,1)} %copy-done.7), kind=kOutput, calls=%fused_computation.48 | convolution fusion | flops 404750336 | bytes 5373952 | tf_op jit(solution)/shard_map/dot_general | solution.py:211
  79.1 3.7 %convolution_add_fusion = f32[512,1024]{1,0:T(8,128)} fusion(f32[512,1024]{1,0:T(8,128)S(1)} %fusion.27, bf16[256,256]{0,1:T(8,128)(2,1)S(1)} %get-tuple-element.37, bf16[1024,256]{1,0:T(8,128)(2,1)S(1)} %copy-done.2, f32[512,1024]{1,0:T(8,128)} %get-tuple-element.69, f32[512,1024]{1,0:T(8,128)} %get-tuple-element.21, bf16[512,256]{1,0:T(8,128)(2,1)} %copy-done.7, ...), kind=kOutput, calls=%fused_computation.21 | convolution fusion | flops 405274624 | bytes 7471104 | tf_op jit(solution)/shard_map/dot_general | solution.py:211
  89.2 1.6 %collective-permute-start.13 = (bf16[96,1024]{1,0:T(8,128)(2,1)S(1)}, bf16[96,1024]{1,0:T(8,128)(2,1)S(1)}, u32[]{:S(2)}, u32[]{:S(2)}) collective-permute-start(bf16[96,1024]{1,0:T(8,128)(2,1)S(1)} %get-tuple-element.25), channel_id=1, source_target_pairs={{0,8},{1,9},{2,10},{3,11},{4,12},{5,13},{6,14},{7,15},{8,0},{9,1},... | collective-permute-start | bytes 589832 | tf_op jit(solution)/shard_map/ppermute | solution.py:20
  92.8 4.3 %collective-permute-done.13 = bf16[96,1024]{1,0:T(8,128)(2,1)S(1)} collective-permute-done((bf16[96,1024]{1,0:T(8,128)(2,1)S(1)}, bf16[96,1024]{1,0:T(8,128)(2,1)S(1)}, u32[]{:S(2)}, u32[]{:S(2)}) %collective-permute-start.13) | collective-permute-done | bytes 196640 | tf_op jit(solution)/shard_map/ppermute | solution.py:20
  97.0 4.5 %collective-permute-done.15 = bf16[96,1024]{1,0:T(8,128)(2,1)S(1)} collective-permute-done((bf16[96,1024]{1,0:T(8,128)(2,1)S(1)}, bf16[96,1024]{1,0:T(8,128)(2,1)S(1)}, u32[]{:S(2)}, u32[]{:S(2)}) %collective-permute-start.15) | collective-permute-done | bytes 196640 | tf_op jit(solution)/shard_map/ppermute | solution.py:20
  103.5 2.5 %collective-permute-start.18 = (bf16[24,1024]{1,0:T(8,128)(2,1)S(1)}, bf16[24,1024]{1,0:T(8,128)(2,1)S(1)}, u32[]{:S(2)}, u32[]{:S(2)}) collective-permute-start(bf16[24,1024]{1,0:T(8,128)(2,1)S(1)} %get-tuple-element.40), channel_id=1, source_target_pairs={{0,3},{1,2},{2,1},{3,0},{4,7},{5,6},{6,5},{7,4},{8,11},{9,10},{10,... | collective-permute-start | bytes 147464 | tf_op jit(solution)/shard_map/ppermute | solution.py:20
  107.5 1.9 %collective-permute-done.18 = bf16[24,1024]{1,0:T(8,128)(2,1)S(1)} collective-permute-done((bf16[24,1024]{1,0:T(8,128)(2,1)S(1)}, bf16[24,1024]{1,0:T(8,128)(2,1)S(1)}, u32[]{:S(2)}, u32[]{:S(2)}) %collective-permute-start.18) | collective-permute-done | bytes 49184 | tf_op jit(solution)/shard_map/ppermute | solution.py:20
  109.4 1.6 %collective-permute-done.17 = bf16[24,1024]{1,0:T(8,128)(2,1)S(1)} collective-permute-done((bf16[24,1024]{1,0:T(8,128)(2,1)S(1)}, bf16[24,1024]{1,0:T(8,128)(2,1)S(1)}, u32[]{:S(2)}, u32[]{:S(2)}) %collective-permute-start.17) | collective-permute-done | bytes 49184 | tf_op jit(solution)/shard_map/ppermute | solution.py:20
  111.0 1.5 %collective-permute-start.21 = (bf16[24,1024]{1,0:T(8,128)(2,1)S(1)}, bf16[24,1024]{1,0:T(8,128)(2,1)S(1)}, u32[]{:S(2)}, u32[]{:S(2)}) collective-permute-start(bf16[24,1024]{1,0:T(8,128)(2,1)S(1)} %add_convert_fusion), channel_id=1, source_target_pairs={{0,1},{1,0},{2,3},{3,2},{4,5},{5,4},{6,7},{7,6},{8,9},{9,8},{10,11... | collective-permute-start | bytes 147464 | tf_op jit(solution)/shard_map/ppermute | solution.py:20
  113.8 1.7 %collective-permute-start.19 = (bf16[24,1024]{1,0:T(8,128)(2,1)S(1)}, bf16[24,1024]{1,0:T(8,128)(2,1)S(1)}, u32[]{:S(2)}, u32[]{:S(2)}) collective-permute-start(bf16[24,1024]{1,0:T(8,128)(2,1)S(1)} %add_convert_fusion), channel_id=1, source_target_pairs={{0,3},{1,2},{2,1},{3,0},{4,7},{5,6},{6,5},{7,4},{8,11},{9,10},{10,... | collective-permute-start | bytes 147464 | tf_op jit(solution)/shard_map/ppermute | solution.py:20
  115.5 2.6 %collective-permute-done.20 = bf16[24,1024]{1,0:T(8,128)(2,1)S(1)} collective-permute-done((bf16[24,1024]{1,0:T(8,128)(2,1)S(1)}, bf16[24,1024]{1,0:T(8,128)(2,1)S(1)}, u32[]{:S(2)}, u32[]{:S(2)}) %collective-permute-start.20) | collective-permute-done | bytes 49184 | tf_op jit(solution)/shard_map/ppermute | solution.py:20
  118.0 1.6 %collective-permute-done.19 = bf16[24,1024]{1,0:T(8,128)(2,1)S(1)} collective-permute-done((bf16[24,1024]{1,0:T(8,128)(2,1)S(1)}, bf16[24,1024]{1,0:T(8,128)(2,1)S(1)}, u32[]{:S(2)}, u32[]{:S(2)}) %collective-permute-start.19) | collective-permute-done | bytes 49184 | tf_op jit(solution)/shard_map/ppermute | solution.py:20
  119.7 1.5 %collective-permute-start.24 = (bf16[96,1024]{1,0:T(8,128)(2,1)S(1)}, bf16[96,1024]{1,0:T(8,128)(2,1)S(1)}, u32[]{:S(2)}, u32[]{:S(2)}) collective-permute-start(bf16[96,1024]{1,0:T(8,128)(2,1)S(1)} %pad_maximum_fusion.4), channel_id=1, source_target_pairs={{0,8},{1,9},{2,10},{3,11},{4,12},{5,13},{6,14},{7,15},{8,0},{9,1},... | collective-permute-start | bytes 589832 | tf_op jit(solution)/shard_map/ppermute | solution.py:20
  123.3 2.2 %collective-permute-done.24 = bf16[96,1024]{1,0:T(8,128)(2,1)S(1)} collective-permute-done((bf16[96,1024]{1,0:T(8,128)(2,1)S(1)}, bf16[96,1024]{1,0:T(8,128)(2,1)S(1)}, u32[]{:S(2)}, u32[]{:S(2)}) %collective-permute-start.24) | collective-permute-done | bytes 196640 | tf_op jit(solution)/shard_map/ppermute | solution.py:20
  125.4 3.6 %collective-permute-done.23 = bf16[96,1024]{1,0:T(8,128)(2,1)S(1)} collective-permute-done((bf16[96,1024]{1,0:T(8,128)(2,1)S(1)}, bf16[96,1024]{1,0:T(8,128)(2,1)S(1)}, u32[]{:S(2)}, u32[]{:S(2)}) %collective-permute-start.23) | collective-permute-done | bytes 196640 | tf_op jit(solution)/shard_map/ppermute | solution.py:20
  129.5 2.3 %collective-permute-done.25 = bf16[384,1024]{1,0:T(8,128)(2,1)S(1)} collective-permute-done((bf16[384,1024]{1,0:T(8,128)(2,1)S(1)}, bf16[384,1024]{1,0:T(8,128)(2,1)S(1)}, u32[]{:S(2)}, u32[]{:S(2)}) %collective-permute-start.25) | collective-permute-done | bytes 786464 | tf_op jit(solution)/shard_map/ppermute | solution.py:20
  (122 shorter events, 36.3 us)
Async XLA Ops:
  0.6 42.2 %copy-start = (bf16[256,1024]{1,0:T(8,128)(2,1)S(1)}, bf16[256,1024]{1,0:T(8,128)(2,1)}, u32[]{:S(2)}) copy-start(bf16[256,1024]{1,0:T(8,128)(2,1)} %param.14) | copy-start | bytes 1572868
  3.0 6.5 %copy-start.9 = (s32[4,1024]{1,0:T(4,128)S(1)}, s32[4,1024]{1,0:T(4,128)}, u32[]{:S(2)}) copy-start(s32[4,1024]{1,0:T(4,128)} %param.11) | copy-start | bytes 49156
  3.9 29.6 %collective-permute-start.4 = (s32[1,1024]{1,0:T(1,128)S(1)}, s32[1,1024]{1,0:T(1,128)S(1)}, u32[]{:S(2)}, u32[]{:S(2)}) collective-permute-start(s32[1,1024]{1,0:T(1,128)S(1)} %get-tuple-element.53), channel_id=1, source_target_pairs={{0,1},{1,0},{2,3},{3,2},{4,5},{5,4},{6,7},{7,6},{8,9},{9,8},{10,11... | collective-permute-start | bytes 12296 | tf_op jit(solution)/shard_map/ppermute | solution.py:20
  7.0 18.4 %collective-permute-start.2 = (s32[1,1024]{1,0:T(1,128)S(1)}, s32[1,1024]{1,0:T(1,128)S(1)}, u32[]{:S(2)}, u32[]{:S(2)}) collective-permute-start(s32[1,1024]{1,0:T(1,128)S(1)} %get-tuple-element.54), channel_id=1, source_target_pairs={{0,3},{1,2},{2,1},{3,0},{4,7},{5,6},{6,5},{7,4},{8,11},{9,10},{10,... | collective-permute-start | bytes 12296 | tf_op jit(solution)/shard_map/ppermute | solution.py:20
  9.4 6.4 %collective-permute-start = (s32[1,1024]{1,0:T(1,128)S(1)}, s32[1,1024]{1,0:T(1,128)S(1)}, u32[]{:S(2)}, u32[]{:S(2)}) collective-permute-start(s32[1,1024]{1,0:T(1,128)S(1)} %get-tuple-element.55), channel_id=1, source_target_pairs={{0,2},{1,3},{2,0},{3,1},{4,6},{5,7},{6,4},{7,5},{8,10},{9,11},{10,... | collective-permute-start | bytes 12296 | tf_op jit(solution)/shard_map/ppermute | solution.py:20
  16.3 26.0 %collective-permute-start.1 = (bf16[512,256]{1,0:T(8,128)(2,1)S(1)}, bf16[512,256]{1,0:T(8,128)(2,1)S(1)}, u32[]{:S(2)}, u32[]{:S(2)}) collective-permute-start(bf16[512,256]{1,0:T(8,128)(2,1)S(1)} %fusion.31), channel_id=1, source_target_pairs={{0,2},{1,3},{2,0},{3,1},{4,6},{5,7},{6,4},{7,5},{8,10},{9,11},{10,... | collective-permute-start | bytes 786440 | tf_op jit(solution)/shard_map/ppermute | solution.py:20
  25.9 8.2 %copy-start.4 = (bf16[512,256]{1,0:T(8,128)(2,1)S(1)}, bf16[512,256]{1,0:T(8,128)(2,1)}, u32[]{:S(2)}) copy-start(bf16[512,256]{1,0:T(8,128)(2,1)} %param.8) | copy-start | bytes 786436
  25.9 8.2 %copy-start.8 = (bf16[256,1024]{1,0:T(8,128)(2,1)S(1)}, bf16[256,1024]{1,0:T(8,128)(2,1)}, u32[]{:S(2)}) copy-start(bf16[256,1024]{1,0:T(8,128)(2,1)} %param.13) | copy-start | bytes 1572868
  25.9 16.4 %collective-permute-start.3 = (bf16[512,256]{1,0:T(8,128)(2,1)S(1)}, bf16[512,256]{1,0:T(8,128)(2,1)S(1)}, u32[]{:S(2)}, u32[]{:S(2)}) collective-permute-start(bf16[512,256]{1,0:T(8,128)(2,1)S(1)} %fusion.30), channel_id=1, source_target_pairs={{0,3},{1,2},{2,1},{3,0},{4,7},{5,6},{6,5},{7,4},{8,11},{9,10},{10,... | collective-permute-start | bytes 786440 | tf_op jit(solution)/shard_map/ppermute | solution.py:20
  34.0 8.3 %collective-permute-start.5 = (bf16[512,256]{1,0:T(8,128)(2,1)S(1)}, bf16[512,256]{1,0:T(8,128)(2,1)S(1)}, u32[]{:S(2)}, u32[]{:S(2)}) collective-permute-start(bf16[512,256]{1,0:T(8,128)(2,1)S(1)} %fusion.29), channel_id=1, source_target_pairs={{0,1},{1,0},{2,3},{3,2},{4,5},{5,4},{6,7},{7,6},{8,9},{9,8},{10,11... | collective-permute-start | bytes 786440 | tf_op jit(solution)/shard_map/ppermute | solution.py:20
  43.8 2.7 %copy-start.2 = (bf16[1024,256]{1,0:T(8,128)(2,1)S(1)}, bf16[1024,256]{1,0:T(8,128)(2,1)}, u32[]{:S(2)}) copy-start(bf16[1024,256]{1,0:T(8,128)(2,1)} %param.15) | copy-start | bytes 1572868
  47.3 15.0 %collective-permute-start.9 = (bf16[256,256]{0,1:T(8,128)(2,1)S(1)}, bf16[256,256]{0,1:T(8,128)(2,1)S(1)}, u32[]{:S(2)}, u32[]{:S(2)}) collective-permute-start(bf16[256,256]{0,1:T(8,128)(2,1)S(1)} %get-tuple-element.46), channel_id=1, source_target_pairs={{0,1},{1,0},{2,3},{3,2},{4,5},{5,4},{6,7},{7,6},{8,9},{9,8},{10,11... | collective-permute-start | bytes 393224 | tf_op jit(solution)/shard_map/ppermute | solution.py:20
  49.3 10.0 %collective-permute-start.10 = (bf16[256,256]{0,1:T(8,128)(2,1)S(1)}, bf16[256,256]{0,1:T(8,128)(2,1)S(1)}, u32[]{:S(2)}, u32[]{:S(2)}) collective-permute-start(bf16[256,256]{0,1:T(8,128)(2,1)S(1)} %get-tuple-element.46), channel_id=1, source_target_pairs={{0,2},{1,3},{2,0},{3,1},{4,6},{5,7},{6,4},{7,5},{8,10},{9,11},{10,... | collective-permute-start | bytes 393224 | tf_op jit(solution)/shard_map/ppermute | solution.py:20
  50.4 11.5 %collective-permute-start.7 = (bf16[256,256]{0,1:T(8,128)(2,1)S(1)}, bf16[256,256]{0,1:T(8,128)(2,1)S(1)}, u32[]{:S(2)}, u32[]{:S(2)}) collective-permute-start(bf16[256,256]{0,1:T(8,128)(2,1)S(1)} %get-tuple-element.47), channel_id=1, source_target_pairs={{0,2},{1,3},{2,0},{3,1},{4,6},{5,7},{6,4},{7,5},{8,10},{9,11},{10,... | collective-permute-start | bytes 393224 | tf_op jit(solution)/shard_map/ppermute | solution.py:20
  52.2 12.5 %collective-permute-start.6 = (bf16[256,256]{0,1:T(8,128)(2,1)S(1)}, bf16[256,256]{0,1:T(8,128)(2,1)S(1)}, u32[]{:S(2)}, u32[]{:S(2)}) collective-permute-start(bf16[256,256]{0,1:T(8,128)(2,1)S(1)} %get-tuple-element.47), channel_id=1, source_target_pairs={{0,1},{1,0},{2,3},{3,2},{4,5},{5,4},{6,7},{7,6},{8,9},{9,8},{10,11... | collective-permute-start | bytes 393224 | tf_op jit(solution)/shard_map/ppermute | solution.py:20
  59.3 5.4 %collective-permute-start.11 = (bf16[256,256]{0,1:T(8,128)(2,1)S(1)}, bf16[256,256]{0,1:T(8,128)(2,1)S(1)}, u32[]{:S(2)}, u32[]{:S(2)}) collective-permute-start(bf16[256,256]{0,1:T(8,128)(2,1)S(1)} %collective-permute-done.10), channel_id=1, source_target_pairs={{0,1},{1,0},{2,3},{3,2},{4,5},{5,4},{6,7},{7,6},{8,9},{9,8},{10,11... | collective-permute-start | bytes 393224 | tf_op jit(solution)/shard_map/ppermute | solution.py:20
  61.9 5.0 %collective-permute-start.8 = (bf16[256,256]{0,1:T(8,128)(2,1)S(1)}, bf16[256,256]{0,1:T(8,128)(2,1)S(1)}, u32[]{:S(2)}, u32[]{:S(2)}) collective-permute-start(bf16[256,256]{0,1:T(8,128)(2,1)S(1)} %collective-permute-done.7), channel_id=1, source_target_pairs={{0,1},{1,0},{2,3},{3,2},{4,5},{5,4},{6,7},{7,6},{8,9},{9,8},{10,11... | collective-permute-start | bytes 393224 | tf_op jit(solution)/shard_map/ppermute | solution.py:20
  82.8 3.8 %copy-start.1 = (f32[512,1024]{1,0:T(8,128)S(1)}, f32[512,1024]{1,0:T(8,128)}, u32[]{:S(2)}) copy-start(f32[512,1024]{1,0:T(8,128)} %convolution_add_fusion) | copy-start | bytes 6291460
  85.3 2.5 %collective-permute-start.12 = (bf16[384,1024]{1,0:T(8,128)(2,1)S(1)}, bf16[384,1024]{1,0:T(8,128)(2,1)}, u32[]{:S(2)}, u32[]{:S(2)}) collective-permute-start(bf16[384,1024]{1,0:T(8,128)(2,1)S(1)} %maximum_maximum_fusion), channel_id=1, source_target_pairs={{0,4},{1,5},{2,6},{3,7},{4,0},{5,1},{6,2},{7,3},{8,12},{9,13},{10,... | collective-permute-start | bytes 2359304 | tf_op jit(solution)/shard_map/ppermute | solution.py:20
  89.2 7.8 %collective-permute-start.13 = (bf16[96,1024]{1,0:T(8,128)(2,1)S(1)}, bf16[96,1024]{1,0:T(8,128)(2,1)S(1)}, u32[]{:S(2)}, u32[]{:S(2)}) collective-permute-start(bf16[96,1024]{1,0:T(8,128)(2,1)S(1)} %get-tuple-element.25), channel_id=1, source_target_pairs={{0,8},{1,9},{2,10},{3,11},{4,12},{5,13},{6,14},{7,15},{8,0},{9,1},... | collective-permute-start | bytes 589832 | tf_op jit(solution)/shard_map/ppermute | solution.py:20
  90.8 10.7 %collective-permute-start.15 = (bf16[96,1024]{1,0:T(8,128)(2,1)S(1)}, bf16[96,1024]{1,0:T(8,128)(2,1)S(1)}, u32[]{:S(2)}, u32[]{:S(2)}) collective-permute-start(bf16[96,1024]{1,0:T(8,128)(2,1)S(1)} %get-tuple-element.26), channel_id=1, source_target_pairs={{0,24},{1,25},{2,26},{3,27},{4,28},{5,29},{6,30},{7,31},{8,16},{9,... | collective-permute-start | bytes 589832 | tf_op jit(solution)/shard_map/ppermute | solution.py:20
  92.3 10.6 %collective-permute-start.14 = (bf16[96,1024]{1,0:T(8,128)(2,1)S(1)}, bf16[96,1024]{1,0:T(8,128)(2,1)S(1)}, u32[]{:S(2)}, u32[]{:S(2)}) collective-permute-start(bf16[96,1024]{1,0:T(8,128)(2,1)S(1)} %get-tuple-element.27), channel_id=1, source_target_pairs={{0,16},{1,17},{2,18},{3,19},{4,20},{5,21},{6,22},{7,23},{8,24},{9,... | collective-permute-start | bytes 589832 | tf_op jit(solution)/shard_map/ppermute | solution.py:20
  103.0 4.5 %collective-permute-start.16 = (bf16[24,1024]{1,0:T(8,128)(2,1)S(1)}, bf16[24,1024]{1,0:T(8,128)(2,1)S(1)}, u32[]{:S(2)}, u32[]{:S(2)}) collective-permute-start(bf16[24,1024]{1,0:T(8,128)(2,1)S(1)} %get-tuple-element.39), channel_id=1, source_target_pairs={{0,1},{1,0},{2,3},{3,2},{4,5},{5,4},{6,7},{7,6},{8,9},{9,8},{10,11... | collective-permute-start | bytes 147464 | tf_op jit(solution)/shard_map/ppermute | solution.py:20
  103.5 5.9 %collective-permute-start.18 = (bf16[24,1024]{1,0:T(8,128)(2,1)S(1)}, bf16[24,1024]{1,0:T(8,128)(2,1)S(1)}, u32[]{:S(2)}, u32[]{:S(2)}) collective-permute-start(bf16[24,1024]{1,0:T(8,128)(2,1)S(1)} %get-tuple-element.40), channel_id=1, source_target_pairs={{0,3},{1,2},{2,1},{3,0},{4,7},{5,6},{6,5},{7,4},{8,11},{9,10},{10,... | collective-permute-start | bytes 147464 | tf_op jit(solution)/shard_map/ppermute | solution.py:20
  105.9 5.0 %collective-permute-start.17 = (bf16[24,1024]{1,0:T(8,128)(2,1)S(1)}, bf16[24,1024]{1,0:T(8,128)(2,1)S(1)}, u32[]{:S(2)}, u32[]{:S(2)}) collective-permute-start(bf16[24,1024]{1,0:T(8,128)(2,1)S(1)} %get-tuple-element.41), channel_id=1, source_target_pairs={{0,2},{1,3},{2,0},{3,1},{4,6},{5,7},{6,4},{7,5},{8,10},{9,11},{10,... | collective-permute-start | bytes 147464 | tf_op jit(solution)/shard_map/ppermute | solution.py:20
  111.0 4.5 %collective-permute-start.21 = (bf16[24,1024]{1,0:T(8,128)(2,1)S(1)}, bf16[24,1024]{1,0:T(8,128)(2,1)S(1)}, u32[]{:S(2)}, u32[]{:S(2)}) collective-permute-start(bf16[24,1024]{1,0:T(8,128)(2,1)S(1)} %add_convert_fusion), channel_id=1, source_target_pairs={{0,1},{1,0},{2,3},{3,2},{4,5},{5,4},{6,7},{7,6},{8,9},{9,8},{10,11... | collective-permute-start | bytes 147464 | tf_op jit(solution)/shard_map/ppermute | solution.py:20
  112.5 5.5 %collective-permute-start.20 = (bf16[24,1024]{1,0:T(8,128)(2,1)S(1)}, bf16[24,1024]{1,0:T(8,128)(2,1)S(1)}, u32[]{:S(2)}, u32[]{:S(2)}) collective-permute-start(bf16[24,1024]{1,0:T(8,128)(2,1)S(1)} %add_convert_fusion), channel_id=1, source_target_pairs={{0,2},{1,3},{2,0},{3,1},{4,6},{5,7},{6,4},{7,5},{8,10},{9,11},{10,... | collective-permute-start | bytes 147464 | tf_op jit(solution)/shard_map/ppermute | solution.py:20
  113.8 5.9 %collective-permute-start.19 = (bf16[24,1024]{1,0:T(8,128)(2,1)S(1)}, bf16[24,1024]{1,0:T(8,128)(2,1)S(1)}, u32[]{:S(2)}, u32[]{:S(2)}) collective-permute-start(bf16[24,1024]{1,0:T(8,128)(2,1)S(1)} %add_convert_fusion), channel_id=1, source_target_pairs={{0,3},{1,2},{2,1},{3,0},{4,7},{5,6},{6,5},{7,4},{8,11},{9,10},{10,... | collective-permute-start | bytes 147464 | tf_op jit(solution)/shard_map/ppermute | solution.py:20
  119.7 5.7 %collective-permute-start.24 = (bf16[96,1024]{1,0:T(8,128)(2,1)S(1)}, bf16[96,1024]{1,0:T(8,128)(2,1)S(1)}, u32[]{:S(2)}, u32[]{:S(2)}) collective-permute-start(bf16[96,1024]{1,0:T(8,128)(2,1)S(1)} %pad_maximum_fusion.4), channel_id=1, source_target_pairs={{0,8},{1,9},{2,10},{3,11},{4,12},{5,13},{6,14},{7,15},{8,0},{9,1},... | collective-permute-start | bytes 589832 | tf_op jit(solution)/shard_map/ppermute | solution.py:20
  121.2 7.8 %collective-permute-start.23 = (bf16[96,1024]{1,0:T(8,128)(2,1)S(1)}, bf16[96,1024]{1,0:T(8,128)(2,1)S(1)}, u32[]{:S(2)}, u32[]{:S(2)}) collective-permute-start(bf16[96,1024]{1,0:T(8,128)(2,1)S(1)} %pad_maximum_fusion.4), channel_id=1, source_target_pairs={{0,16},{1,17},{2,18},{3,19},{4,20},{5,21},{6,22},{7,23},{8,24},{9,... | collective-permute-start | bytes 589832 | tf_op jit(solution)/shard_map/ppermute | solution.py:20
  121.8 7.2 %collective-permute-start.22 = (bf16[96,1024]{1,0:T(8,128)(2,1)S(1)}, bf16[96,1024]{1,0:T(8,128)(2,1)S(1)}, u32[]{:S(2)}, u32[]{:S(2)}) collective-permute-start(bf16[96,1024]{1,0:T(8,128)(2,1)S(1)} %pad_maximum_fusion.4), channel_id=1, source_target_pairs={{0,24},{1,25},{2,26},{3,27},{4,28},{5,29},{6,30},{7,31},{8,16},{9,... | collective-permute-start | bytes 589832 | tf_op jit(solution)/shard_map/ppermute | solution.py:20
  129.4 2.4 %collective-permute-start.25 = (bf16[384,1024]{1,0:T(8,128)(2,1)S(1)}, bf16[384,1024]{1,0:T(8,128)(2,1)S(1)}, u32[]{:S(2)}, u32[]{:S(2)}) collective-permute-start(bf16[384,1024]{1,0:T(8,128)(2,1)S(1)} %pad_maximum_fusion), channel_id=1, source_target_pairs={{0,4},{1,5},{2,6},{3,7},{4,0},{5,1},{6,2},{7,3},{8,12},{9,13},{10,... | collective-permute-start | bytes 2359304 | tf_op jit(solution)/shard_map/ppermute | solution.py:20
  (5 other events, 7.0 us)

commit v3 on v2

--- a/solution.py
+++ b/solution.py
@@ -1,6 +1,10 @@
+import functools
+
 import jax
 import jax.numpy as jnp
 from jax import lax
+from jax.experimental import pallas as pl
+from jax.experimental.pallas import tpu as pltpu
 from jax.sharding import PartitionSpec as P
 
 MARGIN = 0.5
@@ -8,6 +12,7 @@
 BF16 = jnp.bfloat16
 F32 = jnp.float32
 OVER_ROWS = (((0,), (0,)), ((), ()))
+LAST_DIMS = (((1,), (1,)), ((), ()))
 
 
 def exchange(value, sizes, flip_dp, flip_blk):
@@ -104,55 +109,142 @@
     return [known[j] for j in range(1, blk_size)]
 
 
-def pair_gradients(queries, items, sizes):
-    pairs = queries.shape[0]
-    scale = queries.shape[1] ** (-0.5)
-    other_items = spread(items, sizes)
-    other_queries = spread(queries, sizes)
-    cycle = jnp.concatenate([items] + other_items, 0)
-    columns = cycle.shape[0]
-
-    def positive_of(q, i):
-        return jnp.sum(q.astype(F32) * i.astype(F32), 1, keepdims=True) * scale
-
-    def weights_of(q, i, positive):
-        scores = lax.dot_general(q, i, (((1,), (1,)), ((), ())), preferred_element_type=F32)
-        return jax.nn.sigmoid(scores * scale - positive + MARGIN) / columns
-
-    weights = weights_of(queries, cycle, positive_of(queries, items))
-    row_total = jnp.sum(weights, 1, keepdims=True)
-    tile = weights.astype(BF16)
-    d_query = (
-        jnp.dot(tile, cycle, preferred_element_type=F32) - row_total * items.astype(F32)
-    ) * scale
-    remote_queries = jnp.concatenate(other_queries, 0)
-    remote_tile = weights_of(
-        remote_queries, items, positive_of(remote_queries, cycle[pairs:])
-    ).astype(BF16)
+def pair_weights(q, i, positive, scale, columns):
+    scores = lax.dot_general(q, i, LAST_DIMS, preferred_element_type=F32)
+    return jax.nn.sigmoid(scores * scale - positive + MARGIN) / columns
+
+
+def positive_of(q, i, scale):
+    return jnp.sum(q.astype(F32) * i.astype(F32), 1, keepdims=True) * scale
+
+
+def through_norm(d_embed, proj, inv):
+    interior = jnp.mean(d_embed * proj, 1, keepdims=True)
+    return (inv * d_embed - proj * inv**3 * interior).astype(BF16)
+
+
+def through_gate(d_proj, pre, w_out):
+    d_hidden = lax.dot_general(d_proj, w_out, LAST_DIMS, preferred_element_type=F32)
+    sig = jax.nn.sigmoid(pre)
+    return (d_hidden * sig * (1.0 + pre * (1.0 - sig))).astype(BF16)
+
+
+def query_kernel(group_size, *refs):
+    queries, items = refs[0], refs[1 : 1 + group_size]
+    proj, inv, pre, w_out, tile, row_total, d_proj, d_pre = refs[1 + group_size :]
+    q, own_items = queries[...], items[0][...]
+    pairs, width = q.shape
+    scale = width ** (-0.5)
+    positive = positive_of(q, own_items, scale)
+    total = jnp.zeros((pairs, 1), F32)
+    d_query = jnp.zeros((pairs, width), F32)
+    for j in range(group_size):
+        block = items[j][...]
+        weights = pair_weights(q, block, positive, scale, group_size * pairs)
+        total += jnp.sum(weights, 1, keepdims=True)
+        rounded = weights.astype(BF16)
+        if j == 0:
+            tile[...] = rounded
+        d_query += jnp.dot(rounded, block, preferred_element_type=F32)
+    row_total[...] = total
+    d_query = (d_query - total * own_items.astype(F32)) * scale
+    d_p = through_norm(d_query, proj[:pairs], inv[:pairs])
+    d_proj[...] = d_p
+    d_pre[...] = through_gate(d_p, pre[:pairs], w_out[...])
+
+
+def item_kernel(group_size, core_ref, *refs):
+    queries, items = refs[:group_size], refs[group_size : 2 * group_size]
+    (tile, row_total, proj, inv, pre, w_out, d_proj_q, d_pre_q, hidden, inputs, keep, give) = refs[
+        2 * group_size :
+    ]
+    own_items, q = items[0][...], queries[0][...]
+    pairs, width = q.shape
+    scale = width ** (-0.5)
     d_item = (
-        lax.dot_general(tile[:, :pairs], queries, OVER_ROWS, preferred_element_type=F32)
-        + lax.dot_general(remote_tile, remote_queries, OVER_ROWS, preferred_element_type=F32)
-        - row_total * queries.astype(F32)
-    ) * scale
-    return d_query, d_item
-
-
-def sum_staged(g_in, g_out, group, own, sizes):
+        lax.dot_general(tile[...], q, OVER_ROWS, preferred_element_type=F32)
+        - row_total[...] * q.astype(F32)
+    )
+    for j in range(1, group_size):
+        block = queries[j][...]
+        positive = positive_of(block, items[j][...], scale)
+        weights = pair_weights(block, own_items, positive, scale, group_size * pairs).astype(BF16)
+        d_item += lax.dot_general(weights, block, OVER_ROWS, preferred_element_type=F32)
+    d_proj = jnp.concatenate(
+        [d_proj_q[...], through_norm(d_item * scale, proj[pairs:], inv[pairs:])], 0
+    )
+    d_pre = jnp.concatenate(
+        [d_pre_q[...], through_gate(d_proj[pairs:], pre[pairs:], w_out[...])], 0
+    )
+    core = core_ref[0]
+    hid = pre.shape[1]
+    cut = hid // 2
+    fold = cut * width // hid
+    for half, out in ((1 - core, give), (core, keep)):
+        grad = lax.dot_general(inputs[half], d_pre, OVER_ROWS, preferred_element_type=F32)
+        out[:width] = grad.astype(out.dtype)
+        for k in range(hid // width):
+            start = pl.multiple_of(half * cut + k * fold, fold)
+            grad = lax.dot_general(
+                hidden[:, pl.ds(start, fold)], d_proj, OVER_ROWS, preferred_element_type=F32
+            )
+            out[width:, k * width : (k + 1) * width] = grad.astype(out.dtype)
+
+
+def call_kernel(kernel, outs, args, flops, scalars=0):
+    moved = sum(a.size * a.dtype.itemsize for a in list(args) + list(outs))
+    specs = [pl.BlockSpec(memory_space=pltpu.SMEM)] * scalars
+    specs += [pl.BlockSpec(memory_space=pltpu.VMEM)] * (len(args) - scalars)
+    return pl.pallas_call(
+        kernel,
+        out_shape=outs,
+        in_specs=specs,
+        out_specs=[pl.BlockSpec(memory_space=pltpu.VMEM)] * len(outs),
+        compiler_params=pltpu.CompilerParams(vmem_limit_bytes=40 * 1024 * 1024),
+        cost_estimate=pl.CostEstimate(flops=flops, bytes_accessed=moved, transcendentals=0),
+    )(*args)
+
+
+def backward(embedding, projected, inv_norm, pre_act, hidden, inputs, w_out, group, sizes):
+    blk_size = sizes[1]
+    nodes, width = embedding.shape
+    hid = pre_act.shape[1]
+    pairs = nodes // 2
+    queries, items = embedding[:pairs], embedding[pairs:]
+    all_items = [items] + spread(items, sizes)
+    all_queries = [queries] + spread(queries, sizes)
+    shape = jax.ShapeDtypeStruct
+    scores = 2 * pairs * pairs * width
+    tile, row_total, d_proj_q, d_pre_q = call_kernel(
+        functools.partial(query_kernel, blk_size),
+        [
+            shape((pairs, pairs), BF16),
+            shape((pairs, 1), F32),
+            shape((pairs, width), BF16),
+            shape((pairs, hid), BF16),
+        ],
+        [queries] + all_items + [projected, inv_norm, pre_act, w_out],
+        2 * scores * blk_size + 2 * pairs * width * hid,
+    )
+    rows = width + width // 2
+    return call_kernel(
+        functools.partial(item_kernel, blk_size),
+        [shape((rows, hid), F32), shape((rows, hid), BF16)],
+        [jnp.reshape(group % 2, (1,))]
+        + all_queries
+        + all_items
+        + [tile, row_total, projected, inv_norm, pre_act, w_out, d_proj_q, d_pre_q, hidden, inputs],
+        2 * scores * blk_size + 2 * pairs * width * hid + 6 * nodes * width * hid,
+        scalars=1,
+    )
+
+
+def sum_staged(keep, give, side, group, own, sizes):
     dp_size, blk_size = sizes
-    width = g_in.shape[1]
-    side = g_out.shape[1]
+    width = keep.shape[1]
     plane = dp_size // 2
     core = group % 2
     across = group // 2
-
-    def half(index):
-        g_in_half = block_of(g_in, index, 2)
-        g_out_half = block_of(g_out, index, 2)
-        rows = g_out_half.shape[0] * side // width
-        folded = jnp.concatenate(
-            [g_out_half[k * rows : (k + 1) * rows] for k in range(width // side)], 1
-        )
-        return jnp.concatenate([g_in_half, folded], 0)
 
     def unfold(folded):
         return jnp.concatenate(
@@ -168,53 +260,41 @@
     def over_blk(v, j):
         return exchange(v, sizes, 0, j)
 
-    total = half(core) + over_core(half(1 - core).astype(BF16), 1).astype(F32)
-    total = reduce_blocks(total, across, plane, over_plane)
-    total = reduce_blocks(total, own, blk_size, over_blk)
-    block = total.astype(BF16)
-    block = gather_blocks(block, own, blk_size, over_blk)
-    block = gather_blocks(block, across, plane, over_plane)
+    total = keep + over_core(give, 1).astype(F32)
+    if plane & (plane - 1) == 0 and keep.shape[0] % (8 * plane * blk_size) == 0:
+        total = reduce_blocks(total, across, plane, over_plane)
+        total = reduce_blocks(total, own, blk_size, over_blk)
+        block = total.astype(BF16)
+        block = gather_blocks(block, own, blk_size, over_blk)
+        block = gather_blocks(block, across, plane, over_plane)
+    else:
+        halves = jnp.stack([jnp.where(core == c, total, 0.0) for c in range(2)])
+        halves = lax.psum(halves, AXES)
+        block = jnp.where(core == 0, halves[0], halves[1]).astype(BF16)
     other = over_core(block, 1)
     first = jnp.where(core == 0, block, other)
     second = jnp.where(core == 0, other, block)
-    cut = g_in.shape[0] // 2
+    cut = side
     grad_out = jnp.concatenate([unfold(first[cut:]), unfold(second[cut:])], 0)
     return (first[:cut].astype(F32), second[:cut].astype(F32), grad_out.astype(F32))
 
 
 def on_device(sizes, self_feat, nbr_mask, neighbour_slot, serve_rows, feat_store, w_self, w_nbr, w_out):
-    dp_size, blk_size = sizes
     group = lax.axis_index("dp")
     own = lax.axis_index("blk")
     pooled = pooled_mean(nbr_mask, neighbour_slot, serve_rows, feat_store, own, sizes)
     pre_act = jnp.dot(self_feat, w_self, preferred_element_type=F32) + jnp.dot(
         pooled, w_nbr, preferred_element_type=F32
     )
-    gate_sig = jax.nn.sigmoid(pre_act)
-    hidden = (pre_act * gate_sig).astype(BF16)
+    hidden = (pre_act * jax.nn.sigmoid(pre_act)).astype(BF16)
     projected = jnp.dot(hidden, w_out, preferred_element_type=F32)
     inv_norm = lax.rsqrt(jnp.mean(projected * projected, 1, keepdims=True) + 1e-06)
     embedding = (projected * inv_norm).astype(BF16)
-    pairs = embedding.shape[0] // 2
-    inputs = jnp.concatenate([self_feat, pooled], 1)
-    g_in = g_out = 0.0
-    for half, d_embed in enumerate(pair_gradients(embedding[:pairs], embedding[pairs:], sizes)):
-        rows = slice(half * pairs, (half + 1) * pairs)
-        inv, proj, pre, sig = inv_norm[rows], projected[rows], pre_act[rows], gate_sig[rows]
-        interior_term = jnp.mean(d_embed * proj, 1, keepdims=True)
-        d_proj = (inv * d_embed - proj * inv**3 * interior_term).astype(BF16)
-        d_hidden = lax.dot_general(
-            d_proj, w_out, (((1,), (1,)), ((), ())), preferred_element_type=F32
-        )
-        d_pre = (d_hidden * sig * (1.0 + pre * (1.0 - sig))).astype(BF16)
-        g_out += lax.dot_general(hidden[rows], d_proj, OVER_ROWS, preferred_element_type=F32)
-        g_in += lax.dot_general(inputs[rows], d_pre, OVER_ROWS, preferred_element_type=F32)
-    staged = (dp_size & (dp_size - 1)) == 0 and dp_size > 1
-    if staged and g_in.shape[0] % (8 * dp_size * blk_size) == 0:
-        return sum_staged(g_in, g_out, group, own, sizes)
-    g_in, grad_out = lax.psum((g_in, g_out), AXES)
-    cut = g_in.shape[0] // 2
-    return (g_in[:cut], g_in[cut:], grad_out)
+    inputs = jnp.stack([self_feat, pooled])
+    keep, give = backward(
+        embedding, projected, inv_norm, pre_act, hidden, inputs, w_out, group, sizes
+    )
+    return sum_staged(keep, give, w_out.shape[1], group, own, sizes)
 
 
 def solution(mesh):

time: 136 us -> 134 us (0.985)
  matrix products: 19.9 us -> 6.4 us
  waiting for transfers between devices: 41.8 us -> 49.8 us
  Pallas kernels: 0 us -> 5.95 us
  other arithmetic: 11.3 us -> 8.56 us
    dot_general x8 -> x0, matrix products: 12.3 us -> none  [the longest x2 6.11 us: on_device(): lax.dot_general(inputs[rows], d_pre, OVER_ROWS, preferred_element_type=F32)]
    ppermute x26, waiting for transfers between devices: 41.8 us -> 49.8 us  [exchange(): return lax.ppermute(value, AXES, pairs)]
    pallas_call x0 -> x2, Pallas kernels: none -> 5.95 us  [call_kernel(): pl.pallas_call(kernel, out_shape=outs, in_specs=specs, out_specs=[pl.Bloc...]
    convert_element_type x2 -> x0, other arithmetic: 2.2 us -> none  [the longest x1 1.12 us: on_device(): d_proj = (inv * d_embed - proj * inv ** 3 * interior_term).astype(BF16)]
    dot_general x1, matrix products: 2.73 us -> 0.72 us  [on_device(): jnp.dot(pooled, w_nbr, preferred_element_type=F32)]
    another operation x2 -> x0, local copies, waits for them, and re-layouts: 1.48 us -> none
  transfers between devices with their start and end apart: 26 -> 26, of which waited for: 16 -> 15; matrix products, arithmetic and copies ran while one was open for 22% -> 22% of each run, Pallas kernels for 0% -> 2%
where the time goes in v3:
time: 134 us
  waiting for transfers between devices  49.8 us (37%)
  starting transfers between devices  31.5 us (24%)
  local copies, waits for them, and re-layouts  30.2 us (23%)
  other arithmetic  8.56 us (6%)
  matrix products  6.4 us (5%)
  Pallas kernels  5.95 us (4%)
    ppermute x26, waiting for transfers between devices, exchange(): return lax.ppermute(value, AXES, pairs)  49.8 us
    ppermute x26, starting transfers between devices, exchange(): return lax.ppermute(value, AXES, pairs)  31.5 us
    gather x4, local copies, waits for them, and re-layouts, pooled_mean(): rows = feat_store.at[served].get(mode='promise_in_bounds')  25 us
    pallas_call x2, Pallas kernels, call_kernel(): pl.pallas_call(kernel, out_shape=outs, in_specs=specs, out_specs=[pl.Bloc...  5.95 us
    unnamed x29, local copies, waits for them, and re-layouts  2.72 us
  transfers between devices with their start and end apart: 26, of which 15 were waited for; matrix products, arithmetic and copies ran while one was open for 22% of the time, Pallas kernels for 2%

profile of v3, /device:TPU:0, one launch (start us, length us, event | category | flops | bytes accessed | tf_op | source)
XLA Modules:
  0.0 133.6 jit_solution(5641290516428421945)
XLA Ops:
  3.9 4.1 %collective-permute-start = (s32[1,1024]{1,0:T(1,128)S(1)}, s32[1,1024]{1,0:T(1,128)S(1)}, u32[]{:S(2)}, u32[]{:S(2)}) collective-permute-start(s32[1,1024]{1,0:T(1,128)S(1)} %get-tuple-element.51), channel_id=1, source_target_pairs={{0,2},{1,3},{2,0},{3,1},{4,6},{5,7},{6,4},{7,5},{8,10},{9,11},{10,... | collective-permute-start | bytes 12296 | tf_op jit(solution)/shard_map/ppermute | solution.py:25
  9.6 6.2 %gather_fusion = bf16[1024,256]{1,0:T(8,128)(2,1)S(1)} fusion(bf16[8192,256]{1,0:T(8,128)(2,1)} %param.12, s32[1024]{0:T(1024)S(1)} %broadcast_clamp_fusion), kind=kCustom, calls=%fused_computation | custom fusion | bytes 1052672 | tf_op jit(solution)/shard_map/gather | solution.py:95
  16.3 6.2 %gather_fusion.1 = bf16[1024,256]{1,0:T(8,128)(2,1)S(1)} fusion(bf16[8192,256]{1,0:T(8,128)(2,1)} %param.12, s32[1024]{0:T(1024)S(1)} %fusion.33), kind=kCustom, calls=%fused_computation.1 | custom fusion | bytes 1052672 | tf_op jit(solution)/shard_map/gather | solution.py:95
  23.0 6.3 %gather_fusion.2 = bf16[1024,256]{1,0:T(8,128)(2,1)S(1)} fusion(bf16[8192,256]{1,0:T(8,128)(2,1)} %param.12, s32[1024]{0:T(1024)S(1)} %fusion.34), kind=kCustom, calls=%fused_computation.2 | custom fusion | bytes 1052672 | tf_op jit(solution)/shard_map/gather | solution.py:95
  29.8 1.8 %collective-permute-start.5 = (bf16[512,256]{1,0:T(8,128)(2,1)S(1)}, bf16[512,256]{1,0:T(8,128)(2,1)S(1)}, u32[]{:S(2)}, u32[]{:S(2)}) collective-permute-start(bf16[512,256]{1,0:T(8,128)(2,1)S(1)} %fusion.8), channel_id=1, source_target_pairs={{0,1},{1,0},{2,3},{3,2},{4,5},{5,4},{6,7},{7,6},{8,9},{9,8},{10,11... | collective-permute-start | bytes 786440 | tf_op jit(solution)/shard_map/ppermute | solution.py:25
  31.6 2.5 %collective-permute-start.3 = (bf16[512,256]{1,0:T(8,128)(2,1)S(1)}, bf16[512,256]{1,0:T(8,128)(2,1)S(1)}, u32[]{:S(2)}, u32[]{:S(2)}) collective-permute-start(bf16[512,256]{1,0:T(8,128)(2,1)S(1)} %fusion.9), channel_id=1, source_target_pairs={{0,3},{1,2},{2,1},{3,0},{4,7},{5,6},{6,5},{7,4},{8,11},{9,10},{10,... | collective-permute-start | bytes 786440 | tf_op jit(solution)/shard_map/ppermute | solution.py:25
  34.1 1.8 %fusion.38 = f32[512,1024]{1,0:T(8,128)} fusion(bf16[512,256]{1,0:T(8,128)(2,1)S(1)} %copy-done.7, bf16[256,1024]{1,0:T(8,128)(2,1)S(1)} %copy-done.8), kind=kOutput, calls=%fused_computation.117 | convolution fusion | flops 268435456 | bytes 2883584 | tf_op jit(solution)/shard_map/dot_general | solution.py:286
  35.9 6.4 %gather_fusion.3 = bf16[1024,256]{1,0:T(8,128)(2,1)S(1)} fusion(bf16[8192,256]{1,0:T(8,128)(2,1)} %param.12, s32[1024]{0:T(1024)S(1)} %fusion.35), kind=kCustom, calls=%fused_computation.3 | custom fusion | bytes 1052672 | tf_op jit(solution)/shard_map/gather | solution.py:95
  42.3 4.7 %collective-permute-done.3 = bf16[512,256]{1,0:T(8,128)(2,1)S(1)} collective-permute-done((bf16[512,256]{1,0:T(8,128)(2,1)S(1)}, bf16[512,256]{1,0:T(8,128)(2,1)S(1)}, u32[]{:S(2)}, u32[]{:S(2)}) %collective-permute-start.3) | collective-permute-done | bytes 262176 | tf_op jit(solution)/shard_map/ppermute | solution.py:25
  47.0 8.3 %collective-permute-done.1 = bf16[512,256]{1,0:T(8,128)(2,1)S(1)} collective-permute-done((bf16[512,256]{1,0:T(8,128)(2,1)S(1)}, bf16[512,256]{1,0:T(8,128)(2,1)S(1)}, u32[]{:S(2)}, u32[]{:S(2)}) %collective-permute-start.1) | collective-permute-done | bytes 262176 | tf_op jit(solution)/shard_map/ppermute | solution.py:25
  60.4 2.9 %collective-permute-start.7 = (bf16[256,256]{1,0:T(8,128)(2,1)}, bf16[256,256]{1,0:T(8,128)(2,1)}, u32[]{:S(2)}, u32[]{:S(2)}) collective-permute-start(bf16[256,256]{1,0:T(8,128)(2,1)} %get-tuple-element.43.refs_0_), channel_id=1, source_target_pairs={{0,2},{1,3},{2,0},{3,1},{4,6},{5,7},{6,4},{7,5},{8,10},{9,11},{10,... | collective-permute-start | bytes 393224 | tf_op jit(solution)/shard_map/ppermute | solution.py:25
  63.6 8.0 %collective-permute-done.10.refs_3_.refs_6_ = bf16[256,256]{1,0:T(8,128)(2,1)} collective-permute-done((bf16[256,256]{1,0:T(8,128)(2,1)S(1)}, bf16[256,256]{1,0:T(8,128)(2,1)}, u32[]{:S(2)}, u32[]{:S(2)}) %collective-permute-start.10) | collective-permute-done | bytes 131104 | tf_op jit(solution)/shard_map/ppermute | solution.py:25
  71.6 2.0 %collective-permute-start.6 = (bf16[256,256]{1,0:T(8,128)(2,1)}, bf16[256,256]{1,0:T(8,128)(2,1)}, u32[]{:S(2)}, u32[]{:S(2)}) collective-permute-start(bf16[256,256]{1,0:T(8,128)(2,1)} %get-tuple-element.43.refs_0_), channel_id=1, source_target_pairs={{0,1},{1,0},{2,3},{3,2},{4,5},{5,4},{6,7},{7,6},{8,9},{9,8},{10,11... | collective-permute-start | bytes 393224 | tf_op jit(solution)/shard_map/ppermute | solution.py:25
  75.1 3.3 %collective-permute-done.11.refs_4_.refs_7_ = bf16[256,256]{1,0:T(8,128)(2,1)} collective-permute-done((bf16[256,256]{1,0:T(8,128)(2,1)}, bf16[256,256]{1,0:T(8,128)(2,1)}, u32[]{:S(2)}, u32[]{:S(2)}) %collective-permute-start.11) | collective-permute-done | bytes 131104 | tf_op jit(solution)/shard_map/ppermute | solution.py:25
  79.4 2.3 %shard_map.103 = (bf16[256,256]{1,0:T(8,128)(2,1)S(1)}, f32[256,1]{1,0:T(8,128)S(1)}, bf16[256,256]{1,0:T(8,128)(2,1)S(1)}, bf16[256,1024]{1,0:T(8,128)(2,1)S(1)}) custom-call(bf16[256,256]{1,0:T(8,128)(2,1)} %get-tuple-element.43.refs_0_, bf16[256,256]{1,0:T(8,128)(2,1)S(1)} %get-tuple-element.42.refs_1_.refs_4_, ...), custom_call_target="tpu_custom_call" | custom-call | flops 402653184 | bytes 4590592 | tf_op jit(solution)/shard_map/pallas_call | solution.py:198
  81.7 3.7 %shard_map.104 = (f32[384,1024]{1,0:T(8,128)S(1)}, bf16[384,1024]{1,0:T(8,128)(2,1)}) custom-call(s32[1]{0:T(128)} %bitcast.core_ref, bf16[256,256]{1,0:T(8,128)(2,1)} %get-tuple-element.43.refs_0_, bf16[256,256]{1,0:T(8,128)(2,1)} %collective-permute-done.6.refs_1_, bf16[256,256]{1,0:T(8,128)(2,1)} %collective-permute-done.7.refs_2_, ...), custom_call_target="tpu_custom_call" | custom-call | flops 1207959552 | bytes 8915972 | tf_op jit(solution)/shard_map/pallas_call | solution.py:198
  86.6 2.5 %collective-permute-done.12 = bf16[384,1024]{1,0:T(8,128)(2,1)S(1)} collective-permute-done((bf16[384,1024]{1,0:T(8,128)(2,1)}, bf16[384,1024]{1,0:T(8,128)(2,1)S(1)}, u32[]{:S(2)}, u32[]{:S(2)}) %collective-permute-start.12) | collective-permute-done | bytes 786464 | tf_op jit(solution)/shard_map/ppermute | solution.py:25
  89.1 1.6 %convert_add_fusion = f32[384,1024]{1,0:T(8,128)S(1)} fusion(f32[384,1024]{1,0:T(8,128)} %copy-done.5, bf16[384,1024]{1,0:T(8,128)(2,1)S(1)} %collective-permute-done.12), kind=kLoop, calls=%fused_computation.21 | loop fusion | flops 786432 | bytes 3932160 | tf_op jit(solution)/shard_map/add | solution.py:263
  90.8 1.5 %collective-permute-start.13 = (bf16[96,1024]{1,0:T(8,128)(2,1)S(1)}, bf16[96,1024]{1,0:T(8,128)(2,1)S(1)}, u32[]{:S(2)}, u32[]{:S(2)}) collective-permute-start(bf16[96,1024]{1,0:T(8,128)(2,1)S(1)} %get-tuple-element.33), channel_id=1, source_target_pairs={{0,8},{1,9},{2,10},{3,11},{4,12},{5,13},{6,14},{7,15},{8,0},{9,1},... | collective-permute-start | bytes 589832 | tf_op jit(solution)/shard_map/ppermute | solution.py:25
  92.4 1.5 %collective-permute-start.14 = (bf16[96,1024]{1,0:T(8,128)(2,1)S(1)}, bf16[96,1024]{1,0:T(8,128)(2,1)S(1)}, u32[]{:S(2)}, u32[]{:S(2)}) collective-permute-start(bf16[96,1024]{1,0:T(8,128)(2,1)S(1)} %get-tuple-element.35), channel_id=1, source_target_pairs={{0,16},{1,17},{2,18},{3,19},{4,20},{5,21},{6,22},{7,23},{8,24},{9,... | collective-permute-start | bytes 589832 | tf_op jit(solution)/shard_map/ppermute | solution.py:25
  94.4 4.3 %collective-permute-done.13 = bf16[96,1024]{1,0:T(8,128)(2,1)S(1)} collective-permute-done((bf16[96,1024]{1,0:T(8,128)(2,1)S(1)}, bf16[96,1024]{1,0:T(8,128)(2,1)S(1)}, u32[]{:S(2)}, u32[]{:S(2)}) %collective-permute-start.13) | collective-permute-done | bytes 196640 | tf_op jit(solution)/shard_map/ppermute | solution.py:25
  98.6 4.6 %collective-permute-done.14 = bf16[96,1024]{1,0:T(8,128)(2,1)S(1)} collective-permute-done((bf16[96,1024]{1,0:T(8,128)(2,1)S(1)}, bf16[96,1024]{1,0:T(8,128)(2,1)S(1)}, u32[]{:S(2)}, u32[]{:S(2)}) %collective-permute-start.14) | collective-permute-done | bytes 196640 | tf_op jit(solution)/shard_map/ppermute | solution.py:25
  103.4 2.0 %collective-permute-start.17 = (bf16[24,1024]{1,0:T(8,128)(2,1)S(1)}, bf16[24,1024]{1,0:T(8,128)(2,1)S(1)}, u32[]{:S(2)}, u32[]{:S(2)}) collective-permute-start(bf16[24,1024]{1,0:T(8,128)(2,1)S(1)} %get-tuple-element.41), channel_id=1, source_target_pairs={{0,2},{1,3},{2,0},{3,1},{4,6},{5,7},{6,4},{7,5},{8,10},{9,11},{10,... | collective-permute-start | bytes 147464 | tf_op jit(solution)/shard_map/ppermute | solution.py:25
  105.5 2.4 %collective-permute-start.18 = (bf16[24,1024]{1,0:T(8,128)(2,1)S(1)}, bf16[24,1024]{1,0:T(8,128)(2,1)S(1)}, u32[]{:S(2)}, u32[]{:S(2)}) collective-permute-start(bf16[24,1024]{1,0:T(8,128)(2,1)S(1)} %get-tuple-element.40), channel_id=1, source_target_pairs={{0,3},{1,2},{2,1},{3,0},{4,7},{5,6},{6,5},{7,4},{8,11},{9,10},{10,... | collective-permute-start | bytes 147464 | tf_op jit(solution)/shard_map/ppermute | solution.py:25
  109.0 2.3 %collective-permute-done.18 = bf16[24,1024]{1,0:T(8,128)(2,1)S(1)} collective-permute-done((bf16[24,1024]{1,0:T(8,128)(2,1)S(1)}, bf16[24,1024]{1,0:T(8,128)(2,1)S(1)}, u32[]{:S(2)}, u32[]{:S(2)}) %collective-permute-start.18) | collective-permute-done | bytes 49184 | tf_op jit(solution)/shard_map/ppermute | solution.py:25
  111.4 2.4 %collective-permute-start.19 = (bf16[24,1024]{1,0:T(8,128)(2,1)S(1)}, bf16[24,1024]{1,0:T(8,128)(2,1)S(1)}, u32[]{:S(2)}, u32[]{:S(2)}) collective-permute-start(bf16[24,1024]{1,0:T(8,128)(2,1)S(1)} %add_convert_fusion), channel_id=1, source_target_pairs={{0,3},{1,2},{2,1},{3,0},{4,7},{5,6},{6,5},{7,4},{8,11},{9,10},{10,... | collective-permute-start | bytes 147464 | tf_op jit(solution)/shard_map/ppermute | solution.py:25
  113.8 2.0 %collective-permute-start.21 = (bf16[24,1024]{1,0:T(8,128)(2,1)S(1)}, bf16[24,1024]{1,0:T(8,128)(2,1)S(1)}, u32[]{:S(2)}, u32[]{:S(2)}) collective-permute-start(bf16[24,1024]{1,0:T(8,128)(2,1)S(1)} %add_convert_fusion), channel_id=1, source_target_pairs={{0,1},{1,0},{2,3},{3,2},{4,5},{5,4},{6,7},{7,6},{8,9},{9,8},{10,11... | collective-permute-start | bytes 147464 | tf_op jit(solution)/shard_map/ppermute | solution.py:25
  118.9 1.6 %collective-permute-start.22 = (bf16[96,1024]{1,0:T(8,128)(2,1)S(1)}, bf16[96,1024]{1,0:T(8,128)(2,1)S(1)}, u32[]{:S(2)}, u32[]{:S(2)}) collective-permute-start(bf16[96,1024]{1,0:T(8,128)(2,1)S(1)} %pad_maximum_fusion.2), channel_id=1, source_target_pairs={{0,24},{1,25},{2,26},{3,27},{4,28},{5,29},{6,30},{7,31},{8,16},{9,... | collective-permute-start | bytes 589832 | tf_op jit(solution)/shard_map/ppermute | solution.py:25
  122.4 3.2 %collective-permute-done.22 = bf16[96,1024]{1,0:T(8,128)(2,1)S(1)} collective-permute-done((bf16[96,1024]{1,0:T(8,128)(2,1)S(1)}, bf16[96,1024]{1,0:T(8,128)(2,1)S(1)}, u32[]{:S(2)}, u32[]{:S(2)}) %collective-permute-start.22) | collective-permute-done | bytes 196640 | tf_op jit(solution)/shard_map/ppermute | solution.py:25
  125.6 2.0 %collective-permute-done.23 = bf16[96,1024]{1,0:T(8,128)(2,1)S(1)} collective-permute-done((bf16[96,1024]{1,0:T(8,128)(2,1)S(1)}, bf16[96,1024]{1,0:T(8,128)(2,1)S(1)}, u32[]{:S(2)}, u32[]{:S(2)}) %collective-permute-start.23) | collective-permute-done | bytes 196640 | tf_op jit(solution)/shard_map/ppermute | solution.py:25
  128.2 2.3 %collective-permute-done.25 = bf16[384,1024]{1,0:T(8,128)(2,1)S(1)} collective-permute-done((bf16[384,1024]{1,0:T(8,128)(2,1)S(1)}, bf16[384,1024]{1,0:T(8,128)(2,1)S(1)}, u32[]{:S(2)}, u32[]{:S(2)}) %collective-permute-start.25) | collective-permute-done | bytes 786464 | tf_op jit(solution)/shard_map/ppermute | solution.py:25
  130.9 1.6 %slice_convert_fusion = (f32[256,1024]{1,0:T(8,128)}, f32[256,1024]{1,0:T(8,128)}) fusion(bf16[384,1024]{1,0:T(8,128)(2,1)S(1)} %get-tuple-element.31, bf16[384,1024]{1,0:T(8,128)(2,1)S(1)} %get-tuple-element.32), kind=kLoop, calls=%fused_computation.33 | loop fusion | flops 524288 | bytes 3145728 | tf_op jit(solution)/shard_map/convert_element_type | solution.py:279
  (100 shorter events, 24.1 us)
Async XLA Ops:
  0.6 55.2 %copy-start = (bf16[256,1024]{1,0:T(8,128)(2,1)S(1)}, bf16[256,1024]{1,0:T(8,128)(2,1)}, u32[]{:S(2)}) copy-start(bf16[256,1024]{1,0:T(8,128)(2,1)} %param.14) | copy-start | bytes 1572868
  3.0 6.5 %copy-start.10 = (s32[4,1024]{1,0:T(4,128)S(1)}, s32[4,1024]{1,0:T(4,128)}, u32[]{:S(2)}) copy-start(s32[4,1024]{1,0:T(4,128)} %param.11) | copy-start | bytes 49156
  3.9 11.9 %collective-permute-start = (s32[1,1024]{1,0:T(1,128)S(1)}, s32[1,1024]{1,0:T(1,128)S(1)}, u32[]{:S(2)}, u32[]{:S(2)}) collective-permute-start(s32[1,1024]{1,0:T(1,128)S(1)} %get-tuple-element.51), channel_id=1, source_target_pairs={{0,2},{1,3},{2,0},{3,1},{4,6},{5,7},{6,4},{7,5},{8,10},{9,11},{10,... | collective-permute-start | bytes 12296 | tf_op jit(solution)/shard_map/ppermute | solution.py:25
  8.0 14.5 %collective-permute-start.2 = (s32[1,1024]{1,0:T(1,128)S(1)}, s32[1,1024]{1,0:T(1,128)S(1)}, u32[]{:S(2)}, u32[]{:S(2)}) collective-permute-start(s32[1,1024]{1,0:T(1,128)S(1)} %get-tuple-element.50), channel_id=1, source_target_pairs={{0,3},{1,2},{2,1},{3,0},{4,7},{5,6},{6,5},{7,4},{8,11},{9,10},{10,... | collective-permute-start | bytes 12296 | tf_op jit(solution)/shard_map/ppermute | solution.py:25
  9.3 20.0 %collective-permute-start.4 = (s32[1,1024]{1,0:T(1,128)S(1)}, s32[1,1024]{1,0:T(1,128)S(1)}, u32[]{:S(2)}, u32[]{:S(2)}) collective-permute-start(s32[1,1024]{1,0:T(1,128)S(1)} %get-tuple-element.49), channel_id=1, source_target_pairs={{0,1},{1,0},{2,3},{3,2},{4,5},{5,4},{6,7},{7,6},{8,9},{9,8},{10,11... | collective-permute-start | bytes 12296 | tf_op jit(solution)/shard_map/ppermute | solution.py:25
  23.0 11.1 %copy-start.7 = (bf16[512,256]{1,0:T(8,128)(2,1)S(1)}, bf16[512,256]{1,0:T(8,128)(2,1)}, u32[]{:S(2)}) copy-start(bf16[512,256]{1,0:T(8,128)(2,1)} %param.8) | copy-start | bytes 786436
  23.0 11.1 %copy-start.8 = (bf16[256,1024]{1,0:T(8,128)(2,1)S(1)}, bf16[256,1024]{1,0:T(8,128)(2,1)}, u32[]{:S(2)}) copy-start(bf16[256,1024]{1,0:T(8,128)(2,1)} %param.13) | copy-start | bytes 1572868
  29.8 12.5 %collective-permute-start.5 = (bf16[512,256]{1,0:T(8,128)(2,1)S(1)}, bf16[512,256]{1,0:T(8,128)(2,1)S(1)}, u32[]{:S(2)}, u32[]{:S(2)}) collective-permute-start(bf16[512,256]{1,0:T(8,128)(2,1)S(1)} %fusion.8), channel_id=1, source_target_pairs={{0,1},{1,0},{2,3},{3,2},{4,5},{5,4},{6,7},{7,6},{8,9},{9,8},{10,11... | collective-permute-start | bytes 786440 | tf_op jit(solution)/shard_map/ppermute | solution.py:25
  31.6 15.4 %collective-permute-start.3 = (bf16[512,256]{1,0:T(8,128)(2,1)S(1)}, bf16[512,256]{1,0:T(8,128)(2,1)S(1)}, u32[]{:S(2)}, u32[]{:S(2)}) collective-permute-start(bf16[512,256]{1,0:T(8,128)(2,1)S(1)} %fusion.9), channel_id=1, source_target_pairs={{0,3},{1,2},{2,1},{3,0},{4,7},{5,6},{6,5},{7,4},{8,11},{9,10},{10,... | collective-permute-start | bytes 786440 | tf_op jit(solution)/shard_map/ppermute | solution.py:25
  34.1 21.2 %collective-permute-start.1 = (bf16[512,256]{1,0:T(8,128)(2,1)S(1)}, bf16[512,256]{1,0:T(8,128)(2,1)S(1)}, u32[]{:S(2)}, u32[]{:S(2)}) collective-permute-start(bf16[512,256]{1,0:T(8,128)(2,1)S(1)} %fusion.10), channel_id=1, source_target_pairs={{0,2},{1,3},{2,0},{3,1},{4,6},{5,7},{6,4},{7,5},{8,10},{9,11},{10,... | collective-permute-start | bytes 786440 | tf_op jit(solution)/shard_map/ppermute | solution.py:25
  42.3 13.6 %copy-start.6 = (f32[512,1024]{1,0:T(8,128)S(1)}, f32[512,1024]{1,0:T(8,128)}, u32[]{:S(2)}) copy-start(f32[512,1024]{1,0:T(8,128)} %fusion.38) | copy-start | bytes 6291460
  60.4 11.2 %collective-permute-start.10 = (bf16[256,256]{1,0:T(8,128)(2,1)S(1)}, bf16[256,256]{1,0:T(8,128)(2,1)}, u32[]{:S(2)}, u32[]{:S(2)}) collective-permute-start(bf16[256,256]{1,0:T(8,128)(2,1)S(1)} %get-tuple-element.42.refs_1_.refs_4_), channel_id=1, source_target_pairs={{0,2},{1,3},{2,0},{3,1},{4,6},{5,7},{6,4},{7,5},{8,10},{9,11},{10,... | collective-permute-start | bytes 393224 | tf_op jit(solution)/shard_map/ppermute | solution.py:25
  60.4 13.4 %collective-permute-start.7 = (bf16[256,256]{1,0:T(8,128)(2,1)}, bf16[256,256]{1,0:T(8,128)(2,1)}, u32[]{:S(2)}, u32[]{:S(2)}) collective-permute-start(bf16[256,256]{1,0:T(8,128)(2,1)} %get-tuple-element.43.refs_0_), channel_id=1, source_target_pairs={{0,2},{1,3},{2,0},{3,1},{4,6},{5,7},{6,4},{7,5},{8,10},{9,11},{10,... | collective-permute-start | bytes 393224 | tf_op jit(solution)/shard_map/ppermute | solution.py:25
  63.3 11.8 %collective-permute-start.9 = (bf16[256,256]{1,0:T(8,128)(2,1)S(1)}, bf16[256,256]{1,0:T(8,128)(2,1)}, u32[]{:S(2)}, u32[]{:S(2)}) collective-permute-start(bf16[256,256]{1,0:T(8,128)(2,1)S(1)} %get-tuple-element.42.refs_1_.refs_4_), channel_id=1, source_target_pairs={{0,1},{1,0},{2,3},{3,2},{4,5},{5,4},{6,7},{7,6},{8,9},{9,8},{10,11... | collective-permute-start | bytes 393224 | tf_op jit(solution)/shard_map/ppermute | solution.py:25
  71.6 6.8 %collective-permute-start.11 = (bf16[256,256]{1,0:T(8,128)(2,1)}, bf16[256,256]{1,0:T(8,128)(2,1)}, u32[]{:S(2)}, u32[]{:S(2)}) collective-permute-start(bf16[256,256]{1,0:T(8,128)(2,1)} %collective-permute-done.10.refs_3_.refs_6_), channel_id=1, source_target_pairs={{0,1},{1,0},{2,3},{3,2},{4,5},{5,4},{6,7},{7,6},{8,9},{9,8},{10,11... | collective-permute-start | bytes 393224 | tf_op jit(solution)/shard_map/ppermute | solution.py:25
  71.6 10.1 %collective-permute-start.6 = (bf16[256,256]{1,0:T(8,128)(2,1)}, bf16[256,256]{1,0:T(8,128)(2,1)}, u32[]{:S(2)}, u32[]{:S(2)}) collective-permute-start(bf16[256,256]{1,0:T(8,128)(2,1)} %get-tuple-element.43.refs_0_), channel_id=1, source_target_pairs={{0,1},{1,0},{2,3},{3,2},{4,5},{5,4},{6,7},{7,6},{8,9},{9,8},{10,11... | collective-permute-start | bytes 393224 | tf_op jit(solution)/shard_map/ppermute | solution.py:25
  73.8 7.9 %collective-permute-start.8 = (bf16[256,256]{1,0:T(8,128)(2,1)}, bf16[256,256]{1,0:T(8,128)(2,1)S(1)}, u32[]{:S(2)}, u32[]{:S(2)}) collective-permute-start(bf16[256,256]{1,0:T(8,128)(2,1)} %collective-permute-done.7.refs_2_), channel_id=1, source_target_pairs={{0,1},{1,0},{2,3},{3,2},{4,5},{5,4},{6,7},{7,6},{8,9},{9,8},{10,11... | collective-permute-start | bytes 393224 | tf_op jit(solution)/shard_map/ppermute | solution.py:25
  73.9 7.8 %copy-start.4 = (bf16[512,1024]{1,0:T(8,128)(2,1)S(1)}, bf16[512,1024]{1,0:T(8,128)(2,1)}, u32[]{:S(2)}) copy-start(bf16[512,1024]{1,0:T(8,128)(2,1)} %copy-done.3) | copy-start | bytes 3145732
  86.6 2.5 %collective-permute-start.12 = (bf16[384,1024]{1,0:T(8,128)(2,1)}, bf16[384,1024]{1,0:T(8,128)(2,1)S(1)}, u32[]{:S(2)}, u32[]{:S(2)}) collective-permute-start(bf16[384,1024]{1,0:T(8,128)(2,1)} %get-tuple-element.26), channel_id=1, source_target_pairs={{0,4},{1,5},{2,6},{3,7},{4,0},{5,1},{6,2},{7,3},{8,12},{9,13},{10,... | collective-permute-start | bytes 2359304 | tf_op jit(solution)/shard_map/ppermute | solution.py:25
  90.8 7.8 %collective-permute-start.13 = (bf16[96,1024]{1,0:T(8,128)(2,1)S(1)}, bf16[96,1024]{1,0:T(8,128)(2,1)S(1)}, u32[]{:S(2)}, u32[]{:S(2)}) collective-permute-start(bf16[96,1024]{1,0:T(8,128)(2,1)S(1)} %get-tuple-element.33), channel_id=1, source_target_pairs={{0,8},{1,9},{2,10},{3,11},{4,12},{5,13},{6,14},{7,15},{8,0},{9,1},... | collective-permute-start | bytes 589832 | tf_op jit(solution)/shard_map/ppermute | solution.py:25
  92.4 10.9 %collective-permute-start.14 = (bf16[96,1024]{1,0:T(8,128)(2,1)S(1)}, bf16[96,1024]{1,0:T(8,128)(2,1)S(1)}, u32[]{:S(2)}, u32[]{:S(2)}) collective-permute-start(bf16[96,1024]{1,0:T(8,128)(2,1)S(1)} %get-tuple-element.35), channel_id=1, source_target_pairs={{0,16},{1,17},{2,18},{3,19},{4,20},{5,21},{6,22},{7,23},{8,24},{9,... | collective-permute-start | bytes 589832 | tf_op jit(solution)/shard_map/ppermute | solution.py:25
  93.9 9.4 %collective-permute-start.15 = (bf16[96,1024]{1,0:T(8,128)(2,1)S(1)}, bf16[96,1024]{1,0:T(8,128)(2,1)S(1)}, u32[]{:S(2)}, u32[]{:S(2)}) collective-permute-start(bf16[96,1024]{1,0:T(8,128)(2,1)S(1)} %get-tuple-element.34), channel_id=1, source_target_pairs={{0,24},{1,25},{2,26},{3,27},{4,28},{5,29},{6,30},{7,31},{8,16},{9,... | collective-permute-start | bytes 589832 | tf_op jit(solution)/shard_map/ppermute | solution.py:25
  103.4 4.5 %collective-permute-start.16 = (bf16[24,1024]{1,0:T(8,128)(2,1)S(1)}, bf16[24,1024]{1,0:T(8,128)(2,1)S(1)}, u32[]{:S(2)}, u32[]{:S(2)}) collective-permute-start(bf16[24,1024]{1,0:T(8,128)(2,1)S(1)} %get-tuple-element.39), channel_id=1, source_target_pairs={{0,1},{1,0},{2,3},{3,2},{4,5},{5,4},{6,7},{7,6},{8,9},{9,8},{10,11... | collective-permute-start | bytes 147464 | tf_op jit(solution)/shard_map/ppermute | solution.py:25
  103.4 5.6 %collective-permute-start.17 = (bf16[24,1024]{1,0:T(8,128)(2,1)S(1)}, bf16[24,1024]{1,0:T(8,128)(2,1)S(1)}, u32[]{:S(2)}, u32[]{:S(2)}) collective-permute-start(bf16[24,1024]{1,0:T(8,128)(2,1)S(1)} %get-tuple-element.41), channel_id=1, source_target_pairs={{0,2},{1,3},{2,0},{3,1},{4,6},{5,7},{6,4},{7,5},{8,10},{9,11},{10,... | collective-permute-start | bytes 147464 | tf_op jit(solution)/shard_map/ppermute | solution.py:25
  105.5 5.9 %collective-permute-start.18 = (bf16[24,1024]{1,0:T(8,128)(2,1)S(1)}, bf16[24,1024]{1,0:T(8,128)(2,1)S(1)}, u32[]{:S(2)}, u32[]{:S(2)}) collective-permute-start(bf16[24,1024]{1,0:T(8,128)(2,1)S(1)} %get-tuple-element.40), channel_id=1, source_target_pairs={{0,3},{1,2},{2,1},{3,0},{4,7},{5,6},{6,5},{7,4},{8,11},{9,10},{10,... | collective-permute-start | bytes 147464 | tf_op jit(solution)/shard_map/ppermute | solution.py:25
  111.4 6.0 %collective-permute-start.19 = (bf16[24,1024]{1,0:T(8,128)(2,1)S(1)}, bf16[24,1024]{1,0:T(8,128)(2,1)S(1)}, u32[]{:S(2)}, u32[]{:S(2)}) collective-permute-start(bf16[24,1024]{1,0:T(8,128)(2,1)S(1)} %add_convert_fusion), channel_id=1, source_target_pairs={{0,3},{1,2},{2,1},{3,0},{4,7},{5,6},{6,5},{7,4},{8,11},{9,10},{10,... | collective-permute-start | bytes 147464 | tf_op jit(solution)/shard_map/ppermute | solution.py:25
  113.8 5.0 %collective-permute-start.20 = (bf16[24,1024]{1,0:T(8,128)(2,1)S(1)}, bf16[24,1024]{1,0:T(8,128)(2,1)S(1)}, u32[]{:S(2)}, u32[]{:S(2)}) collective-permute-start(bf16[24,1024]{1,0:T(8,128)(2,1)S(1)} %add_convert_fusion), channel_id=1, source_target_pairs={{0,2},{1,3},{2,0},{3,1},{4,6},{5,7},{6,4},{7,5},{8,10},{9,11},{10,... | collective-permute-start | bytes 147464 | tf_op jit(solution)/shard_map/ppermute | solution.py:25
  113.8 5.0 %collective-permute-start.21 = (bf16[24,1024]{1,0:T(8,128)(2,1)S(1)}, bf16[24,1024]{1,0:T(8,128)(2,1)S(1)}, u32[]{:S(2)}, u32[]{:S(2)}) collective-permute-start(bf16[24,1024]{1,0:T(8,128)(2,1)S(1)} %add_convert_fusion), channel_id=1, source_target_pairs={{0,1},{1,0},{2,3},{3,2},{4,5},{5,4},{6,7},{7,6},{8,9},{9,8},{10,11... | collective-permute-start | bytes 147464 | tf_op jit(solution)/shard_map/ppermute | solution.py:25
  118.9 6.7 %collective-permute-start.22 = (bf16[96,1024]{1,0:T(8,128)(2,1)S(1)}, bf16[96,1024]{1,0:T(8,128)(2,1)S(1)}, u32[]{:S(2)}, u32[]{:S(2)}) collective-permute-start(bf16[96,1024]{1,0:T(8,128)(2,1)S(1)} %pad_maximum_fusion.2), channel_id=1, source_target_pairs={{0,24},{1,25},{2,26},{3,27},{4,28},{5,29},{6,30},{7,31},{8,16},{9,... | collective-permute-start | bytes 589832 | tf_op jit(solution)/shard_map/ppermute | solution.py:25
  120.4 7.2 %collective-permute-start.23 = (bf16[96,1024]{1,0:T(8,128)(2,1)S(1)}, bf16[96,1024]{1,0:T(8,128)(2,1)S(1)}, u32[]{:S(2)}, u32[]{:S(2)}) collective-permute-start(bf16[96,1024]{1,0:T(8,128)(2,1)S(1)} %pad_maximum_fusion.2), channel_id=1, source_target_pairs={{0,16},{1,17},{2,18},{3,19},{4,20},{5,21},{6,22},{7,23},{8,24},{9,... | collective-permute-start | bytes 589832 | tf_op jit(solution)/shard_map/ppermute | solution.py:25
  121.7 6.0 %collective-permute-start.24 = (bf16[96,1024]{1,0:T(8,128)(2,1)S(1)}, bf16[96,1024]{1,0:T(8,128)(2,1)S(1)}, u32[]{:S(2)}, u32[]{:S(2)}) collective-permute-start(bf16[96,1024]{1,0:T(8,128)(2,1)S(1)} %pad_maximum_fusion.2), channel_id=1, source_target_pairs={{0,8},{1,9},{2,10},{3,11},{4,12},{5,13},{6,14},{7,15},{8,0},{9,1},... | collective-permute-start | bytes 589832 | tf_op jit(solution)/shard_map/ppermute | solution.py:25
  128.1 2.4 %collective-permute-start.25 = (bf16[384,1024]{1,0:T(8,128)(2,1)S(1)}, bf16[384,1024]{1,0:T(8,128)(2,1)S(1)}, u32[]{:S(2)}, u32[]{:S(2)}) collective-permute-start(bf16[384,1024]{1,0:T(8,128)(2,1)S(1)} %pad_maximum_fusion), channel_id=1, source_target_pairs={{0,4},{1,5},{2,6},{3,7},{4,0},{5,1},{6,2},{7,3},{8,12},{9,13},{10,... | collective-permute-start | bytes 2359304 | tf_op jit(solution)/shard_map/ppermute | solution.py:25
  (5 other events, 5.8 us)

commit v4 on v3

--- a/solution.py
+++ b/solution.py
@@ -71,6 +71,58 @@
     return ((found[:, :low] - 1) * 16 + found[:, low:]).reshape(count, slots // count)
 
 
+def call_kernel(kernel, outs, args, flops=0, scalars=0, scratch=()):
+    moved = sum(a.size * a.dtype.itemsize for a in list(args) + list(outs)) if flops else 0
+    specs = [pl.BlockSpec(memory_space=pltpu.SMEM)] * scalars
+    specs += [pl.BlockSpec(memory_space=pltpu.VMEM)] * (len(args) - scalars)
+    return pl.pallas_call(
+        kernel,
+        out_shape=outs,
+        in_specs=specs,
+        out_specs=[pl.BlockSpec(memory_space=pltpu.VMEM)] * len(outs),
+        scratch_shapes=list(scratch),
+        compiler_params=pltpu.CompilerParams(vmem_limit_bytes=24 * 1024 * 1024),
+        cost_estimate=pl.CostEstimate(flops=flops, bytes_accessed=moved, transcendentals=0),
+    )(*args)
+
+
+def split_kernel(store, left, right):
+    rows, side = left.shape
+    step = rows // 16
+
+    def some_rows(i, carry):
+        at = pl.ds(pl.multiple_of(i * step, step), step)
+        block = store[at, :].astype(F32)
+        left[at, :] = block[:, :side]
+        right[at, :] = block[:, side:]
+        return carry
+
+    lax.fori_loop(0, 16, some_rows, 0)
+
+
+def partial_kernel(requester, serve_rows, node_at, left, right, out, got_left, got_right):
+    count = node_at.shape[1]
+    first = requester[0] * count
+
+    def some_rows(i, carry):
+        base = i * 32
+        wanted = [serve_rows[first + base + u] for u in range(32)]
+        for tile in range(0, 32, 8):
+            at = pl.ds(pl.multiple_of(base + tile, 8), 8)
+            to_left, to_right = got_left.at[at, :], got_right.at[at, :]
+            for u in range(8):
+                row = pl.ds(wanted[tile + u], 1)
+                to_left[u : u + 1, :] = left[row, :]
+                to_right[u : u + 1, :] = right[row, :]
+        return carry
+
+    lax.fori_loop(0, count // 32, some_rows, 0)
+    nodes = lax.broadcasted_iota(jnp.int32, (out.shape[0], count), 0)
+    pick = (nodes == node_at[...]).astype(BF16)
+    rows = jnp.concatenate([got_left[...], got_right[...]], 1).astype(BF16)
+    out[...] = jnp.dot(pick, rows, preferred_element_type=F32).astype(out.dtype)
+
+
 def pooled_mean(nbr_mask, neighbour_slot, serve_rows, feat_store, own, sizes):
     blk_size = sizes[1]
     nodes = nbr_mask.shape[0]
@@ -78,25 +130,44 @@
     valid = jnp.where(first_col, 1, nbr_mask)
     live_count = jnp.sum(valid.astype(F32), 1, keepdims=True)
     node_at = node_of_arrival(neighbour_slot, valid, blk_size)
-    order = sorted(range(1, blk_size), key=lambda j: (j < blk_size // 2, j))
+    order = list(range(blk_size - 1, 0, -1))
     wanted = {
         j: exchange(block_of(node_at, own ^ j, blk_size), sizes, 0, j) for j in order
     }
+    wanted = dict(zip(wanted, lax.optimization_barrier(tuple(wanted.values()))))
     wanted[0] = block_of(node_at, own, blk_size)
-    row_node = lax.broadcasted_iota(jnp.int32, (nodes, serve_rows.shape[1]), 0)
-    total = None
-    sent = None
+    width = feat_store.shape[1]
+    cap = serve_rows.shape[1]
+    shape = jax.ShapeDtypeStruct
+    halves = call_kernel(
+        split_kernel, [shape((feat_store.shape[0], width // 2), F32)] * 2, [feat_store]
+    )
+    served = serve_rows.reshape(-1)
+    parts = {}
     for j in order + [0]:
-        served = block_of(serve_rows, own ^ j, blk_size)[0]
-        if sent is not None:
-            served, sent = lax.optimization_barrier((served, sent))
-            arrived = exchange(sent, sizes, 0, previous).astype(F32)
-            total = arrived if total is None else total + arrived
-        rows = feat_store.at[served].get(mode="promise_in_bounds")
-        pick = (row_node == wanted[j]).astype(BF16)
-        part = jnp.dot(pick, rows, preferred_element_type=F32)
-        sent, previous = part.astype(BF16), j
-    return ((total + part) / live_count).astype(BF16)
+        (parts[j],) = call_kernel(
+            partial_kernel,
+            [shape((nodes, width), BF16 if j % 2 else F32)],
+            [jnp.reshape(own ^ j, (1,)), served, wanted[j]] + list(halves),
+            scalars=2,
+            scratch=[pltpu.VMEM((cap, width // 2), F32)] * 2,
+        )
+        if j:
+            served, parts[j] = lax.optimization_barrier((served, parts[j]))
+    for_own = []
+    bit = 1
+    while bit < blk_size:
+        for j in [j for j in order if j & bit and j in parts]:
+            arrived = exchange(parts.pop(j).astype(BF16), sizes, 0, bit)
+            if j == bit:
+                for_own.append(arrived)
+            else:
+                parts[j ^ bit] = parts[j ^ bit] + arrived.astype(F32)
+        bit *= 2
+    total = parts[0]
+    for part in for_own:
+        total = total + part.astype(F32)
+    return (total / live_count).astype(BF16)
 
 
 def spread(block, sizes):
@@ -155,7 +226,7 @@
 
 def item_kernel(group_size, core_ref, *refs):
     queries, items = refs[:group_size], refs[group_size : 2 * group_size]
-    (tile, row_total, proj, inv, pre, w_out, d_proj_q, d_pre_q, hidden, inputs, keep, give) = refs[
+    (tile, row_total, proj, inv, pre, w_out, d_proj_q, d_pre_q, hidden, feat, pooled, keep, give) = refs[
         2 * group_size :
     ]
     own_items, q = items[0][...], queries[0][...]
@@ -181,7 +252,8 @@
     cut = hid // 2
     fold = cut * width // hid
     for half, out in ((1 - core, give), (core, keep)):
-        grad = lax.dot_general(inputs[half], d_pre, OVER_ROWS, preferred_element_type=F32)
+        rows = jnp.where(half == 0, feat[...], pooled[...])
+        grad = lax.dot_general(rows, d_pre, OVER_ROWS, preferred_element_type=F32)
         out[:width] = grad.astype(out.dtype)
         for k in range(hid // width):
             start = pl.multiple_of(half * cut + k * fold, fold)
@@ -191,26 +263,10 @@
             out[width:, k * width : (k + 1) * width] = grad.astype(out.dtype)
 
 
-def call_kernel(kernel, outs, args, flops, scalars=0):
-    moved = sum(a.size * a.dtype.itemsize for a in list(args) + list(outs))
-    specs = [pl.BlockSpec(memory_space=pltpu.SMEM)] * scalars
-    specs += [pl.BlockSpec(memory_space=pltpu.VMEM)] * (len(args) - scalars)
-    return pl.pallas_call(
-        kernel,
-        out_shape=outs,
-        in_specs=specs,
-        out_specs=[pl.BlockSpec(memory_space=pltpu.VMEM)] * len(outs),
-        compiler_params=pltpu.CompilerParams(vmem_limit_bytes=40 * 1024 * 1024),
-        cost_estimate=pl.CostEstimate(flops=flops, bytes_accessed=moved, transcendentals=0),
-    )(*args)
-
-
-def backward(embedding, projected, inv_norm, pre_act, hidden, inputs, w_out, group, sizes):
+def backward(queries, items, projected, inv_norm, pre_act, hidden, feat, pooled, w_out, group, sizes):
     blk_size = sizes[1]
-    nodes, width = embedding.shape
-    hid = pre_act.shape[1]
-    pairs = nodes // 2
-    queries, items = embedding[:pairs], embedding[pairs:]
+    nodes, hid = pre_act.shape
+    pairs, width = queries.shape
     all_items = [items] + spread(items, sizes)
     all_queries = [queries] + spread(queries, sizes)
     shape = jax.ShapeDtypeStruct
@@ -233,7 +289,8 @@
         [jnp.reshape(group % 2, (1,))]
         + all_queries
         + all_items
-        + [tile, row_total, projected, inv_norm, pre_act, w_out, d_proj_q, d_pre_q, hidden, inputs],
+        + [tile, row_total, projected, inv_norm, pre_act, w_out, d_proj_q, d_pre_q]
+        + [hidden, feat, pooled],
         2 * scores * blk_size + 2 * pairs * width * hid + 6 * nodes * width * hid,
         scalars=1,
     )
@@ -290,9 +347,10 @@
     projected = jnp.dot(hidden, w_out, preferred_element_type=F32)
     inv_norm = lax.rsqrt(jnp.mean(projected * projected, 1, keepdims=True) + 1e-06)
     embedding = (projected * inv_norm).astype(BF16)
-    inputs = jnp.stack([self_feat, pooled])
+    pairs = embedding.shape[0] // 2
+    queries, items = embedding[:pairs], embedding[pairs:]
     keep, give = backward(
-        embedding, projected, inv_norm, pre_act, hidden, inputs, w_out, group, sizes
+        queries, items, projected, inv_norm, pre_act, hidden, self_feat, pooled, w_out, group, sizes
     )
     return sum_staged(keep, give, w_out.shape[1], group, own, sizes)
 

time: 134 us -> 115 us (0.86)
  local copies, waits for them, and re-layouts: 30.2 us -> 7.51 us
  Pallas kernels: 5.95 us -> 16.7 us
  waiting for transfers between devices: 49.8 us -> 44.2 us
  matrix products: 6.4 us -> 3.18 us
  starting transfers between devices: 31.5 us -> 34 us
    gather x4 -> x0, local copies, waits for them, and re-layouts: 25 us -> none  [pooled_mean(): rows = feat_store.at[served].get(mode='promise_in_bounds')]
    pallas_call x2 -> x7, Pallas kernels: 5.95 us -> 16.7 us  [call_kernel(): pl.pallas_call(kernel, out_shape=outs, in_specs=specs, out_specs=[pl.Bloc...]
    ppermute x26, waiting for transfers between devices: 49.8 us -> 44.2 us  [exchange(): return lax.ppermute(value, AXES, pairs)]
    ppermute x26, starting transfers between devices: 31.5 us -> 34 us  [exchange(): return lax.ppermute(value, AXES, pairs)]
    unnamed x29 -> x34, local copies, waits for them, and re-layouts: 2.72 us -> 5.02 us
    dot_general x4 -> x0, matrix products: 1.9 us -> none  [pooled_mean(): part = jnp.dot(pick, rows, preferred_element_type=F32)]
  transfers between devices with their start and end apart: 26 -> 26, of which waited for: 15 -> 15; matrix products, arithmetic and copies ran while one was open for 22% -> 1% of each run, Pallas kernels for 2% -> 9%
where the time goes in v4:
time: 115 us; the launch traced here: 114 us
  waiting for transfers between devices  44.2 us (38%)
  starting transfers between devices  34 us (30%)
  Pallas kernels  16.7 us (15%)
  other arithmetic  7.58 us (7%)
  local copies, waits for them, and re-layouts  7.51 us (7%)
  matrix products  3.18 us (3%)
    ppermute x26, waiting for transfers between devices, exchange(): return lax.ppermute(value, AXES, pairs)  44.2 us
    ppermute x26, starting transfers between devices, exchange(): return lax.ppermute(value, AXES, pairs)  34 us
    pallas_call x7, Pallas kernels, call_kernel(): pl.pallas_call(kernel, out_shape=outs, in_specs=specs, out_specs=[pl.Bloc...  16.7 us
    unnamed x34, local copies, waits for them, and re-layouts  5.02 us
  transfers between devices with their start and end apart: 26, of which 15 were waited for; matrix products, arithmetic and copies ran while one was open for 1% of the time, Pallas kernels for 9%

profile of v4, /device:TPU:0, one launch (start us, length us, event | category | flops | bytes accessed | tf_op | source)
XLA Modules:
  0.0 114.3 jit_solution(12230272050900888986)
XLA Ops:
  3.8 5.1 %collective-permute-start = (s32[1,1024]{1,0:T(1,128)S(1)}, s32[1,1024]{1,0:T(1,128)S(1)}, u32[]{:S(2)}, u32[]{:S(2)}) collective-permute-start(s32[1,1024]{1,0:T(1,128)S(1)} %get-tuple-element.61), channel_id=1, source_target_pairs={{0,3},{1,2},{2,1},{3,0},{4,7},{5,6},{6,5},{7,4},{8,11},{9,10},{10,... | collective-permute-start | bytes 12296 | tf_op jit(solution)/shard_map/ppermute | solution.py:25
  9.6 2.2 %copy-done.3 = bf16[8192,256]{1,0:T(8,128)(2,1)S(1)} copy-done((bf16[8192,256]{1,0:T(8,128)(2,1)S(1)}, bf16[8192,256]{1,0:T(8,128)(2,1)}, u32[]{:S(2)}) %copy-start.3) | copy-done | bytes 4194328
  13.5 2.5 %shard_map.104 = bf16[512,256]{1,0:T(8,128)(2,1)S(1)} custom-call(s32[1]{0:T(128)} %bitcast.2.requester, s32[4096]{0:T(1024)S(1)} %bitcast.18, s32[1,1024]{1,0:T(1,128)S(1)} %collective-permute-done.node_at, f32[8192,128]{1,0:T(8,128)S(1)} %get-tuple-element.21.left, f32[8192,128]{1,0:T(8,128)S(1)} %get-tuple-element.22.right), custom_call_target="tpu_custom_call" | custom-call | tf_op jit(solution)/shard_map/pallas_call | solution.py:78
  16.5 2.5 %shard_map.105 = f32[512,256]{1,0:T(8,128)S(1)} custom-call(s32[1]{0:T(128)} %bitcast.5.requester, s32[4096]{0:T(1024)S(1)} %bitcast.19, s32[1,1024]{1,0:T(1,128)S(1)} %collective-permute-done.1.node_at, f32[8192,128]{1,0:T(8,128)S(1)} %get-tuple-element.21.left, f32[8192,128]{1,0:T(8,128)S(1)} %get-tuple-element.22.right), custom_call_target="tpu_custom_call" | custom-call | tf_op jit(solution)/shard_map/pallas_call | solution.py:78
  19.0 2.5 %shard_map.106 = bf16[512,256]{1,0:T(8,128)(2,1)S(1)} custom-call(s32[1]{0:T(128)} %bitcast.6.requester, s32[4096]{0:T(1024)S(1)} %bitcast.20, s32[1,1024]{1,0:T(1,128)S(1)} %collective-permute-done.2.node_at, f32[8192,128]{1,0:T(8,128)S(1)} %get-tuple-element.21.left, f32[8192,128]{1,0:T(8,128)S(1)} %get-tuple-element.22.right), custom_call_target="tpu_custom_call" | custom-call | tf_op jit(solution)/shard_map/pallas_call | solution.py:78
  21.5 1.6 %collective-permute-start.3 = (bf16[512,256]{1,0:T(8,128)(2,1)S(1)}, bf16[512,256]{1,0:T(8,128)(2,1)S(1)}, u32[]{:S(2)}, u32[]{:S(2)}) collective-permute-start(bf16[512,256]{1,0:T(8,128)(2,1)S(1)} %shard_map.106), channel_id=1, source_target_pairs={{0,1},{1,0},{2,3},{3,2},{4,5},{5,4},{6,7},{7,6},{8,9},{9,8},{10,11... | collective-permute-start | bytes 786440 | tf_op jit(solution)/shard_map/ppermute | solution.py:25
  23.3 2.1 %collective-permute-start.5 = (bf16[512,256]{1,0:T(8,128)(2,1)S(1)}, bf16[512,256]{1,0:T(8,128)(2,1)S(1)}, u32[]{:S(2)}, u32[]{:S(2)}) collective-permute-start(bf16[512,256]{1,0:T(8,128)(2,1)S(1)} %add_convert_fusion), channel_id=1, source_target_pairs={{0,2},{1,3},{2,0},{3,1},{4,6},{5,7},{6,4},{7,5},{8,10},{9,11},{10,... | collective-permute-start | bytes 786440 | tf_op jit(solution)/shard_map/ppermute | solution.py:25
  25.8 2.5 %shard_map.107 = f32[512,256]{1,0:T(8,128)S(1)} custom-call(s32[1]{0:T(128)} %bitcast.1.requester, s32[4096]{0:T(1024)S(1)} %bitcast.21, s32[1,1024]{1,0:T(1,128)S(1)} %get-tuple-element.58.node_at, f32[8192,128]{1,0:T(8,128)S(1)} %get-tuple-element.21.left, f32[8192,128]{1,0:T(8,128)S(1)} %get-tuple-element.22.right), custom_call_target="tpu_custom_call" | custom-call | tf_op jit(solution)/shard_map/pallas_call | solution.py:78
  28.3 6.1 %collective-permute-done.3 = bf16[512,256]{1,0:T(8,128)(2,1)S(1)} collective-permute-done((bf16[512,256]{1,0:T(8,128)(2,1)S(1)}, bf16[512,256]{1,0:T(8,128)(2,1)S(1)}, u32[]{:S(2)}, u32[]{:S(2)}) %collective-permute-start.3) | collective-permute-done | bytes 262176 | tf_op jit(solution)/shard_map/ppermute | solution.py:25
  39.1 1.7 %collective-permute-start.10 = (bf16[256,256]{1,0:T(8,128)(2,1)S(1)}, bf16[256,256]{1,0:T(8,128)(2,1)}, u32[]{:S(2)}, u32[]{:S(2)}) collective-permute-start(bf16[256,256]{1,0:T(8,128)(2,1)S(1)} %get-tuple-element.52.refs_1_.refs_4_), channel_id=1, source_target_pairs={{0,2},{1,3},{2,0},{3,1},{4,6},{5,7},{6,4},{7,5},{8,10},{9,11},{10,... | collective-permute-start | bytes 393224 | tf_op jit(solution)/shard_map/ppermute | solution.py:25
  42.1 2.6 %collective-permute-start.9 = (bf16[256,256]{1,0:T(8,128)(2,1)S(1)}, bf16[256,256]{1,0:T(8,128)(2,1)}, u32[]{:S(2)}, u32[]{:S(2)}) collective-permute-start(bf16[256,256]{1,0:T(8,128)(2,1)S(1)} %get-tuple-element.52.refs_1_.refs_4_), channel_id=1, source_target_pairs={{0,1},{1,0},{2,3},{3,2},{4,5},{5,4},{6,7},{7,6},{8,9},{9,8},{10,11... | collective-permute-start | bytes 393224 | tf_op jit(solution)/shard_map/ppermute | solution.py:25
  44.7 5.9 %collective-permute-done.10.refs_3_.refs_6_ = bf16[256,256]{1,0:T(8,128)(2,1)} collective-permute-done((bf16[256,256]{1,0:T(8,128)(2,1)S(1)}, bf16[256,256]{1,0:T(8,128)(2,1)}, u32[]{:S(2)}, u32[]{:S(2)}) %collective-permute-start.10) | collective-permute-done | bytes 131104 | tf_op jit(solution)/shard_map/ppermute | solution.py:25
  50.6 2.0 %collective-permute-start.6 = (bf16[256,256]{1,0:T(8,128)(2,1)}, bf16[256,256]{1,0:T(8,128)(2,1)}, u32[]{:S(2)}, u32[]{:S(2)}) collective-permute-start(bf16[256,256]{1,0:T(8,128)(2,1)} %get-tuple-element.53.refs_0_), channel_id=1, source_target_pairs={{0,1},{1,0},{2,3},{3,2},{4,5},{5,4},{6,7},{7,6},{8,9},{9,8},{10,11... | collective-permute-start | bytes 393224 | tf_op jit(solution)/shard_map/ppermute | solution.py:25
  52.8 4.2 %collective-permute-done.11.refs_4_.refs_7_ = bf16[256,256]{1,0:T(8,128)(2,1)} collective-permute-done((bf16[256,256]{1,0:T(8,128)(2,1)}, bf16[256,256]{1,0:T(8,128)(2,1)}, u32[]{:S(2)}, u32[]{:S(2)}) %collective-permute-start.11) | collective-permute-done | bytes 131104 | tf_op jit(solution)/shard_map/ppermute | solution.py:25
  58.1 2.4 %shard_map.108 = (bf16[256,256]{1,0:T(8,128)(2,1)S(1)}, f32[256,1]{1,0:T(8,128)S(1)}, bf16[256,256]{1,0:T(8,128)(2,1)S(1)}, bf16[256,1024]{1,0:T(8,128)(2,1)S(1)}) custom-call(bf16[256,256]{1,0:T(8,128)(2,1)} %get-tuple-element.53.refs_0_, bf16[256,256]{1,0:T(8,128)(2,1)S(1)} %get-tuple-element.52.refs_1_.refs_4_, ...), custom_call_target="tpu_custom_call" | custom-call | flops 402653184 | bytes 4590592 | tf_op jit(solution)/shard_map/pallas_call | solution.py:78
  60.5 3.7 %shard_map.109 = (f32[384,1024]{1,0:T(8,128)S(1)}, bf16[384,1024]{1,0:T(8,128)(2,1)}) custom-call(s32[1]{0:T(128)} %bitcast.core_ref, bf16[256,256]{1,0:T(8,128)(2,1)} %get-tuple-element.53.refs_0_, bf16[256,256]{1,0:T(8,128)(2,1)} %collective-permute-done.6.refs_1_, bf16[256,256]{1,0:T(8,128)(2,1)} %collective-permute-done.7.refs_2_, ...), custom_call_target="tpu_custom_call" | custom-call | flops 1207959552 | bytes 8915972 | tf_op jit(solution)/shard_map/pallas_call | solution.py:78
  65.4 2.5 %collective-permute-done.12 = bf16[384,1024]{1,0:T(8,128)(2,1)S(1)} collective-permute-done((bf16[384,1024]{1,0:T(8,128)(2,1)}, bf16[384,1024]{1,0:T(8,128)(2,1)S(1)}, u32[]{:S(2)}, u32[]{:S(2)}) %collective-permute-start.12) | collective-permute-done | bytes 786464 | tf_op jit(solution)/shard_map/ppermute | solution.py:25
  67.9 1.6 %convert_add_fusion = f32[384,1024]{1,0:T(8,128)S(1)} fusion(f32[384,1024]{1,0:T(8,128)} %copy-done.6, bf16[384,1024]{1,0:T(8,128)(2,1)S(1)} %collective-permute-done.12), kind=kLoop, calls=%fused_computation.9 | loop fusion | flops 786432 | bytes 3932160 | tf_op jit(solution)/shard_map/add | solution.py:320
  69.6 1.6 %collective-permute-start.13 = (bf16[96,1024]{1,0:T(8,128)(2,1)S(1)}, bf16[96,1024]{1,0:T(8,128)(2,1)S(1)}, u32[]{:S(2)}, u32[]{:S(2)}) collective-permute-start(bf16[96,1024]{1,0:T(8,128)(2,1)S(1)} %get-tuple-element.43), channel_id=1, source_target_pairs={{0,8},{1,9},{2,10},{3,11},{4,12},{5,13},{6,14},{7,15},{8,0},{9,1},... | collective-permute-start | bytes 589832 | tf_op jit(solution)/shard_map/ppermute | solution.py:25
  71.2 1.5 %collective-permute-start.14 = (bf16[96,1024]{1,0:T(8,128)(2,1)S(1)}, bf16[96,1024]{1,0:T(8,128)(2,1)S(1)}, u32[]{:S(2)}, u32[]{:S(2)}) collective-permute-start(bf16[96,1024]{1,0:T(8,128)(2,1)S(1)} %get-tuple-element.45), channel_id=1, source_target_pairs={{0,16},{1,17},{2,18},{3,19},{4,20},{5,21},{6,22},{7,23},{8,24},{9,... | collective-permute-start | bytes 589832 | tf_op jit(solution)/shard_map/ppermute | solution.py:25
  73.2 4.3 %collective-permute-done.13 = bf16[96,1024]{1,0:T(8,128)(2,1)S(1)} collective-permute-done((bf16[96,1024]{1,0:T(8,128)(2,1)S(1)}, bf16[96,1024]{1,0:T(8,128)(2,1)S(1)}, u32[]{:S(2)}, u32[]{:S(2)}) %collective-permute-start.13) | collective-permute-done | bytes 196640 | tf_op jit(solution)/shard_map/ppermute | solution.py:25
  77.4 4.6 %collective-permute-done.14 = bf16[96,1024]{1,0:T(8,128)(2,1)S(1)} collective-permute-done((bf16[96,1024]{1,0:T(8,128)(2,1)S(1)}, bf16[96,1024]{1,0:T(8,128)(2,1)S(1)}, u32[]{:S(2)}, u32[]{:S(2)}) %collective-permute-start.14) | collective-permute-done | bytes 196640 | tf_op jit(solution)/shard_map/ppermute | solution.py:25
  82.3 4.6 %collective-permute-start.17 = (bf16[24,1024]{1,0:T(8,128)(2,1)S(1)}, bf16[24,1024]{1,0:T(8,128)(2,1)S(1)}, u32[]{:S(2)}, u32[]{:S(2)}) collective-permute-start(bf16[24,1024]{1,0:T(8,128)(2,1)S(1)} %get-tuple-element.51), channel_id=1, source_target_pairs={{0,2},{1,3},{2,0},{3,1},{4,6},{5,7},{6,4},{7,5},{8,10},{9,11},{10,... | collective-permute-start | bytes 147464 | tf_op jit(solution)/shard_map/ppermute | solution.py:25
  86.9 2.6 %collective-permute-done.17 = bf16[24,1024]{1,0:T(8,128)(2,1)S(1)} collective-permute-done((bf16[24,1024]{1,0:T(8,128)(2,1)S(1)}, bf16[24,1024]{1,0:T(8,128)(2,1)S(1)}, u32[]{:S(2)}, u32[]{:S(2)}) %collective-permute-start.17) | collective-permute-done | bytes 49184 | tf_op jit(solution)/shard_map/ppermute | solution.py:25
  89.5 3.3 %collective-permute-done.18 = bf16[24,1024]{1,0:T(8,128)(2,1)S(1)} collective-permute-done((bf16[24,1024]{1,0:T(8,128)(2,1)S(1)}, bf16[24,1024]{1,0:T(8,128)(2,1)S(1)}, u32[]{:S(2)}, u32[]{:S(2)}) %collective-permute-start.18) | collective-permute-done | bytes 49184 | tf_op jit(solution)/shard_map/ppermute | solution.py:25
  93.5 3.8 %collective-permute-start.21 = (bf16[24,1024]{1,0:T(8,128)(2,1)S(1)}, bf16[24,1024]{1,0:T(8,128)(2,1)S(1)}, u32[]{:S(2)}, u32[]{:S(2)}) collective-permute-start(bf16[24,1024]{1,0:T(8,128)(2,1)S(1)} %add_convert_fusion.1), channel_id=1, source_target_pairs={{0,1},{1,0},{2,3},{3,2},{4,5},{5,4},{6,7},{7,6},{8,9},{9,8},{10,11... | collective-permute-start | bytes 147464 | tf_op jit(solution)/shard_map/ppermute | solution.py:25
  97.3 1.6 %collective-permute-done.19 = bf16[24,1024]{1,0:T(8,128)(2,1)S(1)} collective-permute-done((bf16[24,1024]{1,0:T(8,128)(2,1)S(1)}, bf16[24,1024]{1,0:T(8,128)(2,1)S(1)}, u32[]{:S(2)}, u32[]{:S(2)}) %collective-permute-start.19) | collective-permute-done | bytes 49184 | tf_op jit(solution)/shard_map/ppermute | solution.py:25
  99.6 1.6 %collective-permute-start.22 = (bf16[96,1024]{1,0:T(8,128)(2,1)S(1)}, bf16[96,1024]{1,0:T(8,128)(2,1)S(1)}, u32[]{:S(2)}, u32[]{:S(2)}) collective-permute-start(bf16[96,1024]{1,0:T(8,128)(2,1)S(1)} %pad_maximum_fusion.1), channel_id=1, source_target_pairs={{0,24},{1,25},{2,26},{3,27},{4,28},{5,29},{6,30},{7,31},{8,16},{9,... | collective-permute-start | bytes 589832 | tf_op jit(solution)/shard_map/ppermute | solution.py:25
  103.1 3.2 %collective-permute-done.22 = bf16[96,1024]{1,0:T(8,128)(2,1)S(1)} collective-permute-done((bf16[96,1024]{1,0:T(8,128)(2,1)S(1)}, bf16[96,1024]{1,0:T(8,128)(2,1)S(1)}, u32[]{:S(2)}, u32[]{:S(2)}) %collective-permute-start.22) | collective-permute-done | bytes 196640 | tf_op jit(solution)/shard_map/ppermute | solution.py:25
  106.3 2.0 %collective-permute-done.23 = bf16[96,1024]{1,0:T(8,128)(2,1)S(1)} collective-permute-done((bf16[96,1024]{1,0:T(8,128)(2,1)S(1)}, bf16[96,1024]{1,0:T(8,128)(2,1)S(1)}, u32[]{:S(2)}, u32[]{:S(2)}) %collective-permute-start.23) | collective-permute-done | bytes 196640 | tf_op jit(solution)/shard_map/ppermute | solution.py:25
  108.9 2.3 %collective-permute-done.25 = bf16[384,1024]{1,0:T(8,128)(2,1)S(1)} collective-permute-done((bf16[384,1024]{1,0:T(8,128)(2,1)S(1)}, bf16[384,1024]{1,0:T(8,128)(2,1)S(1)}, u32[]{:S(2)}, u32[]{:S(2)}) %collective-permute-start.25) | collective-permute-done | bytes 786464 | tf_op jit(solution)/shard_map/ppermute | solution.py:25
  111.6 1.6 %slice_convert_fusion = (f32[256,1024]{1,0:T(8,128)}, f32[256,1024]{1,0:T(8,128)}) fusion(bf16[384,1024]{1,0:T(8,128)(2,1)S(1)} %get-tuple-element.41, bf16[384,1024]{1,0:T(8,128)(2,1)S(1)} %get-tuple-element.42), kind=kLoop, calls=%fused_computation.14 | loop fusion | flops 524288 | bytes 3145728 | tf_op jit(solution)/shard_map/convert_element_type | solution.py:336
  (97 shorter events, 20.9 us)
Async XLA Ops:
  0.6 34.0 %copy-start = (bf16[256,1024]{1,0:T(8,128)(2,1)S(1)}, bf16[256,1024]{1,0:T(8,128)(2,1)}, u32[]{:S(2)}) copy-start(bf16[256,1024]{1,0:T(8,128)(2,1)} %param.14) | copy-start | bytes 1572868
  3.8 8.7 %collective-permute-start = (s32[1,1024]{1,0:T(1,128)S(1)}, s32[1,1024]{1,0:T(1,128)S(1)}, u32[]{:S(2)}, u32[]{:S(2)}) collective-permute-start(s32[1,1024]{1,0:T(1,128)S(1)} %get-tuple-element.61), channel_id=1, source_target_pairs={{0,3},{1,2},{2,1},{3,0},{4,7},{5,6},{6,5},{7,4},{8,11},{9,10},{10,... | collective-permute-start | bytes 12296 | tf_op jit(solution)/shard_map/ppermute | solution.py:25
  9.0 4.5 %collective-permute-start.1 = (s32[1,1024]{1,0:T(1,128)S(1)}, s32[1,1024]{1,0:T(1,128)S(1)}, u32[]{:S(2)}, u32[]{:S(2)}) collective-permute-start(s32[1,1024]{1,0:T(1,128)S(1)} %get-tuple-element.60), channel_id=1, source_target_pairs={{0,2},{1,3},{2,0},{3,1},{4,6},{5,7},{6,4},{7,5},{8,10},{9,11},{10,... | collective-permute-start | bytes 12296 | tf_op jit(solution)/shard_map/ppermute | solution.py:25
  9.0 4.5 %collective-permute-start.2 = (s32[1,1024]{1,0:T(1,128)S(1)}, s32[1,1024]{1,0:T(1,128)S(1)}, u32[]{:S(2)}, u32[]{:S(2)}) collective-permute-start(s32[1,1024]{1,0:T(1,128)S(1)} %get-tuple-element.59), channel_id=1, source_target_pairs={{0,1},{1,0},{2,3},{3,2},{4,5},{5,4},{6,7},{7,6},{8,9},{9,8},{10,11... | collective-permute-start | bytes 12296 | tf_op jit(solution)/shard_map/ppermute | solution.py:25
  16.0 7.2 %collective-permute-start.4 = (bf16[512,256]{1,0:T(8,128)(2,1)S(1)}, bf16[512,256]{1,0:T(8,128)(2,1)S(1)}, u32[]{:S(2)}, u32[]{:S(2)}) collective-permute-start(bf16[512,256]{1,0:T(8,128)(2,1)S(1)} %shard_map.104), channel_id=1, source_target_pairs={{0,1},{1,0},{2,3},{3,2},{4,5},{5,4},{6,7},{7,6},{8,9},{9,8},{10,11... | collective-permute-start | bytes 786440 | tf_op jit(solution)/shard_map/ppermute | solution.py:25
  19.0 6.3 %copy-start.9 = (bf16[512,256]{1,0:T(8,128)(2,1)S(1)}, bf16[512,256]{1,0:T(8,128)(2,1)}, u32[]{:S(2)}) copy-start(bf16[512,256]{1,0:T(8,128)(2,1)} %refs_17_.1) | copy-start | bytes 786436
  19.0 6.3 %copy-start.11 = (bf16[256,1024]{1,0:T(8,128)(2,1)S(1)}, bf16[256,1024]{1,0:T(8,128)(2,1)}, u32[]{:S(2)}) copy-start(bf16[256,1024]{1,0:T(8,128)(2,1)} %param.13) | copy-start | bytes 1572868
  21.5 12.9 %collective-permute-start.3 = (bf16[512,256]{1,0:T(8,128)(2,1)S(1)}, bf16[512,256]{1,0:T(8,128)(2,1)S(1)}, u32[]{:S(2)}, u32[]{:S(2)}) collective-permute-start(bf16[512,256]{1,0:T(8,128)(2,1)S(1)} %shard_map.106), channel_id=1, source_target_pairs={{0,1},{1,0},{2,3},{3,2},{4,5},{5,4},{6,7},{7,6},{8,9},{9,8},{10,11... | collective-permute-start | bytes 786440 | tf_op jit(solution)/shard_map/ppermute | solution.py:25
  23.3 11.2 %collective-permute-start.5 = (bf16[512,256]{1,0:T(8,128)(2,1)S(1)}, bf16[512,256]{1,0:T(8,128)(2,1)S(1)}, u32[]{:S(2)}, u32[]{:S(2)}) collective-permute-start(bf16[512,256]{1,0:T(8,128)(2,1)S(1)} %add_convert_fusion), channel_id=1, source_target_pairs={{0,2},{1,3},{2,0},{3,1},{4,6},{5,7},{6,4},{7,5},{8,10},{9,11},{10,... | collective-permute-start | bytes 786440 | tf_op jit(solution)/shard_map/ppermute | solution.py:25
  39.1 11.4 %collective-permute-start.10 = (bf16[256,256]{1,0:T(8,128)(2,1)S(1)}, bf16[256,256]{1,0:T(8,128)(2,1)}, u32[]{:S(2)}, u32[]{:S(2)}) collective-permute-start(bf16[256,256]{1,0:T(8,128)(2,1)S(1)} %get-tuple-element.52.refs_1_.refs_4_), channel_id=1, source_target_pairs={{0,2},{1,3},{2,0},{3,1},{4,6},{5,7},{6,4},{7,5},{8,10},{9,11},{10,... | collective-permute-start | bytes 393224 | tf_op jit(solution)/shard_map/ppermute | solution.py:25
  40.8 11.8 %collective-permute-start.7 = (bf16[256,256]{1,0:T(8,128)(2,1)}, bf16[256,256]{1,0:T(8,128)(2,1)}, u32[]{:S(2)}, u32[]{:S(2)}) collective-permute-start(bf16[256,256]{1,0:T(8,128)(2,1)} %get-tuple-element.53.refs_0_), channel_id=1, source_target_pairs={{0,2},{1,3},{2,0},{3,1},{4,6},{5,7},{6,4},{7,5},{8,10},{9,11},{10,... | collective-permute-start | bytes 393224 | tf_op jit(solution)/shard_map/ppermute | solution.py:25
  42.1 10.7 %collective-permute-start.9 = (bf16[256,256]{1,0:T(8,128)(2,1)S(1)}, bf16[256,256]{1,0:T(8,128)(2,1)}, u32[]{:S(2)}, u32[]{:S(2)}) collective-permute-start(bf16[256,256]{1,0:T(8,128)(2,1)S(1)} %get-tuple-element.52.refs_1_.refs_4_), channel_id=1, source_target_pairs={{0,1},{1,0},{2,3},{3,2},{4,5},{5,4},{6,7},{7,6},{8,9},{9,8},{10,11... | collective-permute-start | bytes 393224 | tf_op jit(solution)/shard_map/ppermute | solution.py:25
  50.6 6.4 %collective-permute-start.11 = (bf16[256,256]{1,0:T(8,128)(2,1)}, bf16[256,256]{1,0:T(8,128)(2,1)}, u32[]{:S(2)}, u32[]{:S(2)}) collective-permute-start(bf16[256,256]{1,0:T(8,128)(2,1)} %collective-permute-done.10.refs_3_.refs_6_), channel_id=1, source_target_pairs={{0,1},{1,0},{2,3},{3,2},{4,5},{5,4},{6,7},{7,6},{8,9},{9,8},{10,11... | collective-permute-start | bytes 393224 | tf_op jit(solution)/shard_map/ppermute | solution.py:25
  50.6 9.9 %collective-permute-start.6 = (bf16[256,256]{1,0:T(8,128)(2,1)}, bf16[256,256]{1,0:T(8,128)(2,1)}, u32[]{:S(2)}, u32[]{:S(2)}) collective-permute-start(bf16[256,256]{1,0:T(8,128)(2,1)} %get-tuple-element.53.refs_0_), channel_id=1, source_target_pairs={{0,1},{1,0},{2,3},{3,2},{4,5},{5,4},{6,7},{7,6},{8,9},{9,8},{10,11... | collective-permute-start | bytes 393224 | tf_op jit(solution)/shard_map/ppermute | solution.py:25
  52.6 7.9 %collective-permute-start.8 = (bf16[256,256]{1,0:T(8,128)(2,1)}, bf16[256,256]{1,0:T(8,128)(2,1)}, u32[]{:S(2)}, u32[]{:S(2)}) collective-permute-start(bf16[256,256]{1,0:T(8,128)(2,1)} %collective-permute-done.7.refs_2_), channel_id=1, source_target_pairs={{0,1},{1,0},{2,3},{3,2},{4,5},{5,4},{6,7},{7,6},{8,9},{9,8},{10,11... | collective-permute-start | bytes 393224 | tf_op jit(solution)/shard_map/ppermute | solution.py:25
  58.0 2.4 %copy-start.5 = (bf16[512,1024]{1,0:T(8,128)(2,1)S(1)}, bf16[512,1024]{1,0:T(8,128)(2,1)}, u32[]{:S(2)}) copy-start(bf16[512,1024]{1,0:T(8,128)(2,1)} %copy-done.4) | copy-start | bytes 3145732
  58.1 2.4 %copy-start.8 = (bf16[512,256]{1,0:T(8,128)(2,1)S(1)}, bf16[512,256]{1,0:T(8,128)(2,1)}, u32[]{:S(2)}) copy-start(bf16[512,256]{1,0:T(8,128)(2,1)} %copy-done.7) | copy-start | bytes 786436
  58.1 2.5 %copy-start.10 = (bf16[512,256]{1,0:T(8,128)(2,1)S(1)}, bf16[512,256]{1,0:T(8,128)(2,1)}, u32[]{:S(2)}) copy-start(bf16[512,256]{1,0:T(8,128)(2,1)} %refs_17_.1) | copy-start | bytes 786436
  65.4 2.5 %collective-permute-start.12 = (bf16[384,1024]{1,0:T(8,128)(2,1)}, bf16[384,1024]{1,0:T(8,128)(2,1)S(1)}, u32[]{:S(2)}, u32[]{:S(2)}) collective-permute-start(bf16[384,1024]{1,0:T(8,128)(2,1)} %get-tuple-element.36), channel_id=1, source_target_pairs={{0,4},{1,5},{2,6},{3,7},{4,0},{5,1},{6,2},{7,3},{8,12},{9,13},{10,... | collective-permute-start | bytes 2359304 | tf_op jit(solution)/shard_map/ppermute | solution.py:25
  69.6 7.8 %collective-permute-start.13 = (bf16[96,1024]{1,0:T(8,128)(2,1)S(1)}, bf16[96,1024]{1,0:T(8,128)(2,1)S(1)}, u32[]{:S(2)}, u32[]{:S(2)}) collective-permute-start(bf16[96,1024]{1,0:T(8,128)(2,1)S(1)} %get-tuple-element.43), channel_id=1, source_target_pairs={{0,8},{1,9},{2,10},{3,11},{4,12},{5,13},{6,14},{7,15},{8,0},{9,1},... | collective-permute-start | bytes 589832 | tf_op jit(solution)/shard_map/ppermute | solution.py:25
  71.2 10.9 %collective-permute-start.14 = (bf16[96,1024]{1,0:T(8,128)(2,1)S(1)}, bf16[96,1024]{1,0:T(8,128)(2,1)S(1)}, u32[]{:S(2)}, u32[]{:S(2)}) collective-permute-start(bf16[96,1024]{1,0:T(8,128)(2,1)S(1)} %get-tuple-element.45), channel_id=1, source_target_pairs={{0,16},{1,17},{2,18},{3,19},{4,20},{5,21},{6,22},{7,23},{8,24},{9,... | collective-permute-start | bytes 589832 | tf_op jit(solution)/shard_map/ppermute | solution.py:25
  72.7 9.4 %collective-permute-start.15 = (bf16[96,1024]{1,0:T(8,128)(2,1)S(1)}, bf16[96,1024]{1,0:T(8,128)(2,1)S(1)}, u32[]{:S(2)}, u32[]{:S(2)}) collective-permute-start(bf16[96,1024]{1,0:T(8,128)(2,1)S(1)} %get-tuple-element.44), channel_id=1, source_target_pairs={{0,24},{1,25},{2,26},{3,27},{4,28},{5,29},{6,30},{7,31},{8,16},{9,... | collective-permute-start | bytes 589832 | tf_op jit(solution)/shard_map/ppermute | solution.py:25
  82.2 4.7 %collective-permute-start.16 = (bf16[24,1024]{1,0:T(8,128)(2,1)S(1)}, bf16[24,1024]{1,0:T(8,128)(2,1)S(1)}, u32[]{:S(2)}, u32[]{:S(2)}) collective-permute-start(bf16[24,1024]{1,0:T(8,128)(2,1)S(1)} %get-tuple-element.49), channel_id=1, source_target_pairs={{0,1},{1,0},{2,3},{3,2},{4,5},{5,4},{6,7},{7,6},{8,9},{9,8},{10,11... | collective-permute-start | bytes 147464 | tf_op jit(solution)/shard_map/ppermute | solution.py:25
  82.3 7.2 %collective-permute-start.17 = (bf16[24,1024]{1,0:T(8,128)(2,1)S(1)}, bf16[24,1024]{1,0:T(8,128)(2,1)S(1)}, u32[]{:S(2)}, u32[]{:S(2)}) collective-permute-start(bf16[24,1024]{1,0:T(8,128)(2,1)S(1)} %get-tuple-element.51), channel_id=1, source_target_pairs={{0,2},{1,3},{2,0},{3,1},{4,6},{5,7},{6,4},{7,5},{8,10},{9,11},{10,... | collective-permute-start | bytes 147464 | tf_op jit(solution)/shard_map/ppermute | solution.py:25
  86.9 5.9 %collective-permute-start.18 = (bf16[24,1024]{1,0:T(8,128)(2,1)S(1)}, bf16[24,1024]{1,0:T(8,128)(2,1)S(1)}, u32[]{:S(2)}, u32[]{:S(2)}) collective-permute-start(bf16[24,1024]{1,0:T(8,128)(2,1)S(1)} %get-tuple-element.50), channel_id=1, source_target_pairs={{0,3},{1,2},{2,1},{3,0},{4,7},{5,6},{6,5},{7,4},{8,11},{9,10},{10,... | collective-permute-start | bytes 147464 | tf_op jit(solution)/shard_map/ppermute | solution.py:25
  92.8 6.1 %collective-permute-start.19 = (bf16[24,1024]{1,0:T(8,128)(2,1)S(1)}, bf16[24,1024]{1,0:T(8,128)(2,1)S(1)}, u32[]{:S(2)}, u32[]{:S(2)}) collective-permute-start(bf16[24,1024]{1,0:T(8,128)(2,1)S(1)} %add_convert_fusion.1), channel_id=1, source_target_pairs={{0,3},{1,2},{2,1},{3,0},{4,7},{5,6},{6,5},{7,4},{8,11},{9,10},{10,... | collective-permute-start | bytes 147464 | tf_op jit(solution)/shard_map/ppermute | solution.py:25
  93.5 6.0 %collective-permute-start.20 = (bf16[24,1024]{1,0:T(8,128)(2,1)S(1)}, bf16[24,1024]{1,0:T(8,128)(2,1)S(1)}, u32[]{:S(2)}, u32[]{:S(2)}) collective-permute-start(bf16[24,1024]{1,0:T(8,128)(2,1)S(1)} %add_convert_fusion.1), channel_id=1, source_target_pairs={{0,2},{1,3},{2,0},{3,1},{4,6},{5,7},{6,4},{7,5},{8,10},{9,11},{10,... | collective-permute-start | bytes 147464 | tf_op jit(solution)/shard_map/ppermute | solution.py:25
  93.5 6.0 %collective-permute-start.21 = (bf16[24,1024]{1,0:T(8,128)(2,1)S(1)}, bf16[24,1024]{1,0:T(8,128)(2,1)S(1)}, u32[]{:S(2)}, u32[]{:S(2)}) collective-permute-start(bf16[24,1024]{1,0:T(8,128)(2,1)S(1)} %add_convert_fusion.1), channel_id=1, source_target_pairs={{0,1},{1,0},{2,3},{3,2},{4,5},{5,4},{6,7},{7,6},{8,9},{9,8},{10,11... | collective-permute-start | bytes 147464 | tf_op jit(solution)/shard_map/ppermute | solution.py:25
  99.6 6.7 %collective-permute-start.22 = (bf16[96,1024]{1,0:T(8,128)(2,1)S(1)}, bf16[96,1024]{1,0:T(8,128)(2,1)S(1)}, u32[]{:S(2)}, u32[]{:S(2)}) collective-permute-start(bf16[96,1024]{1,0:T(8,128)(2,1)S(1)} %pad_maximum_fusion.1), channel_id=1, source_target_pairs={{0,24},{1,25},{2,26},{3,27},{4,28},{5,29},{6,30},{7,31},{8,16},{9,... | collective-permute-start | bytes 589832 | tf_op jit(solution)/shard_map/ppermute | solution.py:25
  101.1 7.2 %collective-permute-start.23 = (bf16[96,1024]{1,0:T(8,128)(2,1)S(1)}, bf16[96,1024]{1,0:T(8,128)(2,1)S(1)}, u32[]{:S(2)}, u32[]{:S(2)}) collective-permute-start(bf16[96,1024]{1,0:T(8,128)(2,1)S(1)} %pad_maximum_fusion.1), channel_id=1, source_target_pairs={{0,16},{1,17},{2,18},{3,19},{4,20},{5,21},{6,22},{7,23},{8,24},{9,... | collective-permute-start | bytes 589832 | tf_op jit(solution)/shard_map/ppermute | solution.py:25
  102.4 6.0 %collective-permute-start.24 = (bf16[96,1024]{1,0:T(8,128)(2,1)S(1)}, bf16[96,1024]{1,0:T(8,128)(2,1)S(1)}, u32[]{:S(2)}, u32[]{:S(2)}) collective-permute-start(bf16[96,1024]{1,0:T(8,128)(2,1)S(1)} %pad_maximum_fusion.1), channel_id=1, source_target_pairs={{0,8},{1,9},{2,10},{3,11},{4,12},{5,13},{6,14},{7,15},{8,0},{9,1},... | collective-permute-start | bytes 589832 | tf_op jit(solution)/shard_map/ppermute | solution.py:25
  108.8 2.4 %collective-permute-start.25 = (bf16[384,1024]{1,0:T(8,128)(2,1)S(1)}, bf16[384,1024]{1,0:T(8,128)(2,1)S(1)}, u32[]{:S(2)}, u32[]{:S(2)}) collective-permute-start(bf16[384,1024]{1,0:T(8,128)(2,1)S(1)} %pad_maximum_fusion), channel_id=1, source_target_pairs={{0,4},{1,5},{2,6},{3,7},{4,0},{5,1},{6,2},{7,3},{8,12},{9,13},{10,... | collective-permute-start | bytes 2359304 | tf_op jit(solution)/shard_map/ppermute | solution.py:25
  (7 other events, 8.7 us)

commit v5 on v4

--- a/solution.py
+++ b/solution.py
@@ -4,6 +4,7 @@
 import jax.numpy as jnp
 from jax import lax
 from jax.experimental import pallas as pl
+from jax.experimental.layout import Layout, with_layout_constraint
 from jax.experimental.pallas import tpu as pltpu
 from jax.sharding import PartitionSpec as P
 
@@ -71,15 +72,16 @@
     return ((found[:, :low] - 1) * 16 + found[:, low:]).reshape(count, slots // count)
 
 
-def call_kernel(kernel, outs, args, flops=0, scalars=0, scratch=()):
+SPACES = {"s": pltpu.SMEM, "v": pltpu.VMEM, "a": pl.ANY}
+
+
+def call_kernel(kernel, outs, args, flops=0, spaces="", outs_in="", scratch=()):
     moved = sum(a.size * a.dtype.itemsize for a in list(args) + list(outs)) if flops else 0
-    specs = [pl.BlockSpec(memory_space=pltpu.SMEM)] * scalars
-    specs += [pl.BlockSpec(memory_space=pltpu.VMEM)] * (len(args) - scalars)
     return pl.pallas_call(
         kernel,
         out_shape=outs,
-        in_specs=specs,
-        out_specs=[pl.BlockSpec(memory_space=pltpu.VMEM)] * len(outs),
+        in_specs=[pl.BlockSpec(memory_space=SPACES[c]) for c in spaces.ljust(len(args), "v")],
+        out_specs=[pl.BlockSpec(memory_space=SPACES[c]) for c in outs_in.ljust(len(outs), "v")],
         scratch_shapes=list(scratch),
         compiler_params=pltpu.CompilerParams(vmem_limit_bytes=24 * 1024 * 1024),
         cost_estimate=pl.CostEstimate(flops=flops, bytes_accessed=moved, transcendentals=0),
@@ -149,7 +151,7 @@
             partial_kernel,
             [shape((nodes, width), BF16 if j % 2 else F32)],
             [jnp.reshape(own ^ j, (1,)), served, wanted[j]] + list(halves),
-            scalars=2,
+            spaces="ss",
             scratch=[pltpu.VMEM((cap, width // 2), F32)] * 2,
         )
         if j:
@@ -263,7 +265,39 @@
             out[width:, k * width : (k + 1) * width] = grad.astype(out.dtype)
 
 
-def backward(queries, items, projected, inv_norm, pre_act, hidden, feat, pooled, w_out, group, sizes):
+def cut_kernel(place, keep, arrived, *refs):
+    pieces = refs
+    rows = pieces[0].shape[0]
+    for j, piece in enumerate(pieces):
+        at = pl.ds(pl.multiple_of((place[0] ^ j) * rows, rows), rows)
+        piece[...] = (keep[at, :].astype(F32) + arrived[at, :].astype(F32)).astype(piece.dtype)
+
+
+def finish_kernel(place, block, other, *refs):
+    outs, held, done = refs[:3], refs[3:6], refs[6]
+    hid, width = held[2].shape
+    cut = held[0].shape[0]
+    fold = block.shape[0] - cut
+    own = place[0]
+    copies = [pltpu.make_async_copy(held[n], outs[n], done.at[n]) for n in range(3)]
+
+    def half(index, at):
+        return jnp.where(own == index, block[at], other[at]).astype(F32)
+
+    for index in range(2):
+        held[index][...] = half(index, (slice(0, cut), slice(None)))
+        copies[index].start()
+    for index in range(2):
+        for k in range(hid // width):
+            at = (slice(cut, cut + fold), slice(k * width, (k + 1) * width))
+            start = index * (hid // 2) + k * fold
+            held[2][start : start + fold, :] = half(index, at)
+    copies[2].start()
+    for copy in copies:
+        copy.wait()
+
+
+def backward(queries, items, projected, inv_norm, pre_act, hidden, feat, pooled, w_out, group, own, sizes):
     blk_size = sizes[1]
     nodes, hid = pre_act.shape
     pairs, width = queries.shape
@@ -283,30 +317,34 @@
         2 * scores * blk_size + 2 * pairs * width * hid,
     )
     rows = width + width // 2
-    return call_kernel(
+    plane = sizes[0] // 2
+    core = group % 2
+    across = group // 2
+    if plane & (plane - 1) or rows % (16 * plane) or rows % (8 * plane * blk_size):
+        plane = 1
+    keep, give = call_kernel(
         functools.partial(item_kernel, blk_size),
         [shape((rows, hid), F32), shape((rows, hid), BF16)],
-        [jnp.reshape(group % 2, (1,))]
+        [jnp.reshape(core, (1,))]
         + all_queries
         + all_items
         + [tile, row_total, projected, inv_norm, pre_act, w_out, d_proj_q, d_pre_q]
         + [hidden, feat, pooled],
         2 * scores * blk_size + 2 * pairs * width * hid + 6 * nodes * width * hid,
-        scalars=1,
-    )
-
-
-def sum_staged(keep, give, side, group, own, sizes):
-    dp_size, blk_size = sizes
-    width = keep.shape[1]
-    plane = dp_size // 2
-    core = group % 2
-    across = group // 2
-
-    def unfold(folded):
-        return jnp.concatenate(
-            [folded[:, k * side : (k + 1) * side] for k in range(width // side)], 0
-        )
+        spaces="s",
+    )
+    pieces = call_kernel(
+        cut_kernel,
+        [shape((rows // plane, hid), BF16 if j else F32) for j in range(plane)],
+        [jnp.reshape(across % plane, (1,)), keep, exchange(give, sizes, 1, 0)],
+        spaces="s",
+    )
+    return sum_staged(pieces, core, across, own, sizes)
+
+
+def sum_staged(pieces, core, across, own, sizes):
+    blk_size = sizes[1]
+    plane = len(pieces)
 
     def over_core(v, j):
         return exchange(v, sizes, j, 0)
@@ -317,9 +355,10 @@
     def over_blk(v, j):
         return exchange(v, sizes, 0, j)
 
-    total = keep + over_core(give, 1).astype(F32)
-    if plane & (plane - 1) == 0 and keep.shape[0] % (8 * plane * blk_size) == 0:
-        total = reduce_blocks(total, across, plane, over_plane)
+    total = pieces[0]
+    if plane > 1:
+        for j in range(1, plane):
+            total = total + over_plane(pieces[j], j).astype(F32)
         total = reduce_blocks(total, own, blk_size, over_blk)
         block = total.astype(BF16)
         block = gather_blocks(block, own, blk_size, over_blk)
@@ -329,11 +368,19 @@
         halves = lax.psum(halves, AXES)
         block = jnp.where(core == 0, halves[0], halves[1]).astype(BF16)
     other = over_core(block, 1)
-    first = jnp.where(core == 0, block, other)
-    second = jnp.where(core == 0, other, block)
-    cut = side
-    grad_out = jnp.concatenate([unfold(first[cut:]), unfold(second[cut:])], 0)
-    return (first[:cut].astype(F32), second[:cut].astype(F32), grad_out.astype(F32))
+    rows, hid = block.shape
+    width = rows * 2 // 3
+    outs = [(width, hid), (width, hid), (hid, width)]
+    return tuple(
+        call_kernel(
+            finish_kernel,
+            [jax.ShapeDtypeStruct(o, F32) for o in outs],
+            [jnp.reshape(core, (1,)), block, other],
+            spaces="s",
+            outs_in="aaa",
+            scratch=[pltpu.VMEM(o, F32) for o in outs] + [pltpu.SemaphoreType.DMA((3,))],
+        )
+    )
 
 
 def on_device(sizes, self_feat, nbr_mask, neighbour_slot, serve_rows, feat_store, w_self, w_nbr, w_out):
@@ -344,15 +391,16 @@
         pooled, w_nbr, preferred_element_type=F32
     )
     hidden = (pre_act * jax.nn.sigmoid(pre_act)).astype(BF16)
-    projected = jnp.dot(hidden, w_out, preferred_element_type=F32)
+    projected = with_layout_constraint(
+        jnp.dot(hidden, w_out, preferred_element_type=F32), Layout((0, 1))
+    )
     inv_norm = lax.rsqrt(jnp.mean(projected * projected, 1, keepdims=True) + 1e-06)
     embedding = (projected * inv_norm).astype(BF16)
     pairs = embedding.shape[0] // 2
     queries, items = embedding[:pairs], embedding[pairs:]
-    keep, give = backward(
-        queries, items, projected, inv_norm, pre_act, hidden, self_feat, pooled, w_out, group, sizes
-    )
-    return sum_staged(keep, give, w_out.shape[1], group, own, sizes)
+    return backward(
+        queries, items, projected, inv_norm, pre_act, hidden, self_feat, pooled, w_out, group, own, sizes
+    )
 
 
 def solution(mesh):

time: 115 us -> 111 us (0.965)
  other arithmetic: 7.58 us -> 2.98 us
  Pallas kernels: 16.7 us -> 18.6 us
    convert_element_type x2 -> x0, other arithmetic: 2.61 us -> none  [the longest x1 1.56 us: sum_staged(): second[:cut].astype(F32)]
    pallas_call x7 -> x9, Pallas kernels: 16.7 us -> 18.6 us  [call_kernel(): pl.pallas_call(kernel, out_shape=outs, in_specs=[pl.BlockSpec(memory_spac...]
    add x2 -> x1, other arithmetic: 1.7 us -> 0.09 us  [sum_staged(): total = total + over_plane(pieces[j], j).astype(F32)]
    unnamed x34 -> x29, local copies, waits for them, and re-layouts: 5.02 us -> 6.35 us
    dot_general x1 -> x0, local copies, waits for them, and re-layouts: 1.24 us -> none  [on_device(): projected = jnp.dot(hidden, w_out, preferred_element_type=F32)]
where the time goes in v5:
time: 111 us
  waiting for transfers between devices  44.2 us (40%)
  starting transfers between devices  34 us (31%)
  Pallas kernels  18.6 us (17%)
  local copies, waits for them, and re-layouts  7.5 us (7%)
  other arithmetic  2.98 us (3%)
  matrix products  2.44 us (2%)
    ppermute x26, waiting for transfers between devices, exchange(): return lax.ppermute(value, AXES, pairs)  44.2 us
    ppermute x26, starting transfers between devices, exchange(): return lax.ppermute(value, AXES, pairs)  34 us
    pallas_call x9, Pallas kernels, call_kernel(): pl.pallas_call(kernel, out_shape=outs, in_specs=[pl.BlockSpec(memory_spac...  18.6 us
    unnamed x29, local copies, waits for them, and re-layouts  6.35 us
  transfers between devices with their start and end apart: 26, of which 15 were waited for; matrix products, arithmetic and copies ran while one was open for 1% of the time, Pallas kernels for 9%

profile of v5, /device:TPU:0, one launch (start us, length us, event | category | flops | bytes accessed | tf_op | source)
XLA Modules:
  0.0 110.7 jit_solution(838012771924301465)
XLA Ops:
  3.8 5.1 %collective-permute-start = (s32[1,1024]{1,0:T(1,128)S(1)}, s32[1,1024]{1,0:T(1,128)S(1)}, u32[]{:S(2)}, u32[]{:S(2)}) collective-permute-start(s32[1,1024]{1,0:T(1,128)S(1)} %get-tuple-element.64), channel_id=1, source_target_pairs={{0,3},{1,2},{2,1},{3,0},{4,7},{5,6},{6,5},{7,4},{8,11},{9,10},{10,... | collective-permute-start | bytes 12296 | tf_op jit(solution)/shard_map/ppermute | solution.py:26
  9.6 2.2 %copy-done.1 = bf16[8192,256]{1,0:T(8,128)(2,1)S(1)} copy-done((bf16[8192,256]{1,0:T(8,128)(2,1)S(1)}, bf16[8192,256]{1,0:T(8,128)(2,1)}, u32[]{:S(2)}) %copy-start.1) | copy-done | bytes 4194328
  13.5 2.5 %shard_map.104 = bf16[512,256]{1,0:T(8,128)(2,1)S(1)} custom-call(s32[1]{0:T(128)} %bitcast.3.requester, s32[4096]{0:T(1024)S(1)} %bitcast.19, s32[1,1024]{1,0:T(1,128)S(1)} %collective-permute-done.node_at, f32[8192,128]{1,0:T(8,128)S(1)} %get-tuple-element.25.left, f32[8192,128]{1,0:T(8,128)S(1)} %get-tuple-element.26.right), custom_call_target="tpu_custom_call" | custom-call | tf_op jit(solution)/shard_map/pallas_call | solution.py:80
  16.5 2.5 %shard_map.105 = f32[512,256]{1,0:T(8,128)S(1)} custom-call(s32[1]{0:T(128)} %bitcast.6.requester, s32[4096]{0:T(1024)S(1)} %bitcast.20, s32[1,1024]{1,0:T(1,128)S(1)} %collective-permute-done.1.node_at, f32[8192,128]{1,0:T(8,128)S(1)} %get-tuple-element.25.left, f32[8192,128]{1,0:T(8,128)S(1)} %get-tuple-element.26.right), custom_call_target="tpu_custom_call" | custom-call | tf_op jit(solution)/shard_map/pallas_call | solution.py:80
  19.0 2.5 %shard_map.106 = bf16[512,256]{1,0:T(8,128)(2,1)S(1)} custom-call(s32[1]{0:T(128)} %bitcast.7.requester, s32[4096]{0:T(1024)S(1)} %bitcast.21, s32[1,1024]{1,0:T(1,128)S(1)} %collective-permute-done.2.node_at, f32[8192,128]{1,0:T(8,128)S(1)} %get-tuple-element.25.left, f32[8192,128]{1,0:T(8,128)S(1)} %get-tuple-element.26.right), custom_call_target="tpu_custom_call" | custom-call | tf_op jit(solution)/shard_map/pallas_call | solution.py:80
  21.5 1.6 %collective-permute-start.3 = (bf16[512,256]{1,0:T(8,128)(2,1)S(1)}, bf16[512,256]{1,0:T(8,128)(2,1)S(1)}, u32[]{:S(2)}, u32[]{:S(2)}) collective-permute-start(bf16[512,256]{1,0:T(8,128)(2,1)S(1)} %shard_map.106), channel_id=1, source_target_pairs={{0,1},{1,0},{2,3},{3,2},{4,5},{5,4},{6,7},{7,6},{8,9},{9,8},{10,11... | collective-permute-start | bytes 786440 | tf_op jit(solution)/shard_map/ppermute | solution.py:26
  23.3 2.1 %collective-permute-start.5 = (bf16[512,256]{1,0:T(8,128)(2,1)S(1)}, bf16[512,256]{1,0:T(8,128)(2,1)S(1)}, u32[]{:S(2)}, u32[]{:S(2)}) collective-permute-start(bf16[512,256]{1,0:T(8,128)(2,1)S(1)} %add_convert_fusion), channel_id=1, source_target_pairs={{0,2},{1,3},{2,0},{3,1},{4,6},{5,7},{6,4},{7,5},{8,10},{9,11},{10,... | collective-permute-start | bytes 786440 | tf_op jit(solution)/shard_map/ppermute | solution.py:26
  25.8 2.5 %shard_map.107 = f32[512,256]{1,0:T(8,128)S(1)} custom-call(s32[1]{0:T(128)} %bitcast.2.requester, s32[4096]{0:T(1024)S(1)} %bitcast.22, s32[1,1024]{1,0:T(1,128)S(1)} %get-tuple-element.61.node_at, f32[8192,128]{1,0:T(8,128)S(1)} %get-tuple-element.25.left, f32[8192,128]{1,0:T(8,128)S(1)} %get-tuple-element.26.right), custom_call_target="tpu_custom_call" | custom-call | tf_op jit(solution)/shard_map/pallas_call | solution.py:80
  28.3 6.1 %collective-permute-done.3 = bf16[512,256]{1,0:T(8,128)(2,1)S(1)} collective-permute-done((bf16[512,256]{1,0:T(8,128)(2,1)S(1)}, bf16[512,256]{1,0:T(8,128)(2,1)S(1)}, u32[]{:S(2)}, u32[]{:S(2)}) %collective-permute-start.3) | collective-permute-done | bytes 262176 | tf_op jit(solution)/shard_map/ppermute | solution.py:26
  37.1 1.7 %collective-permute-start.10 = (bf16[256,256]{1,0:T(8,128)(2,1)S(1)}, bf16[256,256]{1,0:T(8,128)(2,1)}, u32[]{:S(2)}, u32[]{:S(2)}) collective-permute-start(bf16[256,256]{1,0:T(8,128)(2,1)S(1)} %get-tuple-element.55.refs_1_.refs_4_), channel_id=1, source_target_pairs={{0,2},{1,3},{2,0},{3,1},{4,6},{5,7},{6,4},{7,5},{8,10},{9,11},{10,... | collective-permute-start | bytes 393224 | tf_op jit(solution)/shard_map/ppermute | solution.py:26
  40.1 2.6 %collective-permute-start.9 = (bf16[256,256]{1,0:T(8,128)(2,1)S(1)}, bf16[256,256]{1,0:T(8,128)(2,1)}, u32[]{:S(2)}, u32[]{:S(2)}) collective-permute-start(bf16[256,256]{1,0:T(8,128)(2,1)S(1)} %get-tuple-element.55.refs_1_.refs_4_), channel_id=1, source_target_pairs={{0,1},{1,0},{2,3},{3,2},{4,5},{5,4},{6,7},{7,6},{8,9},{9,8},{10,11... | collective-permute-start | bytes 393224 | tf_op jit(solution)/shard_map/ppermute | solution.py:26
  42.7 5.9 %collective-permute-done.10.refs_3_.refs_6_ = bf16[256,256]{1,0:T(8,128)(2,1)} collective-permute-done((bf16[256,256]{1,0:T(8,128)(2,1)S(1)}, bf16[256,256]{1,0:T(8,128)(2,1)}, u32[]{:S(2)}, u32[]{:S(2)}) %collective-permute-start.10) | collective-permute-done | bytes 131104 | tf_op jit(solution)/shard_map/ppermute | solution.py:26
  48.6 2.0 %collective-permute-start.6 = (bf16[256,256]{1,0:T(8,128)(2,1)}, bf16[256,256]{1,0:T(8,128)(2,1)}, u32[]{:S(2)}, u32[]{:S(2)}) collective-permute-start(bf16[256,256]{1,0:T(8,128)(2,1)} %get-tuple-element.56.refs_0_), channel_id=1, source_target_pairs={{0,1},{1,0},{2,3},{3,2},{4,5},{5,4},{6,7},{7,6},{8,9},{9,8},{10,11... | collective-permute-start | bytes 393224 | tf_op jit(solution)/shard_map/ppermute | solution.py:26
  50.8 4.2 %collective-permute-done.11.refs_4_.refs_7_ = bf16[256,256]{1,0:T(8,128)(2,1)} collective-permute-done((bf16[256,256]{1,0:T(8,128)(2,1)}, bf16[256,256]{1,0:T(8,128)(2,1)}, u32[]{:S(2)}, u32[]{:S(2)}) %collective-permute-start.11) | collective-permute-done | bytes 131104 | tf_op jit(solution)/shard_map/ppermute | solution.py:26
  56.1 2.4 %shard_map.108 = (bf16[256,256]{1,0:T(8,128)(2,1)S(1)}, f32[256,1]{1,0:T(8,128)S(1)}, bf16[256,256]{1,0:T(8,128)(2,1)S(1)}, bf16[256,1024]{1,0:T(8,128)(2,1)S(1)}) custom-call(bf16[256,256]{1,0:T(8,128)(2,1)} %get-tuple-element.56.refs_0_, bf16[256,256]{1,0:T(8,128)(2,1)S(1)} %get-tuple-element.55.refs_1_.refs_4_, ...), custom_call_target="tpu_custom_call" | custom-call | flops 402653184 | bytes 4590592 | tf_op jit(solution)/shard_map/pallas_call | solution.py:80
  58.5 3.7 %shard_map.109 = (f32[384,1024]{1,0:T(8,128)S(1)}, bf16[384,1024]{1,0:T(8,128)(2,1)}) custom-call(s32[1]{0:T(128)} %bitcast.core_ref.place, bf16[256,256]{1,0:T(8,128)(2,1)} %get-tuple-element.56.refs_0_, bf16[256,256]{1,0:T(8,128)(2,1)} %collective-permute-done.6.refs_1_, bf16[256,256]{1,0:T(8,128)(2,1)} %collective-permute-done.7.refs_2_, ...), custom_call_target="tpu_custom_call" | custom-call | flops 1207959552 | bytes 8915972 | tf_op jit(solution)/shard_map/pallas_call | solution.py:80
  63.4 2.5 %collective-permute-done.12.arrived = bf16[384,1024]{1,0:T(8,128)(2,1)S(1)} collective-permute-done((bf16[384,1024]{1,0:T(8,128)(2,1)}, bf16[384,1024]{1,0:T(8,128)(2,1)S(1)}, u32[]{:S(2)}, u32[]{:S(2)}) %collective-permute-start.12) | collective-permute-done | bytes 786464 | tf_op jit(solution)/shard_map/ppermute | solution.py:26
  65.9 1.4 %copy-done.5 = f32[384,1024]{1,0:T(8,128)S(1)} copy-done((f32[384,1024]{1,0:T(8,128)S(1)}, f32[384,1024]{1,0:T(8,128)}, u32[]{:S(2)}) %copy-start.5) | copy-done | bytes 1572888
  67.5 1.5 %collective-permute-start.13 = (bf16[96,1024]{1,0:T(8,128)(2,1)S(1)}, bf16[96,1024]{1,0:T(8,128)(2,1)S(1)}, u32[]{:S(2)}, u32[]{:S(2)}) collective-permute-start(bf16[96,1024]{1,0:T(8,128)(2,1)S(1)} %get-tuple-element.42), channel_id=1, source_target_pairs={{0,8},{1,9},{2,10},{3,11},{4,12},{5,13},{6,14},{7,15},{8,0},{9,1},... | collective-permute-start | bytes 589832 | tf_op jit(solution)/shard_map/ppermute | solution.py:26
  69.0 1.5 %collective-permute-start.14 = (bf16[96,1024]{1,0:T(8,128)(2,1)S(1)}, bf16[96,1024]{1,0:T(8,128)(2,1)S(1)}, u32[]{:S(2)}, u32[]{:S(2)}) collective-permute-start(bf16[96,1024]{1,0:T(8,128)(2,1)S(1)} %get-tuple-element.43), channel_id=1, source_target_pairs={{0,16},{1,17},{2,18},{3,19},{4,20},{5,21},{6,22},{7,23},{8,24},{9,... | collective-permute-start | bytes 589832 | tf_op jit(solution)/shard_map/ppermute | solution.py:26
  71.0 4.3 %collective-permute-done.13 = bf16[96,1024]{1,0:T(8,128)(2,1)S(1)} collective-permute-done((bf16[96,1024]{1,0:T(8,128)(2,1)S(1)}, bf16[96,1024]{1,0:T(8,128)(2,1)S(1)}, u32[]{:S(2)}, u32[]{:S(2)}) %collective-permute-start.13) | collective-permute-done | bytes 196640 | tf_op jit(solution)/shard_map/ppermute | solution.py:26
  75.3 4.6 %collective-permute-done.14 = bf16[96,1024]{1,0:T(8,128)(2,1)S(1)} collective-permute-done((bf16[96,1024]{1,0:T(8,128)(2,1)S(1)}, bf16[96,1024]{1,0:T(8,128)(2,1)S(1)}, u32[]{:S(2)}, u32[]{:S(2)}) %collective-permute-start.14) | collective-permute-done | bytes 196640 | tf_op jit(solution)/shard_map/ppermute | solution.py:26
  80.1 4.6 %collective-permute-start.17 = (bf16[24,1024]{1,0:T(8,128)(2,1)S(1)}, bf16[24,1024]{1,0:T(8,128)(2,1)S(1)}, u32[]{:S(2)}, u32[]{:S(2)}) collective-permute-start(bf16[24,1024]{1,0:T(8,128)(2,1)S(1)} %get-tuple-element.54), channel_id=1, source_target_pairs={{0,2},{1,3},{2,0},{3,1},{4,6},{5,7},{6,4},{7,5},{8,10},{9,11},{10,... | collective-permute-start | bytes 147464 | tf_op jit(solution)/shard_map/ppermute | solution.py:26
  84.8 2.6 %collective-permute-done.17 = bf16[24,1024]{1,0:T(8,128)(2,1)S(1)} collective-permute-done((bf16[24,1024]{1,0:T(8,128)(2,1)S(1)}, bf16[24,1024]{1,0:T(8,128)(2,1)S(1)}, u32[]{:S(2)}, u32[]{:S(2)}) %collective-permute-start.17) | collective-permute-done | bytes 49184 | tf_op jit(solution)/shard_map/ppermute | solution.py:26
  87.3 3.3 %collective-permute-done.18 = bf16[24,1024]{1,0:T(8,128)(2,1)S(1)} collective-permute-done((bf16[24,1024]{1,0:T(8,128)(2,1)S(1)}, bf16[24,1024]{1,0:T(8,128)(2,1)S(1)}, u32[]{:S(2)}, u32[]{:S(2)}) %collective-permute-start.18) | collective-permute-done | bytes 49184 | tf_op jit(solution)/shard_map/ppermute | solution.py:26
  91.3 3.8 %collective-permute-start.21 = (bf16[24,1024]{1,0:T(8,128)(2,1)S(1)}, bf16[24,1024]{1,0:T(8,128)(2,1)S(1)}, u32[]{:S(2)}, u32[]{:S(2)}) collective-permute-start(bf16[24,1024]{1,0:T(8,128)(2,1)S(1)} %add_convert_fusion.1), channel_id=1, source_target_pairs={{0,1},{1,0},{2,3},{3,2},{4,5},{5,4},{6,7},{7,6},{8,9},{9,8},{10,11... | collective-permute-start | bytes 147464 | tf_op jit(solution)/shard_map/ppermute | solution.py:26
  95.2 1.6 %collective-permute-done.19 = bf16[24,1024]{1,0:T(8,128)(2,1)S(1)} collective-permute-done((bf16[24,1024]{1,0:T(8,128)(2,1)S(1)}, bf16[24,1024]{1,0:T(8,128)(2,1)S(1)}, u32[]{:S(2)}, u32[]{:S(2)}) %collective-permute-start.19) | collective-permute-done | bytes 49184 | tf_op jit(solution)/shard_map/ppermute | solution.py:26
  97.4 1.6 %collective-permute-start.22 = (bf16[96,1024]{1,0:T(8,128)(2,1)S(1)}, bf16[96,1024]{1,0:T(8,128)(2,1)S(1)}, u32[]{:S(2)}, u32[]{:S(2)}) collective-permute-start(bf16[96,1024]{1,0:T(8,128)(2,1)S(1)} %pad_maximum_fusion.1), channel_id=1, source_target_pairs={{0,24},{1,25},{2,26},{3,27},{4,28},{5,29},{6,30},{7,31},{8,16},{9,... | collective-permute-start | bytes 589832 | tf_op jit(solution)/shard_map/ppermute | solution.py:26
  101.0 3.2 %collective-permute-done.22 = bf16[96,1024]{1,0:T(8,128)(2,1)S(1)} collective-permute-done((bf16[96,1024]{1,0:T(8,128)(2,1)S(1)}, bf16[96,1024]{1,0:T(8,128)(2,1)S(1)}, u32[]{:S(2)}, u32[]{:S(2)}) %collective-permute-start.22) | collective-permute-done | bytes 196640 | tf_op jit(solution)/shard_map/ppermute | solution.py:26
  104.1 2.0 %collective-permute-done.23 = bf16[96,1024]{1,0:T(8,128)(2,1)S(1)} collective-permute-done((bf16[96,1024]{1,0:T(8,128)(2,1)S(1)}, bf16[96,1024]{1,0:T(8,128)(2,1)S(1)}, u32[]{:S(2)}, u32[]{:S(2)}) %collective-permute-start.23) | collective-permute-done | bytes 196640 | tf_op jit(solution)/shard_map/ppermute | solution.py:26
  106.7 2.3 %collective-permute-done.25.other = bf16[384,1024]{1,0:T(8,128)(2,1)S(1)} collective-permute-done((bf16[384,1024]{1,0:T(8,128)(2,1)S(1)}, bf16[384,1024]{1,0:T(8,128)(2,1)S(1)}, u32[]{:S(2)}, u32[]{:S(2)}) %collective-permute-start.25) | collective-permute-done | bytes 786464 | tf_op jit(solution)/shard_map/ppermute | solution.py:26
  109.0 1.8 %shard_map.111 = (f32[256,1024]{1,0:T(8,128)}, f32[256,1024]{1,0:T(8,128)}, f32[1024,256]{1,0:T(8,128)}) custom-call(s32[1]{0:T(128)} %bitcast.core_ref.place, bf16[384,1024]{1,0:T(8,128)(2,1)S(1)} %pad_maximum_fusion.block, bf16[384,1024]{1,0:T(8,128)(2,1)S(1)} %collective-permute-done.25.other), custom_call_target="tpu_custom_call" | custom-call | tf_op jit(solution)/shard_map/pallas_call | solution.py:80
  (87 shorter events, 17.5 us)
Async XLA Ops:
  0.6 34.0 %copy-start = (bf16[256,1024]{1,0:T(8,128)(2,1)S(1)}, bf16[256,1024]{1,0:T(8,128)(2,1)}, u32[]{:S(2)}) copy-start(bf16[256,1024]{1,0:T(8,128)(2,1)} %param.14) | copy-start | bytes 1572868
  3.8 8.7 %collective-permute-start = (s32[1,1024]{1,0:T(1,128)S(1)}, s32[1,1024]{1,0:T(1,128)S(1)}, u32[]{:S(2)}, u32[]{:S(2)}) collective-permute-start(s32[1,1024]{1,0:T(1,128)S(1)} %get-tuple-element.64), channel_id=1, source_target_pairs={{0,3},{1,2},{2,1},{3,0},{4,7},{5,6},{6,5},{7,4},{8,11},{9,10},{10,... | collective-permute-start | bytes 12296 | tf_op jit(solution)/shard_map/ppermute | solution.py:26
  9.0 4.5 %collective-permute-start.1 = (s32[1,1024]{1,0:T(1,128)S(1)}, s32[1,1024]{1,0:T(1,128)S(1)}, u32[]{:S(2)}, u32[]{:S(2)}) collective-permute-start(s32[1,1024]{1,0:T(1,128)S(1)} %get-tuple-element.63), channel_id=1, source_target_pairs={{0,2},{1,3},{2,0},{3,1},{4,6},{5,7},{6,4},{7,5},{8,10},{9,11},{10,... | collective-permute-start | bytes 12296 | tf_op jit(solution)/shard_map/ppermute | solution.py:26
  9.0 4.5 %collective-permute-start.2 = (s32[1,1024]{1,0:T(1,128)S(1)}, s32[1,1024]{1,0:T(1,128)S(1)}, u32[]{:S(2)}, u32[]{:S(2)}) collective-permute-start(s32[1,1024]{1,0:T(1,128)S(1)} %get-tuple-element.62), channel_id=1, source_target_pairs={{0,1},{1,0},{2,3},{3,2},{4,5},{5,4},{6,7},{7,6},{8,9},{9,8},{10,11... | collective-permute-start | bytes 12296 | tf_op jit(solution)/shard_map/ppermute | solution.py:26
  16.0 7.2 %collective-permute-start.4 = (bf16[512,256]{1,0:T(8,128)(2,1)S(1)}, bf16[512,256]{1,0:T(8,128)(2,1)S(1)}, u32[]{:S(2)}, u32[]{:S(2)}) collective-permute-start(bf16[512,256]{1,0:T(8,128)(2,1)S(1)} %shard_map.104), channel_id=1, source_target_pairs={{0,1},{1,0},{2,3},{3,2},{4,5},{5,4},{6,7},{7,6},{8,9},{9,8},{10,11... | collective-permute-start | bytes 786440 | tf_op jit(solution)/shard_map/ppermute | solution.py:26
  19.0 6.3 %copy-start.10 = (bf16[512,256]{1,0:T(8,128)(2,1)S(1)}, bf16[512,256]{1,0:T(8,128)(2,1)}, u32[]{:S(2)}) copy-start(bf16[512,256]{1,0:T(8,128)(2,1)} %refs_17_.1) | copy-start | bytes 786436
  19.0 6.3 %copy-start.12 = (bf16[256,1024]{1,0:T(8,128)(2,1)S(1)}, bf16[256,1024]{1,0:T(8,128)(2,1)}, u32[]{:S(2)}) copy-start(bf16[256,1024]{1,0:T(8,128)(2,1)} %param.13) | copy-start | bytes 1572868
  21.5 12.9 %collective-permute-start.3 = (bf16[512,256]{1,0:T(8,128)(2,1)S(1)}, bf16[512,256]{1,0:T(8,128)(2,1)S(1)}, u32[]{:S(2)}, u32[]{:S(2)}) collective-permute-start(bf16[512,256]{1,0:T(8,128)(2,1)S(1)} %shard_map.106), channel_id=1, source_target_pairs={{0,1},{1,0},{2,3},{3,2},{4,5},{5,4},{6,7},{7,6},{8,9},{9,8},{10,11... | collective-permute-start | bytes 786440 | tf_op jit(solution)/shard_map/ppermute | solution.py:26
  23.3 11.2 %collective-permute-start.5 = (bf16[512,256]{1,0:T(8,128)(2,1)S(1)}, bf16[512,256]{1,0:T(8,128)(2,1)S(1)}, u32[]{:S(2)}, u32[]{:S(2)}) collective-permute-start(bf16[512,256]{1,0:T(8,128)(2,1)S(1)} %add_convert_fusion), channel_id=1, source_target_pairs={{0,2},{1,3},{2,0},{3,1},{4,6},{5,7},{6,4},{7,5},{8,10},{9,11},{10,... | collective-permute-start | bytes 786440 | tf_op jit(solution)/shard_map/ppermute | solution.py:26
  35.4 13.2 %copy-start.8 = (bf16[512,1024]{1,0:T(8,128)(2,1)}, bf16[512,1024]{1,0:T(8,128)(2,1)S(1)}, u32[]{:S(2)}) copy-start(bf16[512,1024]{1,0:T(8,128)(2,1)S(1)} %get-tuple-element.69.refs_16_) | copy-start | bytes 3145732
  37.1 11.4 %collective-permute-start.10 = (bf16[256,256]{1,0:T(8,128)(2,1)S(1)}, bf16[256,256]{1,0:T(8,128)(2,1)}, u32[]{:S(2)}, u32[]{:S(2)}) collective-permute-start(bf16[256,256]{1,0:T(8,128)(2,1)S(1)} %get-tuple-element.55.refs_1_.refs_4_), channel_id=1, source_target_pairs={{0,2},{1,3},{2,0},{3,1},{4,6},{5,7},{6,4},{7,5},{8,10},{9,11},{10,... | collective-permute-start | bytes 393224 | tf_op jit(solution)/shard_map/ppermute | solution.py:26
  38.8 11.8 %collective-permute-start.7 = (bf16[256,256]{1,0:T(8,128)(2,1)}, bf16[256,256]{1,0:T(8,128)(2,1)}, u32[]{:S(2)}, u32[]{:S(2)}) collective-permute-start(bf16[256,256]{1,0:T(8,128)(2,1)} %get-tuple-element.56.refs_0_), channel_id=1, source_target_pairs={{0,2},{1,3},{2,0},{3,1},{4,6},{5,7},{6,4},{7,5},{8,10},{9,11},{10,... | collective-permute-start | bytes 393224 | tf_op jit(solution)/shard_map/ppermute | solution.py:26
  40.1 10.7 %collective-permute-start.9 = (bf16[256,256]{1,0:T(8,128)(2,1)S(1)}, bf16[256,256]{1,0:T(8,128)(2,1)}, u32[]{:S(2)}, u32[]{:S(2)}) collective-permute-start(bf16[256,256]{1,0:T(8,128)(2,1)S(1)} %get-tuple-element.55.refs_1_.refs_4_), channel_id=1, source_target_pairs={{0,1},{1,0},{2,3},{3,2},{4,5},{5,4},{6,7},{7,6},{8,9},{9,8},{10,11... | collective-permute-start | bytes 393224 | tf_op jit(solution)/shard_map/ppermute | solution.py:26
  48.6 6.4 %collective-permute-start.11 = (bf16[256,256]{1,0:T(8,128)(2,1)}, bf16[256,256]{1,0:T(8,128)(2,1)}, u32[]{:S(2)}, u32[]{:S(2)}) collective-permute-start(bf16[256,256]{1,0:T(8,128)(2,1)} %collective-permute-done.10.refs_3_.refs_6_), channel_id=1, source_target_pairs={{0,1},{1,0},{2,3},{3,2},{4,5},{5,4},{6,7},{7,6},{8,9},{9,8},{10,11... | collective-permute-start | bytes 393224 | tf_op jit(solution)/shard_map/ppermute | solution.py:26
  48.6 9.9 %collective-permute-start.6 = (bf16[256,256]{1,0:T(8,128)(2,1)}, bf16[256,256]{1,0:T(8,128)(2,1)}, u32[]{:S(2)}, u32[]{:S(2)}) collective-permute-start(bf16[256,256]{1,0:T(8,128)(2,1)} %get-tuple-element.56.refs_0_), channel_id=1, source_target_pairs={{0,1},{1,0},{2,3},{3,2},{4,5},{5,4},{6,7},{7,6},{8,9},{9,8},{10,11... | collective-permute-start | bytes 393224 | tf_op jit(solution)/shard_map/ppermute | solution.py:26
  50.6 7.9 %collective-permute-start.8 = (bf16[256,256]{1,0:T(8,128)(2,1)}, bf16[256,256]{1,0:T(8,128)(2,1)}, u32[]{:S(2)}, u32[]{:S(2)}) collective-permute-start(bf16[256,256]{1,0:T(8,128)(2,1)} %collective-permute-done.7.refs_2_), channel_id=1, source_target_pairs={{0,1},{1,0},{2,3},{3,2},{4,5},{5,4},{6,7},{7,6},{8,9},{9,8},{10,11... | collective-permute-start | bytes 393224 | tf_op jit(solution)/shard_map/ppermute | solution.py:26
  56.1 2.4 %copy-start.9 = (bf16[512,1024]{1,0:T(8,128)(2,1)S(1)}, bf16[512,1024]{1,0:T(8,128)(2,1)}, u32[]{:S(2)}) copy-start(bf16[512,1024]{1,0:T(8,128)(2,1)} %copy-done.8) | copy-start | bytes 3145732
  56.1 2.4 %copy-start.11 = (bf16[512,256]{1,0:T(8,128)(2,1)S(1)}, bf16[512,256]{1,0:T(8,128)(2,1)}, u32[]{:S(2)}) copy-start(bf16[512,256]{1,0:T(8,128)(2,1)} %refs_17_.1) | copy-start | bytes 786436
  63.4 2.5 %collective-permute-start.12 = (bf16[384,1024]{1,0:T(8,128)(2,1)}, bf16[384,1024]{1,0:T(8,128)(2,1)S(1)}, u32[]{:S(2)}, u32[]{:S(2)}) collective-permute-start(bf16[384,1024]{1,0:T(8,128)(2,1)} %get-tuple-element.40), channel_id=1, source_target_pairs={{0,4},{1,5},{2,6},{3,7},{4,0},{5,1},{6,2},{7,3},{8,12},{9,13},{10,... | collective-permute-start | bytes 2359304 | tf_op jit(solution)/shard_map/ppermute | solution.py:26
  67.5 7.8 %collective-permute-start.13 = (bf16[96,1024]{1,0:T(8,128)(2,1)S(1)}, bf16[96,1024]{1,0:T(8,128)(2,1)S(1)}, u32[]{:S(2)}, u32[]{:S(2)}) collective-permute-start(bf16[96,1024]{1,0:T(8,128)(2,1)S(1)} %get-tuple-element.42), channel_id=1, source_target_pairs={{0,8},{1,9},{2,10},{3,11},{4,12},{5,13},{6,14},{7,15},{8,0},{9,1},... | collective-permute-start | bytes 589832 | tf_op jit(solution)/shard_map/ppermute | solution.py:26
  69.0 10.9 %collective-permute-start.14 = (bf16[96,1024]{1,0:T(8,128)(2,1)S(1)}, bf16[96,1024]{1,0:T(8,128)(2,1)S(1)}, u32[]{:S(2)}, u32[]{:S(2)}) collective-permute-start(bf16[96,1024]{1,0:T(8,128)(2,1)S(1)} %get-tuple-element.43), channel_id=1, source_target_pairs={{0,16},{1,17},{2,18},{3,19},{4,20},{5,21},{6,22},{7,23},{8,24},{9,... | collective-permute-start | bytes 589832 | tf_op jit(solution)/shard_map/ppermute | solution.py:26
  70.5 9.4 %collective-permute-start.15 = (bf16[96,1024]{1,0:T(8,128)(2,1)S(1)}, bf16[96,1024]{1,0:T(8,128)(2,1)S(1)}, u32[]{:S(2)}, u32[]{:S(2)}) collective-permute-start(bf16[96,1024]{1,0:T(8,128)(2,1)S(1)} %get-tuple-element.44), channel_id=1, source_target_pairs={{0,24},{1,25},{2,26},{3,27},{4,28},{5,29},{6,30},{7,31},{8,16},{9,... | collective-permute-start | bytes 589832 | tf_op jit(solution)/shard_map/ppermute | solution.py:26
  80.0 4.8 %collective-permute-start.16 = (bf16[24,1024]{1,0:T(8,128)(2,1)S(1)}, bf16[24,1024]{1,0:T(8,128)(2,1)S(1)}, u32[]{:S(2)}, u32[]{:S(2)}) collective-permute-start(bf16[24,1024]{1,0:T(8,128)(2,1)S(1)} %get-tuple-element.52), channel_id=1, source_target_pairs={{0,1},{1,0},{2,3},{3,2},{4,5},{5,4},{6,7},{7,6},{8,9},{9,8},{10,11... | collective-permute-start | bytes 147464 | tf_op jit(solution)/shard_map/ppermute | solution.py:26
  80.1 7.2 %collective-permute-start.17 = (bf16[24,1024]{1,0:T(8,128)(2,1)S(1)}, bf16[24,1024]{1,0:T(8,128)(2,1)S(1)}, u32[]{:S(2)}, u32[]{:S(2)}) collective-permute-start(bf16[24,1024]{1,0:T(8,128)(2,1)S(1)} %get-tuple-element.54), channel_id=1, source_target_pairs={{0,2},{1,3},{2,0},{3,1},{4,6},{5,7},{6,4},{7,5},{8,10},{9,11},{10,... | collective-permute-start | bytes 147464 | tf_op jit(solution)/shard_map/ppermute | solution.py:26
  84.8 5.9 %collective-permute-start.18 = (bf16[24,1024]{1,0:T(8,128)(2,1)S(1)}, bf16[24,1024]{1,0:T(8,128)(2,1)S(1)}, u32[]{:S(2)}, u32[]{:S(2)}) collective-permute-start(bf16[24,1024]{1,0:T(8,128)(2,1)S(1)} %get-tuple-element.53), channel_id=1, source_target_pairs={{0,3},{1,2},{2,1},{3,0},{4,7},{5,6},{6,5},{7,4},{8,11},{9,10},{10,... | collective-permute-start | bytes 147464 | tf_op jit(solution)/shard_map/ppermute | solution.py:26
  90.7 6.1 %collective-permute-start.19 = (bf16[24,1024]{1,0:T(8,128)(2,1)S(1)}, bf16[24,1024]{1,0:T(8,128)(2,1)S(1)}, u32[]{:S(2)}, u32[]{:S(2)}) collective-permute-start(bf16[24,1024]{1,0:T(8,128)(2,1)S(1)} %add_convert_fusion.1), channel_id=1, source_target_pairs={{0,3},{1,2},{2,1},{3,0},{4,7},{5,6},{6,5},{7,4},{8,11},{9,10},{10,... | collective-permute-start | bytes 147464 | tf_op jit(solution)/shard_map/ppermute | solution.py:26
  91.3 6.0 %collective-permute-start.20 = (bf16[24,1024]{1,0:T(8,128)(2,1)S(1)}, bf16[24,1024]{1,0:T(8,128)(2,1)S(1)}, u32[]{:S(2)}, u32[]{:S(2)}) collective-permute-start(bf16[24,1024]{1,0:T(8,128)(2,1)S(1)} %add_convert_fusion.1), channel_id=1, source_target_pairs={{0,2},{1,3},{2,0},{3,1},{4,6},{5,7},{6,4},{7,5},{8,10},{9,11},{10,... | collective-permute-start | bytes 147464 | tf_op jit(solution)/shard_map/ppermute | solution.py:26
  91.3 6.0 %collective-permute-start.21 = (bf16[24,1024]{1,0:T(8,128)(2,1)S(1)}, bf16[24,1024]{1,0:T(8,128)(2,1)S(1)}, u32[]{:S(2)}, u32[]{:S(2)}) collective-permute-start(bf16[24,1024]{1,0:T(8,128)(2,1)S(1)} %add_convert_fusion.1), channel_id=1, source_target_pairs={{0,1},{1,0},{2,3},{3,2},{4,5},{5,4},{6,7},{7,6},{8,9},{9,8},{10,11... | collective-permute-start | bytes 147464 | tf_op jit(solution)/shard_map/ppermute | solution.py:26
  97.4 6.7 %collective-permute-start.22 = (bf16[96,1024]{1,0:T(8,128)(2,1)S(1)}, bf16[96,1024]{1,0:T(8,128)(2,1)S(1)}, u32[]{:S(2)}, u32[]{:S(2)}) collective-permute-start(bf16[96,1024]{1,0:T(8,128)(2,1)S(1)} %pad_maximum_fusion.1), channel_id=1, source_target_pairs={{0,24},{1,25},{2,26},{3,27},{4,28},{5,29},{6,30},{7,31},{8,16},{9,... | collective-permute-start | bytes 589832 | tf_op jit(solution)/shard_map/ppermute | solution.py:26
  99.0 7.2 %collective-permute-start.23 = (bf16[96,1024]{1,0:T(8,128)(2,1)S(1)}, bf16[96,1024]{1,0:T(8,128)(2,1)S(1)}, u32[]{:S(2)}, u32[]{:S(2)}) collective-permute-start(bf16[96,1024]{1,0:T(8,128)(2,1)S(1)} %pad_maximum_fusion.1), channel_id=1, source_target_pairs={{0,16},{1,17},{2,18},{3,19},{4,20},{5,21},{6,22},{7,23},{8,24},{9,... | collective-permute-start | bytes 589832 | tf_op jit(solution)/shard_map/ppermute | solution.py:26
  100.3 6.0 %collective-permute-start.24 = (bf16[96,1024]{1,0:T(8,128)(2,1)S(1)}, bf16[96,1024]{1,0:T(8,128)(2,1)S(1)}, u32[]{:S(2)}, u32[]{:S(2)}) collective-permute-start(bf16[96,1024]{1,0:T(8,128)(2,1)S(1)} %pad_maximum_fusion.1), channel_id=1, source_target_pairs={{0,8},{1,9},{2,10},{3,11},{4,12},{5,13},{6,14},{7,15},{8,0},{9,1},... | collective-permute-start | bytes 589832 | tf_op jit(solution)/shard_map/ppermute | solution.py:26
  106.6 2.4 %collective-permute-start.25 = (bf16[384,1024]{1,0:T(8,128)(2,1)S(1)}, bf16[384,1024]{1,0:T(8,128)(2,1)S(1)}, u32[]{:S(2)}, u32[]{:S(2)}) collective-permute-start(bf16[384,1024]{1,0:T(8,128)(2,1)S(1)} %pad_maximum_fusion.block), channel_id=1, source_target_pairs={{0,4},{1,5},{2,6},{3,7},{4,0},{5,1},{6,2},{7,3},{8,12},{9,13},{10,... | collective-permute-start | bytes 2359304 | tf_op jit(solution)/shard_map/ppermute | solution.py:26
  (8 other events, 10.9 us)

commit v6 on v5

--- a/solution.py
+++ b/solution.py
@@ -125,7 +125,7 @@
     out[...] = jnp.dot(pick, rows, preferred_element_type=F32).astype(out.dtype)
 
 
-def pooled_mean(nbr_mask, neighbour_slot, serve_rows, feat_store, own, sizes):
+def pooled_sums(nbr_mask, neighbour_slot, serve_rows, feat_store, own, sizes):
     blk_size = sizes[1]
     nodes = nbr_mask.shape[0]
     first_col = lax.broadcasted_iota(jnp.int32, nbr_mask.shape, 1) == 0
@@ -156,20 +156,44 @@
         )
         if j:
             served, parts[j] = lax.optimization_barrier((served, parts[j]))
+    halves = (slice(nodes // 2, nodes), slice(0, nodes // 2))
     for_own = []
     bit = 1
     while bit < blk_size:
         for j in [j for j in order if j & bit and j in parts]:
-            arrived = exchange(parts.pop(j).astype(BF16), sizes, 0, bit)
+            part = parts.pop(j)
+            if j == bit and 2 * bit >= blk_size:
+                for_own.append([exchange(part[h].astype(BF16), sizes, 0, bit) for h in halves])
+                continue
+            arrived = exchange(part.astype(BF16), sizes, 0, bit)
             if j == bit:
-                for_own.append(arrived)
+                for_own.append([arrived[h] for h in halves])
             else:
                 parts[j ^ bit] = parts[j ^ bit] + arrived.astype(F32)
         bit *= 2
-    total = parts[0]
-    for part in for_own:
+    return (
+        [parts[0][h] for h in halves],
+        [[arrived[n] for arrived in for_own] for n in range(2)],
+        [live_count[h] for h in halves],
+    )
+
+
+def mean_of(own_part, arrived, live_count):
+    total = own_part
+    for part in arrived:
         total = total + part.astype(F32)
     return (total / live_count).astype(BF16)
+
+
+def forward(own_part, pooled, w_nbr, w_out):
+    pre_act = own_part + jnp.dot(pooled, w_nbr, preferred_element_type=F32)
+    hidden = (pre_act * jax.nn.sigmoid(pre_act)).astype(BF16)
+    projected = with_layout_constraint(
+        jnp.dot(hidden, w_out, preferred_element_type=F32), Layout((0, 1))
+    )
+    inv_norm = lax.rsqrt(jnp.mean(projected * projected, 1, keepdims=True) + 1e-06)
+    embedding = (projected * inv_norm).astype(BF16)
+    return embedding, projected, pre_act, hidden
 
 
 def spread(block, sizes):
@@ -191,7 +215,8 @@
     return jnp.sum(q.astype(F32) * i.astype(F32), 1, keepdims=True) * scale
 
 
-def through_norm(d_embed, proj, inv):
+def through_norm(d_embed, proj):
+    inv = lax.rsqrt(jnp.mean(proj * proj, 1, keepdims=True) + 1e-06)
     interior = jnp.mean(d_embed * proj, 1, keepdims=True)
     return (inv * d_embed - proj * inv**3 * interior).astype(BF16)
 
@@ -204,7 +229,7 @@
 
 def query_kernel(group_size, *refs):
     queries, items = refs[0], refs[1 : 1 + group_size]
-    proj, inv, pre, w_out, tile, row_total, d_proj, d_pre = refs[1 + group_size :]
+    proj, pre, w_out, tile, row_total, d_proj, d_pre = refs[1 + group_size :]
     q, own_items = queries[...], items[0][...]
     pairs, width = q.shape
     scale = width ** (-0.5)
@@ -221,16 +246,15 @@
         d_query += jnp.dot(rounded, block, preferred_element_type=F32)
     row_total[...] = total
     d_query = (d_query - total * own_items.astype(F32)) * scale
-    d_p = through_norm(d_query, proj[:pairs], inv[:pairs])
+    d_p = through_norm(d_query, proj[...])
     d_proj[...] = d_p
-    d_pre[...] = through_gate(d_p, pre[:pairs], w_out[...])
+    d_pre[...] = through_gate(d_p, pre[...], w_out[...])
 
 
 def item_kernel(group_size, core_ref, *refs):
     queries, items = refs[:group_size], refs[group_size : 2 * group_size]
-    (tile, row_total, proj, inv, pre, w_out, d_proj_q, d_pre_q, hidden, feat, pooled, keep, give) = refs[
-        2 * group_size :
-    ]
+    tile, row_total, proj, pre, w_out, d_proj_q, d_pre_q = refs[2 * group_size :][:7]
+    hidden_q, hidden_i, feat, pooled_q, pooled_i, keep, give = refs[2 * group_size + 7 :]
     own_items, q = items[0][...], queries[0][...]
     pairs, width = q.shape
     scale = width ** (-0.5)
@@ -243,25 +267,29 @@
         positive = positive_of(block, items[j][...], scale)
         weights = pair_weights(block, own_items, positive, scale, group_size * pairs).astype(BF16)
         d_item += lax.dot_general(weights, block, OVER_ROWS, preferred_element_type=F32)
-    d_proj = jnp.concatenate(
-        [d_proj_q[...], through_norm(d_item * scale, proj[pairs:], inv[pairs:])], 0
-    )
-    d_pre = jnp.concatenate(
-        [d_pre_q[...], through_gate(d_proj[pairs:], pre[pairs:], w_out[...])], 0
-    )
+    d_proj_i = through_norm(d_item * scale, proj[...])
+    d_proj = (d_proj_q[...], d_proj_i)
+    d_pre = (d_pre_q[...], through_gate(d_proj_i, pre[...], w_out[...]))
+    feats = (feat[:pairs], feat[pairs:])
+    pooled = (pooled_q[...], pooled_i[...])
+    hiddens = (hidden_q, hidden_i)
+
+    def over_nodes(left, right):
+        return sum(
+            lax.dot_general(a, b, OVER_ROWS, preferred_element_type=F32)
+            for a, b in zip(left, right)
+        )
+
     core = core_ref[0]
     hid = pre.shape[1]
     cut = hid // 2
     fold = cut * width // hid
     for half, out in ((1 - core, give), (core, keep)):
-        rows = jnp.where(half == 0, feat[...], pooled[...])
-        grad = lax.dot_general(rows, d_pre, OVER_ROWS, preferred_element_type=F32)
-        out[:width] = grad.astype(out.dtype)
+        rows = [jnp.where(half == 0, a, b) for a, b in zip(feats, pooled)]
+        out[:width] = over_nodes(rows, d_pre).astype(out.dtype)
         for k in range(hid // width):
-            start = pl.multiple_of(half * cut + k * fold, fold)
-            grad = lax.dot_general(
-                hidden[:, pl.ds(start, fold)], d_proj, OVER_ROWS, preferred_element_type=F32
-            )
+            columns = pl.ds(pl.multiple_of(half * cut + k * fold, fold), fold)
+            grad = over_nodes([h[:, columns] for h in hiddens], d_proj)
             out[width:, k * width : (k + 1) * width] = grad.astype(out.dtype)
 
 
@@ -297,10 +325,12 @@
         copy.wait()
 
 
-def backward(queries, items, projected, inv_norm, pre_act, hidden, feat, pooled, w_out, group, own, sizes):
+def backward(query_side, item_side, feat, pooled_q, pooled_i, w_out, group, own, sizes):
     blk_size = sizes[1]
-    nodes, hid = pre_act.shape
+    queries, *saved_q, hidden_q = query_side
+    items, *saved_i, hidden_i = item_side
     pairs, width = queries.shape
+    nodes, hid = 2 * pairs, hidden_q.shape[1]
     all_items = [items] + spread(items, sizes)
     all_queries = [queries] + spread(queries, sizes)
     shape = jax.ShapeDtypeStruct
@@ -313,7 +343,7 @@
             shape((pairs, width), BF16),
             shape((pairs, hid), BF16),
         ],
-        [queries] + all_items + [projected, inv_norm, pre_act, w_out],
+        [queries] + all_items + saved_q + [w_out],
         2 * scores * blk_size + 2 * pairs * width * hid,
     )
     rows = width + width // 2
@@ -328,8 +358,9 @@
         [jnp.reshape(core, (1,))]
         + all_queries
         + all_items
-        + [tile, row_total, projected, inv_norm, pre_act, w_out, d_proj_q, d_pre_q]
-        + [hidden, feat, pooled],
+        + [tile, row_total]
+        + saved_i
+        + [w_out, d_proj_q, d_pre_q, hidden_q, hidden_i, feat, pooled_q, pooled_i],
         2 * scores * blk_size + 2 * pairs * width * hid + 6 * nodes * width * hid,
         spaces="s",
     )
@@ -386,20 +417,19 @@
 def on_device(sizes, self_feat, nbr_mask, neighbour_slot, serve_rows, feat_store, w_self, w_nbr, w_out):
     group = lax.axis_index("dp")
     own = lax.axis_index("blk")
-    pooled = pooled_mean(nbr_mask, neighbour_slot, serve_rows, feat_store, own, sizes)
-    pre_act = jnp.dot(self_feat, w_self, preferred_element_type=F32) + jnp.dot(
-        pooled, w_nbr, preferred_element_type=F32
-    )
-    hidden = (pre_act * jax.nn.sigmoid(pre_act)).astype(BF16)
-    projected = with_layout_constraint(
-        jnp.dot(hidden, w_out, preferred_element_type=F32), Layout((0, 1))
-    )
-    inv_norm = lax.rsqrt(jnp.mean(projected * projected, 1, keepdims=True) + 1e-06)
-    embedding = (projected * inv_norm).astype(BF16)
-    pairs = embedding.shape[0] // 2
-    queries, items = embedding[:pairs], embedding[pairs:]
+    own_sums, arrived, live = pooled_sums(
+        nbr_mask, neighbour_slot, serve_rows, feat_store, own, sizes
+    )
+    pairs = self_feat.shape[0] // 2
+    own_part = lax.optimization_barrier(jnp.dot(self_feat, w_self, preferred_element_type=F32))
+    pooled_i = mean_of(own_sums[0], arrived[0], live[0])
+    items, *item_side = forward(own_part[pairs:], pooled_i, w_nbr, w_out)
+    _, later = lax.optimization_barrier((items, arrived[1]))
+    pooled_q = mean_of(own_sums[1], later, live[1])
+    item_side = (items, *item_side)
+    query_side = forward(own_part[:pairs], pooled_q, w_nbr, w_out)
     return backward(
-        queries, items, projected, inv_norm, pre_act, hidden, self_feat, pooled, w_out, group, own, sizes
+        query_side, item_side, self_feat, pooled_q, pooled_i, w_out, group, own, sizes
     )
 
 

time: 111 us -> 110 us (level)
  waiting for transfers between devices: 44.2 us -> 36.9 us
  starting transfers between devices: 34 us -> 39 us
  matrix products: 2.44 us -> 4.63 us
    ppermute x26 -> x27, waiting for transfers between devices: 44.2 us -> 36.9 us  [exchange(): return lax.ppermute(value, AXES, pairs)]
    ppermute x26 -> x27, starting transfers between devices: 34 us -> 39 us  [exchange(): return lax.ppermute(value, AXES, pairs)]
    dot_general x2 -> x4, matrix products: 1.28 us -> 3.47 us  [the longest x2 2.71 us: forward(): pre_act = own_part + jnp.dot(pooled, w_nbr, preferred_element_type=F32)]
    unnamed x29 -> x21, local copies, waits for them, and re-layouts: 6.35 us -> 6.04 us
  transfers between devices with their start and end apart: 26 -> 27, of which waited for: 15 -> 16; matrix products, arithmetic and copies ran while one was open for 1% -> 4% of each run, Pallas kernels for 9% -> 9%
where the time goes in v6:
time: 110 us
  starting transfers between devices  39 us (35%)
  waiting for transfers between devices  36.9 us (34%)
  Pallas kernels  18.5 us (17%)
  local copies, waits for them, and re-layouts  6.4 us (6%)
  matrix products  4.63 us (4%)
  other arithmetic  3.13 us (3%)
    ppermute x27, starting transfers between devices, exchange(): return lax.ppermute(value, AXES, pairs)  39 us
    ppermute x27, waiting for transfers between devices, exchange(): return lax.ppermute(value, AXES, pairs)  36.9 us
    pallas_call x9, Pallas kernels, call_kernel(): pl.pallas_call(kernel, out_shape=outs, in_specs=[pl.BlockSpec(memory_spac...  18.5 us
    unnamed x21, local copies, waits for them, and re-layouts  6.04 us
    dot_general x2, matrix products, forward(): pre_act = own_part + jnp.dot(pooled, w_nbr, preferred_element_type=F32)  2.71 us
  transfers between devices with their start and end apart: 27, of which 16 were waited for; matrix products, arithmetic and copies ran while one was open for 4% of the time, Pallas kernels for 9%

profile of v6, /device:TPU:0, one launch (start us, length us, event | category | flops | bytes accessed | tf_op | source)
XLA Modules:
  0.0 109.7 jit_solution(3334342420474122620)
XLA Ops:
  3.9 5.1 %collective-permute-start = (s32[1,1024]{1,0:T(1,128)S(1)}, s32[1,1024]{1,0:T(1,128)S(1)}, u32[]{:S(2)}, u32[]{:S(2)}) collective-permute-start(s32[1,1024]{1,0:T(1,128)S(1)} %get-tuple-element.68), channel_id=1, source_target_pairs={{0,3},{1,2},{2,1},{3,0},{4,7},{5,6},{6,5},{7,4},{8,11},{9,10},{10,... | collective-permute-start | bytes 12296 | tf_op jit(solution)/shard_map/ppermute | solution.py:26
  9.6 2.2 %copy-done.2 = bf16[8192,256]{1,0:T(8,128)(2,1)S(1)} copy-done((bf16[8192,256]{1,0:T(8,128)(2,1)S(1)}, bf16[8192,256]{1,0:T(8,128)(2,1)}, u32[]{:S(2)}) %copy-start.2) | copy-done | bytes 4194328
  13.5 2.5 %shard_map.104 = bf16[512,256]{1,0:T(8,128)(2,1)S(1)} custom-call(s32[1]{0:T(128)} %bitcast.3.requester, s32[4096]{0:T(1024)S(1)} %bitcast.22, s32[1,1024]{1,0:T(1,128)S(1)} %collective-permute-done.node_at, f32[8192,128]{1,0:T(8,128)S(1)} %get-tuple-element.27.left, f32[8192,128]{1,0:T(8,128)S(1)} %get-tuple-element.28.right), custom_call_target="tpu_custom_call" | custom-call | tf_op jit(solution)/shard_map/pallas_call | solution.py:80
  16.9 2.5 %shard_map.105 = f32[512,256]{1,0:T(8,128)S(1)} custom-call(s32[1]{0:T(128)} %bitcast.6.requester, s32[4096]{0:T(1024)S(1)} %bitcast.23, s32[1,1024]{1,0:T(1,128)S(1)} %collective-permute-done.1.node_at, f32[8192,128]{1,0:T(8,128)S(1)} %get-tuple-element.27.left, f32[8192,128]{1,0:T(8,128)S(1)} %get-tuple-element.28.right), custom_call_target="tpu_custom_call" | custom-call | tf_op jit(solution)/shard_map/pallas_call | solution.py:80
  19.4 2.5 %shard_map.106 = bf16[512,256]{1,0:T(8,128)(2,1)S(1)} custom-call(s32[1]{0:T(128)} %bitcast.7.requester, s32[4096]{0:T(1024)S(1)} %bitcast.24, s32[1,1024]{1,0:T(1,128)S(1)} %collective-permute-done.2.node_at, f32[8192,128]{1,0:T(8,128)S(1)} %get-tuple-element.27.left, f32[8192,128]{1,0:T(8,128)S(1)} %get-tuple-element.28.right), custom_call_target="tpu_custom_call" | custom-call | tf_op jit(solution)/shard_map/pallas_call | solution.py:80
  21.9 1.7 %collective-permute-start.3 = (bf16[512,256]{1,0:T(8,128)(2,1)S(1)}, bf16[512,256]{1,0:T(8,128)(2,1)S(1)}, u32[]{:S(2)}, u32[]{:S(2)}) collective-permute-start(bf16[512,256]{1,0:T(8,128)(2,1)S(1)} %shard_map.106), channel_id=1, source_target_pairs={{0,1},{1,0},{2,3},{3,2},{4,5},{5,4},{6,7},{7,6},{8,9},{9,8},{10,11... | collective-permute-start | bytes 786440 | tf_op jit(solution)/shard_map/ppermute | solution.py:26
  23.7 2.1 %collective-permute-start.5 = (bf16[256,256]{1,0:T(8,128)(2,1)S(1)}, bf16[256,256]{1,0:T(8,128)(2,1)S(1)}, u32[]{:S(2)}, u32[]{:S(2)}) collective-permute-start(bf16[256,256]{1,0:T(8,128)(2,1)S(1)} %get-tuple-element.60), channel_id=1, source_target_pairs={{0,2},{1,3},{2,0},{3,1},{4,6},{5,7},{6,4},{7,5},{8,10},{9,11},{10,... | collective-permute-start | bytes 393224 | tf_op jit(solution)/shard_map/ppermute | solution.py:26
  25.8 2.5 %shard_map.107 = f32[512,256]{1,0:T(8,128)S(1)} custom-call(s32[1]{0:T(128)} %bitcast.2.requester, s32[4096]{0:T(1024)S(1)} %bitcast.25, s32[1,1024]{1,0:T(1,128)S(1)} %get-tuple-element.65.node_at, f32[8192,128]{1,0:T(8,128)S(1)} %get-tuple-element.27.left, f32[8192,128]{1,0:T(8,128)S(1)} %get-tuple-element.28.right), custom_call_target="tpu_custom_call" | custom-call | tf_op jit(solution)/shard_map/pallas_call | solution.py:80
  29.3 4.3 %collective-permute-done.3 = bf16[512,256]{1,0:T(8,128)(2,1)S(1)} collective-permute-done((bf16[512,256]{1,0:T(8,128)(2,1)S(1)}, bf16[512,256]{1,0:T(8,128)(2,1)S(1)}, u32[]{:S(2)}, u32[]{:S(2)}) %collective-permute-start.3) | collective-permute-done | bytes 262176 | tf_op jit(solution)/shard_map/ppermute | solution.py:26
  35.6 1.6 %collective-permute-start.11 = (bf16[256,256]{1,0:T(8,128)(2,1)S(1)}, bf16[256,256]{1,0:T(8,128)(2,1)S(1)}, u32[]{:S(2)}, u32[]{:S(2)}) collective-permute-start(bf16[256,256]{1,0:T(8,128)(2,1)S(1)} %multiply_convert_fusion.3.refs_1_.refs_4_), channel_id=1, source_target_pairs={{0,2},{1,3},{2,0},{3,1},{4,6},{5,7},{6,4},{7,5},{8,10},{9,11},{10,... | collective-permute-start | bytes 393224 | tf_op jit(solution)/shard_map/ppermute | solution.py:26
  37.2 3.5 %collective-permute-done.6 = bf16[256,256]{1,0:T(8,128)(2,1)S(1)} collective-permute-done((bf16[256,256]{1,0:T(8,128)(2,1)S(1)}, bf16[256,256]{1,0:T(8,128)(2,1)S(1)}, u32[]{:S(2)}, u32[]{:S(2)}) %collective-permute-start.6) | collective-permute-done | bytes 131104 | tf_op jit(solution)/shard_map/ppermute | solution.py:26
  42.7 5.4 %collective-permute-start.10 = (bf16[256,256]{1,0:T(8,128)(2,1)S(1)}, bf16[256,256]{1,0:T(8,128)(2,1)}, u32[]{:S(2)}, u32[]{:S(2)}) collective-permute-start(bf16[256,256]{1,0:T(8,128)(2,1)S(1)} %multiply_convert_fusion.3.refs_1_.refs_4_), channel_id=1, source_target_pairs={{0,1},{1,0},{2,3},{3,2},{4,5},{5,4},{6,7},{7,6},{8,9},{9,8},{10,11... | collective-permute-start | bytes 393224 | tf_op jit(solution)/shard_map/ppermute | solution.py:26
  48.1 2.0 %collective-permute-start.7 = (bf16[256,256]{1,0:T(8,128)(2,1)S(1)}, bf16[256,256]{1,0:T(8,128)(2,1)}, u32[]{:S(2)}, u32[]{:S(2)}) collective-permute-start(bf16[256,256]{1,0:T(8,128)(2,1)S(1)} %multiply_convert_fusion.2.refs_0_), channel_id=1, source_target_pairs={{0,1},{1,0},{2,3},{3,2},{4,5},{5,4},{6,7},{7,6},{8,9},{9,8},{10,11... | collective-permute-start | bytes 393224 | tf_op jit(solution)/shard_map/ppermute | solution.py:26
  50.1 2.5 %collective-permute-start.9 = (bf16[256,256]{1,0:T(8,128)(2,1)}, bf16[256,256]{1,0:T(8,128)(2,1)}, u32[]{:S(2)}, u32[]{:S(2)}) collective-permute-start(bf16[256,256]{1,0:T(8,128)(2,1)} %collective-permute-done.8.refs_2_), channel_id=1, source_target_pairs={{0,1},{1,0},{2,3},{3,2},{4,5},{5,4},{6,7},{7,6},{8,9},{9,8},{10,11... | collective-permute-start | bytes 393224 | tf_op jit(solution)/shard_map/ppermute | solution.py:26
  55.1 2.2 %shard_map.108 = (bf16[256,256]{1,0:T(8,128)(2,1)S(1)}, f32[256,1]{1,0:T(8,128)S(1)}, bf16[256,256]{1,0:T(8,128)(2,1)S(1)}, bf16[256,1024]{1,0:T(8,128)(2,1)S(1)}) custom-call(bf16[256,256]{1,0:T(8,128)(2,1)S(1)} %multiply_convert_fusion.2.refs_0_, bf16[256,256]{1,0:T(8,128)(2,1)S(1)} %multiply_convert_fusion.3.refs_1_.refs_4_, ...), custom_call_target="tpu_custom_call" | custom-call | flops 402653184 | bytes 3277824 | tf_op jit(solution)/shard_map/pallas_call | solution.py:80
  57.3 3.9 %shard_map.109 = (f32[384,1024]{1,0:T(8,128)S(1)}, bf16[384,1024]{1,0:T(8,128)(2,1)}) custom-call(s32[1]{0:T(128)} %bitcast.core_ref.place, bf16[256,256]{1,0:T(8,128)(2,1)S(1)} %multiply_convert_fusion.2.refs_0_, bf16[256,256]{1,0:T(8,128)(2,1)} %collective-permute-done.7.refs_1_, bf16[256,256]{1,0:T(8,128)(2,1)} %collective-permute-done.8.refs_2_, ...), custom_call_target="tpu_custom_call" | custom-call | flops 1207959552 | bytes 7603204 | tf_op jit(solution)/shard_map/pallas_call | solution.py:80
  62.4 2.5 %collective-permute-done.13.arrived = bf16[384,1024]{1,0:T(8,128)(2,1)S(1)} collective-permute-done((bf16[384,1024]{1,0:T(8,128)(2,1)}, bf16[384,1024]{1,0:T(8,128)(2,1)S(1)}, u32[]{:S(2)}, u32[]{:S(2)}) %collective-permute-start.13) | collective-permute-done | bytes 786464 | tf_op jit(solution)/shard_map/ppermute | solution.py:26
  66.4 2.5 %collective-permute-start.16 = (bf16[96,1024]{1,0:T(8,128)(2,1)S(1)}, bf16[96,1024]{1,0:T(8,128)(2,1)S(1)}, u32[]{:S(2)}, u32[]{:S(2)}) collective-permute-start(bf16[96,1024]{1,0:T(8,128)(2,1)S(1)} %get-tuple-element.48), channel_id=1, source_target_pairs={{0,24},{1,25},{2,26},{3,27},{4,28},{5,29},{6,30},{7,31},{8,16},{9,... | collective-permute-start | bytes 589832 | tf_op jit(solution)/shard_map/ppermute | solution.py:26
  70.0 5.2 %collective-permute-done.16 = bf16[96,1024]{1,0:T(8,128)(2,1)S(1)} collective-permute-done((bf16[96,1024]{1,0:T(8,128)(2,1)S(1)}, bf16[96,1024]{1,0:T(8,128)(2,1)S(1)}, u32[]{:S(2)}, u32[]{:S(2)}) %collective-permute-start.16) | collective-permute-done | bytes 196640 | tf_op jit(solution)/shard_map/ppermute | solution.py:26
  75.2 3.4 %collective-permute-done.15 = bf16[96,1024]{1,0:T(8,128)(2,1)S(1)} collective-permute-done((bf16[96,1024]{1,0:T(8,128)(2,1)S(1)}, bf16[96,1024]{1,0:T(8,128)(2,1)S(1)}, u32[]{:S(2)}, u32[]{:S(2)}) %collective-permute-start.15) | collective-permute-done | bytes 196640 | tf_op jit(solution)/shard_map/ppermute | solution.py:26
  78.8 4.3 %collective-permute-start.19 = (bf16[24,1024]{1,0:T(8,128)(2,1)S(1)}, bf16[24,1024]{1,0:T(8,128)(2,1)S(1)}, u32[]{:S(2)}, u32[]{:S(2)}) collective-permute-start(bf16[24,1024]{1,0:T(8,128)(2,1)S(1)} %get-tuple-element.57), channel_id=1, source_target_pairs={{0,3},{1,2},{2,1},{3,0},{4,7},{5,6},{6,5},{7,4},{8,11},{9,10},{10,... | collective-permute-start | bytes 147464 | tf_op jit(solution)/shard_map/ppermute | solution.py:26
  83.7 1.7 %collective-permute-done.19 = bf16[24,1024]{1,0:T(8,128)(2,1)S(1)} collective-permute-done((bf16[24,1024]{1,0:T(8,128)(2,1)S(1)}, bf16[24,1024]{1,0:T(8,128)(2,1)S(1)}, u32[]{:S(2)}, u32[]{:S(2)}) %collective-permute-start.19) | collective-permute-done | bytes 49184 | tf_op jit(solution)/shard_map/ppermute | solution.py:26
  85.4 2.6 %collective-permute-done.18 = bf16[24,1024]{1,0:T(8,128)(2,1)S(1)} collective-permute-done((bf16[24,1024]{1,0:T(8,128)(2,1)S(1)}, bf16[24,1024]{1,0:T(8,128)(2,1)S(1)}, u32[]{:S(2)}, u32[]{:S(2)}) %collective-permute-start.18) | collective-permute-done | bytes 49184 | tf_op jit(solution)/shard_map/ppermute | solution.py:26
  88.1 2.0 %collective-permute-start.20 = (bf16[24,1024]{1,0:T(8,128)(2,1)S(1)}, bf16[24,1024]{1,0:T(8,128)(2,1)S(1)}, u32[]{:S(2)}, u32[]{:S(2)}) collective-permute-start(bf16[24,1024]{1,0:T(8,128)(2,1)S(1)} %add_convert_fusion.1), channel_id=1, source_target_pairs={{0,3},{1,2},{2,1},{3,0},{4,7},{5,6},{6,5},{7,4},{8,11},{9,10},{10,... | collective-permute-start | bytes 147464 | tf_op jit(solution)/shard_map/ppermute | solution.py:26
  90.3 2.2 %collective-permute-start.22 = (bf16[24,1024]{1,0:T(8,128)(2,1)S(1)}, bf16[24,1024]{1,0:T(8,128)(2,1)S(1)}, u32[]{:S(2)}, u32[]{:S(2)}) collective-permute-start(bf16[24,1024]{1,0:T(8,128)(2,1)S(1)} %add_convert_fusion.1), channel_id=1, source_target_pairs={{0,1},{1,0},{2,3},{3,2},{4,5},{5,4},{6,7},{7,6},{8,9},{9,8},{10,11... | collective-permute-start | bytes 147464 | tf_op jit(solution)/shard_map/ppermute | solution.py:26
  92.5 1.7 %collective-permute-done.20 = bf16[24,1024]{1,0:T(8,128)(2,1)S(1)} collective-permute-done((bf16[24,1024]{1,0:T(8,128)(2,1)S(1)}, bf16[24,1024]{1,0:T(8,128)(2,1)S(1)}, u32[]{:S(2)}, u32[]{:S(2)}) %collective-permute-start.20) | collective-permute-done | bytes 49184 | tf_op jit(solution)/shard_map/ppermute | solution.py:26
  94.2 1.4 %collective-permute-done.21 = bf16[24,1024]{1,0:T(8,128)(2,1)S(1)} collective-permute-done((bf16[24,1024]{1,0:T(8,128)(2,1)S(1)}, bf16[24,1024]{1,0:T(8,128)(2,1)S(1)}, u32[]{:S(2)}, u32[]{:S(2)}) %collective-permute-start.21) | collective-permute-done | bytes 49184 | tf_op jit(solution)/shard_map/ppermute | solution.py:26
  96.9 1.8 %collective-permute-start.24 = (bf16[96,1024]{1,0:T(8,128)(2,1)S(1)}, bf16[96,1024]{1,0:T(8,128)(2,1)S(1)}, u32[]{:S(2)}, u32[]{:S(2)}) collective-permute-start(bf16[96,1024]{1,0:T(8,128)(2,1)S(1)} %pad_maximum_fusion.1), channel_id=1, source_target_pairs={{0,16},{1,17},{2,18},{3,19},{4,20},{5,21},{6,22},{7,23},{8,24},{9,... | collective-permute-start | bytes 589832 | tf_op jit(solution)/shard_map/ppermute | solution.py:26
  99.2 3.8 %collective-permute-done.23 = bf16[96,1024]{1,0:T(8,128)(2,1)S(1)} collective-permute-done((bf16[96,1024]{1,0:T(8,128)(2,1)S(1)}, bf16[96,1024]{1,0:T(8,128)(2,1)S(1)}, u32[]{:S(2)}, u32[]{:S(2)}) %collective-permute-start.23) | collective-permute-done | bytes 196640 | tf_op jit(solution)/shard_map/ppermute | solution.py:26
  103.1 2.0 %collective-permute-done.24 = bf16[96,1024]{1,0:T(8,128)(2,1)S(1)} collective-permute-done((bf16[96,1024]{1,0:T(8,128)(2,1)S(1)}, bf16[96,1024]{1,0:T(8,128)(2,1)S(1)}, u32[]{:S(2)}, u32[]{:S(2)}) %collective-permute-start.24) | collective-permute-done | bytes 196640 | tf_op jit(solution)/shard_map/ppermute | solution.py:26
  105.6 2.3 %collective-permute-done.26.other = bf16[384,1024]{1,0:T(8,128)(2,1)S(1)} collective-permute-done((bf16[384,1024]{1,0:T(8,128)(2,1)S(1)}, bf16[384,1024]{1,0:T(8,128)(2,1)S(1)}, u32[]{:S(2)}, u32[]{:S(2)}) %collective-permute-start.26) | collective-permute-done | bytes 786464 | tf_op jit(solution)/shard_map/ppermute | solution.py:26
  107.9 1.8 %shard_map.111 = (f32[256,1024]{1,0:T(8,128)}, f32[256,1024]{1,0:T(8,128)}, f32[1024,256]{1,0:T(8,128)}) custom-call(s32[1]{0:T(128)} %bitcast.core_ref.place, bf16[384,1024]{1,0:T(8,128)(2,1)S(1)} %pad_maximum_fusion.block, bf16[384,1024]{1,0:T(8,128)(2,1)S(1)} %collective-permute-done.26.other), custom_call_target="tpu_custom_call" | custom-call | tf_op jit(solution)/shard_map/pallas_call | solution.py:80
  (87 shorter events, 21.2 us)
Async XLA Ops:
  0.6 33.1 %copy-start = (bf16[256,1024]{1,0:T(8,128)(2,1)S(1)}, bf16[256,1024]{1,0:T(8,128)(2,1)}, u32[]{:S(2)}) copy-start(bf16[256,1024]{1,0:T(8,128)(2,1)} %param.14) | copy-start | bytes 1572868
  3.0 6.6 %copy-start.9 = (s32[4,1024]{1,0:T(4,128)S(1)}, s32[4,1024]{1,0:T(4,128)}, u32[]{:S(2)}) copy-start(s32[4,1024]{1,0:T(4,128)} %param.11) | copy-start | bytes 49156
  3.9 8.5 %collective-permute-start = (s32[1,1024]{1,0:T(1,128)S(1)}, s32[1,1024]{1,0:T(1,128)S(1)}, u32[]{:S(2)}, u32[]{:S(2)}) collective-permute-start(s32[1,1024]{1,0:T(1,128)S(1)} %get-tuple-element.68), channel_id=1, source_target_pairs={{0,3},{1,2},{2,1},{3,0},{4,7},{5,6},{6,5},{7,4},{8,11},{9,10},{10,... | collective-permute-start | bytes 12296 | tf_op jit(solution)/shard_map/ppermute | solution.py:26
  9.0 4.5 %collective-permute-start.1 = (s32[1,1024]{1,0:T(1,128)S(1)}, s32[1,1024]{1,0:T(1,128)S(1)}, u32[]{:S(2)}, u32[]{:S(2)}) collective-permute-start(s32[1,1024]{1,0:T(1,128)S(1)} %get-tuple-element.67), channel_id=1, source_target_pairs={{0,2},{1,3},{2,0},{3,1},{4,6},{5,7},{6,4},{7,5},{8,10},{9,11},{10,... | collective-permute-start | bytes 12296 | tf_op jit(solution)/shard_map/ppermute | solution.py:26
  9.0 4.5 %collective-permute-start.2 = (s32[1,1024]{1,0:T(1,128)S(1)}, s32[1,1024]{1,0:T(1,128)S(1)}, u32[]{:S(2)}, u32[]{:S(2)}) collective-permute-start(s32[1,1024]{1,0:T(1,128)S(1)} %get-tuple-element.66), channel_id=1, source_target_pairs={{0,1},{1,0},{2,3},{3,2},{4,5},{5,4},{6,7},{7,6},{8,9},{9,8},{10,11... | collective-permute-start | bytes 12296 | tf_op jit(solution)/shard_map/ppermute | solution.py:26
  9.6 2.2 %copy-start.2 = (bf16[8192,256]{1,0:T(8,128)(2,1)S(1)}, bf16[8192,256]{1,0:T(8,128)(2,1)}, u32[]{:S(2)}) copy-start(bf16[8192,256]{1,0:T(8,128)(2,1)} %store.1) | copy-start | bytes 12582916
  13.5 2.9 %copy-start.7 = (bf16[512,256]{1,0:T(8,128)(2,1)S(1)}, bf16[512,256]{1,0:T(8,128)(2,1)}, u32[]{:S(2)}) copy-start(bf16[512,256]{1,0:T(8,128)(2,1)} %refs_17_.1) | copy-start | bytes 786436
  13.5 2.9 %copy-start.8 = (bf16[256,1024]{1,0:T(8,128)(2,1)S(1)}, bf16[256,1024]{1,0:T(8,128)(2,1)}, u32[]{:S(2)}) copy-start(bf16[256,1024]{1,0:T(8,128)(2,1)} %param.13) | copy-start | bytes 1572868
  16.0 7.6 %collective-permute-start.4 = (bf16[512,256]{1,0:T(8,128)(2,1)S(1)}, bf16[512,256]{1,0:T(8,128)(2,1)S(1)}, u32[]{:S(2)}, u32[]{:S(2)}) collective-permute-start(bf16[512,256]{1,0:T(8,128)(2,1)S(1)} %shard_map.104), channel_id=1, source_target_pairs={{0,1},{1,0},{2,3},{3,2},{4,5},{5,4},{6,7},{7,6},{8,9},{9,8},{10,11... | collective-permute-start | bytes 786440 | tf_op jit(solution)/shard_map/ppermute | solution.py:26
  21.9 11.7 %collective-permute-start.3 = (bf16[512,256]{1,0:T(8,128)(2,1)S(1)}, bf16[512,256]{1,0:T(8,128)(2,1)S(1)}, u32[]{:S(2)}, u32[]{:S(2)}) collective-permute-start(bf16[512,256]{1,0:T(8,128)(2,1)S(1)} %shard_map.106), channel_id=1, source_target_pairs={{0,1},{1,0},{2,3},{3,2},{4,5},{5,4},{6,7},{7,6},{8,9},{9,8},{10,11... | collective-permute-start | bytes 786440 | tf_op jit(solution)/shard_map/ppermute | solution.py:26
  23.7 9.8 %collective-permute-start.5 = (bf16[256,256]{1,0:T(8,128)(2,1)S(1)}, bf16[256,256]{1,0:T(8,128)(2,1)S(1)}, u32[]{:S(2)}, u32[]{:S(2)}) collective-permute-start(bf16[256,256]{1,0:T(8,128)(2,1)S(1)} %get-tuple-element.60), channel_id=1, source_target_pairs={{0,2},{1,3},{2,0},{3,1},{4,6},{5,7},{6,4},{7,5},{8,10},{9,11},{10,... | collective-permute-start | bytes 393224 | tf_op jit(solution)/shard_map/ppermute | solution.py:26
  28.3 12.3 %collective-permute-start.6 = (bf16[256,256]{1,0:T(8,128)(2,1)S(1)}, bf16[256,256]{1,0:T(8,128)(2,1)S(1)}, u32[]{:S(2)}, u32[]{:S(2)}) collective-permute-start(bf16[256,256]{1,0:T(8,128)(2,1)S(1)} %get-tuple-element.59), channel_id=1, source_target_pairs={{0,2},{1,3},{2,0},{3,1},{4,6},{5,7},{6,4},{7,5},{8,10},{9,11},{10,... | collective-permute-start | bytes 393224 | tf_op jit(solution)/shard_map/ppermute | solution.py:26
  35.6 12.4 %collective-permute-start.11 = (bf16[256,256]{1,0:T(8,128)(2,1)S(1)}, bf16[256,256]{1,0:T(8,128)(2,1)S(1)}, u32[]{:S(2)}, u32[]{:S(2)}) collective-permute-start(bf16[256,256]{1,0:T(8,128)(2,1)S(1)} %multiply_convert_fusion.3.refs_1_.refs_4_), channel_id=1, source_target_pairs={{0,2},{1,3},{2,0},{3,1},{4,6},{5,7},{6,4},{7,5},{8,10},{9,11},{10,... | collective-permute-start | bytes 393224 | tf_op jit(solution)/shard_map/ppermute | solution.py:26
  42.6 7.5 %collective-permute-start.8 = (bf16[256,256]{1,0:T(8,128)(2,1)S(1)}, bf16[256,256]{1,0:T(8,128)(2,1)}, u32[]{:S(2)}, u32[]{:S(2)}) collective-permute-start(bf16[256,256]{1,0:T(8,128)(2,1)S(1)} %multiply_convert_fusion.2.refs_0_), channel_id=1, source_target_pairs={{0,2},{1,3},{2,0},{3,1},{4,6},{5,7},{6,4},{7,5},{8,10},{9,11},{10,... | collective-permute-start | bytes 393224 | tf_op jit(solution)/shard_map/ppermute | solution.py:26
  42.7 9.9 %collective-permute-start.10 = (bf16[256,256]{1,0:T(8,128)(2,1)S(1)}, bf16[256,256]{1,0:T(8,128)(2,1)}, u32[]{:S(2)}, u32[]{:S(2)}) collective-permute-start(bf16[256,256]{1,0:T(8,128)(2,1)S(1)} %multiply_convert_fusion.3.refs_1_.refs_4_), channel_id=1, source_target_pairs={{0,1},{1,0},{2,3},{3,2},{4,5},{5,4},{6,7},{7,6},{8,9},{9,8},{10,11... | collective-permute-start | bytes 393224 | tf_op jit(solution)/shard_map/ppermute | solution.py:26
  48.0 5.9 %collective-permute-start.12 = (bf16[256,256]{1,0:T(8,128)(2,1)S(1)}, bf16[256,256]{1,0:T(8,128)(2,1)}, u32[]{:S(2)}, u32[]{:S(2)}) collective-permute-start(bf16[256,256]{1,0:T(8,128)(2,1)S(1)} %collective-permute-done.11.refs_3_.refs_6_), channel_id=1, source_target_pairs={{0,1},{1,0},{2,3},{3,2},{4,5},{5,4},{6,7},{7,6},{8,9},{9,8},{10,11... | collective-permute-start | bytes 393224 | tf_op jit(solution)/shard_map/ppermute | solution.py:26
  48.1 9.2 %collective-permute-start.7 = (bf16[256,256]{1,0:T(8,128)(2,1)S(1)}, bf16[256,256]{1,0:T(8,128)(2,1)}, u32[]{:S(2)}, u32[]{:S(2)}) collective-permute-start(bf16[256,256]{1,0:T(8,128)(2,1)S(1)} %multiply_convert_fusion.2.refs_0_), channel_id=1, source_target_pairs={{0,1},{1,0},{2,3},{3,2},{4,5},{5,4},{6,7},{7,6},{8,9},{9,8},{10,11... | collective-permute-start | bytes 393224 | tf_op jit(solution)/shard_map/ppermute | solution.py:26
  50.1 7.2 %collective-permute-start.9 = (bf16[256,256]{1,0:T(8,128)(2,1)}, bf16[256,256]{1,0:T(8,128)(2,1)}, u32[]{:S(2)}, u32[]{:S(2)}) collective-permute-start(bf16[256,256]{1,0:T(8,128)(2,1)} %collective-permute-done.8.refs_2_), channel_id=1, source_target_pairs={{0,1},{1,0},{2,3},{3,2},{4,5},{5,4},{6,7},{7,6},{8,9},{9,8},{10,11... | collective-permute-start | bytes 393224 | tf_op jit(solution)/shard_map/ppermute | solution.py:26
  62.4 2.5 %collective-permute-start.13 = (bf16[384,1024]{1,0:T(8,128)(2,1)}, bf16[384,1024]{1,0:T(8,128)(2,1)S(1)}, u32[]{:S(2)}, u32[]{:S(2)}) collective-permute-start(bf16[384,1024]{1,0:T(8,128)(2,1)} %get-tuple-element.44), channel_id=1, source_target_pairs={{0,4},{1,5},{2,6},{3,7},{4,0},{5,1},{6,2},{7,3},{8,12},{9,13},{10,... | collective-permute-start | bytes 2359304 | tf_op jit(solution)/shard_map/ppermute | solution.py:26
  66.4 8.8 %collective-permute-start.16 = (bf16[96,1024]{1,0:T(8,128)(2,1)S(1)}, bf16[96,1024]{1,0:T(8,128)(2,1)S(1)}, u32[]{:S(2)}, u32[]{:S(2)}) collective-permute-start(bf16[96,1024]{1,0:T(8,128)(2,1)S(1)} %get-tuple-element.48), channel_id=1, source_target_pairs={{0,24},{1,25},{2,26},{3,27},{4,28},{5,29},{6,30},{7,31},{8,16},{9,... | collective-permute-start | bytes 589832 | tf_op jit(solution)/shard_map/ppermute | solution.py:26
  68.9 9.6 %collective-permute-start.15 = (bf16[96,1024]{1,0:T(8,128)(2,1)S(1)}, bf16[96,1024]{1,0:T(8,128)(2,1)S(1)}, u32[]{:S(2)}, u32[]{:S(2)}) collective-permute-start(bf16[96,1024]{1,0:T(8,128)(2,1)S(1)} %get-tuple-element.47), channel_id=1, source_target_pairs={{0,16},{1,17},{2,18},{3,19},{4,20},{5,21},{6,22},{7,23},{8,24},{9,... | collective-permute-start | bytes 589832 | tf_op jit(solution)/shard_map/ppermute | solution.py:26
  69.4 9.2 %collective-permute-start.14 = (bf16[96,1024]{1,0:T(8,128)(2,1)S(1)}, bf16[96,1024]{1,0:T(8,128)(2,1)S(1)}, u32[]{:S(2)}, u32[]{:S(2)}) collective-permute-start(bf16[96,1024]{1,0:T(8,128)(2,1)S(1)} %get-tuple-element.46), channel_id=1, source_target_pairs={{0,8},{1,9},{2,10},{3,11},{4,12},{5,13},{6,14},{7,15},{8,0},{9,1},... | collective-permute-start | bytes 589832 | tf_op jit(solution)/shard_map/ppermute | solution.py:26
  78.8 6.7 %collective-permute-start.19 = (bf16[24,1024]{1,0:T(8,128)(2,1)S(1)}, bf16[24,1024]{1,0:T(8,128)(2,1)S(1)}, u32[]{:S(2)}, u32[]{:S(2)}) collective-permute-start(bf16[24,1024]{1,0:T(8,128)(2,1)S(1)} %get-tuple-element.57), channel_id=1, source_target_pairs={{0,3},{1,2},{2,1},{3,0},{4,7},{5,6},{6,5},{7,4},{8,11},{9,10},{10,... | collective-permute-start | bytes 147464 | tf_op jit(solution)/shard_map/ppermute | solution.py:26
  83.0 5.0 %collective-permute-start.18 = (bf16[24,1024]{1,0:T(8,128)(2,1)S(1)}, bf16[24,1024]{1,0:T(8,128)(2,1)S(1)}, u32[]{:S(2)}, u32[]{:S(2)}) collective-permute-start(bf16[24,1024]{1,0:T(8,128)(2,1)S(1)} %get-tuple-element.58), channel_id=1, source_target_pairs={{0,2},{1,3},{2,0},{3,1},{4,6},{5,7},{6,4},{7,5},{8,10},{9,11},{10,... | collective-permute-start | bytes 147464 | tf_op jit(solution)/shard_map/ppermute | solution.py:26
  83.0 5.0 %collective-permute-start.17 = (bf16[24,1024]{1,0:T(8,128)(2,1)S(1)}, bf16[24,1024]{1,0:T(8,128)(2,1)S(1)}, u32[]{:S(2)}, u32[]{:S(2)}) collective-permute-start(bf16[24,1024]{1,0:T(8,128)(2,1)S(1)} %get-tuple-element.56), channel_id=1, source_target_pairs={{0,1},{1,0},{2,3},{3,2},{4,5},{5,4},{6,7},{7,6},{8,9},{9,8},{10,11... | collective-permute-start | bytes 147464 | tf_op jit(solution)/shard_map/ppermute | solution.py:26
  88.1 6.1 %collective-permute-start.20 = (bf16[24,1024]{1,0:T(8,128)(2,1)S(1)}, bf16[24,1024]{1,0:T(8,128)(2,1)S(1)}, u32[]{:S(2)}, u32[]{:S(2)}) collective-permute-start(bf16[24,1024]{1,0:T(8,128)(2,1)S(1)} %add_convert_fusion.1), channel_id=1, source_target_pairs={{0,3},{1,2},{2,1},{3,0},{4,7},{5,6},{6,5},{7,4},{8,11},{9,10},{10,... | collective-permute-start | bytes 147464 | tf_op jit(solution)/shard_map/ppermute | solution.py:26
  90.1 5.5 %collective-permute-start.21 = (bf16[24,1024]{1,0:T(8,128)(2,1)S(1)}, bf16[24,1024]{1,0:T(8,128)(2,1)S(1)}, u32[]{:S(2)}, u32[]{:S(2)}) collective-permute-start(bf16[24,1024]{1,0:T(8,128)(2,1)S(1)} %add_convert_fusion.1), channel_id=1, source_target_pairs={{0,2},{1,3},{2,0},{3,1},{4,6},{5,7},{6,4},{7,5},{8,10},{9,11},{10,... | collective-permute-start | bytes 147464 | tf_op jit(solution)/shard_map/ppermute | solution.py:26
  90.3 5.3 %collective-permute-start.22 = (bf16[24,1024]{1,0:T(8,128)(2,1)S(1)}, bf16[24,1024]{1,0:T(8,128)(2,1)S(1)}, u32[]{:S(2)}, u32[]{:S(2)}) collective-permute-start(bf16[24,1024]{1,0:T(8,128)(2,1)S(1)} %add_convert_fusion.1), channel_id=1, source_target_pairs={{0,1},{1,0},{2,3},{3,2},{4,5},{5,4},{6,7},{7,6},{8,9},{9,8},{10,11... | collective-permute-start | bytes 147464 | tf_op jit(solution)/shard_map/ppermute | solution.py:26
  95.7 7.4 %collective-permute-start.23 = (bf16[96,1024]{1,0:T(8,128)(2,1)S(1)}, bf16[96,1024]{1,0:T(8,128)(2,1)S(1)}, u32[]{:S(2)}, u32[]{:S(2)}) collective-permute-start(bf16[96,1024]{1,0:T(8,128)(2,1)S(1)} %pad_maximum_fusion.1), channel_id=1, source_target_pairs={{0,24},{1,25},{2,26},{3,27},{4,28},{5,29},{6,30},{7,31},{8,16},{9,... | collective-permute-start | bytes 589832 | tf_op jit(solution)/shard_map/ppermute | solution.py:26
  96.9 8.1 %collective-permute-start.24 = (bf16[96,1024]{1,0:T(8,128)(2,1)S(1)}, bf16[96,1024]{1,0:T(8,128)(2,1)S(1)}, u32[]{:S(2)}, u32[]{:S(2)}) collective-permute-start(bf16[96,1024]{1,0:T(8,128)(2,1)S(1)} %pad_maximum_fusion.1), channel_id=1, source_target_pairs={{0,16},{1,17},{2,18},{3,19},{4,20},{5,21},{6,22},{7,23},{8,24},{9,... | collective-permute-start | bytes 589832 | tf_op jit(solution)/shard_map/ppermute | solution.py:26
  98.7 6.5 %collective-permute-start.25 = (bf16[96,1024]{1,0:T(8,128)(2,1)S(1)}, bf16[96,1024]{1,0:T(8,128)(2,1)S(1)}, u32[]{:S(2)}, u32[]{:S(2)}) collective-permute-start(bf16[96,1024]{1,0:T(8,128)(2,1)S(1)} %pad_maximum_fusion.1), channel_id=1, source_target_pairs={{0,8},{1,9},{2,10},{3,11},{4,12},{5,13},{6,14},{7,15},{8,0},{9,1},... | collective-permute-start | bytes 589832 | tf_op jit(solution)/shard_map/ppermute | solution.py:26
  105.5 2.4 %collective-permute-start.26 = (bf16[384,1024]{1,0:T(8,128)(2,1)S(1)}, bf16[384,1024]{1,0:T(8,128)(2,1)S(1)}, u32[]{:S(2)}, u32[]{:S(2)}) collective-permute-start(bf16[384,1024]{1,0:T(8,128)(2,1)S(1)} %pad_maximum_fusion.block), channel_id=1, source_target_pairs={{0,4},{1,5},{2,6},{3,7},{4,0},{5,1},{6,2},{7,3},{8,12},{9,13},{10,... | collective-permute-start | bytes 2359304 | tf_op jit(solution)/shard_map/ppermute | solution.py:26
  (5 other events, 7.4 us)

commit v7 on v6

--- a/solution.py
+++ b/solution.py
@@ -55,11 +55,11 @@
 
 def node_of_arrival(neighbour_slot, valid, count):
     slots = neighbour_slot.shape[1]
-    low = 128
+    low = 64
     node = lax.broadcasted_iota(jnp.int32, (1, slots), 1) // (slots // valid.shape[0])
     flat_valid = valid.reshape(1, slots)
-    high_hot = lax.broadcasted_iota(jnp.int32, (slots // low, slots), 0) == neighbour_slot // low
-    low_hot = lax.broadcasted_iota(jnp.int32, (low, slots), 0) == neighbour_slot % low
+    high_hot = lax.broadcasted_iota(jnp.int32, (slots // low, slots), 0) == neighbour_slot >> (low.bit_length() - 1)
+    low_hot = lax.broadcasted_iota(jnp.int32, (low, slots), 0) == neighbour_slot & (low - 1)
     upper = ((node // 16 + 1) * flat_valid).astype(F32)
     lower = ((node % 16) * flat_valid).astype(F32)
     codes = jnp.concatenate(
@@ -354,7 +354,7 @@
         plane = 1
     keep, give = call_kernel(
         functools.partial(item_kernel, blk_size),
-        [shape((rows, hid), F32), shape((rows, hid), BF16)],
+        [shape((rows, hid), BF16), shape((rows, hid), BF16)],
         [jnp.reshape(core, (1,))]
         + all_queries
         + all_items

time: 110 us -> 109 us (level)
  no operation moved by 1% of the time
where the time goes in v7:
time: 109 us
  starting transfers between devices  39 us (36%)
  waiting for transfers between devices  37 us (34%)
  Pallas kernels  18.6 us (17%)
  local copies, waits for them, and re-layouts  5.89 us (5%)
  matrix products  4.39 us (4%)
  other arithmetic  2.92 us (3%)
    ppermute x27, starting transfers between devices, exchange(): return lax.ppermute(value, AXES, pairs)  39 us
    ppermute x27, waiting for transfers between devices, exchange(): return lax.ppermute(value, AXES, pairs)  37 us
    pallas_call x9, Pallas kernels, call_kernel(): pl.pallas_call(kernel, out_shape=outs, in_specs=[pl.BlockSpec(memory_spac...  18.6 us
    unnamed x21, local copies, waits for them, and re-layouts  5.46 us
    dot_general x2, matrix products, forward(): pre_act = own_part + jnp.dot(pooled, w_nbr, preferred_element_type=F32)  2.71 us
  transfers between devices with their start and end apart: 27, of which 16 were waited for; matrix products, arithmetic and copies ran while one was open for 4% of the time, Pallas kernels for 9%

profile of v7, /device:TPU:0, one launch (start us, length us, event | category | flops | bytes accessed | tf_op | source)
XLA Modules:
  0.0 108.7 jit_solution(10609021123143300085)
XLA Ops:
  3.4 5.1 %collective-permute-start = (s32[1,1024]{1,0:T(1,128)S(1)}, s32[1,1024]{1,0:T(1,128)S(1)}, u32[]{:S(2)}, u32[]{:S(2)}) collective-permute-start(s32[1,1024]{1,0:T(1,128)S(1)} %get-tuple-element.66), channel_id=1, source_target_pairs={{0,3},{1,2},{2,1},{3,0},{4,7},{5,6},{6,5},{7,4},{8,11},{9,10},{10,... | collective-permute-start | bytes 12296 | tf_op jit(solution)/shard_map/ppermute | solution.py:26
  9.2 2.2 %copy-done.2 = bf16[8192,256]{1,0:T(8,128)(2,1)S(1)} copy-done((bf16[8192,256]{1,0:T(8,128)(2,1)S(1)}, bf16[8192,256]{1,0:T(8,128)(2,1)}, u32[]{:S(2)}) %copy-start.2) | copy-done | bytes 4194328
  13.1 2.5 %shard_map.104 = bf16[512,256]{1,0:T(8,128)(2,1)S(1)} custom-call(s32[1]{0:T(128)} %bitcast.3.requester, s32[4096]{0:T(1024)S(1)} %bitcast.22, s32[1,1024]{1,0:T(1,128)S(1)} %collective-permute-done.node_at, f32[8192,128]{1,0:T(8,128)S(1)} %get-tuple-element.27.left, f32[8192,128]{1,0:T(8,128)S(1)} %get-tuple-element.28.right), custom_call_target="tpu_custom_call" | custom-call | tf_op jit(solution)/shard_map/pallas_call | solution.py:80
  16.4 2.5 %shard_map.105 = f32[512,256]{1,0:T(8,128)S(1)} custom-call(s32[1]{0:T(128)} %bitcast.6.requester, s32[4096]{0:T(1024)S(1)} %bitcast.23, s32[1,1024]{1,0:T(1,128)S(1)} %collective-permute-done.1.node_at, f32[8192,128]{1,0:T(8,128)S(1)} %get-tuple-element.27.left, f32[8192,128]{1,0:T(8,128)S(1)} %get-tuple-element.28.right), custom_call_target="tpu_custom_call" | custom-call | tf_op jit(solution)/shard_map/pallas_call | solution.py:80
  19.0 2.5 %shard_map.106 = bf16[512,256]{1,0:T(8,128)(2,1)S(1)} custom-call(s32[1]{0:T(128)} %bitcast.7.requester, s32[4096]{0:T(1024)S(1)} %bitcast.24, s32[1,1024]{1,0:T(1,128)S(1)} %collective-permute-done.2.node_at, f32[8192,128]{1,0:T(8,128)S(1)} %get-tuple-element.27.left, f32[8192,128]{1,0:T(8,128)S(1)} %get-tuple-element.28.right), custom_call_target="tpu_custom_call" | custom-call | tf_op jit(solution)/shard_map/pallas_call | solution.py:80
  21.5 1.7 %collective-permute-start.3 = (bf16[512,256]{1,0:T(8,128)(2,1)S(1)}, bf16[512,256]{1,0:T(8,128)(2,1)S(1)}, u32[]{:S(2)}, u32[]{:S(2)}) collective-permute-start(bf16[512,256]{1,0:T(8,128)(2,1)S(1)} %shard_map.106), channel_id=1, source_target_pairs={{0,1},{1,0},{2,3},{3,2},{4,5},{5,4},{6,7},{7,6},{8,9},{9,8},{10,11... | collective-permute-start | bytes 786440 | tf_op jit(solution)/shard_map/ppermute | solution.py:26
  23.3 2.1 %collective-permute-start.5 = (bf16[256,256]{1,0:T(8,128)(2,1)S(1)}, bf16[256,256]{1,0:T(8,128)(2,1)S(1)}, u32[]{:S(2)}, u32[]{:S(2)}) collective-permute-start(bf16[256,256]{1,0:T(8,128)(2,1)S(1)} %get-tuple-element.58), channel_id=1, source_target_pairs={{0,2},{1,3},{2,0},{3,1},{4,6},{5,7},{6,4},{7,5},{8,10},{9,11},{10,... | collective-permute-start | bytes 393224 | tf_op jit(solution)/shard_map/ppermute | solution.py:26
  25.4 2.5 %shard_map.107 = f32[512,256]{1,0:T(8,128)S(1)} custom-call(s32[1]{0:T(128)} %bitcast.2.requester, s32[4096]{0:T(1024)S(1)} %bitcast.25, s32[1,1024]{1,0:T(1,128)S(1)} %get-tuple-element.63.node_at, f32[8192,128]{1,0:T(8,128)S(1)} %get-tuple-element.27.left, f32[8192,128]{1,0:T(8,128)S(1)} %get-tuple-element.28.right), custom_call_target="tpu_custom_call" | custom-call | tf_op jit(solution)/shard_map/pallas_call | solution.py:80
  28.9 4.3 %collective-permute-done.3 = bf16[512,256]{1,0:T(8,128)(2,1)S(1)} collective-permute-done((bf16[512,256]{1,0:T(8,128)(2,1)S(1)}, bf16[512,256]{1,0:T(8,128)(2,1)S(1)}, u32[]{:S(2)}, u32[]{:S(2)}) %collective-permute-start.3) | collective-permute-done | bytes 262176 | tf_op jit(solution)/shard_map/ppermute | solution.py:26
  35.2 1.6 %collective-permute-start.11 = (bf16[256,256]{1,0:T(8,128)(2,1)S(1)}, bf16[256,256]{1,0:T(8,128)(2,1)S(1)}, u32[]{:S(2)}, u32[]{:S(2)}) collective-permute-start(bf16[256,256]{1,0:T(8,128)(2,1)S(1)} %multiply_convert_fusion.3.refs_1_.refs_4_), channel_id=1, source_target_pairs={{0,2},{1,3},{2,0},{3,1},{4,6},{5,7},{6,4},{7,5},{8,10},{9,11},{10,... | collective-permute-start | bytes 393224 | tf_op jit(solution)/shard_map/ppermute | solution.py:26
  36.7 3.5 %collective-permute-done.6 = bf16[256,256]{1,0:T(8,128)(2,1)S(1)} collective-permute-done((bf16[256,256]{1,0:T(8,128)(2,1)S(1)}, bf16[256,256]{1,0:T(8,128)(2,1)S(1)}, u32[]{:S(2)}, u32[]{:S(2)}) %collective-permute-start.6) | collective-permute-done | bytes 131104 | tf_op jit(solution)/shard_map/ppermute | solution.py:26
  42.3 5.3 %collective-permute-start.10 = (bf16[256,256]{1,0:T(8,128)(2,1)S(1)}, bf16[256,256]{1,0:T(8,128)(2,1)}, u32[]{:S(2)}, u32[]{:S(2)}) collective-permute-start(bf16[256,256]{1,0:T(8,128)(2,1)S(1)} %multiply_convert_fusion.3.refs_1_.refs_4_), channel_id=1, source_target_pairs={{0,1},{1,0},{2,3},{3,2},{4,5},{5,4},{6,7},{7,6},{8,9},{9,8},{10,11... | collective-permute-start | bytes 393224 | tf_op jit(solution)/shard_map/ppermute | solution.py:26
  47.6 2.0 %collective-permute-start.7 = (bf16[256,256]{1,0:T(8,128)(2,1)S(1)}, bf16[256,256]{1,0:T(8,128)(2,1)}, u32[]{:S(2)}, u32[]{:S(2)}) collective-permute-start(bf16[256,256]{1,0:T(8,128)(2,1)S(1)} %multiply_convert_fusion.2.refs_0_), channel_id=1, source_target_pairs={{0,1},{1,0},{2,3},{3,2},{4,5},{5,4},{6,7},{7,6},{8,9},{9,8},{10,11... | collective-permute-start | bytes 393224 | tf_op jit(solution)/shard_map/ppermute | solution.py:26
  49.6 2.5 %collective-permute-start.9 = (bf16[256,256]{1,0:T(8,128)(2,1)}, bf16[256,256]{1,0:T(8,128)(2,1)}, u32[]{:S(2)}, u32[]{:S(2)}) collective-permute-start(bf16[256,256]{1,0:T(8,128)(2,1)} %collective-permute-done.8.refs_2_), channel_id=1, source_target_pairs={{0,1},{1,0},{2,3},{3,2},{4,5},{5,4},{6,7},{7,6},{8,9},{9,8},{10,11... | collective-permute-start | bytes 393224 | tf_op jit(solution)/shard_map/ppermute | solution.py:26
  54.7 2.2 %shard_map.108 = (bf16[256,256]{1,0:T(8,128)(2,1)S(1)}, f32[256,1]{1,0:T(8,128)S(1)}, bf16[256,256]{1,0:T(8,128)(2,1)S(1)}, bf16[256,1024]{1,0:T(8,128)(2,1)S(1)}) custom-call(bf16[256,256]{1,0:T(8,128)(2,1)S(1)} %multiply_convert_fusion.2.refs_0_, bf16[256,256]{1,0:T(8,128)(2,1)S(1)} %multiply_convert_fusion.3.refs_1_.refs_4_, ...), custom_call_target="tpu_custom_call" | custom-call | flops 402653184 | bytes 3277824 | tf_op jit(solution)/shard_map/pallas_call | solution.py:80
  56.9 3.9 %shard_map.109 = (bf16[384,1024]{1,0:T(8,128)(2,1)S(1)}, bf16[384,1024]{1,0:T(8,128)(2,1)}) custom-call(s32[1]{0:T(128)} %bitcast.core_ref.place, bf16[256,256]{1,0:T(8,128)(2,1)S(1)} %multiply_convert_fusion.2.refs_0_, bf16[256,256]{1,0:T(8,128)(2,1)} %collective-permute-done.7.refs_1_, bf16[256,256]{1,0:T(8,128)(2,1)} %collective-permute-done.8.refs_2_, ...), custom_call_target="tpu_custom_call" | custom-call | flops 1207959552 | bytes 6816772 | tf_op jit(solution)/shard_map/pallas_call | solution.py:80
  61.7 2.5 %collective-permute-done.13.arrived = bf16[384,1024]{1,0:T(8,128)(2,1)S(1)} collective-permute-done((bf16[384,1024]{1,0:T(8,128)(2,1)}, bf16[384,1024]{1,0:T(8,128)(2,1)S(1)}, u32[]{:S(2)}, u32[]{:S(2)}) %collective-permute-start.13) | collective-permute-done | bytes 786464 | tf_op jit(solution)/shard_map/ppermute | solution.py:26
  65.5 2.5 %collective-permute-start.16 = (bf16[96,1024]{1,0:T(8,128)(2,1)S(1)}, bf16[96,1024]{1,0:T(8,128)(2,1)S(1)}, u32[]{:S(2)}, u32[]{:S(2)}) collective-permute-start(bf16[96,1024]{1,0:T(8,128)(2,1)S(1)} %get-tuple-element.48), channel_id=1, source_target_pairs={{0,24},{1,25},{2,26},{3,27},{4,28},{5,29},{6,30},{7,31},{8,16},{9,... | collective-permute-start | bytes 589832 | tf_op jit(solution)/shard_map/ppermute | solution.py:26
  69.1 5.2 %collective-permute-done.16 = bf16[96,1024]{1,0:T(8,128)(2,1)S(1)} collective-permute-done((bf16[96,1024]{1,0:T(8,128)(2,1)S(1)}, bf16[96,1024]{1,0:T(8,128)(2,1)S(1)}, u32[]{:S(2)}, u32[]{:S(2)}) %collective-permute-start.16) | collective-permute-done | bytes 196640 | tf_op jit(solution)/shard_map/ppermute | solution.py:26
  74.3 3.4 %collective-permute-done.15 = bf16[96,1024]{1,0:T(8,128)(2,1)S(1)} collective-permute-done((bf16[96,1024]{1,0:T(8,128)(2,1)S(1)}, bf16[96,1024]{1,0:T(8,128)(2,1)S(1)}, u32[]{:S(2)}, u32[]{:S(2)}) %collective-permute-start.15) | collective-permute-done | bytes 196640 | tf_op jit(solution)/shard_map/ppermute | solution.py:26
  77.8 4.3 %collective-permute-start.19 = (bf16[24,1024]{1,0:T(8,128)(2,1)S(1)}, bf16[24,1024]{1,0:T(8,128)(2,1)S(1)}, u32[]{:S(2)}, u32[]{:S(2)}) collective-permute-start(bf16[24,1024]{1,0:T(8,128)(2,1)S(1)} %get-tuple-element.55), channel_id=1, source_target_pairs={{0,3},{1,2},{2,1},{3,0},{4,7},{5,6},{6,5},{7,4},{8,11},{9,10},{10,... | collective-permute-start | bytes 147464 | tf_op jit(solution)/shard_map/ppermute | solution.py:26
  82.8 1.7 %collective-permute-done.19 = bf16[24,1024]{1,0:T(8,128)(2,1)S(1)} collective-permute-done((bf16[24,1024]{1,0:T(8,128)(2,1)S(1)}, bf16[24,1024]{1,0:T(8,128)(2,1)S(1)}, u32[]{:S(2)}, u32[]{:S(2)}) %collective-permute-start.19) | collective-permute-done | bytes 49184 | tf_op jit(solution)/shard_map/ppermute | solution.py:26
  84.5 2.6 %collective-permute-done.18 = bf16[24,1024]{1,0:T(8,128)(2,1)S(1)} collective-permute-done((bf16[24,1024]{1,0:T(8,128)(2,1)S(1)}, bf16[24,1024]{1,0:T(8,128)(2,1)S(1)}, u32[]{:S(2)}, u32[]{:S(2)}) %collective-permute-start.18) | collective-permute-done | bytes 49184 | tf_op jit(solution)/shard_map/ppermute | solution.py:26
  87.2 2.0 %collective-permute-start.20 = (bf16[24,1024]{1,0:T(8,128)(2,1)S(1)}, bf16[24,1024]{1,0:T(8,128)(2,1)S(1)}, u32[]{:S(2)}, u32[]{:S(2)}) collective-permute-start(bf16[24,1024]{1,0:T(8,128)(2,1)S(1)} %add_convert_fusion.1), channel_id=1, source_target_pairs={{0,3},{1,2},{2,1},{3,0},{4,7},{5,6},{6,5},{7,4},{8,11},{9,10},{10,... | collective-permute-start | bytes 147464 | tf_op jit(solution)/shard_map/ppermute | solution.py:26
  89.4 2.2 %collective-permute-start.22 = (bf16[24,1024]{1,0:T(8,128)(2,1)S(1)}, bf16[24,1024]{1,0:T(8,128)(2,1)S(1)}, u32[]{:S(2)}, u32[]{:S(2)}) collective-permute-start(bf16[24,1024]{1,0:T(8,128)(2,1)S(1)} %add_convert_fusion.1), channel_id=1, source_target_pairs={{0,1},{1,0},{2,3},{3,2},{4,5},{5,4},{6,7},{7,6},{8,9},{9,8},{10,11... | collective-permute-start | bytes 147464 | tf_op jit(solution)/shard_map/ppermute | solution.py:26
  91.6 1.6 %collective-permute-done.20 = bf16[24,1024]{1,0:T(8,128)(2,1)S(1)} collective-permute-done((bf16[24,1024]{1,0:T(8,128)(2,1)S(1)}, bf16[24,1024]{1,0:T(8,128)(2,1)S(1)}, u32[]{:S(2)}, u32[]{:S(2)}) %collective-permute-start.20) | collective-permute-done | bytes 49184 | tf_op jit(solution)/shard_map/ppermute | solution.py:26
  93.2 1.4 %collective-permute-done.21 = bf16[24,1024]{1,0:T(8,128)(2,1)S(1)} collective-permute-done((bf16[24,1024]{1,0:T(8,128)(2,1)S(1)}, bf16[24,1024]{1,0:T(8,128)(2,1)S(1)}, u32[]{:S(2)}, u32[]{:S(2)}) %collective-permute-start.21) | collective-permute-done | bytes 49184 | tf_op jit(solution)/shard_map/ppermute | solution.py:26
  96.0 1.8 %collective-permute-start.24 = (bf16[96,1024]{1,0:T(8,128)(2,1)S(1)}, bf16[96,1024]{1,0:T(8,128)(2,1)S(1)}, u32[]{:S(2)}, u32[]{:S(2)}) collective-permute-start(bf16[96,1024]{1,0:T(8,128)(2,1)S(1)} %pad_maximum_fusion.1), channel_id=1, source_target_pairs={{0,16},{1,17},{2,18},{3,19},{4,20},{5,21},{6,22},{7,23},{8,24},{9,... | collective-permute-start | bytes 589832 | tf_op jit(solution)/shard_map/ppermute | solution.py:26
  98.3 3.8 %collective-permute-done.23 = bf16[96,1024]{1,0:T(8,128)(2,1)S(1)} collective-permute-done((bf16[96,1024]{1,0:T(8,128)(2,1)S(1)}, bf16[96,1024]{1,0:T(8,128)(2,1)S(1)}, u32[]{:S(2)}, u32[]{:S(2)}) %collective-permute-start.23) | collective-permute-done | bytes 196640 | tf_op jit(solution)/shard_map/ppermute | solution.py:26
  102.1 2.0 %collective-permute-done.24 = bf16[96,1024]{1,0:T(8,128)(2,1)S(1)} collective-permute-done((bf16[96,1024]{1,0:T(8,128)(2,1)S(1)}, bf16[96,1024]{1,0:T(8,128)(2,1)S(1)}, u32[]{:S(2)}, u32[]{:S(2)}) %collective-permute-start.24) | collective-permute-done | bytes 196640 | tf_op jit(solution)/shard_map/ppermute | solution.py:26
  104.7 2.3 %collective-permute-done.26.other = bf16[384,1024]{1,0:T(8,128)(2,1)S(1)} collective-permute-done((bf16[384,1024]{1,0:T(8,128)(2,1)S(1)}, bf16[384,1024]{1,0:T(8,128)(2,1)S(1)}, u32[]{:S(2)}, u32[]{:S(2)}) %collective-permute-start.26) | collective-permute-done | bytes 786464 | tf_op jit(solution)/shard_map/ppermute | solution.py:26
  107.0 1.8 %shard_map.111 = (f32[256,1024]{1,0:T(8,128)}, f32[256,1024]{1,0:T(8,128)}, f32[1024,256]{1,0:T(8,128)}) custom-call(s32[1]{0:T(128)} %bitcast.core_ref.place, bf16[384,1024]{1,0:T(8,128)(2,1)S(1)} %pad_maximum_fusion.block, bf16[384,1024]{1,0:T(8,128)(2,1)S(1)} %collective-permute-done.26.other), custom_call_target="tpu_custom_call" | custom-call | tf_op jit(solution)/shard_map/pallas_call | solution.py:80
  (86 shorter events, 20.3 us)
Async XLA Ops:
  0.6 32.6 %copy-start = (bf16[256,1024]{1,0:T(8,128)(2,1)S(1)}, bf16[256,1024]{1,0:T(8,128)(2,1)}, u32[]{:S(2)}) copy-start(bf16[256,1024]{1,0:T(8,128)(2,1)} %param.14) | copy-start | bytes 1572868
  0.6 8.6 %copy-start.9 = (s32[4,1024]{1,0:T(4,128)S(1)}, s32[4,1024]{1,0:T(4,128)}, u32[]{:S(2)}) copy-start(s32[4,1024]{1,0:T(4,128)} %param.11) | copy-start | bytes 49156
  3.4 8.5 %collective-permute-start = (s32[1,1024]{1,0:T(1,128)S(1)}, s32[1,1024]{1,0:T(1,128)S(1)}, u32[]{:S(2)}, u32[]{:S(2)}) collective-permute-start(s32[1,1024]{1,0:T(1,128)S(1)} %get-tuple-element.66), channel_id=1, source_target_pairs={{0,3},{1,2},{2,1},{3,0},{4,7},{5,6},{6,5},{7,4},{8,11},{9,10},{10,... | collective-permute-start | bytes 12296 | tf_op jit(solution)/shard_map/ppermute | solution.py:26
  8.6 4.5 %collective-permute-start.1 = (s32[1,1024]{1,0:T(1,128)S(1)}, s32[1,1024]{1,0:T(1,128)S(1)}, u32[]{:S(2)}, u32[]{:S(2)}) collective-permute-start(s32[1,1024]{1,0:T(1,128)S(1)} %get-tuple-element.65), channel_id=1, source_target_pairs={{0,2},{1,3},{2,0},{3,1},{4,6},{5,7},{6,4},{7,5},{8,10},{9,11},{10,... | collective-permute-start | bytes 12296 | tf_op jit(solution)/shard_map/ppermute | solution.py:26
  8.6 4.5 %collective-permute-start.2 = (s32[1,1024]{1,0:T(1,128)S(1)}, s32[1,1024]{1,0:T(1,128)S(1)}, u32[]{:S(2)}, u32[]{:S(2)}) collective-permute-start(s32[1,1024]{1,0:T(1,128)S(1)} %get-tuple-element.64), channel_id=1, source_target_pairs={{0,1},{1,0},{2,3},{3,2},{4,5},{5,4},{6,7},{7,6},{8,9},{9,8},{10,11... | collective-permute-start | bytes 12296 | tf_op jit(solution)/shard_map/ppermute | solution.py:26
  9.2 2.2 %copy-start.2 = (bf16[8192,256]{1,0:T(8,128)(2,1)S(1)}, bf16[8192,256]{1,0:T(8,128)(2,1)}, u32[]{:S(2)}) copy-start(bf16[8192,256]{1,0:T(8,128)(2,1)} %store.1) | copy-start | bytes 12582916
  13.1 2.9 %copy-start.5 = (bf16[512,256]{1,0:T(8,128)(2,1)S(1)}, bf16[512,256]{1,0:T(8,128)(2,1)}, u32[]{:S(2)}) copy-start(bf16[512,256]{1,0:T(8,128)(2,1)} %refs_17_.1) | copy-start | bytes 786436
  13.1 2.9 %copy-start.8 = (bf16[256,1024]{1,0:T(8,128)(2,1)S(1)}, bf16[256,1024]{1,0:T(8,128)(2,1)}, u32[]{:S(2)}) copy-start(bf16[256,1024]{1,0:T(8,128)(2,1)} %param.13) | copy-start | bytes 1572868
  15.6 7.6 %collective-permute-start.4 = (bf16[512,256]{1,0:T(8,128)(2,1)S(1)}, bf16[512,256]{1,0:T(8,128)(2,1)S(1)}, u32[]{:S(2)}, u32[]{:S(2)}) collective-permute-start(bf16[512,256]{1,0:T(8,128)(2,1)S(1)} %shard_map.104), channel_id=1, source_target_pairs={{0,1},{1,0},{2,3},{3,2},{4,5},{5,4},{6,7},{7,6},{8,9},{9,8},{10,11... | collective-permute-start | bytes 786440 | tf_op jit(solution)/shard_map/ppermute | solution.py:26
  21.5 11.7 %collective-permute-start.3 = (bf16[512,256]{1,0:T(8,128)(2,1)S(1)}, bf16[512,256]{1,0:T(8,128)(2,1)S(1)}, u32[]{:S(2)}, u32[]{:S(2)}) collective-permute-start(bf16[512,256]{1,0:T(8,128)(2,1)S(1)} %shard_map.106), channel_id=1, source_target_pairs={{0,1},{1,0},{2,3},{3,2},{4,5},{5,4},{6,7},{7,6},{8,9},{9,8},{10,11... | collective-permute-start | bytes 786440 | tf_op jit(solution)/shard_map/ppermute | solution.py:26
  23.3 9.8 %collective-permute-start.5 = (bf16[256,256]{1,0:T(8,128)(2,1)S(1)}, bf16[256,256]{1,0:T(8,128)(2,1)S(1)}, u32[]{:S(2)}, u32[]{:S(2)}) collective-permute-start(bf16[256,256]{1,0:T(8,128)(2,1)S(1)} %get-tuple-element.58), channel_id=1, source_target_pairs={{0,2},{1,3},{2,0},{3,1},{4,6},{5,7},{6,4},{7,5},{8,10},{9,11},{10,... | collective-permute-start | bytes 393224 | tf_op jit(solution)/shard_map/ppermute | solution.py:26
  27.9 12.3 %collective-permute-start.6 = (bf16[256,256]{1,0:T(8,128)(2,1)S(1)}, bf16[256,256]{1,0:T(8,128)(2,1)S(1)}, u32[]{:S(2)}, u32[]{:S(2)}) collective-permute-start(bf16[256,256]{1,0:T(8,128)(2,1)S(1)} %get-tuple-element.57), channel_id=1, source_target_pairs={{0,2},{1,3},{2,0},{3,1},{4,6},{5,7},{6,4},{7,5},{8,10},{9,11},{10,... | collective-permute-start | bytes 393224 | tf_op jit(solution)/shard_map/ppermute | solution.py:26
  35.2 12.4 %collective-permute-start.11 = (bf16[256,256]{1,0:T(8,128)(2,1)S(1)}, bf16[256,256]{1,0:T(8,128)(2,1)S(1)}, u32[]{:S(2)}, u32[]{:S(2)}) collective-permute-start(bf16[256,256]{1,0:T(8,128)(2,1)S(1)} %multiply_convert_fusion.3.refs_1_.refs_4_), channel_id=1, source_target_pairs={{0,2},{1,3},{2,0},{3,1},{4,6},{5,7},{6,4},{7,5},{8,10},{9,11},{10,... | collective-permute-start | bytes 393224 | tf_op jit(solution)/shard_map/ppermute | solution.py:26
  42.2 7.5 %collective-permute-start.8 = (bf16[256,256]{1,0:T(8,128)(2,1)S(1)}, bf16[256,256]{1,0:T(8,128)(2,1)}, u32[]{:S(2)}, u32[]{:S(2)}) collective-permute-start(bf16[256,256]{1,0:T(8,128)(2,1)S(1)} %multiply_convert_fusion.2.refs_0_), channel_id=1, source_target_pairs={{0,2},{1,3},{2,0},{3,1},{4,6},{5,7},{6,4},{7,5},{8,10},{9,11},{10,... | collective-permute-start | bytes 393224 | tf_op jit(solution)/shard_map/ppermute | solution.py:26
  42.3 9.9 %collective-permute-start.10 = (bf16[256,256]{1,0:T(8,128)(2,1)S(1)}, bf16[256,256]{1,0:T(8,128)(2,1)}, u32[]{:S(2)}, u32[]{:S(2)}) collective-permute-start(bf16[256,256]{1,0:T(8,128)(2,1)S(1)} %multiply_convert_fusion.3.refs_1_.refs_4_), channel_id=1, source_target_pairs={{0,1},{1,0},{2,3},{3,2},{4,5},{5,4},{6,7},{7,6},{8,9},{9,8},{10,11... | collective-permute-start | bytes 393224 | tf_op jit(solution)/shard_map/ppermute | solution.py:26
  47.6 5.9 %collective-permute-start.12 = (bf16[256,256]{1,0:T(8,128)(2,1)S(1)}, bf16[256,256]{1,0:T(8,128)(2,1)}, u32[]{:S(2)}, u32[]{:S(2)}) collective-permute-start(bf16[256,256]{1,0:T(8,128)(2,1)S(1)} %collective-permute-done.11.refs_3_.refs_6_), channel_id=1, source_target_pairs={{0,1},{1,0},{2,3},{3,2},{4,5},{5,4},{6,7},{7,6},{8,9},{9,8},{10,11... | collective-permute-start | bytes 393224 | tf_op jit(solution)/shard_map/ppermute | solution.py:26
  47.6 9.2 %collective-permute-start.7 = (bf16[256,256]{1,0:T(8,128)(2,1)S(1)}, bf16[256,256]{1,0:T(8,128)(2,1)}, u32[]{:S(2)}, u32[]{:S(2)}) collective-permute-start(bf16[256,256]{1,0:T(8,128)(2,1)S(1)} %multiply_convert_fusion.2.refs_0_), channel_id=1, source_target_pairs={{0,1},{1,0},{2,3},{3,2},{4,5},{5,4},{6,7},{7,6},{8,9},{9,8},{10,11... | collective-permute-start | bytes 393224 | tf_op jit(solution)/shard_map/ppermute | solution.py:26
  49.6 7.2 %collective-permute-start.9 = (bf16[256,256]{1,0:T(8,128)(2,1)}, bf16[256,256]{1,0:T(8,128)(2,1)}, u32[]{:S(2)}, u32[]{:S(2)}) collective-permute-start(bf16[256,256]{1,0:T(8,128)(2,1)} %collective-permute-done.8.refs_2_), channel_id=1, source_target_pairs={{0,1},{1,0},{2,3},{3,2},{4,5},{5,4},{6,7},{7,6},{8,9},{9,8},{10,11... | collective-permute-start | bytes 393224 | tf_op jit(solution)/shard_map/ppermute | solution.py:26
  61.7 2.5 %collective-permute-start.13 = (bf16[384,1024]{1,0:T(8,128)(2,1)}, bf16[384,1024]{1,0:T(8,128)(2,1)S(1)}, u32[]{:S(2)}, u32[]{:S(2)}) collective-permute-start(bf16[384,1024]{1,0:T(8,128)(2,1)} %get-tuple-element.44), channel_id=1, source_target_pairs={{0,4},{1,5},{2,6},{3,7},{4,0},{5,1},{6,2},{7,3},{8,12},{9,13},{10,... | collective-permute-start | bytes 2359304 | tf_op jit(solution)/shard_map/ppermute | solution.py:26
  65.5 8.8 %collective-permute-start.16 = (bf16[96,1024]{1,0:T(8,128)(2,1)S(1)}, bf16[96,1024]{1,0:T(8,128)(2,1)S(1)}, u32[]{:S(2)}, u32[]{:S(2)}) collective-permute-start(bf16[96,1024]{1,0:T(8,128)(2,1)S(1)} %get-tuple-element.48), channel_id=1, source_target_pairs={{0,24},{1,25},{2,26},{3,27},{4,28},{5,29},{6,30},{7,31},{8,16},{9,... | collective-permute-start | bytes 589832 | tf_op jit(solution)/shard_map/ppermute | solution.py:26
  68.0 9.6 %collective-permute-start.15 = (bf16[96,1024]{1,0:T(8,128)(2,1)S(1)}, bf16[96,1024]{1,0:T(8,128)(2,1)S(1)}, u32[]{:S(2)}, u32[]{:S(2)}) collective-permute-start(bf16[96,1024]{1,0:T(8,128)(2,1)S(1)} %get-tuple-element.47), channel_id=1, source_target_pairs={{0,16},{1,17},{2,18},{3,19},{4,20},{5,21},{6,22},{7,23},{8,24},{9,... | collective-permute-start | bytes 589832 | tf_op jit(solution)/shard_map/ppermute | solution.py:26
  68.5 9.2 %collective-permute-start.14 = (bf16[96,1024]{1,0:T(8,128)(2,1)S(1)}, bf16[96,1024]{1,0:T(8,128)(2,1)S(1)}, u32[]{:S(2)}, u32[]{:S(2)}) collective-permute-start(bf16[96,1024]{1,0:T(8,128)(2,1)S(1)} %get-tuple-element.46), channel_id=1, source_target_pairs={{0,8},{1,9},{2,10},{3,11},{4,12},{5,13},{6,14},{7,15},{8,0},{9,1},... | collective-permute-start | bytes 589832 | tf_op jit(solution)/shard_map/ppermute | solution.py:26
  77.8 6.6 %collective-permute-start.19 = (bf16[24,1024]{1,0:T(8,128)(2,1)S(1)}, bf16[24,1024]{1,0:T(8,128)(2,1)S(1)}, u32[]{:S(2)}, u32[]{:S(2)}) collective-permute-start(bf16[24,1024]{1,0:T(8,128)(2,1)S(1)} %get-tuple-element.55), channel_id=1, source_target_pairs={{0,3},{1,2},{2,1},{3,0},{4,7},{5,6},{6,5},{7,4},{8,11},{9,10},{10,... | collective-permute-start | bytes 147464 | tf_op jit(solution)/shard_map/ppermute | solution.py:26
  82.1 5.0 %collective-permute-start.18 = (bf16[24,1024]{1,0:T(8,128)(2,1)S(1)}, bf16[24,1024]{1,0:T(8,128)(2,1)S(1)}, u32[]{:S(2)}, u32[]{:S(2)}) collective-permute-start(bf16[24,1024]{1,0:T(8,128)(2,1)S(1)} %get-tuple-element.56), channel_id=1, source_target_pairs={{0,2},{1,3},{2,0},{3,1},{4,6},{5,7},{6,4},{7,5},{8,10},{9,11},{10,... | collective-permute-start | bytes 147464 | tf_op jit(solution)/shard_map/ppermute | solution.py:26
  82.1 5.0 %collective-permute-start.17 = (bf16[24,1024]{1,0:T(8,128)(2,1)S(1)}, bf16[24,1024]{1,0:T(8,128)(2,1)S(1)}, u32[]{:S(2)}, u32[]{:S(2)}) collective-permute-start(bf16[24,1024]{1,0:T(8,128)(2,1)S(1)} %get-tuple-element.54), channel_id=1, source_target_pairs={{0,1},{1,0},{2,3},{3,2},{4,5},{5,4},{6,7},{7,6},{8,9},{9,8},{10,11... | collective-permute-start | bytes 147464 | tf_op jit(solution)/shard_map/ppermute | solution.py:26
  87.2 6.1 %collective-permute-start.20 = (bf16[24,1024]{1,0:T(8,128)(2,1)S(1)}, bf16[24,1024]{1,0:T(8,128)(2,1)S(1)}, u32[]{:S(2)}, u32[]{:S(2)}) collective-permute-start(bf16[24,1024]{1,0:T(8,128)(2,1)S(1)} %add_convert_fusion.1), channel_id=1, source_target_pairs={{0,3},{1,2},{2,1},{3,0},{4,7},{5,6},{6,5},{7,4},{8,11},{9,10},{10,... | collective-permute-start | bytes 147464 | tf_op jit(solution)/shard_map/ppermute | solution.py:26
  89.2 5.5 %collective-permute-start.21 = (bf16[24,1024]{1,0:T(8,128)(2,1)S(1)}, bf16[24,1024]{1,0:T(8,128)(2,1)S(1)}, u32[]{:S(2)}, u32[]{:S(2)}) collective-permute-start(bf16[24,1024]{1,0:T(8,128)(2,1)S(1)} %add_convert_fusion.1), channel_id=1, source_target_pairs={{0,2},{1,3},{2,0},{3,1},{4,6},{5,7},{6,4},{7,5},{8,10},{9,11},{10,... | collective-permute-start | bytes 147464 | tf_op jit(solution)/shard_map/ppermute | solution.py:26
  89.4 5.3 %collective-permute-start.22 = (bf16[24,1024]{1,0:T(8,128)(2,1)S(1)}, bf16[24,1024]{1,0:T(8,128)(2,1)S(1)}, u32[]{:S(2)}, u32[]{:S(2)}) collective-permute-start(bf16[24,1024]{1,0:T(8,128)(2,1)S(1)} %add_convert_fusion.1), channel_id=1, source_target_pairs={{0,1},{1,0},{2,3},{3,2},{4,5},{5,4},{6,7},{7,6},{8,9},{9,8},{10,11... | collective-permute-start | bytes 147464 | tf_op jit(solution)/shard_map/ppermute | solution.py:26
  94.7 7.4 %collective-permute-start.23 = (bf16[96,1024]{1,0:T(8,128)(2,1)S(1)}, bf16[96,1024]{1,0:T(8,128)(2,1)S(1)}, u32[]{:S(2)}, u32[]{:S(2)}) collective-permute-start(bf16[96,1024]{1,0:T(8,128)(2,1)S(1)} %pad_maximum_fusion.1), channel_id=1, source_target_pairs={{0,24},{1,25},{2,26},{3,27},{4,28},{5,29},{6,30},{7,31},{8,16},{9,... | collective-permute-start | bytes 589832 | tf_op jit(solution)/shard_map/ppermute | solution.py:26
  96.0 8.1 %collective-permute-start.24 = (bf16[96,1024]{1,0:T(8,128)(2,1)S(1)}, bf16[96,1024]{1,0:T(8,128)(2,1)S(1)}, u32[]{:S(2)}, u32[]{:S(2)}) collective-permute-start(bf16[96,1024]{1,0:T(8,128)(2,1)S(1)} %pad_maximum_fusion.1), channel_id=1, source_target_pairs={{0,16},{1,17},{2,18},{3,19},{4,20},{5,21},{6,22},{7,23},{8,24},{9,... | collective-permute-start | bytes 589832 | tf_op jit(solution)/shard_map/ppermute | solution.py:26
  97.8 6.5 %collective-permute-start.25 = (bf16[96,1024]{1,0:T(8,128)(2,1)S(1)}, bf16[96,1024]{1,0:T(8,128)(2,1)S(1)}, u32[]{:S(2)}, u32[]{:S(2)}) collective-permute-start(bf16[96,1024]{1,0:T(8,128)(2,1)S(1)} %pad_maximum_fusion.1), channel_id=1, source_target_pairs={{0,8},{1,9},{2,10},{3,11},{4,12},{5,13},{6,14},{7,15},{8,0},{9,1},... | collective-permute-start | bytes 589832 | tf_op jit(solution)/shard_map/ppermute | solution.py:26
  104.6 2.4 %collective-permute-start.26 = (bf16[384,1024]{1,0:T(8,128)(2,1)S(1)}, bf16[384,1024]{1,0:T(8,128)(2,1)S(1)}, u32[]{:S(2)}, u32[]{:S(2)}) collective-permute-start(bf16[384,1024]{1,0:T(8,128)(2,1)S(1)} %pad_maximum_fusion.block), channel_id=1, source_target_pairs={{0,4},{1,5},{2,6},{3,7},{4,0},{5,1},{6,2},{7,3},{8,12},{9,13},{10,... | collective-permute-start | bytes 2359304 | tf_op jit(solution)/shard_map/ppermute | solution.py:26
  (5 other events, 6.8 us)

commit v8 on v7

--- a/solution.py
+++ b/solution.py
@@ -89,8 +89,8 @@
 
 
 def split_kernel(store, left, right):
-    rows, side = left.shape
-    step = rows // 16
+    side = left.shape[1]
+    step = store.shape[0] // 16
 
     def some_rows(i, carry):
         at = pl.ds(pl.multiple_of(i * step, step), step)
@@ -121,7 +121,7 @@
     lax.fori_loop(0, count // 32, some_rows, 0)
     nodes = lax.broadcasted_iota(jnp.int32, (out.shape[0], count), 0)
     pick = (nodes == node_at[...]).astype(BF16)
-    rows = jnp.concatenate([got_left[...], got_right[...]], 1).astype(BF16)
+    rows = jnp.concatenate([got_left[:count], got_right[:count]], 1).astype(BF16)
     out[...] = jnp.dot(pick, rows, preferred_element_type=F32).astype(out.dtype)
 
 
@@ -141,8 +141,9 @@
     width = feat_store.shape[1]
     cap = serve_rows.shape[1]
     shape = jax.ShapeDtypeStruct
+    tile = 8
     halves = call_kernel(
-        split_kernel, [shape((feat_store.shape[0], width // 2), F32)] * 2, [feat_store]
+        split_kernel, [shape((feat_store.shape[0] + tile, width // 2), F32)] * 2, [feat_store]
     )
     served = serve_rows.reshape(-1)
     parts = {}
@@ -152,7 +153,7 @@
             [shape((nodes, width), BF16 if j % 2 else F32)],
             [jnp.reshape(own ^ j, (1,)), served, wanted[j]] + list(halves),
             spaces="ss",
-            scratch=[pltpu.VMEM((cap, width // 2), F32)] * 2,
+            scratch=[pltpu.VMEM((cap + tile, width // 2), F32)] * 2,
         )
         if j:
             served, parts[j] = lax.optimization_barrier((served, parts[j]))

time: 109 us -> 109 us (level)
  no operation moved by 1% of the time
where the time goes in v8:
time: 109 us
  starting transfers between devices  39 us (36%)
  waiting for transfers between devices  37 us (34%)
  Pallas kernels  18.6 us (17%)
  local copies, waits for them, and re-layouts  5.89 us (5%)
  matrix products  4.37 us (4%)
  other arithmetic  2.91 us (3%)
    ppermute x27, starting transfers between devices, exchange(): return lax.ppermute(value, AXES, pairs)  39 us
    ppermute x27, waiting for transfers between devices, exchange(): return lax.ppermute(value, AXES, pairs)  37 us
    pallas_call x9, Pallas kernels, call_kernel(): pl.pallas_call(kernel, out_shape=outs, in_specs=[pl.BlockSpec(memory_spac...  18.6 us
    unnamed x21, local copies, waits for them, and re-layouts  5.46 us
    dot_general x2, matrix products, forward(): pre_act = own_part + jnp.dot(pooled, w_nbr, preferred_element_type=F32)  2.69 us
  transfers between devices with their start and end apart: 27, of which 16 were waited for; matrix products, arithmetic and copies ran while one was open for 4% of the time, Pallas kernels for 9%

profile of v8, /device:TPU:0, one launch (start us, length us, event | category | flops | bytes accessed | tf_op | source)
XLA Modules:
  0.0 108.7 jit_solution(5632792656038239927)
XLA Ops:
  3.4 5.1 %collective-permute-start = (s32[1,1024]{1,0:T(1,128)S(1)}, s32[1,1024]{1,0:T(1,128)S(1)}, u32[]{:S(2)}, u32[]{:S(2)}) collective-permute-start(s32[1,1024]{1,0:T(1,128)S(1)} %get-tuple-element.66), channel_id=1, source_target_pairs={{0,3},{1,2},{2,1},{3,0},{4,7},{5,6},{6,5},{7,4},{8,11},{9,10},{10,... | collective-permute-start | bytes 12296 | tf_op jit(solution)/shard_map/ppermute | solution.py:26
  9.2 2.2 %copy-done.2 = bf16[8192,256]{1,0:T(8,128)(2,1)S(1)} copy-done((bf16[8192,256]{1,0:T(8,128)(2,1)S(1)}, bf16[8192,256]{1,0:T(8,128)(2,1)}, u32[]{:S(2)}) %copy-start.2) | copy-done | bytes 4194328
  13.1 2.5 %shard_map.104 = bf16[512,256]{1,0:T(8,128)(2,1)S(1)} custom-call(s32[1]{0:T(128)} %bitcast.3.requester, s32[4096]{0:T(1024)S(1)} %bitcast.22, s32[1,1024]{1,0:T(1,128)S(1)} %collective-permute-done.node_at, f32[8200,128]{1,0:T(8,128)S(1)} %get-tuple-element.27.left, f32[8200,128]{1,0:T(8,128)S(1)} %get-tuple-element.28.right), custom_call_target="tpu_custom_call" | custom-call | tf_op jit(solution)/shard_map/pallas_call | solution.py:80
  16.4 2.5 %shard_map.105 = f32[512,256]{1,0:T(8,128)S(1)} custom-call(s32[1]{0:T(128)} %bitcast.6.requester, s32[4096]{0:T(1024)S(1)} %bitcast.23, s32[1,1024]{1,0:T(1,128)S(1)} %collective-permute-done.1.node_at, f32[8200,128]{1,0:T(8,128)S(1)} %get-tuple-element.27.left, f32[8200,128]{1,0:T(8,128)S(1)} %get-tuple-element.28.right), custom_call_target="tpu_custom_call" | custom-call | tf_op jit(solution)/shard_map/pallas_call | solution.py:80
  19.0 2.5 %shard_map.106 = bf16[512,256]{1,0:T(8,128)(2,1)S(1)} custom-call(s32[1]{0:T(128)} %bitcast.7.requester, s32[4096]{0:T(1024)S(1)} %bitcast.24, s32[1,1024]{1,0:T(1,128)S(1)} %collective-permute-done.2.node_at, f32[8200,128]{1,0:T(8,128)S(1)} %get-tuple-element.27.left, f32[8200,128]{1,0:T(8,128)S(1)} %get-tuple-element.28.right), custom_call_target="tpu_custom_call" | custom-call | tf_op jit(solution)/shard_map/pallas_call | solution.py:80
  21.5 1.7 %collective-permute-start.3 = (bf16[512,256]{1,0:T(8,128)(2,1)S(1)}, bf16[512,256]{1,0:T(8,128)(2,1)S(1)}, u32[]{:S(2)}, u32[]{:S(2)}) collective-permute-start(bf16[512,256]{1,0:T(8,128)(2,1)S(1)} %shard_map.106), channel_id=1, source_target_pairs={{0,1},{1,0},{2,3},{3,2},{4,5},{5,4},{6,7},{7,6},{8,9},{9,8},{10,11... | collective-permute-start | bytes 786440 | tf_op jit(solution)/shard_map/ppermute | solution.py:26
  23.3 2.1 %collective-permute-start.5 = (bf16[256,256]{1,0:T(8,128)(2,1)S(1)}, bf16[256,256]{1,0:T(8,128)(2,1)S(1)}, u32[]{:S(2)}, u32[]{:S(2)}) collective-permute-start(bf16[256,256]{1,0:T(8,128)(2,1)S(1)} %get-tuple-element.58), channel_id=1, source_target_pairs={{0,2},{1,3},{2,0},{3,1},{4,6},{5,7},{6,4},{7,5},{8,10},{9,11},{10,... | collective-permute-start | bytes 393224 | tf_op jit(solution)/shard_map/ppermute | solution.py:26
  25.4 2.5 %shard_map.107 = f32[512,256]{1,0:T(8,128)S(1)} custom-call(s32[1]{0:T(128)} %bitcast.2.requester, s32[4096]{0:T(1024)S(1)} %bitcast.25, s32[1,1024]{1,0:T(1,128)S(1)} %get-tuple-element.63.node_at, f32[8200,128]{1,0:T(8,128)S(1)} %get-tuple-element.27.left, f32[8200,128]{1,0:T(8,128)S(1)} %get-tuple-element.28.right), custom_call_target="tpu_custom_call" | custom-call | tf_op jit(solution)/shard_map/pallas_call | solution.py:80
  28.9 4.3 %collective-permute-done.3 = bf16[512,256]{1,0:T(8,128)(2,1)S(1)} collective-permute-done((bf16[512,256]{1,0:T(8,128)(2,1)S(1)}, bf16[512,256]{1,0:T(8,128)(2,1)S(1)}, u32[]{:S(2)}, u32[]{:S(2)}) %collective-permute-start.3) | collective-permute-done | bytes 262176 | tf_op jit(solution)/shard_map/ppermute | solution.py:26
  35.2 1.6 %collective-permute-start.11 = (bf16[256,256]{1,0:T(8,128)(2,1)S(1)}, bf16[256,256]{1,0:T(8,128)(2,1)S(1)}, u32[]{:S(2)}, u32[]{:S(2)}) collective-permute-start(bf16[256,256]{1,0:T(8,128)(2,1)S(1)} %multiply_convert_fusion.3.refs_1_.refs_4_), channel_id=1, source_target_pairs={{0,2},{1,3},{2,0},{3,1},{4,6},{5,7},{6,4},{7,5},{8,10},{9,11},{10,... | collective-permute-start | bytes 393224 | tf_op jit(solution)/shard_map/ppermute | solution.py:26
  36.7 3.5 %collective-permute-done.6 = bf16[256,256]{1,0:T(8,128)(2,1)S(1)} collective-permute-done((bf16[256,256]{1,0:T(8,128)(2,1)S(1)}, bf16[256,256]{1,0:T(8,128)(2,1)S(1)}, u32[]{:S(2)}, u32[]{:S(2)}) %collective-permute-start.6) | collective-permute-done | bytes 131104 | tf_op jit(solution)/shard_map/ppermute | solution.py:26
  42.2 5.3 %collective-permute-start.10 = (bf16[256,256]{1,0:T(8,128)(2,1)S(1)}, bf16[256,256]{1,0:T(8,128)(2,1)}, u32[]{:S(2)}, u32[]{:S(2)}) collective-permute-start(bf16[256,256]{1,0:T(8,128)(2,1)S(1)} %multiply_convert_fusion.3.refs_1_.refs_4_), channel_id=1, source_target_pairs={{0,1},{1,0},{2,3},{3,2},{4,5},{5,4},{6,7},{7,6},{8,9},{9,8},{10,11... | collective-permute-start | bytes 393224 | tf_op jit(solution)/shard_map/ppermute | solution.py:26
  47.6 2.0 %collective-permute-start.7 = (bf16[256,256]{1,0:T(8,128)(2,1)S(1)}, bf16[256,256]{1,0:T(8,128)(2,1)}, u32[]{:S(2)}, u32[]{:S(2)}) collective-permute-start(bf16[256,256]{1,0:T(8,128)(2,1)S(1)} %multiply_convert_fusion.2.refs_0_), channel_id=1, source_target_pairs={{0,1},{1,0},{2,3},{3,2},{4,5},{5,4},{6,7},{7,6},{8,9},{9,8},{10,11... | collective-permute-start | bytes 393224 | tf_op jit(solution)/shard_map/ppermute | solution.py:26
  49.6 2.5 %collective-permute-start.9 = (bf16[256,256]{1,0:T(8,128)(2,1)}, bf16[256,256]{1,0:T(8,128)(2,1)}, u32[]{:S(2)}, u32[]{:S(2)}) collective-permute-start(bf16[256,256]{1,0:T(8,128)(2,1)} %collective-permute-done.8.refs_2_), channel_id=1, source_target_pairs={{0,1},{1,0},{2,3},{3,2},{4,5},{5,4},{6,7},{7,6},{8,9},{9,8},{10,11... | collective-permute-start | bytes 393224 | tf_op jit(solution)/shard_map/ppermute | solution.py:26
  54.7 2.2 %shard_map.108 = (bf16[256,256]{1,0:T(8,128)(2,1)S(1)}, f32[256,1]{1,0:T(8,128)S(1)}, bf16[256,256]{1,0:T(8,128)(2,1)S(1)}, bf16[256,1024]{1,0:T(8,128)(2,1)S(1)}) custom-call(bf16[256,256]{1,0:T(8,128)(2,1)S(1)} %multiply_convert_fusion.2.refs_0_, bf16[256,256]{1,0:T(8,128)(2,1)S(1)} %multiply_convert_fusion.3.refs_1_.refs_4_, ...), custom_call_target="tpu_custom_call" | custom-call | flops 402653184 | bytes 3277824 | tf_op jit(solution)/shard_map/pallas_call | solution.py:80
  56.9 3.9 %shard_map.109 = (bf16[384,1024]{1,0:T(8,128)(2,1)S(1)}, bf16[384,1024]{1,0:T(8,128)(2,1)}) custom-call(s32[1]{0:T(128)} %bitcast.core_ref.place, bf16[256,256]{1,0:T(8,128)(2,1)S(1)} %multiply_convert_fusion.2.refs_0_, bf16[256,256]{1,0:T(8,128)(2,1)} %collective-permute-done.7.refs_1_, bf16[256,256]{1,0:T(8,128)(2,1)} %collective-permute-done.8.refs_2_, ...), custom_call_target="tpu_custom_call" | custom-call | flops 1207959552 | bytes 6816772 | tf_op jit(solution)/shard_map/pallas_call | solution.py:80
  61.7 2.5 %collective-permute-done.13.arrived = bf16[384,1024]{1,0:T(8,128)(2,1)S(1)} collective-permute-done((bf16[384,1024]{1,0:T(8,128)(2,1)}, bf16[384,1024]{1,0:T(8,128)(2,1)S(1)}, u32[]{:S(2)}, u32[]{:S(2)}) %collective-permute-start.13) | collective-permute-done | bytes 786464 | tf_op jit(solution)/shard_map/ppermute | solution.py:26
  65.5 2.5 %collective-permute-start.16 = (bf16[96,1024]{1,0:T(8,128)(2,1)S(1)}, bf16[96,1024]{1,0:T(8,128)(2,1)S(1)}, u32[]{:S(2)}, u32[]{:S(2)}) collective-permute-start(bf16[96,1024]{1,0:T(8,128)(2,1)S(1)} %get-tuple-element.48), channel_id=1, source_target_pairs={{0,24},{1,25},{2,26},{3,27},{4,28},{5,29},{6,30},{7,31},{8,16},{9,... | collective-permute-start | bytes 589832 | tf_op jit(solution)/shard_map/ppermute | solution.py:26
  69.0 5.2 %collective-permute-done.16 = bf16[96,1024]{1,0:T(8,128)(2,1)S(1)} collective-permute-done((bf16[96,1024]{1,0:T(8,128)(2,1)S(1)}, bf16[96,1024]{1,0:T(8,128)(2,1)S(1)}, u32[]{:S(2)}, u32[]{:S(2)}) %collective-permute-start.16) | collective-permute-done | bytes 196640 | tf_op jit(solution)/shard_map/ppermute | solution.py:26
  74.2 3.4 %collective-permute-done.15 = bf16[96,1024]{1,0:T(8,128)(2,1)S(1)} collective-permute-done((bf16[96,1024]{1,0:T(8,128)(2,1)S(1)}, bf16[96,1024]{1,0:T(8,128)(2,1)S(1)}, u32[]{:S(2)}, u32[]{:S(2)}) %collective-permute-start.15) | collective-permute-done | bytes 196640 | tf_op jit(solution)/shard_map/ppermute | solution.py:26
  77.8 4.3 %collective-permute-start.19 = (bf16[24,1024]{1,0:T(8,128)(2,1)S(1)}, bf16[24,1024]{1,0:T(8,128)(2,1)S(1)}, u32[]{:S(2)}, u32[]{:S(2)}) collective-permute-start(bf16[24,1024]{1,0:T(8,128)(2,1)S(1)} %get-tuple-element.55), channel_id=1, source_target_pairs={{0,3},{1,2},{2,1},{3,0},{4,7},{5,6},{6,5},{7,4},{8,11},{9,10},{10,... | collective-permute-start | bytes 147464 | tf_op jit(solution)/shard_map/ppermute | solution.py:26
  82.8 1.7 %collective-permute-done.19 = bf16[24,1024]{1,0:T(8,128)(2,1)S(1)} collective-permute-done((bf16[24,1024]{1,0:T(8,128)(2,1)S(1)}, bf16[24,1024]{1,0:T(8,128)(2,1)S(1)}, u32[]{:S(2)}, u32[]{:S(2)}) %collective-permute-start.19) | collective-permute-done | bytes 49184 | tf_op jit(solution)/shard_map/ppermute | solution.py:26
  84.5 2.6 %collective-permute-done.18 = bf16[24,1024]{1,0:T(8,128)(2,1)S(1)} collective-permute-done((bf16[24,1024]{1,0:T(8,128)(2,1)S(1)}, bf16[24,1024]{1,0:T(8,128)(2,1)S(1)}, u32[]{:S(2)}, u32[]{:S(2)}) %collective-permute-start.18) | collective-permute-done | bytes 49184 | tf_op jit(solution)/shard_map/ppermute | solution.py:26
  87.2 2.0 %collective-permute-start.20 = (bf16[24,1024]{1,0:T(8,128)(2,1)S(1)}, bf16[24,1024]{1,0:T(8,128)(2,1)S(1)}, u32[]{:S(2)}, u32[]{:S(2)}) collective-permute-start(bf16[24,1024]{1,0:T(8,128)(2,1)S(1)} %add_convert_fusion.1), channel_id=1, source_target_pairs={{0,3},{1,2},{2,1},{3,0},{4,7},{5,6},{6,5},{7,4},{8,11},{9,10},{10,... | collective-permute-start | bytes 147464 | tf_op jit(solution)/shard_map/ppermute | solution.py:26
  89.4 2.2 %collective-permute-start.22 = (bf16[24,1024]{1,0:T(8,128)(2,1)S(1)}, bf16[24,1024]{1,0:T(8,128)(2,1)S(1)}, u32[]{:S(2)}, u32[]{:S(2)}) collective-permute-start(bf16[24,1024]{1,0:T(8,128)(2,1)S(1)} %add_convert_fusion.1), channel_id=1, source_target_pairs={{0,1},{1,0},{2,3},{3,2},{4,5},{5,4},{6,7},{7,6},{8,9},{9,8},{10,11... | collective-permute-start | bytes 147464 | tf_op jit(solution)/shard_map/ppermute | solution.py:26
  91.6 1.6 %collective-permute-done.20 = bf16[24,1024]{1,0:T(8,128)(2,1)S(1)} collective-permute-done((bf16[24,1024]{1,0:T(8,128)(2,1)S(1)}, bf16[24,1024]{1,0:T(8,128)(2,1)S(1)}, u32[]{:S(2)}, u32[]{:S(2)}) %collective-permute-start.20) | collective-permute-done | bytes 49184 | tf_op jit(solution)/shard_map/ppermute | solution.py:26
  93.3 1.4 %collective-permute-done.21 = bf16[24,1024]{1,0:T(8,128)(2,1)S(1)} collective-permute-done((bf16[24,1024]{1,0:T(8,128)(2,1)S(1)}, bf16[24,1024]{1,0:T(8,128)(2,1)S(1)}, u32[]{:S(2)}, u32[]{:S(2)}) %collective-permute-start.21) | collective-permute-done | bytes 49184 | tf_op jit(solution)/shard_map/ppermute | solution.py:26
  96.0 1.8 %collective-permute-start.24 = (bf16[96,1024]{1,0:T(8,128)(2,1)S(1)}, bf16[96,1024]{1,0:T(8,128)(2,1)S(1)}, u32[]{:S(2)}, u32[]{:S(2)}) collective-permute-start(bf16[96,1024]{1,0:T(8,128)(2,1)S(1)} %pad_maximum_fusion.1), channel_id=1, source_target_pairs={{0,16},{1,17},{2,18},{3,19},{4,20},{5,21},{6,22},{7,23},{8,24},{9,... | collective-permute-start | bytes 589832 | tf_op jit(solution)/shard_map/ppermute | solution.py:26
  98.3 3.8 %collective-permute-done.23 = bf16[96,1024]{1,0:T(8,128)(2,1)S(1)} collective-permute-done((bf16[96,1024]{1,0:T(8,128)(2,1)S(1)}, bf16[96,1024]{1,0:T(8,128)(2,1)S(1)}, u32[]{:S(2)}, u32[]{:S(2)}) %collective-permute-start.23) | collective-permute-done | bytes 196640 | tf_op jit(solution)/shard_map/ppermute | solution.py:26
  102.1 2.0 %collective-permute-done.24 = bf16[96,1024]{1,0:T(8,128)(2,1)S(1)} collective-permute-done((bf16[96,1024]{1,0:T(8,128)(2,1)S(1)}, bf16[96,1024]{1,0:T(8,128)(2,1)S(1)}, u32[]{:S(2)}, u32[]{:S(2)}) %collective-permute-start.24) | collective-permute-done | bytes 196640 | tf_op jit(solution)/shard_map/ppermute | solution.py:26
  104.7 2.3 %collective-permute-done.26.other = bf16[384,1024]{1,0:T(8,128)(2,1)S(1)} collective-permute-done((bf16[384,1024]{1,0:T(8,128)(2,1)S(1)}, bf16[384,1024]{1,0:T(8,128)(2,1)S(1)}, u32[]{:S(2)}, u32[]{:S(2)}) %collective-permute-start.26) | collective-permute-done | bytes 786464 | tf_op jit(solution)/shard_map/ppermute | solution.py:26
  107.0 1.8 %shard_map.111 = (f32[256,1024]{1,0:T(8,128)}, f32[256,1024]{1,0:T(8,128)}, f32[1024,256]{1,0:T(8,128)}) custom-call(s32[1]{0:T(128)} %bitcast.core_ref.place, bf16[384,1024]{1,0:T(8,128)(2,1)S(1)} %pad_maximum_fusion.block, bf16[384,1024]{1,0:T(8,128)(2,1)S(1)} %collective-permute-done.26.other), custom_call_target="tpu_custom_call" | custom-call | tf_op jit(solution)/shard_map/pallas_call | solution.py:80
  (86 shorter events, 20.3 us)
Async XLA Ops:
  0.6 32.6 %copy-start = (bf16[256,1024]{1,0:T(8,128)(2,1)S(1)}, bf16[256,1024]{1,0:T(8,128)(2,1)}, u32[]{:S(2)}) copy-start(bf16[256,1024]{1,0:T(8,128)(2,1)} %param.14) | copy-start | bytes 1572868
  0.6 8.6 %copy-start.9 = (s32[4,1024]{1,0:T(4,128)S(1)}, s32[4,1024]{1,0:T(4,128)}, u32[]{:S(2)}) copy-start(s32[4,1024]{1,0:T(4,128)} %param.11) | copy-start | bytes 49156
  3.4 8.5 %collective-permute-start = (s32[1,1024]{1,0:T(1,128)S(1)}, s32[1,1024]{1,0:T(1,128)S(1)}, u32[]{:S(2)}, u32[]{:S(2)}) collective-permute-start(s32[1,1024]{1,0:T(1,128)S(1)} %get-tuple-element.66), channel_id=1, source_target_pairs={{0,3},{1,2},{2,1},{3,0},{4,7},{5,6},{6,5},{7,4},{8,11},{9,10},{10,... | collective-permute-start | bytes 12296 | tf_op jit(solution)/shard_map/ppermute | solution.py:26
  8.6 4.5 %collective-permute-start.1 = (s32[1,1024]{1,0:T(1,128)S(1)}, s32[1,1024]{1,0:T(1,128)S(1)}, u32[]{:S(2)}, u32[]{:S(2)}) collective-permute-start(s32[1,1024]{1,0:T(1,128)S(1)} %get-tuple-element.65), channel_id=1, source_target_pairs={{0,2},{1,3},{2,0},{3,1},{4,6},{5,7},{6,4},{7,5},{8,10},{9,11},{10,... | collective-permute-start | bytes 12296 | tf_op jit(solution)/shard_map/ppermute | solution.py:26
  8.6 4.5 %collective-permute-start.2 = (s32[1,1024]{1,0:T(1,128)S(1)}, s32[1,1024]{1,0:T(1,128)S(1)}, u32[]{:S(2)}, u32[]{:S(2)}) collective-permute-start(s32[1,1024]{1,0:T(1,128)S(1)} %get-tuple-element.64), channel_id=1, source_target_pairs={{0,1},{1,0},{2,3},{3,2},{4,5},{5,4},{6,7},{7,6},{8,9},{9,8},{10,11... | collective-permute-start | bytes 12296 | tf_op jit(solution)/shard_map/ppermute | solution.py:26
  9.2 2.2 %copy-start.2 = (bf16[8192,256]{1,0:T(8,128)(2,1)S(1)}, bf16[8192,256]{1,0:T(8,128)(2,1)}, u32[]{:S(2)}) copy-start(bf16[8192,256]{1,0:T(8,128)(2,1)} %store.1) | copy-start | bytes 12582916
  13.1 2.9 %copy-start.5 = (bf16[512,256]{1,0:T(8,128)(2,1)S(1)}, bf16[512,256]{1,0:T(8,128)(2,1)}, u32[]{:S(2)}) copy-start(bf16[512,256]{1,0:T(8,128)(2,1)} %refs_17_.1) | copy-start | bytes 786436
  13.1 2.9 %copy-start.8 = (bf16[256,1024]{1,0:T(8,128)(2,1)S(1)}, bf16[256,1024]{1,0:T(8,128)(2,1)}, u32[]{:S(2)}) copy-start(bf16[256,1024]{1,0:T(8,128)(2,1)} %param.13) | copy-start | bytes 1572868
  15.6 7.6 %collective-permute-start.4 = (bf16[512,256]{1,0:T(8,128)(2,1)S(1)}, bf16[512,256]{1,0:T(8,128)(2,1)S(1)}, u32[]{:S(2)}, u32[]{:S(2)}) collective-permute-start(bf16[512,256]{1,0:T(8,128)(2,1)S(1)} %shard_map.104), channel_id=1, source_target_pairs={{0,1},{1,0},{2,3},{3,2},{4,5},{5,4},{6,7},{7,6},{8,9},{9,8},{10,11... | collective-permute-start | bytes 786440 | tf_op jit(solution)/shard_map/ppermute | solution.py:26
  21.5 11.7 %collective-permute-start.3 = (bf16[512,256]{1,0:T(8,128)(2,1)S(1)}, bf16[512,256]{1,0:T(8,128)(2,1)S(1)}, u32[]{:S(2)}, u32[]{:S(2)}) collective-permute-start(bf16[512,256]{1,0:T(8,128)(2,1)S(1)} %shard_map.106), channel_id=1, source_target_pairs={{0,1},{1,0},{2,3},{3,2},{4,5},{5,4},{6,7},{7,6},{8,9},{9,8},{10,11... | collective-permute-start | bytes 786440 | tf_op jit(solution)/shard_map/ppermute | solution.py:26
  23.3 9.8 %collective-permute-start.5 = (bf16[256,256]{1,0:T(8,128)(2,1)S(1)}, bf16[256,256]{1,0:T(8,128)(2,1)S(1)}, u32[]{:S(2)}, u32[]{:S(2)}) collective-permute-start(bf16[256,256]{1,0:T(8,128)(2,1)S(1)} %get-tuple-element.58), channel_id=1, source_target_pairs={{0,2},{1,3},{2,0},{3,1},{4,6},{5,7},{6,4},{7,5},{8,10},{9,11},{10,... | collective-permute-start | bytes 393224 | tf_op jit(solution)/shard_map/ppermute | solution.py:26
  27.9 12.3 %collective-permute-start.6 = (bf16[256,256]{1,0:T(8,128)(2,1)S(1)}, bf16[256,256]{1,0:T(8,128)(2,1)S(1)}, u32[]{:S(2)}, u32[]{:S(2)}) collective-permute-start(bf16[256,256]{1,0:T(8,128)(2,1)S(1)} %get-tuple-element.57), channel_id=1, source_target_pairs={{0,2},{1,3},{2,0},{3,1},{4,6},{5,7},{6,4},{7,5},{8,10},{9,11},{10,... | collective-permute-start | bytes 393224 | tf_op jit(solution)/shard_map/ppermute | solution.py:26
  35.2 12.4 %collective-permute-start.11 = (bf16[256,256]{1,0:T(8,128)(2,1)S(1)}, bf16[256,256]{1,0:T(8,128)(2,1)S(1)}, u32[]{:S(2)}, u32[]{:S(2)}) collective-permute-start(bf16[256,256]{1,0:T(8,128)(2,1)S(1)} %multiply_convert_fusion.3.refs_1_.refs_4_), channel_id=1, source_target_pairs={{0,2},{1,3},{2,0},{3,1},{4,6},{5,7},{6,4},{7,5},{8,10},{9,11},{10,... | collective-permute-start | bytes 393224 | tf_op jit(solution)/shard_map/ppermute | solution.py:26
  42.2 7.5 %collective-permute-start.8 = (bf16[256,256]{1,0:T(8,128)(2,1)S(1)}, bf16[256,256]{1,0:T(8,128)(2,1)}, u32[]{:S(2)}, u32[]{:S(2)}) collective-permute-start(bf16[256,256]{1,0:T(8,128)(2,1)S(1)} %multiply_convert_fusion.2.refs_0_), channel_id=1, source_target_pairs={{0,2},{1,3},{2,0},{3,1},{4,6},{5,7},{6,4},{7,5},{8,10},{9,11},{10,... | collective-permute-start | bytes 393224 | tf_op jit(solution)/shard_map/ppermute | solution.py:26
  42.2 9.9 %collective-permute-start.10 = (bf16[256,256]{1,0:T(8,128)(2,1)S(1)}, bf16[256,256]{1,0:T(8,128)(2,1)}, u32[]{:S(2)}, u32[]{:S(2)}) collective-permute-start(bf16[256,256]{1,0:T(8,128)(2,1)S(1)} %multiply_convert_fusion.3.refs_1_.refs_4_), channel_id=1, source_target_pairs={{0,1},{1,0},{2,3},{3,2},{4,5},{5,4},{6,7},{7,6},{8,9},{9,8},{10,11... | collective-permute-start | bytes 393224 | tf_op jit(solution)/shard_map/ppermute | solution.py:26
  47.6 5.9 %collective-permute-start.12 = (bf16[256,256]{1,0:T(8,128)(2,1)S(1)}, bf16[256,256]{1,0:T(8,128)(2,1)}, u32[]{:S(2)}, u32[]{:S(2)}) collective-permute-start(bf16[256,256]{1,0:T(8,128)(2,1)S(1)} %collective-permute-done.11.refs_3_.refs_6_), channel_id=1, source_target_pairs={{0,1},{1,0},{2,3},{3,2},{4,5},{5,4},{6,7},{7,6},{8,9},{9,8},{10,11... | collective-permute-start | bytes 393224 | tf_op jit(solution)/shard_map/ppermute | solution.py:26
  47.6 9.2 %collective-permute-start.7 = (bf16[256,256]{1,0:T(8,128)(2,1)S(1)}, bf16[256,256]{1,0:T(8,128)(2,1)}, u32[]{:S(2)}, u32[]{:S(2)}) collective-permute-start(bf16[256,256]{1,0:T(8,128)(2,1)S(1)} %multiply_convert_fusion.2.refs_0_), channel_id=1, source_target_pairs={{0,1},{1,0},{2,3},{3,2},{4,5},{5,4},{6,7},{7,6},{8,9},{9,8},{10,11... | collective-permute-start | bytes 393224 | tf_op jit(solution)/shard_map/ppermute | solution.py:26
  49.6 7.3 %collective-permute-start.9 = (bf16[256,256]{1,0:T(8,128)(2,1)}, bf16[256,256]{1,0:T(8,128)(2,1)}, u32[]{:S(2)}, u32[]{:S(2)}) collective-permute-start(bf16[256,256]{1,0:T(8,128)(2,1)} %collective-permute-done.8.refs_2_), channel_id=1, source_target_pairs={{0,1},{1,0},{2,3},{3,2},{4,5},{5,4},{6,7},{7,6},{8,9},{9,8},{10,11... | collective-permute-start | bytes 393224 | tf_op jit(solution)/shard_map/ppermute | solution.py:26
  61.7 2.5 %collective-permute-start.13 = (bf16[384,1024]{1,0:T(8,128)(2,1)}, bf16[384,1024]{1,0:T(8,128)(2,1)S(1)}, u32[]{:S(2)}, u32[]{:S(2)}) collective-permute-start(bf16[384,1024]{1,0:T(8,128)(2,1)} %get-tuple-element.44), channel_id=1, source_target_pairs={{0,4},{1,5},{2,6},{3,7},{4,0},{5,1},{6,2},{7,3},{8,12},{9,13},{10,... | collective-permute-start | bytes 2359304 | tf_op jit(solution)/shard_map/ppermute | solution.py:26
  65.5 8.8 %collective-permute-start.16 = (bf16[96,1024]{1,0:T(8,128)(2,1)S(1)}, bf16[96,1024]{1,0:T(8,128)(2,1)S(1)}, u32[]{:S(2)}, u32[]{:S(2)}) collective-permute-start(bf16[96,1024]{1,0:T(8,128)(2,1)S(1)} %get-tuple-element.48), channel_id=1, source_target_pairs={{0,24},{1,25},{2,26},{3,27},{4,28},{5,29},{6,30},{7,31},{8,16},{9,... | collective-permute-start | bytes 589832 | tf_op jit(solution)/shard_map/ppermute | solution.py:26
  68.0 9.6 %collective-permute-start.15 = (bf16[96,1024]{1,0:T(8,128)(2,1)S(1)}, bf16[96,1024]{1,0:T(8,128)(2,1)S(1)}, u32[]{:S(2)}, u32[]{:S(2)}) collective-permute-start(bf16[96,1024]{1,0:T(8,128)(2,1)S(1)} %get-tuple-element.47), channel_id=1, source_target_pairs={{0,16},{1,17},{2,18},{3,19},{4,20},{5,21},{6,22},{7,23},{8,24},{9,... | collective-permute-start | bytes 589832 | tf_op jit(solution)/shard_map/ppermute | solution.py:26
  68.5 9.2 %collective-permute-start.14 = (bf16[96,1024]{1,0:T(8,128)(2,1)S(1)}, bf16[96,1024]{1,0:T(8,128)(2,1)S(1)}, u32[]{:S(2)}, u32[]{:S(2)}) collective-permute-start(bf16[96,1024]{1,0:T(8,128)(2,1)S(1)} %get-tuple-element.46), channel_id=1, source_target_pairs={{0,8},{1,9},{2,10},{3,11},{4,12},{5,13},{6,14},{7,15},{8,0},{9,1},... | collective-permute-start | bytes 589832 | tf_op jit(solution)/shard_map/ppermute | solution.py:26
  77.8 6.7 %collective-permute-start.19 = (bf16[24,1024]{1,0:T(8,128)(2,1)S(1)}, bf16[24,1024]{1,0:T(8,128)(2,1)S(1)}, u32[]{:S(2)}, u32[]{:S(2)}) collective-permute-start(bf16[24,1024]{1,0:T(8,128)(2,1)S(1)} %get-tuple-element.55), channel_id=1, source_target_pairs={{0,3},{1,2},{2,1},{3,0},{4,7},{5,6},{6,5},{7,4},{8,11},{9,10},{10,... | collective-permute-start | bytes 147464 | tf_op jit(solution)/shard_map/ppermute | solution.py:26
  82.1 5.0 %collective-permute-start.18 = (bf16[24,1024]{1,0:T(8,128)(2,1)S(1)}, bf16[24,1024]{1,0:T(8,128)(2,1)S(1)}, u32[]{:S(2)}, u32[]{:S(2)}) collective-permute-start(bf16[24,1024]{1,0:T(8,128)(2,1)S(1)} %get-tuple-element.56), channel_id=1, source_target_pairs={{0,2},{1,3},{2,0},{3,1},{4,6},{5,7},{6,4},{7,5},{8,10},{9,11},{10,... | collective-permute-start | bytes 147464 | tf_op jit(solution)/shard_map/ppermute | solution.py:26
  82.1 5.0 %collective-permute-start.17 = (bf16[24,1024]{1,0:T(8,128)(2,1)S(1)}, bf16[24,1024]{1,0:T(8,128)(2,1)S(1)}, u32[]{:S(2)}, u32[]{:S(2)}) collective-permute-start(bf16[24,1024]{1,0:T(8,128)(2,1)S(1)} %get-tuple-element.54), channel_id=1, source_target_pairs={{0,1},{1,0},{2,3},{3,2},{4,5},{5,4},{6,7},{7,6},{8,9},{9,8},{10,11... | collective-permute-start | bytes 147464 | tf_op jit(solution)/shard_map/ppermute | solution.py:26
  87.2 6.1 %collective-permute-start.20 = (bf16[24,1024]{1,0:T(8,128)(2,1)S(1)}, bf16[24,1024]{1,0:T(8,128)(2,1)S(1)}, u32[]{:S(2)}, u32[]{:S(2)}) collective-permute-start(bf16[24,1024]{1,0:T(8,128)(2,1)S(1)} %add_convert_fusion.1), channel_id=1, source_target_pairs={{0,3},{1,2},{2,1},{3,0},{4,7},{5,6},{6,5},{7,4},{8,11},{9,10},{10,... | collective-permute-start | bytes 147464 | tf_op jit(solution)/shard_map/ppermute | solution.py:26
  89.2 5.5 %collective-permute-start.21 = (bf16[24,1024]{1,0:T(8,128)(2,1)S(1)}, bf16[24,1024]{1,0:T(8,128)(2,1)S(1)}, u32[]{:S(2)}, u32[]{:S(2)}) collective-permute-start(bf16[24,1024]{1,0:T(8,128)(2,1)S(1)} %add_convert_fusion.1), channel_id=1, source_target_pairs={{0,2},{1,3},{2,0},{3,1},{4,6},{5,7},{6,4},{7,5},{8,10},{9,11},{10,... | collective-permute-start | bytes 147464 | tf_op jit(solution)/shard_map/ppermute | solution.py:26
  89.4 5.3 %collective-permute-start.22 = (bf16[24,1024]{1,0:T(8,128)(2,1)S(1)}, bf16[24,1024]{1,0:T(8,128)(2,1)S(1)}, u32[]{:S(2)}, u32[]{:S(2)}) collective-permute-start(bf16[24,1024]{1,0:T(8,128)(2,1)S(1)} %add_convert_fusion.1), channel_id=1, source_target_pairs={{0,1},{1,0},{2,3},{3,2},{4,5},{5,4},{6,7},{7,6},{8,9},{9,8},{10,11... | collective-permute-start | bytes 147464 | tf_op jit(solution)/shard_map/ppermute | solution.py:26
  94.8 7.4 %collective-permute-start.23 = (bf16[96,1024]{1,0:T(8,128)(2,1)S(1)}, bf16[96,1024]{1,0:T(8,128)(2,1)S(1)}, u32[]{:S(2)}, u32[]{:S(2)}) collective-permute-start(bf16[96,1024]{1,0:T(8,128)(2,1)S(1)} %pad_maximum_fusion.1), channel_id=1, source_target_pairs={{0,24},{1,25},{2,26},{3,27},{4,28},{5,29},{6,30},{7,31},{8,16},{9,... | collective-permute-start | bytes 589832 | tf_op jit(solution)/shard_map/ppermute | solution.py:26
  96.0 8.1 %collective-permute-start.24 = (bf16[96,1024]{1,0:T(8,128)(2,1)S(1)}, bf16[96,1024]{1,0:T(8,128)(2,1)S(1)}, u32[]{:S(2)}, u32[]{:S(2)}) collective-permute-start(bf16[96,1024]{1,0:T(8,128)(2,1)S(1)} %pad_maximum_fusion.1), channel_id=1, source_target_pairs={{0,16},{1,17},{2,18},{3,19},{4,20},{5,21},{6,22},{7,23},{8,24},{9,... | collective-permute-start | bytes 589832 | tf_op jit(solution)/shard_map/ppermute | solution.py:26
  97.8 6.5 %collective-permute-start.25 = (bf16[96,1024]{1,0:T(8,128)(2,1)S(1)}, bf16[96,1024]{1,0:T(8,128)(2,1)S(1)}, u32[]{:S(2)}, u32[]{:S(2)}) collective-permute-start(bf16[96,1024]{1,0:T(8,128)(2,1)S(1)} %pad_maximum_fusion.1), channel_id=1, source_target_pairs={{0,8},{1,9},{2,10},{3,11},{4,12},{5,13},{6,14},{7,15},{8,0},{9,1},... | collective-permute-start | bytes 589832 | tf_op jit(solution)/shard_map/ppermute | solution.py:26
  104.6 2.4 %collective-permute-start.26 = (bf16[384,1024]{1,0:T(8,128)(2,1)S(1)}, bf16[384,1024]{1,0:T(8,128)(2,1)S(1)}, u32[]{:S(2)}, u32[]{:S(2)}) collective-permute-start(bf16[384,1024]{1,0:T(8,128)(2,1)S(1)} %pad_maximum_fusion.block), channel_id=1, source_target_pairs={{0,4},{1,5},{2,6},{3,7},{4,0},{5,1},{6,2},{7,3},{8,12},{9,13},{10,... | collective-permute-start | bytes 2359304 | tf_op jit(solution)/shard_map/ppermute | solution.py:26
  (5 other events, 6.8 us)

commit v9 on v8

--- a/solution.py
+++ b/solution.py
@@ -107,9 +107,9 @@
     first = requester[0] * count
 
     def some_rows(i, carry):
-        base = i * 32
-        wanted = [serve_rows[first + base + u] for u in range(32)]
-        for tile in range(0, 32, 8):
+        base = i * 64
+        wanted = [serve_rows[first + base + u] for u in range(64)]
+        for tile in range(0, 64, 8):
             at = pl.ds(pl.multiple_of(base + tile, 8), 8)
             to_left, to_right = got_left.at[at, :], got_right.at[at, :]
             for u in range(8):
@@ -118,7 +118,7 @@
                 to_right[u : u + 1, :] = right[row, :]
         return carry
 
-    lax.fori_loop(0, count // 32, some_rows, 0)
+    lax.fori_loop(0, count // 64, some_rows, 0)
     nodes = lax.broadcasted_iota(jnp.int32, (out.shape[0], count), 0)
     pick = (nodes == node_at[...]).astype(BF16)
     rows = jnp.concatenate([got_left[:count], got_right[:count]], 1).astype(BF16)

time: 109 us -> 109 us (level)
  no operation moved by 1% of the time
where the time goes in v9:
time: 109 us
  starting transfers between devices  39.1 us (36%)
  waiting for transfers between devices  37 us (34%)
  Pallas kernels  18.3 us (17%)
  local copies, waits for them, and re-layouts  5.89 us (5%)
  matrix products  4.37 us (4%)
  other arithmetic  2.91 us (3%)
    ppermute x27, starting transfers between devices, exchange(): return lax.ppermute(value, AXES, pairs)  39.1 us
    ppermute x27, waiting for transfers between devices, exchange(): return lax.ppermute(value, AXES, pairs)  37 us
    pallas_call x9, Pallas kernels, call_kernel(): pl.pallas_call(kernel, out_shape=outs, in_specs=[pl.BlockSpec(memory_spac...  18.3 us
    unnamed x21, local copies, waits for them, and re-layouts  5.46 us
    dot_general x2, matrix products, forward(): pre_act = own_part + jnp.dot(pooled, w_nbr, preferred_element_type=F32)  2.69 us
  transfers between devices with their start and end apart: 27, of which 16 were waited for; matrix products, arithmetic and copies ran while one was open for 4% of the time, Pallas kernels for 9%

profile of v9, /device:TPU:0, one launch (start us, length us, event | category | flops | bytes accessed | tf_op | source)
XLA Modules:
  0.0 108.5 jit_solution(2639811513020029990)
XLA Ops:
  3.4 5.1 %collective-permute-start = (s32[1,1024]{1,0:T(1,128)S(1)}, s32[1,1024]{1,0:T(1,128)S(1)}, u32[]{:S(2)}, u32[]{:S(2)}) collective-permute-start(s32[1,1024]{1,0:T(1,128)S(1)} %get-tuple-element.66), channel_id=1, source_target_pairs={{0,3},{1,2},{2,1},{3,0},{4,7},{5,6},{6,5},{7,4},{8,11},{9,10},{10,... | collective-permute-start | bytes 12296 | tf_op jit(solution)/shard_map/ppermute | solution.py:26
  9.2 2.2 %copy-done.2 = bf16[8192,256]{1,0:T(8,128)(2,1)S(1)} copy-done((bf16[8192,256]{1,0:T(8,128)(2,1)S(1)}, bf16[8192,256]{1,0:T(8,128)(2,1)}, u32[]{:S(2)}) %copy-start.2) | copy-done | bytes 4194328
  13.1 2.4 %shard_map.104 = bf16[512,256]{1,0:T(8,128)(2,1)S(1)} custom-call(s32[1]{0:T(128)} %bitcast.3.requester, s32[4096]{0:T(1024)S(1)} %bitcast.22, s32[1,1024]{1,0:T(1,128)S(1)} %collective-permute-done.node_at, f32[8200,128]{1,0:T(8,128)S(1)} %get-tuple-element.27.left, f32[8200,128]{1,0:T(8,128)S(1)} %get-tuple-element.28.right), custom_call_target="tpu_custom_call" | custom-call | tf_op jit(solution)/shard_map/pallas_call | solution.py:80
  16.4 2.4 %shard_map.105 = f32[512,256]{1,0:T(8,128)S(1)} custom-call(s32[1]{0:T(128)} %bitcast.6.requester, s32[4096]{0:T(1024)S(1)} %bitcast.23, s32[1,1024]{1,0:T(1,128)S(1)} %collective-permute-done.1.node_at, f32[8200,128]{1,0:T(8,128)S(1)} %get-tuple-element.27.left, f32[8200,128]{1,0:T(8,128)S(1)} %get-tuple-element.28.right), custom_call_target="tpu_custom_call" | custom-call | tf_op jit(solution)/shard_map/pallas_call | solution.py:80
  18.8 2.4 %shard_map.106 = bf16[512,256]{1,0:T(8,128)(2,1)S(1)} custom-call(s32[1]{0:T(128)} %bitcast.7.requester, s32[4096]{0:T(1024)S(1)} %bitcast.24, s32[1,1024]{1,0:T(1,128)S(1)} %collective-permute-done.2.node_at, f32[8200,128]{1,0:T(8,128)S(1)} %get-tuple-element.27.left, f32[8200,128]{1,0:T(8,128)S(1)} %get-tuple-element.28.right), custom_call_target="tpu_custom_call" | custom-call | tf_op jit(solution)/shard_map/pallas_call | solution.py:80
  21.2 1.7 %collective-permute-start.3 = (bf16[512,256]{1,0:T(8,128)(2,1)S(1)}, bf16[512,256]{1,0:T(8,128)(2,1)S(1)}, u32[]{:S(2)}, u32[]{:S(2)}) collective-permute-start(bf16[512,256]{1,0:T(8,128)(2,1)S(1)} %shard_map.106), channel_id=1, source_target_pairs={{0,1},{1,0},{2,3},{3,2},{4,5},{5,4},{6,7},{7,6},{8,9},{9,8},{10,11... | collective-permute-start | bytes 786440 | tf_op jit(solution)/shard_map/ppermute | solution.py:26
  23.1 2.1 %collective-permute-start.5 = (bf16[256,256]{1,0:T(8,128)(2,1)S(1)}, bf16[256,256]{1,0:T(8,128)(2,1)S(1)}, u32[]{:S(2)}, u32[]{:S(2)}) collective-permute-start(bf16[256,256]{1,0:T(8,128)(2,1)S(1)} %get-tuple-element.58), channel_id=1, source_target_pairs={{0,2},{1,3},{2,0},{3,1},{4,6},{5,7},{6,4},{7,5},{8,10},{9,11},{10,... | collective-permute-start | bytes 393224 | tf_op jit(solution)/shard_map/ppermute | solution.py:26
  25.2 2.4 %shard_map.107 = f32[512,256]{1,0:T(8,128)S(1)} custom-call(s32[1]{0:T(128)} %bitcast.2.requester, s32[4096]{0:T(1024)S(1)} %bitcast.25, s32[1,1024]{1,0:T(1,128)S(1)} %get-tuple-element.63.node_at, f32[8200,128]{1,0:T(8,128)S(1)} %get-tuple-element.27.left, f32[8200,128]{1,0:T(8,128)S(1)} %get-tuple-element.28.right), custom_call_target="tpu_custom_call" | custom-call | tf_op jit(solution)/shard_map/pallas_call | solution.py:80
  28.6 4.3 %collective-permute-done.3 = bf16[512,256]{1,0:T(8,128)(2,1)S(1)} collective-permute-done((bf16[512,256]{1,0:T(8,128)(2,1)S(1)}, bf16[512,256]{1,0:T(8,128)(2,1)S(1)}, u32[]{:S(2)}, u32[]{:S(2)}) %collective-permute-start.3) | collective-permute-done | bytes 262176 | tf_op jit(solution)/shard_map/ppermute | solution.py:26
  34.9 1.6 %collective-permute-start.11 = (bf16[256,256]{1,0:T(8,128)(2,1)S(1)}, bf16[256,256]{1,0:T(8,128)(2,1)S(1)}, u32[]{:S(2)}, u32[]{:S(2)}) collective-permute-start(bf16[256,256]{1,0:T(8,128)(2,1)S(1)} %multiply_convert_fusion.3.refs_1_.refs_4_), channel_id=1, source_target_pairs={{0,2},{1,3},{2,0},{3,1},{4,6},{5,7},{6,4},{7,5},{8,10},{9,11},{10,... | collective-permute-start | bytes 393224 | tf_op jit(solution)/shard_map/ppermute | solution.py:26
  36.5 3.5 %collective-permute-done.6 = bf16[256,256]{1,0:T(8,128)(2,1)S(1)} collective-permute-done((bf16[256,256]{1,0:T(8,128)(2,1)S(1)}, bf16[256,256]{1,0:T(8,128)(2,1)S(1)}, u32[]{:S(2)}, u32[]{:S(2)}) %collective-permute-start.6) | collective-permute-done | bytes 131104 | tf_op jit(solution)/shard_map/ppermute | solution.py:26
  42.0 5.4 %collective-permute-start.10 = (bf16[256,256]{1,0:T(8,128)(2,1)S(1)}, bf16[256,256]{1,0:T(8,128)(2,1)}, u32[]{:S(2)}, u32[]{:S(2)}) collective-permute-start(bf16[256,256]{1,0:T(8,128)(2,1)S(1)} %multiply_convert_fusion.3.refs_1_.refs_4_), channel_id=1, source_target_pairs={{0,1},{1,0},{2,3},{3,2},{4,5},{5,4},{6,7},{7,6},{8,9},{9,8},{10,11... | collective-permute-start | bytes 393224 | tf_op jit(solution)/shard_map/ppermute | solution.py:26
  47.4 2.0 %collective-permute-start.7 = (bf16[256,256]{1,0:T(8,128)(2,1)S(1)}, bf16[256,256]{1,0:T(8,128)(2,1)}, u32[]{:S(2)}, u32[]{:S(2)}) collective-permute-start(bf16[256,256]{1,0:T(8,128)(2,1)S(1)} %multiply_convert_fusion.2.refs_0_), channel_id=1, source_target_pairs={{0,1},{1,0},{2,3},{3,2},{4,5},{5,4},{6,7},{7,6},{8,9},{9,8},{10,11... | collective-permute-start | bytes 393224 | tf_op jit(solution)/shard_map/ppermute | solution.py:26
  49.4 2.5 %collective-permute-start.9 = (bf16[256,256]{1,0:T(8,128)(2,1)}, bf16[256,256]{1,0:T(8,128)(2,1)}, u32[]{:S(2)}, u32[]{:S(2)}) collective-permute-start(bf16[256,256]{1,0:T(8,128)(2,1)} %collective-permute-done.8.refs_2_), channel_id=1, source_target_pairs={{0,1},{1,0},{2,3},{3,2},{4,5},{5,4},{6,7},{7,6},{8,9},{9,8},{10,11... | collective-permute-start | bytes 393224 | tf_op jit(solution)/shard_map/ppermute | solution.py:26
  54.5 2.2 %shard_map.108 = (bf16[256,256]{1,0:T(8,128)(2,1)S(1)}, f32[256,1]{1,0:T(8,128)S(1)}, bf16[256,256]{1,0:T(8,128)(2,1)S(1)}, bf16[256,1024]{1,0:T(8,128)(2,1)S(1)}) custom-call(bf16[256,256]{1,0:T(8,128)(2,1)S(1)} %multiply_convert_fusion.2.refs_0_, bf16[256,256]{1,0:T(8,128)(2,1)S(1)} %multiply_convert_fusion.3.refs_1_.refs_4_, ...), custom_call_target="tpu_custom_call" | custom-call | flops 402653184 | bytes 3277824 | tf_op jit(solution)/shard_map/pallas_call | solution.py:80
  56.6 3.9 %shard_map.109 = (bf16[384,1024]{1,0:T(8,128)(2,1)S(1)}, bf16[384,1024]{1,0:T(8,128)(2,1)}) custom-call(s32[1]{0:T(128)} %bitcast.core_ref.place, bf16[256,256]{1,0:T(8,128)(2,1)S(1)} %multiply_convert_fusion.2.refs_0_, bf16[256,256]{1,0:T(8,128)(2,1)} %collective-permute-done.7.refs_1_, bf16[256,256]{1,0:T(8,128)(2,1)} %collective-permute-done.8.refs_2_, ...), custom_call_target="tpu_custom_call" | custom-call | flops 1207959552 | bytes 6816772 | tf_op jit(solution)/shard_map/pallas_call | solution.py:80
  61.5 2.5 %collective-permute-done.13.arrived = bf16[384,1024]{1,0:T(8,128)(2,1)S(1)} collective-permute-done((bf16[384,1024]{1,0:T(8,128)(2,1)}, bf16[384,1024]{1,0:T(8,128)(2,1)S(1)}, u32[]{:S(2)}, u32[]{:S(2)}) %collective-permute-start.13) | collective-permute-done | bytes 786464 | tf_op jit(solution)/shard_map/ppermute | solution.py:26
  65.3 2.5 %collective-permute-start.16 = (bf16[96,1024]{1,0:T(8,128)(2,1)S(1)}, bf16[96,1024]{1,0:T(8,128)(2,1)S(1)}, u32[]{:S(2)}, u32[]{:S(2)}) collective-permute-start(bf16[96,1024]{1,0:T(8,128)(2,1)S(1)} %get-tuple-element.48), channel_id=1, source_target_pairs={{0,24},{1,25},{2,26},{3,27},{4,28},{5,29},{6,30},{7,31},{8,16},{9,... | collective-permute-start | bytes 589832 | tf_op jit(solution)/shard_map/ppermute | solution.py:26
  68.8 5.2 %collective-permute-done.16 = bf16[96,1024]{1,0:T(8,128)(2,1)S(1)} collective-permute-done((bf16[96,1024]{1,0:T(8,128)(2,1)S(1)}, bf16[96,1024]{1,0:T(8,128)(2,1)S(1)}, u32[]{:S(2)}, u32[]{:S(2)}) %collective-permute-start.16) | collective-permute-done | bytes 196640 | tf_op jit(solution)/shard_map/ppermute | solution.py:26
  74.0 3.4 %collective-permute-done.15 = bf16[96,1024]{1,0:T(8,128)(2,1)S(1)} collective-permute-done((bf16[96,1024]{1,0:T(8,128)(2,1)S(1)}, bf16[96,1024]{1,0:T(8,128)(2,1)S(1)}, u32[]{:S(2)}, u32[]{:S(2)}) %collective-permute-start.15) | collective-permute-done | bytes 196640 | tf_op jit(solution)/shard_map/ppermute | solution.py:26
  77.6 4.3 %collective-permute-start.19 = (bf16[24,1024]{1,0:T(8,128)(2,1)S(1)}, bf16[24,1024]{1,0:T(8,128)(2,1)S(1)}, u32[]{:S(2)}, u32[]{:S(2)}) collective-permute-start(bf16[24,1024]{1,0:T(8,128)(2,1)S(1)} %get-tuple-element.55), channel_id=1, source_target_pairs={{0,3},{1,2},{2,1},{3,0},{4,7},{5,6},{6,5},{7,4},{8,11},{9,10},{10,... | collective-permute-start | bytes 147464 | tf_op jit(solution)/shard_map/ppermute | solution.py:26
  82.5 1.7 %collective-permute-done.19 = bf16[24,1024]{1,0:T(8,128)(2,1)S(1)} collective-permute-done((bf16[24,1024]{1,0:T(8,128)(2,1)S(1)}, bf16[24,1024]{1,0:T(8,128)(2,1)S(1)}, u32[]{:S(2)}, u32[]{:S(2)}) %collective-permute-start.19) | collective-permute-done | bytes 49184 | tf_op jit(solution)/shard_map/ppermute | solution.py:26
  84.3 2.6 %collective-permute-done.18 = bf16[24,1024]{1,0:T(8,128)(2,1)S(1)} collective-permute-done((bf16[24,1024]{1,0:T(8,128)(2,1)S(1)}, bf16[24,1024]{1,0:T(8,128)(2,1)S(1)}, u32[]{:S(2)}, u32[]{:S(2)}) %collective-permute-start.18) | collective-permute-done | bytes 49184 | tf_op jit(solution)/shard_map/ppermute | solution.py:26
  86.9 2.0 %collective-permute-start.20 = (bf16[24,1024]{1,0:T(8,128)(2,1)S(1)}, bf16[24,1024]{1,0:T(8,128)(2,1)S(1)}, u32[]{:S(2)}, u32[]{:S(2)}) collective-permute-start(bf16[24,1024]{1,0:T(8,128)(2,1)S(1)} %add_convert_fusion.1), channel_id=1, source_target_pairs={{0,3},{1,2},{2,1},{3,0},{4,7},{5,6},{6,5},{7,4},{8,11},{9,10},{10,... | collective-permute-start | bytes 147464 | tf_op jit(solution)/shard_map/ppermute | solution.py:26
  89.1 2.2 %collective-permute-start.22 = (bf16[24,1024]{1,0:T(8,128)(2,1)S(1)}, bf16[24,1024]{1,0:T(8,128)(2,1)S(1)}, u32[]{:S(2)}, u32[]{:S(2)}) collective-permute-start(bf16[24,1024]{1,0:T(8,128)(2,1)S(1)} %add_convert_fusion.1), channel_id=1, source_target_pairs={{0,1},{1,0},{2,3},{3,2},{4,5},{5,4},{6,7},{7,6},{8,9},{9,8},{10,11... | collective-permute-start | bytes 147464 | tf_op jit(solution)/shard_map/ppermute | solution.py:26
  91.4 1.6 %collective-permute-done.20 = bf16[24,1024]{1,0:T(8,128)(2,1)S(1)} collective-permute-done((bf16[24,1024]{1,0:T(8,128)(2,1)S(1)}, bf16[24,1024]{1,0:T(8,128)(2,1)S(1)}, u32[]{:S(2)}, u32[]{:S(2)}) %collective-permute-start.20) | collective-permute-done | bytes 49184 | tf_op jit(solution)/shard_map/ppermute | solution.py:26
  93.0 1.4 %collective-permute-done.21 = bf16[24,1024]{1,0:T(8,128)(2,1)S(1)} collective-permute-done((bf16[24,1024]{1,0:T(8,128)(2,1)S(1)}, bf16[24,1024]{1,0:T(8,128)(2,1)S(1)}, u32[]{:S(2)}, u32[]{:S(2)}) %collective-permute-start.21) | collective-permute-done | bytes 49184 | tf_op jit(solution)/shard_map/ppermute | solution.py:26
  95.7 1.8 %collective-permute-start.24 = (bf16[96,1024]{1,0:T(8,128)(2,1)S(1)}, bf16[96,1024]{1,0:T(8,128)(2,1)S(1)}, u32[]{:S(2)}, u32[]{:S(2)}) collective-permute-start(bf16[96,1024]{1,0:T(8,128)(2,1)S(1)} %pad_maximum_fusion.1), channel_id=1, source_target_pairs={{0,16},{1,17},{2,18},{3,19},{4,20},{5,21},{6,22},{7,23},{8,24},{9,... | collective-permute-start | bytes 589832 | tf_op jit(solution)/shard_map/ppermute | solution.py:26
  98.1 3.8 %collective-permute-done.23 = bf16[96,1024]{1,0:T(8,128)(2,1)S(1)} collective-permute-done((bf16[96,1024]{1,0:T(8,128)(2,1)S(1)}, bf16[96,1024]{1,0:T(8,128)(2,1)S(1)}, u32[]{:S(2)}, u32[]{:S(2)}) %collective-permute-start.23) | collective-permute-done | bytes 196640 | tf_op jit(solution)/shard_map/ppermute | solution.py:26
  101.9 2.0 %collective-permute-done.24 = bf16[96,1024]{1,0:T(8,128)(2,1)S(1)} collective-permute-done((bf16[96,1024]{1,0:T(8,128)(2,1)S(1)}, bf16[96,1024]{1,0:T(8,128)(2,1)S(1)}, u32[]{:S(2)}, u32[]{:S(2)}) %collective-permute-start.24) | collective-permute-done | bytes 196640 | tf_op jit(solution)/shard_map/ppermute | solution.py:26
  104.5 2.3 %collective-permute-done.26.other = bf16[384,1024]{1,0:T(8,128)(2,1)S(1)} collective-permute-done((bf16[384,1024]{1,0:T(8,128)(2,1)S(1)}, bf16[384,1024]{1,0:T(8,128)(2,1)S(1)}, u32[]{:S(2)}, u32[]{:S(2)}) %collective-permute-start.26) | collective-permute-done | bytes 786464 | tf_op jit(solution)/shard_map/ppermute | solution.py:26
  106.8 1.8 %shard_map.111 = (f32[256,1024]{1,0:T(8,128)}, f32[256,1024]{1,0:T(8,128)}, f32[1024,256]{1,0:T(8,128)}) custom-call(s32[1]{0:T(128)} %bitcast.core_ref.place, bf16[384,1024]{1,0:T(8,128)(2,1)S(1)} %pad_maximum_fusion.block, bf16[384,1024]{1,0:T(8,128)(2,1)S(1)} %collective-permute-done.26.other), custom_call_target="tpu_custom_call" | custom-call | tf_op jit(solution)/shard_map/pallas_call | solution.py:80
  (86 shorter events, 20.2 us)
Async XLA Ops:
  0.6 32.4 %copy-start = (bf16[256,1024]{1,0:T(8,128)(2,1)S(1)}, bf16[256,1024]{1,0:T(8,128)(2,1)}, u32[]{:S(2)}) copy-start(bf16[256,1024]{1,0:T(8,128)(2,1)} %param.14) | copy-start | bytes 1572868
  0.6 8.6 %copy-start.9 = (s32[4,1024]{1,0:T(4,128)S(1)}, s32[4,1024]{1,0:T(4,128)}, u32[]{:S(2)}) copy-start(s32[4,1024]{1,0:T(4,128)} %param.11) | copy-start | bytes 49156
  3.4 8.5 %collective-permute-start = (s32[1,1024]{1,0:T(1,128)S(1)}, s32[1,1024]{1,0:T(1,128)S(1)}, u32[]{:S(2)}, u32[]{:S(2)}) collective-permute-start(s32[1,1024]{1,0:T(1,128)S(1)} %get-tuple-element.66), channel_id=1, source_target_pairs={{0,3},{1,2},{2,1},{3,0},{4,7},{5,6},{6,5},{7,4},{8,11},{9,10},{10,... | collective-permute-start | bytes 12296 | tf_op jit(solution)/shard_map/ppermute | solution.py:26
  8.6 4.5 %collective-permute-start.1 = (s32[1,1024]{1,0:T(1,128)S(1)}, s32[1,1024]{1,0:T(1,128)S(1)}, u32[]{:S(2)}, u32[]{:S(2)}) collective-permute-start(s32[1,1024]{1,0:T(1,128)S(1)} %get-tuple-element.65), channel_id=1, source_target_pairs={{0,2},{1,3},{2,0},{3,1},{4,6},{5,7},{6,4},{7,5},{8,10},{9,11},{10,... | collective-permute-start | bytes 12296 | tf_op jit(solution)/shard_map/ppermute | solution.py:26
  8.6 4.5 %collective-permute-start.2 = (s32[1,1024]{1,0:T(1,128)S(1)}, s32[1,1024]{1,0:T(1,128)S(1)}, u32[]{:S(2)}, u32[]{:S(2)}) collective-permute-start(s32[1,1024]{1,0:T(1,128)S(1)} %get-tuple-element.64), channel_id=1, source_target_pairs={{0,1},{1,0},{2,3},{3,2},{4,5},{5,4},{6,7},{7,6},{8,9},{9,8},{10,11... | collective-permute-start | bytes 12296 | tf_op jit(solution)/shard_map/ppermute | solution.py:26
  9.2 2.2 %copy-start.2 = (bf16[8192,256]{1,0:T(8,128)(2,1)S(1)}, bf16[8192,256]{1,0:T(8,128)(2,1)}, u32[]{:S(2)}) copy-start(bf16[8192,256]{1,0:T(8,128)(2,1)} %store.1) | copy-start | bytes 12582916
  13.1 2.9 %copy-start.5 = (bf16[512,256]{1,0:T(8,128)(2,1)S(1)}, bf16[512,256]{1,0:T(8,128)(2,1)}, u32[]{:S(2)}) copy-start(bf16[512,256]{1,0:T(8,128)(2,1)} %refs_17_.1) | copy-start | bytes 786436
  13.1 2.9 %copy-start.8 = (bf16[256,1024]{1,0:T(8,128)(2,1)S(1)}, bf16[256,1024]{1,0:T(8,128)(2,1)}, u32[]{:S(2)}) copy-start(bf16[256,1024]{1,0:T(8,128)(2,1)} %param.13) | copy-start | bytes 1572868
  15.5 7.5 %collective-permute-start.4 = (bf16[512,256]{1,0:T(8,128)(2,1)S(1)}, bf16[512,256]{1,0:T(8,128)(2,1)S(1)}, u32[]{:S(2)}, u32[]{:S(2)}) collective-permute-start(bf16[512,256]{1,0:T(8,128)(2,1)S(1)} %shard_map.104), channel_id=1, source_target_pairs={{0,1},{1,0},{2,3},{3,2},{4,5},{5,4},{6,7},{7,6},{8,9},{9,8},{10,11... | collective-permute-start | bytes 786440 | tf_op jit(solution)/shard_map/ppermute | solution.py:26
  21.2 11.7 %collective-permute-start.3 = (bf16[512,256]{1,0:T(8,128)(2,1)S(1)}, bf16[512,256]{1,0:T(8,128)(2,1)S(1)}, u32[]{:S(2)}, u32[]{:S(2)}) collective-permute-start(bf16[512,256]{1,0:T(8,128)(2,1)S(1)} %shard_map.106), channel_id=1, source_target_pairs={{0,1},{1,0},{2,3},{3,2},{4,5},{5,4},{6,7},{7,6},{8,9},{9,8},{10,11... | collective-permute-start | bytes 786440 | tf_op jit(solution)/shard_map/ppermute | solution.py:26
  23.1 9.8 %collective-permute-start.5 = (bf16[256,256]{1,0:T(8,128)(2,1)S(1)}, bf16[256,256]{1,0:T(8,128)(2,1)S(1)}, u32[]{:S(2)}, u32[]{:S(2)}) collective-permute-start(bf16[256,256]{1,0:T(8,128)(2,1)S(1)} %get-tuple-element.58), channel_id=1, source_target_pairs={{0,2},{1,3},{2,0},{3,1},{4,6},{5,7},{6,4},{7,5},{8,10},{9,11},{10,... | collective-permute-start | bytes 393224 | tf_op jit(solution)/shard_map/ppermute | solution.py:26
  27.6 12.4 %collective-permute-start.6 = (bf16[256,256]{1,0:T(8,128)(2,1)S(1)}, bf16[256,256]{1,0:T(8,128)(2,1)S(1)}, u32[]{:S(2)}, u32[]{:S(2)}) collective-permute-start(bf16[256,256]{1,0:T(8,128)(2,1)S(1)} %get-tuple-element.57), channel_id=1, source_target_pairs={{0,2},{1,3},{2,0},{3,1},{4,6},{5,7},{6,4},{7,5},{8,10},{9,11},{10,... | collective-permute-start | bytes 393224 | tf_op jit(solution)/shard_map/ppermute | solution.py:26
  34.9 12.5 %collective-permute-start.11 = (bf16[256,256]{1,0:T(8,128)(2,1)S(1)}, bf16[256,256]{1,0:T(8,128)(2,1)S(1)}, u32[]{:S(2)}, u32[]{:S(2)}) collective-permute-start(bf16[256,256]{1,0:T(8,128)(2,1)S(1)} %multiply_convert_fusion.3.refs_1_.refs_4_), channel_id=1, source_target_pairs={{0,2},{1,3},{2,0},{3,1},{4,6},{5,7},{6,4},{7,5},{8,10},{9,11},{10,... | collective-permute-start | bytes 393224 | tf_op jit(solution)/shard_map/ppermute | solution.py:26
  41.9 7.5 %collective-permute-start.8 = (bf16[256,256]{1,0:T(8,128)(2,1)S(1)}, bf16[256,256]{1,0:T(8,128)(2,1)}, u32[]{:S(2)}, u32[]{:S(2)}) collective-permute-start(bf16[256,256]{1,0:T(8,128)(2,1)S(1)} %multiply_convert_fusion.2.refs_0_), channel_id=1, source_target_pairs={{0,2},{1,3},{2,0},{3,1},{4,6},{5,7},{6,4},{7,5},{8,10},{9,11},{10,... | collective-permute-start | bytes 393224 | tf_op jit(solution)/shard_map/ppermute | solution.py:26
  42.0 9.9 %collective-permute-start.10 = (bf16[256,256]{1,0:T(8,128)(2,1)S(1)}, bf16[256,256]{1,0:T(8,128)(2,1)}, u32[]{:S(2)}, u32[]{:S(2)}) collective-permute-start(bf16[256,256]{1,0:T(8,128)(2,1)S(1)} %multiply_convert_fusion.3.refs_1_.refs_4_), channel_id=1, source_target_pairs={{0,1},{1,0},{2,3},{3,2},{4,5},{5,4},{6,7},{7,6},{8,9},{9,8},{10,11... | collective-permute-start | bytes 393224 | tf_op jit(solution)/shard_map/ppermute | solution.py:26
  47.4 5.8 %collective-permute-start.12 = (bf16[256,256]{1,0:T(8,128)(2,1)S(1)}, bf16[256,256]{1,0:T(8,128)(2,1)}, u32[]{:S(2)}, u32[]{:S(2)}) collective-permute-start(bf16[256,256]{1,0:T(8,128)(2,1)S(1)} %collective-permute-done.11.refs_3_.refs_6_), channel_id=1, source_target_pairs={{0,1},{1,0},{2,3},{3,2},{4,5},{5,4},{6,7},{7,6},{8,9},{9,8},{10,11... | collective-permute-start | bytes 393224 | tf_op jit(solution)/shard_map/ppermute | solution.py:26
  47.4 9.2 %collective-permute-start.7 = (bf16[256,256]{1,0:T(8,128)(2,1)S(1)}, bf16[256,256]{1,0:T(8,128)(2,1)}, u32[]{:S(2)}, u32[]{:S(2)}) collective-permute-start(bf16[256,256]{1,0:T(8,128)(2,1)S(1)} %multiply_convert_fusion.2.refs_0_), channel_id=1, source_target_pairs={{0,1},{1,0},{2,3},{3,2},{4,5},{5,4},{6,7},{7,6},{8,9},{9,8},{10,11... | collective-permute-start | bytes 393224 | tf_op jit(solution)/shard_map/ppermute | solution.py:26
  49.4 7.2 %collective-permute-start.9 = (bf16[256,256]{1,0:T(8,128)(2,1)}, bf16[256,256]{1,0:T(8,128)(2,1)}, u32[]{:S(2)}, u32[]{:S(2)}) collective-permute-start(bf16[256,256]{1,0:T(8,128)(2,1)} %collective-permute-done.8.refs_2_), channel_id=1, source_target_pairs={{0,1},{1,0},{2,3},{3,2},{4,5},{5,4},{6,7},{7,6},{8,9},{9,8},{10,11... | collective-permute-start | bytes 393224 | tf_op jit(solution)/shard_map/ppermute | solution.py:26
  61.5 2.5 %collective-permute-start.13 = (bf16[384,1024]{1,0:T(8,128)(2,1)}, bf16[384,1024]{1,0:T(8,128)(2,1)S(1)}, u32[]{:S(2)}, u32[]{:S(2)}) collective-permute-start(bf16[384,1024]{1,0:T(8,128)(2,1)} %get-tuple-element.44), channel_id=1, source_target_pairs={{0,4},{1,5},{2,6},{3,7},{4,0},{5,1},{6,2},{7,3},{8,12},{9,13},{10,... | collective-permute-start | bytes 2359304 | tf_op jit(solution)/shard_map/ppermute | solution.py:26
  65.3 8.8 %collective-permute-start.16 = (bf16[96,1024]{1,0:T(8,128)(2,1)S(1)}, bf16[96,1024]{1,0:T(8,128)(2,1)S(1)}, u32[]{:S(2)}, u32[]{:S(2)}) collective-permute-start(bf16[96,1024]{1,0:T(8,128)(2,1)S(1)} %get-tuple-element.48), channel_id=1, source_target_pairs={{0,24},{1,25},{2,26},{3,27},{4,28},{5,29},{6,30},{7,31},{8,16},{9,... | collective-permute-start | bytes 589832 | tf_op jit(solution)/shard_map/ppermute | solution.py:26
  67.8 9.6 %collective-permute-start.15 = (bf16[96,1024]{1,0:T(8,128)(2,1)S(1)}, bf16[96,1024]{1,0:T(8,128)(2,1)S(1)}, u32[]{:S(2)}, u32[]{:S(2)}) collective-permute-start(bf16[96,1024]{1,0:T(8,128)(2,1)S(1)} %get-tuple-element.47), channel_id=1, source_target_pairs={{0,16},{1,17},{2,18},{3,19},{4,20},{5,21},{6,22},{7,23},{8,24},{9,... | collective-permute-start | bytes 589832 | tf_op jit(solution)/shard_map/ppermute | solution.py:26
  68.3 9.2 %collective-permute-start.14 = (bf16[96,1024]{1,0:T(8,128)(2,1)S(1)}, bf16[96,1024]{1,0:T(8,128)(2,1)S(1)}, u32[]{:S(2)}, u32[]{:S(2)}) collective-permute-start(bf16[96,1024]{1,0:T(8,128)(2,1)S(1)} %get-tuple-element.46), channel_id=1, source_target_pairs={{0,8},{1,9},{2,10},{3,11},{4,12},{5,13},{6,14},{7,15},{8,0},{9,1},... | collective-permute-start | bytes 589832 | tf_op jit(solution)/shard_map/ppermute | solution.py:26
  77.6 6.7 %collective-permute-start.19 = (bf16[24,1024]{1,0:T(8,128)(2,1)S(1)}, bf16[24,1024]{1,0:T(8,128)(2,1)S(1)}, u32[]{:S(2)}, u32[]{:S(2)}) collective-permute-start(bf16[24,1024]{1,0:T(8,128)(2,1)S(1)} %get-tuple-element.55), channel_id=1, source_target_pairs={{0,3},{1,2},{2,1},{3,0},{4,7},{5,6},{6,5},{7,4},{8,11},{9,10},{10,... | collective-permute-start | bytes 147464 | tf_op jit(solution)/shard_map/ppermute | solution.py:26
  81.9 5.0 %collective-permute-start.18 = (bf16[24,1024]{1,0:T(8,128)(2,1)S(1)}, bf16[24,1024]{1,0:T(8,128)(2,1)S(1)}, u32[]{:S(2)}, u32[]{:S(2)}) collective-permute-start(bf16[24,1024]{1,0:T(8,128)(2,1)S(1)} %get-tuple-element.56), channel_id=1, source_target_pairs={{0,2},{1,3},{2,0},{3,1},{4,6},{5,7},{6,4},{7,5},{8,10},{9,11},{10,... | collective-permute-start | bytes 147464 | tf_op jit(solution)/shard_map/ppermute | solution.py:26
  81.9 5.0 %collective-permute-start.17 = (bf16[24,1024]{1,0:T(8,128)(2,1)S(1)}, bf16[24,1024]{1,0:T(8,128)(2,1)S(1)}, u32[]{:S(2)}, u32[]{:S(2)}) collective-permute-start(bf16[24,1024]{1,0:T(8,128)(2,1)S(1)} %get-tuple-element.54), channel_id=1, source_target_pairs={{0,1},{1,0},{2,3},{3,2},{4,5},{5,4},{6,7},{7,6},{8,9},{9,8},{10,11... | collective-permute-start | bytes 147464 | tf_op jit(solution)/shard_map/ppermute | solution.py:26
  86.9 6.1 %collective-permute-start.20 = (bf16[24,1024]{1,0:T(8,128)(2,1)S(1)}, bf16[24,1024]{1,0:T(8,128)(2,1)S(1)}, u32[]{:S(2)}, u32[]{:S(2)}) collective-permute-start(bf16[24,1024]{1,0:T(8,128)(2,1)S(1)} %add_convert_fusion.1), channel_id=1, source_target_pairs={{0,3},{1,2},{2,1},{3,0},{4,7},{5,6},{6,5},{7,4},{8,11},{9,10},{10,... | collective-permute-start | bytes 147464 | tf_op jit(solution)/shard_map/ppermute | solution.py:26
  88.9 5.5 %collective-permute-start.21 = (bf16[24,1024]{1,0:T(8,128)(2,1)S(1)}, bf16[24,1024]{1,0:T(8,128)(2,1)S(1)}, u32[]{:S(2)}, u32[]{:S(2)}) collective-permute-start(bf16[24,1024]{1,0:T(8,128)(2,1)S(1)} %add_convert_fusion.1), channel_id=1, source_target_pairs={{0,2},{1,3},{2,0},{3,1},{4,6},{5,7},{6,4},{7,5},{8,10},{9,11},{10,... | collective-permute-start | bytes 147464 | tf_op jit(solution)/shard_map/ppermute | solution.py:26
  89.1 5.3 %collective-permute-start.22 = (bf16[24,1024]{1,0:T(8,128)(2,1)S(1)}, bf16[24,1024]{1,0:T(8,128)(2,1)S(1)}, u32[]{:S(2)}, u32[]{:S(2)}) collective-permute-start(bf16[24,1024]{1,0:T(8,128)(2,1)S(1)} %add_convert_fusion.1), channel_id=1, source_target_pairs={{0,1},{1,0},{2,3},{3,2},{4,5},{5,4},{6,7},{7,6},{8,9},{9,8},{10,11... | collective-permute-start | bytes 147464 | tf_op jit(solution)/shard_map/ppermute | solution.py:26
  94.5 7.4 %collective-permute-start.23 = (bf16[96,1024]{1,0:T(8,128)(2,1)S(1)}, bf16[96,1024]{1,0:T(8,128)(2,1)S(1)}, u32[]{:S(2)}, u32[]{:S(2)}) collective-permute-start(bf16[96,1024]{1,0:T(8,128)(2,1)S(1)} %pad_maximum_fusion.1), channel_id=1, source_target_pairs={{0,24},{1,25},{2,26},{3,27},{4,28},{5,29},{6,30},{7,31},{8,16},{9,... | collective-permute-start | bytes 589832 | tf_op jit(solution)/shard_map/ppermute | solution.py:26
  95.7 8.1 %collective-permute-start.24 = (bf16[96,1024]{1,0:T(8,128)(2,1)S(1)}, bf16[96,1024]{1,0:T(8,128)(2,1)S(1)}, u32[]{:S(2)}, u32[]{:S(2)}) collective-permute-start(bf16[96,1024]{1,0:T(8,128)(2,1)S(1)} %pad_maximum_fusion.1), channel_id=1, source_target_pairs={{0,16},{1,17},{2,18},{3,19},{4,20},{5,21},{6,22},{7,23},{8,24},{9,... | collective-permute-start | bytes 589832 | tf_op jit(solution)/shard_map/ppermute | solution.py:26
  97.5 6.5 %collective-permute-start.25 = (bf16[96,1024]{1,0:T(8,128)(2,1)S(1)}, bf16[96,1024]{1,0:T(8,128)(2,1)S(1)}, u32[]{:S(2)}, u32[]{:S(2)}) collective-permute-start(bf16[96,1024]{1,0:T(8,128)(2,1)S(1)} %pad_maximum_fusion.1), channel_id=1, source_target_pairs={{0,8},{1,9},{2,10},{3,11},{4,12},{5,13},{6,14},{7,15},{8,0},{9,1},... | collective-permute-start | bytes 589832 | tf_op jit(solution)/shard_map/ppermute | solution.py:26
  104.4 2.4 %collective-permute-start.26 = (bf16[384,1024]{1,0:T(8,128)(2,1)S(1)}, bf16[384,1024]{1,0:T(8,128)(2,1)S(1)}, u32[]{:S(2)}, u32[]{:S(2)}) collective-permute-start(bf16[384,1024]{1,0:T(8,128)(2,1)S(1)} %pad_maximum_fusion.block), channel_id=1, source_target_pairs={{0,4},{1,5},{2,6},{3,7},{4,0},{5,1},{6,2},{7,3},{8,12},{9,13},{10,... | collective-permute-start | bytes 2359304 | tf_op jit(solution)/shard_map/ppermute | solution.py:26
  (5 other events, 6.8 us)
